TPU v7x, 32 devices: a whole 2x2x4 slice. The times are simulated.
32 devices in a mesh: space: 8 (over y, x, core), filt: 4 (over z).
Axes of the slice: x: 2, y: 2, z: 4, core: 2. Of those that a mesh axis runs over, the one named last changes fastest.
Arguments:
- image: bfloat16 [96, 32, 1024], P(None, 'space', 'filt'), may hold values from -6 to 6
- cotangent: bfloat16 [96, 32, 1024], P(None, 'space', 'filt'), may hold values from -6 to 6
- kernel: float32 [96, 7, 7], replicated, may hold values from -0.875 to 0.875
- dw_bias: float32 [96], replicated, may hold values from -0.5 to 0.5
- layer_norm_gain: float32 [96], replicated, may hold values from 0.5 to 1.5
- layer_norm_bias: float32 [96], replicated, may hold values from -3 to 3
- w_expand: bfloat16 [384, 96], replicated, may hold values from -0.625 to 0.625
- b_expand: bfloat16 [384], replicated, may hold values from -3 to 3
- w_reduce: bfloat16 [384, 96], replicated, may hold values from -0.3125 to 0.3125
- b_reduce: float32 [96], replicated, may hold values from -3 to 3
- layer_scale: float32 [96], replicated, may hold values from 0.2 to 1
Outputs:
- output: bfloat16 [96, 32, 1024], P(None, 'space', 'filt')
- image_grad: bfloat16 [96, 32, 1024], P(None, 'space', 'filt')
- kernel_grad: float32 [96, 7, 7], replicated
- dw_bias_grad: float32 [96], replicated
- gain_grad: float32 [96], replicated
- ln_bias_grad: float32 [96], replicated
- expand_grad: float32 [384, 96], P('filt')
- expand_bias_grad: float32 [384], P('filt')
- reduce_grad: float32 [384, 96], P('filt')
- reduce_bias_grad: float32 [96], replicated
- scale_grad: float32 [96], replicated
All inputs are finite; a program needn't handle non-finite values.
Results may differ from a plain program's by a relative error of at most 0.011.
Values may be sent and summed in bfloat16 or wider, within the bound.
No kernel may reach another device: no remote copies, remote signals or barrier semaphores. Data moves between devices by JAX's collectives and lax.ppermute only.
A program may use at most 64 MiB of HBM per device.

v0:
```python
import math

import jax
import jax.numpy as jnp
from jax import lax
from jax.sharding import PartitionSpec as P


def padded_2(x, sides, width):
    for axis, dim in sides:
        size, length = (lax.axis_size(axis), x.shape[dim])
        up = [(i, (i + 1) % size) for i in range(size - 1)]
        down = [(j, i) for i, j in up]
        last = lax.slice_in_dim(x, length - width, length, axis=dim)
        initial = lax.slice_in_dim(x, 0, width, axis=dim)
        before = lax.ppermute(last, axis, up)
        after = lax.ppermute(initial, axis, down)
        x = jnp.concatenate([before, x, after], axis=dim)
    return x


def depthwise(padded, kernel, row_count, col_count):
    total = jnp.zeros((padded.shape[0], row_count, col_count), jnp.float32)
    for shift_row in range(7):
        for shift_col in range(7):
            piece = padded[
                :, shift_row : shift_row + row_count, shift_col : shift_col + col_count
            ].astype(jnp.float32)
            total = total + kernel[:, shift_row, shift_col][:, None, None] * piece
    return total


def conv_back(padded, kernel, row_count, col_count):
    total = jnp.zeros((padded.shape[0], row_count, col_count), jnp.float32)
    for shift_row in range(7):
        for shift_col in range(7):
            piece = padded[
                :,
                6 - shift_row : 6 - shift_row + row_count,
                6 - shift_col : 6 - shift_col + col_count,
            ].astype(jnp.float32)
            total = total + kernel[:, shift_row, shift_col][:, None, None] * piece
    return total


def kernel_terms(padded, convolution_gradient, row_count, col_count):
    lines = []
    for shift_row in range(7):
        entries = []
        for shift_col in range(7):
            piece = padded[
                :, shift_row : shift_row + row_count, shift_col : shift_col + col_count
            ].astype(jnp.float32)
            entries.append(jnp.sum(piece * convolution_gradient, axis=(1, 2)))
        lines.append(jnp.stack(entries, axis=1))
    return jnp.stack(lines, axis=1)


def gelu_exact(value):
    return value * (1.0 + jax.scipy.special.erf(value / math.sqrt(2.0))) * 0.5


def gelu_slope(value):
    return (1.0 + jax.scipy.special.erf(value / math.sqrt(2.0))) * 0.5 + value * jnp.exp(
        -0.5 * value * value
    ) / math.sqrt(2.0 * math.pi)


def shards(
    image,
    cotangent,
    kernel,
    dw_bias,
    layer_norm_gain,
    layer_norm_bias,
    w_expand,
    b_expand,
    w_reduce,
    b_reduce,
    layer_scale,
):
    channels, row_count, col_count = image.shape
    panel_rows = w_expand.shape[0] // lax.axis_size("filt")
    tok_count = row_count * col_count
    padded = padded_2(image, (("space", 1), ("filt", 2)), 3)
    conv = depthwise(padded, kernel, row_count, col_count)
    conv = conv + dw_bias[:, None, None]
    flat = conv.reshape(channels, tok_count)
    average = jnp.mean(flat, axis=0, keepdims=True)
    mean_removed = flat - average
    inverse_deviation = lax.rsqrt(
        jnp.mean(mean_removed * mean_removed, axis=0, keepdims=True) + 1e-06
    )
    standardized_input = mean_removed * inverse_deviation
    normalized_input = (
        standardized_input * layer_norm_gain[:, None] + layer_norm_bias[:, None]
    ).astype(jnp.bfloat16)
    hidden = (
        jnp.dot(w_expand, normalized_input, preferred_element_type=jnp.float32)
        + b_expand.astype(jnp.float32)[:, None]
    )
    active = gelu_exact(hidden).astype(jnp.bfloat16)
    branch = (
        lax.dot_general(
            w_reduce, active, (((0,), (0,)), ((), ())), preferred_element_type=jnp.float32
        )
        + b_reduce[:, None]
    )
    resid = image.reshape(channels, tok_count).astype(jnp.float32)
    output = (
        (resid + layer_scale[:, None] * branch)
        .astype(jnp.bfloat16)
        .reshape(channels, row_count, col_count)
    )
    cot_flat = cotangent.reshape(channels, tok_count).astype(jnp.float32)
    scaled = layer_scale[:, None] * cot_flat
    g_scale = jnp.sum(cot_flat * branch, axis=1)
    g_rbias = jnp.sum(scaled, axis=1)
    d_branch = scaled.astype(jnp.bfloat16)
    g_reduce = lax.dot_general(
        active, d_branch, (((1,), (1,)), ((), ())), preferred_element_type=jnp.float32
    )
    d_active = jnp.dot(w_reduce, d_branch, preferred_element_type=jnp.float32)
    d_hidden = (d_active * gelu_slope(hidden)).astype(jnp.bfloat16)
    g_ebias = jnp.sum(d_hidden.astype(jnp.float32), axis=1)
    g_expand = lax.dot_general(
        d_hidden, normalized_input, (((1,), (1,)), ((), ())), preferred_element_type=jnp.float32
    )
    normalized_gradient = lax.dot_general(
        w_expand, d_hidden, (((0,), (0,)), ((), ())), preferred_element_type=jnp.float32
    )
    norm_gain_gradient = jnp.sum(normalized_gradient * standardized_input, axis=1)
    g_lbias = jnp.sum(normalized_gradient, axis=1)
    standardized_gradient = normalized_gradient * layer_norm_gain[:, None]
    convolution_gradient = inverse_deviation * (
        standardized_gradient
        - jnp.mean(standardized_gradient, axis=0, keepdims=True)
        - standardized_input
        * jnp.mean(standardized_gradient * standardized_input, axis=0, keepdims=True)
    )
    convolution_gradient = convolution_gradient.astype(jnp.bfloat16).reshape(
        channels, row_count, col_count
    )
    d_float = convolution_gradient.astype(jnp.float32)
    g_dbias = jnp.sum(d_float, axis=(1, 2))
    padded_grad = padded_2(convolution_gradient, (("space", 1), ("filt", 2)), 3)
    back = conv_back(padded_grad, kernel, row_count, col_count)
    image_grad = (cotangent.astype(jnp.float32) + back).astype(jnp.bfloat16)
    g_kernel = kernel_terms(padded, d_float, row_count, col_count)
    factor = 1.0 / math.sqrt(tok_count * lax.axis_size("space") * lax.axis_size("filt"))
    (
        g_reduce,
        g_expand,
        g_ebias,
        g_kernel,
        g_dbias,
        norm_gain_gradient,
        g_lbias,
        g_scale,
        g_rbias,
    ) = lax.psum(
        (
            g_reduce,
            g_expand,
            g_ebias,
            g_kernel,
            g_dbias,
            norm_gain_gradient,
            g_lbias,
            g_scale,
            g_rbias,
        ),
        ("space", "filt"),
    )
    start = lax.axis_index("filt") * panel_rows
    g_reduce = lax.dynamic_slice_in_dim(g_reduce, start, panel_rows, 0)
    g_expand = lax.dynamic_slice_in_dim(g_expand, start, panel_rows, 0)
    g_ebias = lax.dynamic_slice_in_dim(g_ebias, start, panel_rows, 0)
    return (
        output,
        image_grad,
        g_kernel * factor,
        g_dbias * factor,
        norm_gain_gradient * factor,
        g_lbias * factor,
        g_expand * factor,
        g_ebias * factor,
        g_reduce * factor,
        g_rbias * factor,
        g_scale * factor,
    )


def solution(mesh):
    in_specs = (
        P(None, "space", "filt"),
        P(None, "space", "filt"),
        P(),
        P(),
        P(),
        P(),
        P(),
        P(),
        P(),
        P(),
        P(),
    )
    out_specs = (
        P(None, "space", "filt"),
        P(None, "space", "filt"),
        P(),
        P(),
        P(),
        P(),
        P("filt", None),
        P("filt"),
        P("filt", None),
        P(),
        P(),
    )
    return jax.shard_map(shards, mesh=mesh, in_specs=in_specs, out_specs=out_specs, check_vma=False)
```

profile of v0, /device:TPU:0, one launch (start us, length us, event | category | flops | bytes accessed | tf_op | source)
XLA Modules:
  0.0 299.4 jit_solution(2297312889227222972)
XLA Ops:
  7.2 0.0 copy-start
  7.2 0.0 all-reduce.4.cloned.1.call-start
  7.2 1.2 fusion.139
  8.5 2.5 collective-permute-start
  11.0 1.3 collective-permute-start.1
  12.3 1.0 slice_bitcast_fusion.48
  13.3 1.6 slice_bitcast_fusion.47
  15.0 1.5 slice_bitcast_fusion.46
  16.6 1.6 pad_maximum_fusion.2
  18.2 0.2 fusion.137
  18.4 4.3 %collective-permute-start.2 = (bf16[96,10,3]{2,1,0:T(8,128)(2,1)S(1)}, bf16[96,10,3]{2,1,0:T(8,128)(2,1)S(1)}, u32[]{:S(2)}, u32[]{:S(2)}) collective-permute-start(bf16[96,10,3]{2,1,0:T(8,128)(2,1)S(1)} %get-tuple-element.88), channel_id=1, source_target_pairs={{0,1},{1,2},{2,3},{4,5},{5,6},{6,7},{8,9},{9,10},{10,11},{12,13},{... | collective-permute-start | bytes 17288 | tf_op jit(solution)/shard_map/ppermute | solution.py:16
  22.7 1.3 collective-permute-start.3
  24.0 2.0 multiply_reduce_fusion.1
  26.1 0.9 copy.22
  27.1 2.9 collective-permute-done.2
  30.0 0.7 copy-done.10
  30.7 4.1 %collective-permute-done.3 = bf16[96,10,3]{2,1,0:T(8,128)(2,1)} collective-permute-done((bf16[96,10,3]{2,1,0:T(8,128)(2,1)S(1)}, bf16[96,10,3]{2,1,0:T(8,128)(2,1)}, u32[]{:S(2)}, u32[]{:S(2)}) %collective-permute-start.3) | collective-permute-done | bytes 5792 | tf_op jit(solution)/shard_map/ppermute | solution.py:17
  34.8 3.4 %maximum_maximum_fusion = (bf16[96,10,259]{2,1,0:T(8,128)(2,1)S(1)}, bf16[96,10,259]{2,1,0:T(8,128)(2,1)S(1)}) fusion(bf16[96,3,256]{2,1,0:T(4,128)(2,1)S(1)} %collective-permute-done.1, bf16[96,4,256]{2,1,0:T(4,128)(2,1)S(1)} %copy-done.1, bf16[96,3,256]{2,1,0:T(4,128)(2,1)S(1)} %collective-permute-done, bf16[96,10,3]{2,1,0:T(8,128)(2,1)} %copy-done.10, ...), kind=kLoop, calls=%fused_computation.67 | loop fusion | flops 3978240 | bytes 1497600 | tf_op jit(solution)/shard_map/concatenate | solution.py:18
  38.6 0.0 copy-start.14
  38.6 11.5 %fusion.134 = (f32[4,256]{1,0:T(4,128)S(1)}, f32[96,4,256]{2,1,0:T(4,128)S(1)}) fusion(f32[96]{0:T(128)S(1)} %copy-done.92, bf16[96,10,259]{2,1,0:T(8,128)(2,1)S(1)} %get-tuple-element.93, f32[96]{0:T(128)S(1)} %copy-done.82, f32[96]{0:T(128)S(1)} %copy-done.84, f32[96]{0:T(128)S(1)} %get-tuple-element.101, ...), kind=kLoop, calls=%fused_computation.346 | loop fusion | flops 16317440 | bytes 9165568 | tf_op jit(solution)/shard_map/reduce_sum | solution.py:89
  50.2 0.2 multiply_reduce_fusion.3
  50.3 0.1 copy.23
  50.5 1.5 fusion.9
  52.0 1.5 convert_reduce_fusion
  53.5 1.1 fusion.133
  54.6 1.0 fusion.120
  55.6 1.4 convert_reduce_fusion.1
  57.1 1.1 reshape.89
  58.1 7.8 %fusion.115 = (f32[96]{0:T(128)}, f32[96]{0:T(128)}, f32[96]{0:T(128)}, f32[96]{0:T(128)}, f32[96]{0:T(128)}, /*index=5*/f32[96]{0:T(128)}, f32[96]{0:T(128)}, f...) fusion(bf16[96,4,256]{2,1,0:T(4,128)(2,1)S(1)} %reshape.89, ...), kind=kLoop, calls=%fused_computation.241 | loop fusion | flops 5404992 | bytes 3742464 | tf_op jit(solution)/shard_map/reduce_sum | solution.py:54
  65.9 9.8 %fusion.119 = (f32[96]{0:T(128)}, f32[96]{0:T(128)}, f32[96]{0:T(128)}, f32[96]{0:T(128)}, f32[96]{0:T(128)}, /*index=5*/f32[96]{0:T(128)}, f32[96]{0:T(128)}, f...) fusion(bf16[96,4,256]{2,1,0:T(4,128)(2,1)S(1)} %reshape.89, ...), kind=kLoop, calls=%fused_computation.245 | loop fusion | flops 5404992 | bytes 3742464 | tf_op jit(solution)/shard_map/reduce_sum | solution.py:54
  75.7 2.8 fusion.73
  78.6 0.9 fusion.138
  79.4 1.1 fusion.132
  80.6 5.9 %fusion.118 = (f32[96]{0:T(128)}, f32[96]{0:T(128)}, f32[96]{0:T(128)}, f32[96]{0:T(128)}, f32[96]{0:T(128)}, /*index=5*/f32[96]{0:T(128)}, f32[96]{0:T(128)}, f32[96]{0:T(128)}, f32[96]{0:T(128)}, f32[96]{0:T(128)}) fusion(bf16[96,4,256]{2,1,0:T(4,128)(2,1)S(1)} %reshape.89, bf16[96,10,259]{2,1,0:T(8,128)(2,1)S(1)} %get-tuple-element.93, ...), kind=kLoop, calls=%fused_computation.244 | loop fusion | flops 4815936 | bytes 1281792 | tf_op jit(solution)/shard_map/reduce_sum | solution.py:54
  86.5 0.8 stack.199
  87.3 0.1 reduce_sum.586
  87.4 0.7 stack.208
  88.1 0.7 stack.217
  88.8 0.7 stack.226
  89.6 0.7 stack.235
  90.3 0.7 stack.244
  91.0 0.7 stack.253
  91.8 1.5 multiply_reduce_fusion
  93.3 43.9 %all-reduce = (f32[96,7,7]{0,2,1:T(8,128)S(1)}, f32[96]{0:T(128)S(1)}, f32[96]{0:T(128)S(1)}, f32[96]{0:T(128)S(1)}, f32[384]{0:T(512)S(1)}, /*index=5*/f32[96]{0:T(128)S(1)}, f32[96]{0:T(128)S(1)}) all-reduce(f32[96,7,7]{0,2,1:T(8,128)S(1)} %constant_dynamic-update-slice_fusion, ...), channel_id=1, replica_groups=mesh['space'=8,'filt'=4] {'space','filt'}, use_global_device_ids=true, to_apply=%region_53.0 | all-reduce | flops 5568 | bytes 44544 | tf_op jit(solution)/shard_map/psum | solution.py:161
  137.2 0.6 broadcast_multiply_fusion
  137.8 0.5 broadcast_multiply_fusion.4
  138.3 0.5 broadcast_multiply_fusion.5
  138.9 0.5 broadcast_multiply_fusion.6
  139.4 0.5 broadcast_multiply_fusion.7
  139.9 1.3 collective-permute-start.4
  141.2 1.3 collective-permute-start.5
  142.5 0.5 broadcast_multiply_fusion.8
  143.0 0.8 reshape.88
  143.8 0.0 all-reduce.4.cloned.1.call-update
  143.8 0.6 dynamic-slice_multiply_fusion.2
  144.4 2.5 collective-permute-done.5
  146.9 0.5 pad_maximum_fusion.3
  147.4 0.2 fusion.136
  147.6 1.3 collective-permute-start.6
  148.9 4.6 %collective-permute-start.7 = (bf16[96,10,3]{2,1,0:T(8,128)(2,1)S(1)}, bf16[96,10,3]{2,1,0:T(8,128)(2,1)S(1)}, u32[]{:S(2)}, u32[]{:S(2)}) collective-permute-start(bf16[96,10,3]{2,1,0:T(8,128)(2,1)S(1)} %get-tuple-element.87), channel_id=1, source_target_pairs={{0,1},{1,2},{2,3},{4,5},{5,6},{6,7},{8,9},{9,10},{10,11},{12,13},{... | collective-permute-start | bytes 17288 | tf_op jit(solution)/shard_map/ppermute | solution.py:16
  153.5 122.9 %all-reduce.4.cloned.1.call-done = (f32[384,96]{1,0:T(8,128)}, f32[384,96]{1,0:T(8,128)}) async-done(((f32[384,96]{1,0:T(8,128)}, f32[384,96]{1,0:T(8,128)}), (f32[384,96]{1,0:T(8,128)}, f32[384,96]{1,0:T(8,128)})) %all-reduce.4.cloned.1.call-update) | async-done | bytes 294928 | tf_op jit(solution)/shard_map/psum | solution.py:161
  276.4 1.5 dynamic-slice_multiply_fusion
  278.2 2.3 pad_maximum_fusion.1
  280.8 11.7 %add_convert_fusion = bf16[96,4,256]{2,1,0:T(4,128)(2,1)} fusion(bf16[96,4,256]{2,1,0:T(4,128)(2,1)S(1)} %reshape.89, bf16[96,3,256]{2,1,0:T(4,128)(2,1)S(1)} %collective-permute-done.4, bf16[96,3,256]{2,1,0:T(4,128)(2,1)S(1)} %collective-permute-done.5, bf16[96,10,259]{2,1,0:T(8,128)(2,1)S(1)} %get-tuple-element.91, ...), kind=kLoop, calls=%fused_computation.252 | loop fusion | flops 16416768 | bytes 9161088 | tf_op jit(solution)/shard_map/convert_element_type | solution.py:148
  (202 shorter events, 0.5 us)
Async XLA Ops:
  7.2 43.3 %copy-start = (bf16[384,96]{0,1:T(8,128)(2,1)S(1)}, bf16[384,96]{0,1:T(8,128)(2,1)}, u32[]{:S(2)}) copy-start(bf16[384,96]{0,1:T(8,128)(2,1)} %param.17) | copy-start | bytes 221188
  7.2 269.2 %all-reduce.4.cloned.1.call-start = ((), (), s32[]{:S(2)}) async-start(), calls=%async_computation | async-start | bytes 786432 | tf_op jit(solution)/shard_map/psum | solution.py:161
  8.4 15.6 %copy-start.8 = (bf16[96,4,256]{2,1,0:T(4,128)(2,1)S(1)}, bf16[96,4,256]{2,1,0:T(4,128)(2,1)}, u32[]{:S(2)}) copy-start(bf16[96,4,256]{2,1,0:T(4,128)(2,1)} %param.12) | copy-start | bytes 589828
  8.4 15.6 %copy-start.15 = (f32[96]{0:T(128)S(1)}, f32[96]{0:T(128)}, u32[]{:S(2)}) copy-start(f32[96]{0:T(128)} %param.21) | copy-start | bytes 1156
  8.5 8.1 %collective-permute-start = (bf16[96,3,256]{2,1,0:T(4,128)(2,1)S(1)}, bf16[96,3,256]{2,1,0:T(4,128)(2,1)S(1)}, u32[]{:S(2)}, u32[]{:S(2)}) collective-permute-start(bf16[96,3,256]{2,1,0:T(4,128)(2,1)S(1)} %get-tuple-element.98), channel_id=1, source_target_pairs={{0,4},{4,8},{8,12},{12,16},{16,20},{20,24},{24,28},{1,5},{5,9},{9,... | collective-permute-start | bytes 442376 | tf_op jit(solution)/shard_map/ppermute | solution.py:16
  11.0 5.6 %collective-permute-start.1 = (bf16[96,3,256]{2,1,0:T(4,128)(2,1)S(1)}, bf16[96,3,256]{2,1,0:T(4,128)(2,1)S(1)}, u32[]{:S(2)}, u32[]{:S(2)}) collective-permute-start(bf16[96,3,256]{2,1,0:T(4,128)(2,1)S(1)} %get-tuple-element.99), channel_id=1, source_target_pairs={{4,0},{8,4},{12,8},{16,12},{20,16},{24,20},{28,24},{5,1},{9,5},{13... | collective-permute-start | bytes 442376 | tf_op jit(solution)/shard_map/ppermute | solution.py:17
  13.2 25.0 %copy-start.16 = (f32[96]{0:T(128)}, f32[96]{0:T(128)S(1)}, u32[]{:S(2)}) copy-start(f32[96]{0:T(128)S(1)} %get-tuple-element.114) | copy-start | bytes 1156
  13.3 25.0 %copy-start.18 = (f32[96]{0:T(128)}, f32[96]{0:T(128)S(1)}, u32[]{:S(2)}) copy-start(f32[96]{0:T(128)S(1)} %get-tuple-element.115) | copy-start | bytes 1156
  13.3 25.0 %copy-start.20 = (f32[96]{0:T(128)}, f32[96]{0:T(128)S(1)}, u32[]{:S(2)}) copy-start(f32[96]{0:T(128)S(1)} %get-tuple-element.116) | copy-start | bytes 1156
  13.3 25.0 %copy-start.22 = (f32[96]{0:T(128)}, f32[96]{0:T(128)S(1)}, u32[]{:S(2)}) copy-start(f32[96]{0:T(128)S(1)} %get-tuple-element.117) | copy-start | bytes 1156
  13.3 25.0 %copy-start.24 = (f32[96]{0:T(128)}, f32[96]{0:T(128)S(1)}, u32[]{:S(2)}) copy-start(f32[96]{0:T(128)S(1)} %get-tuple-element.118) | copy-start | bytes 1156
  14.9 23.4 %copy-start.26 = (f32[96]{0:T(128)}, f32[96]{0:T(128)S(1)}, u32[]{:S(2)}) copy-start(f32[96]{0:T(128)S(1)} %get-tuple-element.119) | copy-start | bytes 1156
  14.9 23.4 %copy-start.28 = (f32[96]{0:T(128)}, f32[96]{0:T(128)S(1)}, u32[]{:S(2)}) copy-start(f32[96]{0:T(128)S(1)} %get-tuple-element.120) | copy-start | bytes 1156
  14.9 23.4 %copy-start.30 = (f32[96]{0:T(128)}, f32[96]{0:T(128)S(1)}, u32[]{:S(2)}) copy-start(f32[96]{0:T(128)S(1)} %get-tuple-element.121) | copy-start | bytes 1156
  14.9 23.4 %copy-start.32 = (f32[96]{0:T(128)}, f32[96]{0:T(128)S(1)}, u32[]{:S(2)}) copy-start(f32[96]{0:T(128)S(1)} %get-tuple-element.122) | copy-start | bytes 1156
  14.9 23.4 %copy-start.34 = (f32[96]{0:T(128)}, f32[96]{0:T(128)S(1)}, u32[]{:S(2)}) copy-start(f32[96]{0:T(128)S(1)} %get-tuple-element.123) | copy-start | bytes 1156
  14.9 23.4 %copy-start.36 = (f32[96]{0:T(128)}, f32[96]{0:T(128)S(1)}, u32[]{:S(2)}) copy-start(f32[96]{0:T(128)S(1)} %get-tuple-element.124) | copy-start | bytes 1156
  15.0 23.4 %copy-start.38 = (f32[96]{0:T(128)}, f32[96]{0:T(128)S(1)}, u32[]{:S(2)}) copy-start(f32[96]{0:T(128)S(1)} %get-tuple-element.125) | copy-start | bytes 1156
  15.0 23.4 %copy-start.40 = (f32[96]{0:T(128)}, f32[96]{0:T(128)S(1)}, u32[]{:S(2)}) copy-start(f32[96]{0:T(128)S(1)} %get-tuple-element.126) | copy-start | bytes 1156
  15.0 23.4 %copy-start.42 = (f32[96]{0:T(128)}, f32[96]{0:T(128)S(1)}, u32[]{:S(2)}) copy-start(f32[96]{0:T(128)S(1)} %get-tuple-element.127) | copy-start | bytes 1156
  15.0 23.4 %copy-start.44 = (f32[96]{0:T(128)}, f32[96]{0:T(128)S(1)}, u32[]{:S(2)}) copy-start(f32[96]{0:T(128)S(1)} %get-tuple-element.128) | copy-start | bytes 1156
  15.0 23.4 %copy-start.46 = (f32[96]{0:T(128)}, f32[96]{0:T(128)S(1)}, u32[]{:S(2)}) copy-start(f32[96]{0:T(128)S(1)} %get-tuple-element.129) | copy-start | bytes 1156
  15.0 23.4 %copy-start.48 = (f32[96]{0:T(128)}, f32[96]{0:T(128)S(1)}, u32[]{:S(2)}) copy-start(f32[96]{0:T(128)S(1)} %get-tuple-element.130) | copy-start | bytes 1156
  15.0 23.4 %copy-start.50 = (f32[96]{0:T(128)}, f32[96]{0:T(128)S(1)}, u32[]{:S(2)}) copy-start(f32[96]{0:T(128)S(1)} %get-tuple-element.131) | copy-start | bytes 1156
  16.5 9.5 %copy-start.91 = (bf16[384]{0:T(512)(128)(2,1)S(1)}, bf16[384]{0:T(512)(128)(2,1)}, u32[]{:S(2)}) copy-start(bf16[384]{0:T(512)(128)(2,1)} %param.18) | copy-start | bytes 2308
  16.5 9.5 %copy-start.1 = (bf16[96,4,256]{2,1,0:T(4,128)(2,1)S(1)}, bf16[96,4,256]{2,1,0:T(4,128)(2,1)}, u32[]{:S(2)}) copy-start(bf16[96,4,256]{2,1,0:T(4,128)(2,1)} %param.11) | copy-start | bytes 589828
  16.6 21.8 %copy-start.7 = (bf16[96,3,256]{2,1,0:T(4,128)(2,1)}, bf16[96,3,256]{2,1,0:T(4,128)(2,1)S(1)}, u32[]{:S(2)}) copy-start(bf16[96,3,256]{2,1,0:T(4,128)(2,1)S(1)} %collective-permute-done.1) | copy-start | bytes 442372
  18.4 11.6 %collective-permute-start.2 = (bf16[96,10,3]{2,1,0:T(8,128)(2,1)S(1)}, bf16[96,10,3]{2,1,0:T(8,128)(2,1)S(1)}, u32[]{:S(2)}, u32[]{:S(2)}) collective-permute-start(bf16[96,10,3]{2,1,0:T(8,128)(2,1)S(1)} %get-tuple-element.88), channel_id=1, source_target_pairs={{0,1},{1,2},{2,3},{4,5},{5,6},{6,7},{8,9},{9,10},{10,11},{12,13},{... | collective-permute-start | bytes 17288 | tf_op jit(solution)/shard_map/ppermute | solution.py:16
  22.7 12.1 %collective-permute-start.3 = (bf16[96,10,3]{2,1,0:T(8,128)(2,1)S(1)}, bf16[96,10,3]{2,1,0:T(8,128)(2,1)}, u32[]{:S(2)}, u32[]{:S(2)}) collective-permute-start(bf16[96,10,3]{2,1,0:T(8,128)(2,1)S(1)} %get-tuple-element.89), channel_id=1, source_target_pairs={{1,0},{2,1},{3,2},{5,4},{6,5},{7,6},{9,8},{10,9},{11,10},{13,12},{... | collective-permute-start | bytes 17288 | tf_op jit(solution)/shard_map/ppermute | solution.py:17
  26.1 25.9 %copy-start.4 = (f32[12,8,4,256]{3,1,2,0:T(8,128)}, f32[12,8,4,256]{3,1,2,0:T(8,128)S(1)}, u32[]{:S(2)}) copy-start(f32[12,8,4,256]{3,1,2,0:T(8,128)S(1)} %copy.26) | copy-start | bytes 1179652
  27.0 11.4 %copy-start.52 = (f32[96]{0:T(128)S(1)}, f32[96]{0:T(128)}, u32[]{:S(2)}) copy-start(f32[96]{0:T(128)} %get-tuple-element.132) | copy-start | bytes 1156
  27.0 11.4 %copy-start.54 = (f32[96]{0:T(128)S(1)}, f32[96]{0:T(128)}, u32[]{:S(2)}) copy-start(f32[96]{0:T(128)} %get-tuple-element.133) | copy-start | bytes 1156
  27.0 11.5 %copy-start.56 = (f32[96]{0:T(128)S(1)}, f32[96]{0:T(128)}, u32[]{:S(2)}) copy-start(f32[96]{0:T(128)} %get-tuple-element.134) | copy-start | bytes 1156
  27.0 11.5 %copy-start.58 = (f32[96]{0:T(128)S(1)}, f32[96]{0:T(128)}, u32[]{:S(2)}) copy-start(f32[96]{0:T(128)} %get-tuple-element.135) | copy-start | bytes 1156
  27.0 11.5 %copy-start.60 = (f32[96]{0:T(128)S(1)}, f32[96]{0:T(128)}, u32[]{:S(2)}) copy-start(f32[96]{0:T(128)} %get-tuple-element.136) | copy-start | bytes 1156
  27.0 11.5 %copy-start.62 = (f32[96]{0:T(128)S(1)}, f32[96]{0:T(128)}, u32[]{:S(2)}) copy-start(f32[96]{0:T(128)} %get-tuple-element.137) | copy-start | bytes 1156
  27.0 11.5 %copy-start.64 = (f32[96]{0:T(128)S(1)}, f32[96]{0:T(128)}, u32[]{:S(2)}) copy-start(f32[96]{0:T(128)} %get-tuple-element.138) | copy-start | bytes 1156
  27.0 11.5 %copy-start.66 = (f32[96]{0:T(128)S(1)}, f32[96]{0:T(128)}, u32[]{:S(2)}) copy-start(f32[96]{0:T(128)} %get-tuple-element.139) | copy-start | bytes 1156
  27.0 11.5 %copy-start.68 = (f32[96]{0:T(128)S(1)}, f32[96]{0:T(128)}, u32[]{:S(2)}) copy-start(f32[96]{0:T(128)} %get-tuple-element.140) | copy-start | bytes 1156
  27.0 11.5 %copy-start.70 = (f32[96]{0:T(128)S(1)}, f32[96]{0:T(128)}, u32[]{:S(2)}) copy-start(f32[96]{0:T(128)} %get-tuple-element.141) | copy-start | bytes 1156
  27.0 11.5 %copy-start.72 = (f32[96]{0:T(128)S(1)}, f32[96]{0:T(128)}, u32[]{:S(2)}) copy-start(f32[96]{0:T(128)} %get-tuple-element.142) | copy-start | bytes 1156
  27.0 11.5 %copy-start.74 = (f32[96]{0:T(128)S(1)}, f32[96]{0:T(128)}, u32[]{:S(2)}) copy-start(f32[96]{0:T(128)} %get-tuple-element.143) | copy-start | bytes 1156
  27.0 11.5 %copy-start.76 = (f32[96]{0:T(128)S(1)}, f32[96]{0:T(128)}, u32[]{:S(2)}) copy-start(f32[96]{0:T(128)} %get-tuple-element.144) | copy-start | bytes 1156
  27.1 11.5 %copy-start.78 = (f32[96]{0:T(128)S(1)}, f32[96]{0:T(128)}, u32[]{:S(2)}) copy-start(f32[96]{0:T(128)} %get-tuple-element.145) | copy-start | bytes 1156
  27.1 11.5 %copy-start.80 = (f32[96]{0:T(128)S(1)}, f32[96]{0:T(128)}, u32[]{:S(2)}) copy-start(f32[96]{0:T(128)} %get-tuple-element.146) | copy-start | bytes 1156
  27.1 11.5 %copy-start.82 = (f32[96]{0:T(128)S(1)}, f32[96]{0:T(128)}, u32[]{:S(2)}) copy-start(f32[96]{0:T(128)} %get-tuple-element.147) | copy-start | bytes 1156
  27.1 11.5 %copy-start.84 = (f32[96]{0:T(128)S(1)}, f32[96]{0:T(128)}, u32[]{:S(2)}) copy-start(f32[96]{0:T(128)} %get-tuple-element.148) | copy-start | bytes 1156
  27.1 11.5 %copy-start.92 = (f32[96]{0:T(128)S(1)}, f32[96]{0:T(128)}, u32[]{:S(2)}) copy-start(f32[96]{0:T(128)} %param.14) | copy-start | bytes 1156
  38.6 11.9 %copy-start.14 = (f32[96]{0:T(128)S(1)}, f32[96]{0:T(128)}, u32[]{:S(2)}) copy-start(f32[96]{0:T(128)} %param.15) | copy-start | bytes 1156
  38.6 11.9 %copy-start.86 = (f32[96]{0:T(128)S(1)}, f32[96]{0:T(128)}, u32[]{:S(2)}) copy-start(f32[96]{0:T(128)} %param.16) | copy-start | bytes 1156
  75.7 3.7 %copy-start.2 = (bf16[384,1024]{0,1:T(8,128)(2,1)S(1)}, bf16[384,1024]{0,1:T(8,128)(2,1)}, u32[]{:S(2)}) copy-start(bf16[384,1024]{0,1:T(8,128)(2,1)} %get-tuple-element.151) | copy-start | bytes 2359300
  75.7 3.7 %copy-start.5 = (f32[12,8,4,256]{3,1,2,0:T(8,128)S(1)}, f32[12,8,4,256]{3,1,2,0:T(8,128)}, u32[]{:S(2)}) copy-start(f32[12,8,4,256]{3,1,2,0:T(8,128)} %copy-done.4) | copy-start | bytes 1179652
  79.4 12.3 %copy-start.3 = (bf16[384,1024]{0,1:T(8,128)(2,1)S(1)}, bf16[384,1024]{0,1:T(8,128)(2,1)}, u32[]{:S(2)}) copy-start(bf16[384,1024]{0,1:T(8,128)(2,1)} %get-tuple-element.151) | copy-start | bytes 2359300
  79.4 12.3 %copy-start.6 = (f32[12,8,4,256]{3,1,2,0:T(8,128)S(1)}, f32[12,8,4,256]{3,1,2,0:T(8,128)}, u32[]{:S(2)}) copy-start(f32[12,8,4,256]{3,1,2,0:T(8,128)} %copy-done.4) | copy-start | bytes 1179652
  86.4 6.8 %copy-start.87 = (f32[96]{0:T(128)S(1)}, f32[96]{0:T(128)}, u32[]{:S(2)}) copy-start(f32[96]{0:T(128)} %multiply_reduce_fusion.1) | copy-start | bytes 1156
  86.4 6.8 %copy-start.88 = (f32[96]{0:T(128)S(1)}, f32[96]{0:T(128)}, u32[]{:S(2)}) copy-start(f32[96]{0:T(128)} %get-tuple-element.53) | copy-start | bytes 1156
  86.4 6.9 %copy-start.89 = (f32[96]{0:T(128)S(1)}, f32[96]{0:T(128)}, u32[]{:S(2)}) copy-start(f32[96]{0:T(128)} %get-tuple-element.82) | copy-start | bytes 1156
  86.4 6.9 %copy-start.90 = (f32[384]{0:T(512)S(1)}, f32[384]{0:T(512)}, u32[]{:S(2)}) copy-start(f32[384]{0:T(512)} %get-tuple-element.154) | copy-start | bytes 4612
  86.4 53.4 %copy-start.12 = (bf16[96,3,256]{2,1,0:T(4,128)(2,1)S(1)}, bf16[96,3,256]{2,1,0:T(4,128)(2,1)}, u32[]{:S(2)}) copy-start(bf16[96,3,256]{2,1,0:T(4,128)(2,1)} %get-tuple-element.97) | copy-start | bytes 442372
  86.4 54.7 %copy-start.11 = (bf16[96,3,256]{2,1,0:T(4,128)(2,1)S(1)}, bf16[96,3,256]{2,1,0:T(4,128)(2,1)}, u32[]{:S(2)}) copy-start(bf16[96,3,256]{2,1,0:T(4,128)(2,1)} %get-tuple-element.96) | copy-start | bytes 442372
  139.9 4.5 %collective-permute-start.4 = (bf16[96,3,256]{2,1,0:T(4,128)(2,1)S(1)}, bf16[96,3,256]{2,1,0:T(4,128)(2,1)S(1)}, u32[]{:S(2)}, u32[]{:S(2)}) collective-permute-start(bf16[96,3,256]{2,1,0:T(4,128)(2,1)S(1)} %copy-done.12), channel_id=1, source_target_pairs={{0,4},{4,8},{8,12},{12,16},{16,20},{20,24},{24,28},{1,5},{5,9},{9,... | collective-permute-start | bytes 442376 | tf_op jit(solution)/shard_map/ppermute | solution.py:16
  141.2 5.7 %collective-permute-start.5 = (bf16[96,3,256]{2,1,0:T(4,128)(2,1)S(1)}, bf16[96,3,256]{2,1,0:T(4,128)(2,1)S(1)}, u32[]{:S(2)}, u32[]{:S(2)}) collective-permute-start(bf16[96,3,256]{2,1,0:T(4,128)(2,1)S(1)} %copy-done.11), channel_id=1, source_target_pairs={{4,0},{8,4},{12,8},{16,12},{20,16},{24,20},{28,24},{5,1},{9,5},{13... | collective-permute-start | bytes 442376 | tf_op jit(solution)/shard_map/ppermute | solution.py:17
  147.6 130.5 %collective-permute-start.6 = (bf16[96,10,3]{2,1,0:T(8,128)(2,1)S(1)}, bf16[96,10,3]{2,1,0:T(8,128)(2,1)S(1)}, u32[]{:S(2)}, u32[]{:S(2)}) collective-permute-start(bf16[96,10,3]{2,1,0:T(8,128)(2,1)S(1)} %get-tuple-element.86), channel_id=1, source_target_pairs={{1,0},{2,1},{3,2},{5,4},{6,5},{7,6},{9,8},{10,9},{11,10},{13,12},{... | collective-permute-start | bytes 17288 | tf_op jit(solution)/shard_map/ppermute | solution.py:17
  148.9 129.2 %collective-permute-start.7 = (bf16[96,10,3]{2,1,0:T(8,128)(2,1)S(1)}, bf16[96,10,3]{2,1,0:T(8,128)(2,1)S(1)}, u32[]{:S(2)}, u32[]{:S(2)}) collective-permute-start(bf16[96,10,3]{2,1,0:T(8,128)(2,1)S(1)} %get-tuple-element.87), channel_id=1, source_target_pairs={{0,1},{1,2},{2,3},{4,5},{5,6},{6,7},{8,9},{9,10},{10,11},{12,13},{... | collective-permute-start | bytes 17288 | tf_op jit(solution)/shard_map/ppermute | solution.py:16
  (38 other events, 98.8 us)
Sparse Core Ops, SparseCore 0:
  144.0 132.3 all-reduce.3
where the time goes:
time: 300 us; the launch traced here: 299 us
  waiting for transfers between devices  132 us (44%)
  other arithmetic  66.2 us (22%)
  blocking collectives  43.9 us (15%)
  starting transfers between devices  17.9 us (6%)
  local copies, waits for them, and re-layouts  15.7 us (5%)
  between operations  15.6 us (5%)
  matrix products  7.76 us (3%)
    psum x1, waiting for transfers between devices, shards(): lax.psum((g_reduce, g_expand, g_ebias, g_kernel, g_dbias, norm_gain_gradi...  123 us
    psum x1, blocking collectives, shards(): lax.psum((g_reduce, g_expand, g_ebias, g_kernel, g_dbias, norm_gain_gradi...  43.9 us
    reduce_sum x4, other arithmetic, kernel_terms(): entries.append(jnp.sum(piece * convolution_gradient, axis=(1, 2)))  26.3 us
    ppermute x4, starting transfers between devices, padded_2(): before = lax.ppermute(last, axis, up)  12.7 us
    convert_element_type x1, other arithmetic, shards(): image_grad = (cotangent.astype(jnp.float32) + back).astype(jnp.bfloat16)  11.7 us
    reduce_sum x1, other arithmetic, shards(): average = jnp.mean(flat, axis=0, keepdims=True)  11.5 us
    concatenate x4, other arithmetic, padded_2(): x = jnp.concatenate([before, x, after], axis=dim)  7.74 us
    ppermute x4, waiting for transfers between devices, padded_2(): after = lax.ppermute(initial, axis, down)  6.56 us
  transfers between devices with their start and end apart: 9, of which 4 were waited for; matrix products, arithmetic and copies ran while one was open for 4% of the time, Pallas kernels for 0%

commit v1 on v0

v1 whole, which is shorter than its diff:
```python
import functools
import math

import jax
import jax.numpy as jnp
from jax import lax
from jax.experimental import pallas as pl
from jax.experimental.pallas import tpu as pltpu
from jax.sharding import PartitionSpec as P

F32 = jnp.float32
BF16 = jnp.bfloat16
SIDE = 7
HALO = 3
LANES = 128
EDGE = 16
PIECES = 8
NT = (((1,), (1,)), ((), ()))
TN = (((0,), (0,)), ((), ()))


def iota(shape, dim):
    return lax.broadcasted_iota(jnp.int32, shape, dim)


def dot(a, b, dims=(((1,), (0,)), ((), ()))):
    return lax.dot_general(a, b, dims, preferred_element_type=F32)


def column(row):
    n = row.shape[1]
    eye = iota((n, n), 0) == iota((n, n), 1)
    return jnp.sum(jnp.where(eye, row, 0.0), axis=1, keepdims=True)


def pack_edges(rows):
    width = rows[0].shape[1]
    q, j = iota((2 * EDGE, width), 0), iota((2 * EDGE, width), 1)
    total = None
    for i, row in enumerate(rows):
        last = (q == HALO * i + j - (width - HALO)) & (j >= width - HALO)
        first = (q == EDGE + HALO * i + j) & (j < HALO)
        pick = jnp.where(last | first, 1.0, 0.0).astype(BF16)
        part = dot(pick, row, NT)
        total = part if total is None else total + part
    return total


def halo_tile(edges, i):
    q, l = iota((2 * EDGE, LANES), 0), iota((2 * EDGE, LANES), 1)
    left = (q == HALO * i + l - (LANES - HALO)) & (l >= LANES - HALO)
    right = (q == EDGE + HALO * i + l) & (l < HALO)
    pick = jnp.where(left | right, 1.0, 0.0).astype(BF16)
    return dot(edges, pick, TN).astype(BF16)


def taps_matrix(taps_ref, line_ref, w_ref, flip):
    channels = taps_ref.shape[2]
    for b in range(SIDE):
        line_ref[0:SIDE, b * channels : (b + 1) * channels] = taps_ref[:, SIDE - 1 - b if flip else b, :]
    lane = iota((1, SIDE * channels), 1)
    for b in range(1, SIDE):
        lane = jnp.where(iota((1, SIDE * channels), 1) >= b * channels, iota((1, SIDE * channels), 1) - b * channels, lane)
    mask = lane == iota((channels, SIDE * channels), 0)
    for m in range(SIDE):
        a = m if flip else SIDE - 1 - m
        w_ref[m * channels : (m + 1) * channels, :] = jnp.where(mask, line_ref[a : a + 1, :], 0.0).astype(BF16)
    return mask


def shifted(x, amount):
    return x if amount % x.shape[1] == 0 else pltpu.roll(x, amount % x.shape[1], 1)


def spread(xs_ref, r, x):
    channels = x.shape[0]
    width = xs_ref.shape[1]
    for b in range(SIDE):
        xs_ref[(r * SIDE + b) * channels : (r * SIDE + b + 1) * channels, :] = shifted(x, HALO - b)[:, :width]


def depthwise(w_ref, xs_ref, acc_ref, row_count, channels):
    deep = SIDE * channels
    acc_ref[...] = jnp.zeros_like(acc_ref)
    for r in range(row_count + 2 * HALO):
        i0, i1 = max(0, r - (SIDE - 1)), min(row_count - 1, r)
        m0 = SIDE - 1 - r + i0
        part = dot(w_ref[m0 * channels : (m0 + i1 - i0 + 1) * channels, :], xs_ref[r * deep : (r + 1) * deep, :])
        acc_ref[i0 * channels : (i1 + 1) * channels, :] += part


def pack_kernel(image_ref, edges_ref):
    rows = image_ref.shape[0]
    edges = pack_edges([image_ref[i] for i in range(rows)]).astype(BF16)
    edges_ref[0] = edges[:EDGE]
    edges_ref[1] = edges[EDGE:]


def widen_kernel(image_ref, left_ref, right_ref, wide_ref, top_ref, bottom_ref):
    rows, _, width = image_ref.shape
    edges = jnp.concatenate([left_ref[...], right_ref[...]], axis=0)
    for i in range(rows):
        row = jnp.concatenate([image_ref[i], halo_tile(edges, i)], axis=1)
        wide_ref[i] = row
        if i < HALO:
            top_ref[i] = row
        if i >= rows - HALO:
            bottom_ref[i - rows + HALO] = row


def gelu_parts(v):
    z = jnp.abs(v)
    t = 1.0 / (1.0 + (0.3275911 / math.sqrt(2.0)) * z)
    e = jnp.exp(-0.5 * (v * v))
    half = 0.5
    poly = t * (
        half * 0.254829592
        + t * (half * -0.284496736 + t * (half * 1.421413741 + t * (half * -1.453152027 + t * (half * 1.061405429))))
    )
    tail = poly * e
    return jnp.where(v >= 0.0, 1.0 - tail, tail), (v * (1.0 / math.sqrt(2.0 * math.pi))) * e


def main_kernel(
    spread_parts,
    axes,
    up_ref,
    mid_ref,
    down_ref,
    cot_ref,
    taps_ref,
    dwb_ref,
    gain_ref,
    lnb_ref,
    we_ref,
    be_ref,
    wr_ref,
    br_ref,
    scale_ref,
    out_ref,
    dconv_ref,
    top_ref,
    bottom_ref,
    *rest,
):
    if spread_parts:
        (block_ref, *scratch) = rest
    else:
        (grads_ref, small_out_ref, edges_ref, *scratch) = rest
    x_ref, xs_ref, w_ref, line_ref, acc_ref, xhat_ref, nm_ref, db_ref, act_ref, dh_ref, we2_ref, wide_ref, dcs_ref, small_ref = scratch
    rows, channels, width = cot_ref.shape
    hidden_n = we_ref.shape[1]
    deep = SIDE * channels
    dwb, gain, lnb, br, scale = (column(ref[...]) for ref in (dwb_ref, gain_ref, lnb_ref, br_ref, scale_ref))
    we_t = we_ref[...]
    wr_t = wr_ref[...]
    we2_ref[0:channels, :] = we_t
    extra = nm_ref.shape[0] - channels
    we2_ref[channels:, :] = jnp.where(iota((extra, hidden_n), 0) == 0, be_ref[...].astype(F32), 0.0).astype(BF16)
    we2 = we2_ref[...].T
    wr = wr_t.T
    mask = taps_matrix(taps_ref, line_ref, w_ref, False)
    for r in range(rows + 2 * HALO):
        if r < HALO:
            x = up_ref[r]
        elif r < HALO + rows:
            x = mid_ref[r - HALO]
        else:
            x = down_ref[r - HALO - rows]
        x_ref[r * channels : (r + 1) * channels, :] = x
        spread(xs_ref, r, x)
    depthwise(w_ref, xs_ref, acc_ref, rows, channels)
    nm_ref[channels:, :] = jnp.where(iota((extra, rows * width), 0) == 0, 1.0, 0.0).astype(BF16)
    zero = jnp.zeros((channels, LANES), F32)
    sums = {k: zero for k in ("dwb", "gain", "lnb", "rb", "scale")}

    def add(name, value):
        for k in range(0, width, LANES):
            sums[name] = sums[name] + value[:, k : k + LANES]

    chunk = 128
    dconv_rows = []
    for i in range(rows):
        cols = slice(i * width, (i + 1) * width)
        conv = acc_ref[i * channels : (i + 1) * channels, :] + dwb
        conv = conv - jnp.mean(conv, axis=0, keepdims=True)
        inv = lax.rsqrt(jnp.mean(conv * conv, axis=0, keepdims=True) + 1e-6)
        xhat = conv * inv
        xhat_ref[...] = xhat
        nm_ref[0:channels, cols] = (xhat * gain + lnb).astype(BF16)
        cot = cot_ref[i].astype(F32)
        add("rb", cot)
        db_ref[:, cols] = (cot * scale).astype(BF16)
        for h0 in range(0, hidden_n, chunk):
            hs = slice(h0, h0 + chunk)
            hidden = dot(we2[hs, :], nm_ref[:, cols])
            back = dot(wr[hs, :], db_ref[:, cols])
            phi, bump = gelu_parts(hidden)
            act_ref[hs, cols] = (hidden * phi).astype(BF16)
            dh_ref[hs, cols] = (back * (phi + bump)).astype(BF16)
        branch = dot(wr_t, act_ref[:, cols]) + br
        out_ref[i] = (mid_ref[i][:, :width].astype(F32) + scale * branch).astype(BF16)
        add("scale", cot * branch)
        d_normed = dot(we_t, dh_ref[:, cols])
        xhat = xhat_ref[...]
        add("lnb", d_normed)
        add("gain", d_normed * xhat)
        d_xhat = d_normed * gain
        m1 = jnp.mean(d_xhat, axis=0, keepdims=True)
        m2 = jnp.mean(d_xhat * xhat, axis=0, keepdims=True)
        dconv = (inv * (d_xhat - m1 - xhat * m2)).astype(BF16)
        add("dwb", dconv.astype(F32))
        dconv_ref[i] = dconv
        if i < HALO:
            top_ref[i] = dconv
        if i >= rows - HALO:
            bottom_ref[i - rows + HALO] = dconv
        dconv_rows.append(dconv)
        padded = jnp.concatenate([dconv, jnp.zeros((channels, LANES), BF16)], axis=1)
        for b in range(SIDE):
            dcs_ref[b * channels : (b + 1) * channels, i * (width + LANES) : (i + 1) * (width + LANES)] = shifted(padded, b - HALO)
    edges = pack_edges(dconv_rows).astype(BF16)
    g_reduce = dot(act_ref[...], db_ref[...], NT)
    g_expand = dot(dh_ref[...], nm_ref[...], NT)
    for i in range(rows):
        wide_ref[:, i * (width + LANES) : (i + 1) * (width + LANES)] = x_ref[i * channels : i * channels + deep, :]
    taps = dot(wide_ref[...], dcs_ref[...], NT)
    small_ref[...] = jnp.zeros_like(small_ref)
    for a in range(SIDE):
        line_ref[a : a + 1, :] = jnp.sum(
            jnp.where(mask, taps[a * channels : (a + 1) * channels, :], 0.0), axis=0, keepdims=True
        )
    for b in range(SIDE):
        small_ref[b * 8 : b * 8 + SIDE, 0:channels] = line_ref[0:SIDE, b * channels : (b + 1) * channels]
    for b, name in enumerate(("dwb", "gain", "lnb", "rb", "scale")):
        total = jnp.sum(sums[name].T, axis=0, keepdims=True)
        small_ref[b * 8 + SIDE : b * 8 + 8, 0:channels] = total * scale_ref[...] if name == "rb" else total
    if not spread_parts:
        grads_ref[...] = jnp.zeros_like(grads_ref)
        grads_ref[0, :, 0:channels] = g_reduce
        grads_ref[1, :, 0 : nm_ref.shape[0]] = g_expand
        small_out_ref[...] = small_ref[...]
        edges_ref[...] = jnp.zeros_like(edges_ref)
        edges_ref[:, 0:channels] = edges
        return
    space, filt = spread_parts
    me = lax.axis_index(axes[1])
    panel = hidden_n // filt
    step = 2 * panel // PIECES
    pad = lambda v: jnp.concatenate([v, jnp.zeros((v.shape[0], LANES - v.shape[1]), v.dtype)], axis=1)
    g_reduce, g_expand = pad(g_reduce), pad(g_expand)
    edges = pad(edges)
    for f in range(filt):
        edge = jnp.where(f > me, edges[:EDGE], edges[EDGE:])
        for s in range(space):
            source = g_reduce if s < PIECES // 2 else g_expand
            at = f * panel + (s % (PIECES // 2)) * step
            head = jnp.concatenate([source[at : at + step], small_ref[s * 8 : s * 8 + 8, :]], axis=0)
            block_ref[s * filt + f, 0 : step + 8, :] = head.astype(BF16)
            block_ref[s * filt + f, step + 8 :, :] = edge


def sum_kernel(axes, sizes, block_ref, total_ref, edges_ref):
    count, _, _ = block_ref.shape
    head = block_ref.shape[1] - EDGE
    total = block_ref[0, :head, :].astype(F32)
    for d in range(1, count):
        total = total + block_ref[d, :head, :].astype(F32)
    for s in range(total_ref.shape[0]):
        total_ref[s] = total
    space, filt = sizes
    s, f = lax.axis_index(axes[0]), lax.axis_index(axes[1])
    for k in range(3):
        for side in range(2):
            ss, ff = s + k - 1, f + 2 * side - 1
            inside = (ss >= 0) & (ss < space) & (ff >= 0) & (ff < filt)
            at = jnp.clip(ss, 0, space - 1) * filt + jnp.clip(ff, 0, filt - 1)
            value = block_ref[at, head:, :]
            edges_ref[k, side * EDGE : (side + 1) * EDGE, :] = jnp.where(inside, value, jnp.zeros_like(value))


def back_kernel(up_ref, mid_ref, down_ref, edges_ref, cot_ref, taps_ref, out_ref, xs_ref, w_ref, line_ref, acc_ref):
    rows, channels, width = cot_ref.shape
    taps_matrix(taps_ref, line_ref, w_ref, True)
    edges = [edges_ref[k][:, 0:channels] for k in range(3)]
    for r in range(rows + 2 * HALO):
        if r < HALO:
            x, h = up_ref[r], halo_tile(edges[0], rows - HALO + r)
        elif r < HALO + rows:
            x, h = mid_ref[r - HALO], halo_tile(edges[1], r - HALO)
        else:
            x, h = down_ref[r - HALO - rows], halo_tile(edges[2], r - HALO - rows)
        spread(xs_ref, r, jnp.concatenate([x, h], axis=1))
    depthwise(w_ref, xs_ref, acc_ref, rows, channels)
    for i in range(rows):
        out_ref[i] = (cot_ref[i].astype(F32) + acc_ref[i * channels : (i + 1) * channels, :]).astype(BF16)


def finish_kernel(factor, total_ref, kg_ref, dwb_ref, gain_ref, lnb_ref, ge_ref, eb_ref, gr_ref, rb_ref, sc_ref):
    channels = kg_ref.shape[2]
    step = total_ref.shape[1] - 8
    for b in range(SIDE):
        kg_ref[:, b, :] = total_ref[b, step : step + SIDE, 0:channels] * factor
    for b, ref in enumerate((dwb_ref, gain_ref, lnb_ref, rb_ref, sc_ref)):
        ref[...] = total_ref[b, step + SIDE :, 0:channels] * factor
    half = PIECES // 2
    for s in range(half):
        gr_ref[s * step : (s + 1) * step, :] = total_ref[s, 0:step, 0:channels] * factor
        part = total_ref[half + s, 0:step, :] * factor
        ge_ref[s * step : (s + 1) * step, :] = part[:, 0:channels]
        eye = iota((step, half * step), 0) + s * step == iota((step, half * step), 1)
        line = jnp.sum(jnp.where(eye, part[:, channels : channels + 1], 0.0), axis=0, keepdims=True)
        eb_ref[...] = line if s == 0 else eb_ref[...] + line


def call(kernel, outs, *args, scratch=(), flops=0):
    moved = sum(math.prod(a.shape) * a.dtype.itemsize for a in args) + sum(
        math.prod(s) * jnp.dtype(d).itemsize for s, d in outs
    )
    return pl.pallas_call(
        kernel,
        out_shape=[jax.ShapeDtypeStruct(s, d) for s, d in outs],
        scratch_shapes=[pltpu.VMEM(s, d) for s, d in scratch],
        compiler_params=pltpu.CompilerParams(vmem_limit_bytes=40 * 2**20),
        cost_estimate=pl.CostEstimate(flops=flops, bytes_accessed=moved, transcendentals=0),
    )(*args)


def moved(x, axis, step):
    size = lax.axis_size(axis)
    return lax.ppermute(x, axis, [(i, i + step) for i in range(size) if 0 <= i + step < size])


def shards(
    axes,
    image,
    cotangent,
    kernel,
    dw_bias,
    layer_norm_gain,
    layer_norm_bias,
    w_expand,
    b_expand,
    w_reduce,
    b_reduce,
    layer_scale,
):
    over_rows, over_cols = axes
    space, filt = lax.axis_size(over_rows), lax.axis_size(over_cols)
    channels, rows, width = image.shape
    hidden_n = w_expand.shape[0]
    panel = hidden_n // filt
    step = 2 * panel // PIECES
    deep = SIDE * channels
    tall = rows + 2 * HALO
    wide = width + LANES
    tokens = rows * width
    direct = space == PIECES
    image_t = jnp.transpose(image, (1, 0, 2))
    cot_t = jnp.transpose(cotangent, (1, 0, 2))
    taps = jnp.transpose(kernel, (1, 2, 0))
    (edges,) = call(pack_kernel, [((2, EDGE, channels), BF16)], image_t)
    left = moved(edges[0], over_cols, 1)
    right = moved(edges[1], over_cols, -1)
    mid, top, bottom = call(
        widen_kernel,
        [((rows, channels, wide), BF16), ((HALO, channels, wide), BF16), ((HALO, channels, wide), BF16)],
        image_t,
        left,
        right,
    )
    up = moved(bottom, over_rows, 1)
    down = moved(top, over_rows, -1)
    row = lambda v: v.reshape(1, -1)
    outs = [
        ((rows, channels, width), BF16),
        ((rows, channels, width), BF16),
        ((HALO, channels, width), BF16),
        ((HALO, channels, width), BF16),
    ]
    if direct:
        outs += [((space * filt, step + 8 + EDGE, LANES), BF16)]
    else:
        outs += [((2, hidden_n, LANES), F32), ((PIECES * 8, LANES), F32), ((2 * EDGE, LANES), BF16)]
    lift = channels + 16
    out_t, dconv, top, bottom, *rest = call(
        functools.partial(main_kernel, (space, filt) if direct else None, axes),
        outs,
        up,
        mid,
        down,
        cot_t,
        taps,
        row(dw_bias),
        row(layer_norm_gain),
        row(layer_norm_bias),
        w_expand.T,
        row(b_expand),
        w_reduce.T,
        row(b_reduce),
        row(layer_scale),
        scratch=[
            ((tall * channels, wide), BF16),
            ((tall * deep, width), BF16),
            ((deep, deep), BF16),
            ((8, deep), F32),
            ((rows * channels, width), F32),
            ((channels, width), F32),
            ((lift, tokens), BF16),
            ((channels, tokens), BF16),
            ((hidden_n, tokens), BF16),
            ((hidden_n, tokens), BF16),
            ((lift, hidden_n), BF16),
            ((deep, rows * wide), BF16),
            ((deep, rows * wide), BF16),
            ((PIECES * 8, LANES), F32),
        ],
    )
    up = moved(bottom, over_rows, 1)
    down = moved(top, over_rows, -1)
    if direct:
        (block,) = rest
        block = lax.all_to_all(block, axes, 0, 0, tiled=True)
        total, edges = call(
            functools.partial(sum_kernel, axes, (space, filt)),
            [((PIECES, step + 8, LANES), F32), ((3, 2 * EDGE, LANES), BF16)],
            block,
        )
        total = lax.all_to_all(total, over_rows, 0, 0, tiled=True)
    else:
        grads, small, edges = rest
        edges = jnp.concatenate([moved(edges[:EDGE], over_cols, 1), moved(edges[EDGE:], over_cols, -1)], axis=0)
        edges = jnp.stack([moved(edges, over_rows, 1), edges, moved(edges, over_rows, -1)])
        grads, small = lax.psum((grads, small), axes)
        grads = lax.dynamic_slice_in_dim(grads, lax.axis_index(over_cols) * panel, panel, 1)
        total = jnp.concatenate([grads.reshape(PIECES, step, LANES), small.reshape(PIECES, 8, LANES)], axis=1)
    (back_t,) = call(
        back_kernel,
        [((rows, channels, width), BF16)],
        up,
        dconv,
        down,
        edges,
        cot_t,
        taps,
        scratch=[
            ((tall * deep, width), BF16),
            ((deep, deep), BF16),
            ((8, deep), F32),
            ((rows * channels, width), F32),
        ],
    )
    factor = 1.0 / math.sqrt(tokens * space * filt)
    line = ((1, channels), F32)
    kg, dwb, gain, lnb, ge, eb, gr, rb, sc = call(
        functools.partial(finish_kernel, factor),
        [
            ((SIDE, SIDE, channels), F32),
            line,
            line,
            line,
            ((panel, channels), F32),
            ((1, panel), F32),
            ((panel, channels), F32),
            line,
            line,
        ],
        total,
    )
    flat = lambda v: v.reshape(-1)
    return (
        jnp.transpose(out_t, (1, 0, 2)),
        jnp.transpose(back_t, (1, 0, 2)),
        jnp.transpose(kg, (2, 0, 1)),
        flat(dwb),
        flat(gain),
        flat(lnb),
        ge,
        flat(eb),
        gr,
        flat(rb),
        flat(sc),
    )


def solution(mesh):
    axes = ("space", "filt")
    pixels = P(None, *axes)
    return jax.shard_map(
        functools.partial(shards, axes),
        mesh=mesh,
        in_specs=(pixels, pixels) + (P(),) * 9,
        out_specs=(pixels, pixels, P(), P(), P(), P(), P("filt", None), P("filt"), P("filt", None), P(), P()),
        check_vma=False,
    )
```

time: 300 us -> 58.9 us (0.20)
  waiting for transfers between devices: 132 us -> 16 us
  other arithmetic: 66.2 us -> 0 us
  blocking collectives: 43.9 us -> 0 us
  between operations: 15.6 us -> 0.85 us
  local copies, waits for them, and re-layouts: 15.7 us -> 3.35 us
  Pallas kernels: 0 us -> 11.5 us
  starting transfers between devices: 17.9 us -> 26.8 us
  matrix products: 7.76 us -> 0 us
    psum x1 -> x0, waiting for transfers between devices: 123 us -> none  [shards(): lax.psum((g_reduce, g_expand, g_ebias, g_kernel, g_dbias, norm_gain_gradi...]
    psum x1 -> x0, blocking collectives: 43.9 us -> none  [shards(): lax.psum((g_reduce, g_expand, g_ebias, g_kernel, g_dbias, norm_gain_gradi...]
    reduce_sum x9 -> x0, other arithmetic: 41.5 us -> none  [the longest x4 26.3 us: kernel_terms(): entries.append(jnp.sum(piece * convolution_gradient, axis=(1, 2)))]
    all_to_all x0 -> x2, starting transfers between devices: none -> 13.8 us  [the longest x1 10.5 us: shards(): block = lax.all_to_all(block, axes, 0, 0, tiled=True)]
    convert_element_type x2 -> x0, other arithmetic: 11.7 us -> none  [the longest x1 11.7 us: shards(): image_grad = (cotangent.astype(jnp.float32) + back).astype(jnp.bfloat16)]
    pallas_call x0 -> x6, Pallas kernels: none -> 11.5 us  [call(): pl.pallas_call(kernel, out_shape=[jax.ShapeDtypeStruct(s, d) for s, d in...]
    all_to_all x0 -> x2, waiting for transfers between devices: none -> 10.6 us  [the longest x1 8.35 us: shards(): block = lax.all_to_all(block, axes, 0, 0, tiled=True)]
    dot_general x6 -> x0, matrix products: 7.76 us -> none  [the longest x1 1.53 us: shards(): d_active = jnp.dot(w_reduce, d_branch, preferred_element_type=jnp.float32)]
  transfers between devices with their start and end apart: 9 -> 8, of which waited for: 4 -> 4; matrix products, arithmetic and copies ran while one was open for 4% -> 3% of each run, Pallas kernels for 0% -> 4%
where the time goes in v1:
time: 58.9 us; the launch traced here: 58.4 us
  starting transfers between devices  26.8 us (46%)
  waiting for transfers between devices  16 us (27%)
  Pallas kernels  11.5 us (20%)
  local copies, waits for them, and re-layouts  3.35 us (6%)
  between operations  0.85 us (1%)
    ppermute x6, starting transfers between devices, moved(): lax.ppermute(x, axis, [(i, i + step) for i in range(size) if 0 <= i + ste...  12.9 us
    pallas_call x6, Pallas kernels, call(): pl.pallas_call(kernel, out_shape=[jax.ShapeDtypeStruct(s, d) for s, d in...  11.5 us
    all_to_all x1, starting transfers between devices, shards(): block = lax.all_to_all(block, axes, 0, 0, tiled=True)  10.5 us
    all_to_all x1, waiting for transfers between devices, shards(): block = lax.all_to_all(block, axes, 0, 0, tiled=True)  8.35 us
    ppermute x6, waiting for transfers between devices, moved(): lax.ppermute(x, axis, [(i, i + step) for i in range(size) if 0 <= i + ste...  5.42 us
    all_to_all x1, starting transfers between devices, shards(): total = lax.all_to_all(total, over_rows, 0, 0, tiled=True)  3.37 us
    unnamed x24, local copies, waits for them, and re-layouts  3.34 us
    all_to_all x1, waiting for transfers between devices, shards(): total = lax.all_to_all(total, over_rows, 0, 0, tiled=True)  2.23 us
  transfers between devices with their start and end apart: 8, of which 4 were waited for; matrix products, arithmetic and copies ran while one was open for 3% of the time, Pallas kernels for 4%

profile of v1, /device:TPU:0, one launch (start us, length us, event | category | flops | bytes accessed | tf_op | source)
XLA Modules:
  0.0 58.4 jit_solution(2853289209259944784)
XLA Ops:
  0.6 0.9 %copy.29 = bf16[96,4,256]{2,0,1:T(8,128)(2,1)S(1)} copy(bf16[96,4,256]{2,1,0:T(4,128)(2,1)} %param.11) | data formatting | bytes 393216 | tf_op args[0]
  1.6 0.0 copy-start.8
  1.6 0.2 shard_map.194
  1.8 1.3 %collective-permute-start.1 = (bf16[16,96]{1,0:T(8,128)(2,1)S(1)}, bf16[16,96]{1,0:T(8,128)(2,1)S(1)}, u32[]{:S(2)}, u32[]{:S(2)}) collective-permute-start(bf16[16,96]{1,0:T(8,128)(2,1)S(1)} %get-tuple-element.60), channel_id=1, source_target_pairs={{1,0},{2,1},{3,2},{5,4},{6,5},{7,6},{9,8},{10,9},{11,10},{13,12},{... | collective-permute-start | bytes 9224 | tf_op jit(solution)/shard_map/ppermute | solution.py:331
  3.1 5.6 %collective-permute-start = (bf16[16,96]{1,0:T(8,128)(2,1)S(1)}, bf16[16,96]{1,0:T(8,128)(2,1)S(1)}, u32[]{:S(2)}, u32[]{:S(2)}) collective-permute-start(bf16[16,96]{1,0:T(8,128)(2,1)S(1)} %get-tuple-element.61), channel_id=1, source_target_pairs={{0,1},{1,2},{2,3},{4,5},{5,6},{6,7},{8,9},{9,10},{10,11},{12,13},{... | collective-permute-start | bytes 9224 | tf_op jit(solution)/shard_map/ppermute | solution.py:331
  8.7 0.0 collective-permute-done.1.right_ref
  8.7 1.3 %collective-permute-done.left_ref = bf16[16,96]{1,0:T(8,128)(2,1)S(1)} collective-permute-done((bf16[16,96]{1,0:T(8,128)(2,1)S(1)}, bf16[16,96]{1,0:T(8,128)(2,1)S(1)}, u32[]{:S(2)}, u32[]{:S(2)}) %collective-permute-start) | collective-permute-done | bytes 3104 | tf_op jit(solution)/shard_map/ppermute | solution.py:331
  10.0 0.2 shard_map.195
  10.2 0.0 copy-start.9
  10.2 1.3 %collective-permute-start.2 = (bf16[3,96,384]{2,1,0:T(8,128)(2,1)S(1)}, bf16[3,96,384]{2,1,0:T(8,128)(2,1)S(1)}, u32[]{:S(2)}, u32[]{:S(2)}) collective-permute-start(bf16[3,96,384]{2,1,0:T(8,128)(2,1)S(1)} %get-tuple-element.30), channel_id=1, source_target_pairs={{0,4},{4,8},{8,12},{12,16},{16,20},{20,24},{24,28},{1,5},{5,9},{9,... | collective-permute-start | bytes 663560 | tf_op jit(solution)/shard_map/ppermute | solution.py:331
  11.5 1.3 %collective-permute-start.3 = (bf16[3,96,384]{2,1,0:T(8,128)(2,1)S(1)}, bf16[3,96,384]{2,1,0:T(8,128)(2,1)S(1)}, u32[]{:S(2)}, u32[]{:S(2)}) collective-permute-start(bf16[3,96,384]{2,1,0:T(8,128)(2,1)S(1)} %get-tuple-element.32), channel_id=1, source_target_pairs={{4,0},{8,4},{12,8},{16,12},{20,16},{24,20},{28,24},{5,1},{9,5},{13... | collective-permute-start | bytes 663560 | tf_op jit(solution)/shard_map/ppermute | solution.py:331
  12.8 0.0 copy-done.9
  12.8 0.0 copy-done.8
  12.8 0.0 copy-start
  12.8 0.0 copy-start.1
  12.9 0.0 copy-start.2
  12.9 0.0 collective-permute-done.2.up_ref
  12.9 4.1 %collective-permute-done.3.down_ref = bf16[3,96,384]{2,1,0:T(8,128)(2,1)S(1)} collective-permute-done((bf16[3,96,384]{2,1,0:T(8,128)(2,1)S(1)}, bf16[3,96,384]{2,1,0:T(8,128)(2,1)S(1)}, u32[]{:S(2)}, u32[]{:S(2)}) %collective-permute-start.3) | collective-permute-done | bytes 221216 | tf_op jit(solution)/shard_map/ppermute | solution.py:331
  17.0 0.0 copy-start.6
  17.0 0.0 copy-start.7
  17.0 0.0 copy-start.3
  17.0 0.0 copy-start.4
  17.0 0.0 copy-start.5
  17.0 0.0 copy-done
  17.1 0.0 copy-done.1
  17.1 0.0 copy-done.2
  17.1 0.6 %copy-done.6 = f32[96]{0:T(128)S(1)} copy-done((f32[96]{0:T(128)S(1)}, f32[96]{0:T(128)}, u32[]{:S(2)}) %copy-start.6) | copy-done | bytes 408
  17.7 0.0 copy-done.7
  17.7 0.0 copy-done.3
  17.7 0.0 copy-done.4
  17.7 0.0 copy-done.5
  17.7 8.1 %shard_map.196 = (bf16[4,96,256]{2,1,0:T(8,128)(2,1)S(1)}, bf16[4,96,256]{2,1,0:T(8,128)(2,1)S(1)}, bf16[3,96,256]{2,1,0:T(8,128)(2,1)S(1)}, bf16[3,96,256]{2,1,0:T(8,128)(2,1)S(1)}, bf16[32,48,128]{2,1,0:T(8,128)(2,1)}) custom-call(bf16[3,96,384]{2,1,0:T(8,128)(2,1)S(1)} %collective-permute-done.2.up_ref, ...), custom_call_target="tpu_custom_call" | custom-call | bytes 2184192 | tf_op jit(solution)/shard_map/pallas_call | solution.py:320
  25.8 10.5 %all-to-all-start = ((bf16[32,48,128]{2,1,0:T(8,128)(2,1)}), bf16[32,48,128]{2,1,0:T(8,128)(2,1)S(1)}, u32[]{:S(2)}, u32[]{:S(2)}) async-start(bf16[32,48,128]{2,1,0:T(8,128)(2,1)} %get-tuple-element.37), calls=%async_computation | async-start | bytes 786432 | tf_op jit(solution)/shard_map/all_to_all | solution.py:423
  36.3 2.2 %collective-permute-start.4 = (bf16[3,96,256]{2,1,0:T(8,128)(2,1)S(1)}, bf16[3,96,256]{2,1,0:T(8,128)(2,1)S(1)}, u32[]{:S(2)}, u32[]{:S(2)}) collective-permute-start(bf16[3,96,256]{2,1,0:T(8,128)(2,1)S(1)} %get-tuple-element.34), channel_id=1, source_target_pairs={{0,4},{4,8},{8,12},{12,16},{16,20},{20,24},{24,28},{1,5},{5,9},{9,... | collective-permute-start | bytes 442376 | tf_op jit(solution)/shard_map/ppermute | solution.py:331
  38.5 1.3 %collective-permute-start.5 = (bf16[3,96,256]{2,1,0:T(8,128)(2,1)S(1)}, bf16[3,96,256]{2,1,0:T(8,128)(2,1)S(1)}, u32[]{:S(2)}, u32[]{:S(2)}) collective-permute-start(bf16[3,96,256]{2,1,0:T(8,128)(2,1)S(1)} %get-tuple-element.36), channel_id=1, source_target_pairs={{4,0},{8,4},{12,8},{16,12},{20,16},{24,20},{28,24},{5,1},{9,5},{13... | collective-permute-start | bytes 442376 | tf_op jit(solution)/shard_map/ppermute | solution.py:331
  39.8 8.4 %all-to-all-done.block_ref = bf16[32,48,128]{2,1,0:T(8,128)(2,1)S(1)} async-done(((bf16[32,48,128]{2,1,0:T(8,128)(2,1)}), bf16[32,48,128]{2,1,0:T(8,128)(2,1)S(1)}, u32[]{:S(2)}, u32[]{:S(2)}) %all-to-all-start) | async-done | bytes 393248 | tf_op jit(solution)/shard_map/all_to_all | solution.py:423
  48.2 0.7 %shard_map.197 = (f32[8,32,128]{2,1,0:T(8,128)}, bf16[3,32,128]{2,1,0:T(8,128)(2,1)S(1)}) custom-call(bf16[32,48,128]{2,1,0:T(8,128)(2,1)S(1)} %all-to-all-done.block_ref), custom_call_target="tpu_custom_call" | custom-call | bytes 548864 | tf_op jit(solution)/shard_map/pallas_call | solution.py:320
  48.8 3.4 %all-to-all-start.1 = ((f32[8,32,128]{2,1,0:T(8,128)}), f32[8,32,128]{2,1,0:T(8,128)S(1)}, u32[]{:S(2)}, u32[]{:S(2)}) async-start(f32[8,32,128]{2,1,0:T(8,128)} %get-tuple-element.39), calls=%async_computation.1 | async-start | bytes 262144 | tf_op jit(solution)/shard_map/all_to_all | solution.py:429
  52.2 0.8 %copy.24 = bf16[96,4,256]{2,1,0:T(4,128)(2,1)} copy(bf16[96,4,256]{2,0,1:T(8,128)(2,1)S(1)} %bitcast.32) | data formatting | bytes 393216
  53.1 0.0 collective-permute-done.4.up_ref
  53.1 0.0 collective-permute-done.5.down_ref
  53.1 1.6 %shard_map.198 = bf16[4,96,256]{2,1,0:T(8,128)(2,1)S(1)} custom-call(bf16[3,96,256]{2,1,0:T(8,128)(2,1)S(1)} %collective-permute-done.4.up_ref, bf16[4,96,256]{2,1,0:T(8,128)(2,1)S(1)} %get-tuple-element.35.mid_ref, bf16[3,96,256]{2,1,0:T(8,128)(2,1)S(1)} %collective-permute-done.5.down_ref, bf16[3,32,128]{2,1,0:T(8,128)(2,1)S(1)} %get-tuple-element.38.edges_ref, ...), custom_call_target="tpu_custom_call" | custom-call | bytes 928128 | tf_op jit(solution)/shard_map/pallas_call | solution.py:320
  54.6 0.8 %copy.25 = bf16[96,4,256]{2,1,0:T(4,128)(2,1)} copy(bf16[96,4,256]{2,0,1:T(8,128)(2,1)S(1)} %bitcast.31) | data formatting | bytes 393216
  55.5 2.2 %all-to-all-done.1.total_ref = f32[8,32,128]{2,1,0:T(8,128)S(1)} async-done(((f32[8,32,128]{2,1,0:T(8,128)}), f32[8,32,128]{2,1,0:T(8,128)S(1)}, u32[]{:S(2)}, u32[]{:S(2)}) %all-to-all-start.1) | async-done | bytes 131104 | tf_op jit(solution)/shard_map/all_to_all | solution.py:429
  57.7 0.7 %shard_map.199 = (f32[7,7,96]{2,1,0:T(8,128)}, f32[1,96]{1,0:T(1,128)}, f32[1,96]{1,0:T(1,128)}, f32[1,96]{1,0:T(1,128)}, f32[96,96]{1,0:T(8,128)}, /*index=5*/f...) custom-call(f32[8,32,128]{2,1,0:T(8,128)S(1)} %all-to-all-done.1.total_ref), custom_call_target="tpu_custom_call" | custom-call | bytes 225920 | tf_op jit(solution)/shard_map/pallas_call | solution.py:320
  (3 shorter events, 0.0 us)
Async XLA Ops:
  1.6 11.2 %copy-start.8 = (bf16[96,4,256]{2,1,0:T(4,128)(2,1)S(1)}, bf16[96,4,256]{2,1,0:T(4,128)(2,1)}, u32[]{:S(2)}) copy-start(bf16[96,4,256]{2,1,0:T(4,128)(2,1)} %param.12) | copy-start | bytes 589828
  1.8 6.9 %collective-permute-start.1 = (bf16[16,96]{1,0:T(8,128)(2,1)S(1)}, bf16[16,96]{1,0:T(8,128)(2,1)S(1)}, u32[]{:S(2)}, u32[]{:S(2)}) collective-permute-start(bf16[16,96]{1,0:T(8,128)(2,1)S(1)} %get-tuple-element.60), channel_id=1, source_target_pairs={{1,0},{2,1},{3,2},{5,4},{6,5},{7,6},{9,8},{10,9},{11,10},{13,12},{... | collective-permute-start | bytes 9224 | tf_op jit(solution)/shard_map/ppermute | solution.py:331
  3.1 6.9 %collective-permute-start = (bf16[16,96]{1,0:T(8,128)(2,1)S(1)}, bf16[16,96]{1,0:T(8,128)(2,1)S(1)}, u32[]{:S(2)}, u32[]{:S(2)}) collective-permute-start(bf16[16,96]{1,0:T(8,128)(2,1)S(1)} %get-tuple-element.61), channel_id=1, source_target_pairs={{0,1},{1,2},{2,3},{4,5},{5,6},{6,7},{8,9},{9,10},{10,11},{12,13},{... | collective-permute-start | bytes 9224 | tf_op jit(solution)/shard_map/ppermute | solution.py:331
  10.2 2.6 %copy-start.9 = (bf16[384]{0:T(512)(128)(2,1)S(1)}, bf16[384]{0:T(512)(128)(2,1)}, u32[]{:S(2)}) copy-start(bf16[384]{0:T(512)(128)(2,1)} %param.18) | copy-start | bytes 2308
  10.2 2.7 %collective-permute-start.2 = (bf16[3,96,384]{2,1,0:T(8,128)(2,1)S(1)}, bf16[3,96,384]{2,1,0:T(8,128)(2,1)S(1)}, u32[]{:S(2)}, u32[]{:S(2)}) collective-permute-start(bf16[3,96,384]{2,1,0:T(8,128)(2,1)S(1)} %get-tuple-element.30), channel_id=1, source_target_pairs={{0,4},{4,8},{8,12},{12,16},{16,20},{20,24},{24,28},{1,5},{5,9},{9,... | collective-permute-start | bytes 663560 | tf_op jit(solution)/shard_map/ppermute | solution.py:331
  11.5 5.5 %collective-permute-start.3 = (bf16[3,96,384]{2,1,0:T(8,128)(2,1)S(1)}, bf16[3,96,384]{2,1,0:T(8,128)(2,1)S(1)}, u32[]{:S(2)}, u32[]{:S(2)}) collective-permute-start(bf16[3,96,384]{2,1,0:T(8,128)(2,1)S(1)} %get-tuple-element.32), channel_id=1, source_target_pairs={{4,0},{8,4},{12,8},{16,12},{20,16},{24,20},{28,24},{5,1},{9,5},{13... | collective-permute-start | bytes 663560 | tf_op jit(solution)/shard_map/ppermute | solution.py:331
  12.8 4.2 %copy-start = (f32[96,7,7]{0,2,1:T(8,128)S(1)}, f32[96,7,7]{0,2,1:T(8,128)}, u32[]{:S(2)}) copy-start(f32[96,7,7]{0,2,1:T(8,128)} %param.13) | copy-start | bytes 56452
  12.8 4.2 %copy-start.1 = (bf16[384,96]{0,1:T(8,128)(2,1)S(1)}, bf16[384,96]{0,1:T(8,128)(2,1)}, u32[]{:S(2)}) copy-start(bf16[384,96]{0,1:T(8,128)(2,1)} %param.17) | copy-start | bytes 221188
  12.9 4.2 %copy-start.2 = (bf16[384,96]{0,1:T(8,128)(2,1)S(1)}, bf16[384,96]{0,1:T(8,128)(2,1)}, u32[]{:S(2)}) copy-start(bf16[384,96]{0,1:T(8,128)(2,1)} %param.19) | copy-start | bytes 221188
  17.0 0.7 %copy-start.6 = (f32[96]{0:T(128)S(1)}, f32[96]{0:T(128)}, u32[]{:S(2)}) copy-start(f32[96]{0:T(128)} %param.20) | copy-start | bytes 1156
  17.0 0.7 %copy-start.7 = (f32[96]{0:T(128)S(1)}, f32[96]{0:T(128)}, u32[]{:S(2)}) copy-start(f32[96]{0:T(128)} %param.21) | copy-start | bytes 1156
  17.0 0.7 %copy-start.3 = (f32[96]{0:T(128)S(1)}, f32[96]{0:T(128)}, u32[]{:S(2)}) copy-start(f32[96]{0:T(128)} %param.14) | copy-start | bytes 1156
  17.0 0.7 %copy-start.4 = (f32[96]{0:T(128)S(1)}, f32[96]{0:T(128)}, u32[]{:S(2)}) copy-start(f32[96]{0:T(128)} %param.15) | copy-start | bytes 1156
  17.0 0.7 %copy-start.5 = (f32[96]{0:T(128)S(1)}, f32[96]{0:T(128)}, u32[]{:S(2)}) copy-start(f32[96]{0:T(128)} %param.16) | copy-start | bytes 1156
  25.8 22.3 %all-to-all-start = ((bf16[32,48,128]{2,1,0:T(8,128)(2,1)}), bf16[32,48,128]{2,1,0:T(8,128)(2,1)S(1)}, u32[]{:S(2)}, u32[]{:S(2)}) async-start(bf16[32,48,128]{2,1,0:T(8,128)(2,1)} %get-tuple-element.37), calls=%async_computation | async-start | bytes 786432 | tf_op jit(solution)/shard_map/all_to_all | solution.py:423
  36.3 16.7 %collective-permute-start.4 = (bf16[3,96,256]{2,1,0:T(8,128)(2,1)S(1)}, bf16[3,96,256]{2,1,0:T(8,128)(2,1)S(1)}, u32[]{:S(2)}, u32[]{:S(2)}) collective-permute-start(bf16[3,96,256]{2,1,0:T(8,128)(2,1)S(1)} %get-tuple-element.34), channel_id=1, source_target_pairs={{0,4},{4,8},{8,12},{12,16},{16,20},{20,24},{24,28},{1,5},{5,9},{9,... | collective-permute-start | bytes 442376 | tf_op jit(solution)/shard_map/ppermute | solution.py:331
  38.5 14.6 %collective-permute-start.5 = (bf16[3,96,256]{2,1,0:T(8,128)(2,1)S(1)}, bf16[3,96,256]{2,1,0:T(8,128)(2,1)S(1)}, u32[]{:S(2)}, u32[]{:S(2)}) collective-permute-start(bf16[3,96,256]{2,1,0:T(8,128)(2,1)S(1)} %get-tuple-element.36), channel_id=1, source_target_pairs={{4,0},{8,4},{12,8},{16,12},{20,16},{24,20},{28,24},{5,1},{9,5},{13... | collective-permute-start | bytes 442376 | tf_op jit(solution)/shard_map/ppermute | solution.py:331
  48.8 8.9 %all-to-all-start.1 = ((f32[8,32,128]{2,1,0:T(8,128)}), f32[8,32,128]{2,1,0:T(8,128)S(1)}, u32[]{:S(2)}, u32[]{:S(2)}) async-start(f32[8,32,128]{2,1,0:T(8,128)} %get-tuple-element.39), calls=%async_computation.1 | async-start | bytes 262144 | tf_op jit(solution)/shard_map/all_to_all | solution.py:429

commit v2 on v1

v2 whole, which is shorter than its diff:
```python
import functools
import math

import jax
import jax.numpy as jnp
from jax import lax
from jax.experimental import pallas as pl
from jax.experimental.pallas import tpu as pltpu
from jax.sharding import Mesh, PartitionSpec as P

F32 = jnp.float32
BF16 = jnp.bfloat16
SIDE = 7
HALO = 3
LANES = 128
GROUP = 32
DEEP = SIDE * GROUP
NT = (((1,), (1,)), ((), ()))
VECTORS = ("dwb", "gain", "lnb", "rb", "scale")


def iota(shape, dim):
    return lax.broadcasted_iota(jnp.int32, shape, dim)


def dot(a, b, dims=(((1,), (0,)), ((), ()))):
    return lax.dot_general(a, b, dims, preferred_element_type=F32)


def column(row):
    n = row.shape[1]
    eye = iota((n, n), 0) == iota((n, n), 1)
    return jnp.sum(jnp.where(eye, row, 0.0), axis=1, keepdims=True)


def widened(value):
    fill = jnp.zeros((value.shape[0], LANES - value.shape[1]), value.dtype)
    return jnp.concatenate([value, fill], axis=1)


def edge_height(rows):
    return -(-HALO * rows // 16) * 16


def pack_edges(rows):
    width, high = rows[0].shape[1], edge_height(len(rows))
    q, j = iota((2 * high, width), 0), iota((2 * high, width), 1)
    total = None
    for i, row in enumerate(rows):
        last = (q == HALO * i + j - (width - HALO)) & (j >= width - HALO)
        first = (q == high + HALO * i + j) & (j < HALO)
        pick = jnp.where(last | first, 1.0, 0.0).astype(BF16)
        part = dot(pick, row, NT)
        total = part if total is None else total + part
    return total.astype(BF16)


def halo_tile(edges_t, i):
    high = edges_t.shape[1] // 2
    q, l = iota((2 * high, LANES), 0), iota((2 * high, LANES), 1)
    left = (q == HALO * i + l - (LANES - HALO)) & (l >= LANES - HALO)
    right = (q == high + HALO * i + l) & (l < HALO)
    pick = jnp.where(left | right, 1.0, 0.0).astype(BF16)
    return dot(edges_t, pick).astype(BF16)


def group_diagonal():
    lane = iota((1, DEEP), 1)
    inner = lane
    for b in range(1, SIDE):
        inner = jnp.where(lane >= b * GROUP, lane - b * GROUP, inner)
    return inner == iota((GROUP, DEEP), 0)


def tap_matrices(taps_ref, line_ref, w_ref, flip):
    diagonal = group_diagonal()
    for g in range(w_ref.shape[0]):
        for b in range(SIDE):
            piece = taps_ref[:, SIDE - 1 - b if flip else b, g * GROUP : (g + 1) * GROUP]
            line_ref[0:SIDE, b * GROUP : (b + 1) * GROUP] = piece
        for m in range(SIDE):
            a = m if flip else SIDE - 1 - m
            w_ref[g, m * GROUP : (m + 1) * GROUP, :] = jnp.where(diagonal, line_ref[a : a + 1, :], 0.0).astype(BF16)


def shifted(x, amount):
    return x if amount % x.shape[1] == 0 else pltpu.roll(x, amount % x.shape[1], 1)


def spread(xs_ref, r, x):
    channels = x.shape[0]
    width = xs_ref.shape[1]
    for b in range(SIDE):
        moved = shifted(x, HALO - b)[:, :width]
        for g in range(channels // GROUP):
            at = r * SIDE * channels + g * DEEP + b * GROUP
            xs_ref[at : at + GROUP, :] = moved[g * GROUP : (g + 1) * GROUP]


def depthwise(w_ref, xs_ref, acc_ref, rows):
    groups = w_ref.shape[0]
    channels = groups * GROUP
    for g in range(groups):
        sums = [None] * rows
        for r in range(rows + 2 * HALO):
            i0, i1 = max(0, r - (SIDE - 1)), min(rows - 1, r)
            m0 = SIDE - 1 - r + i0
            at = r * SIDE * channels + g * DEEP
            part = dot(w_ref[g, m0 * GROUP : (m0 + i1 - i0 + 1) * GROUP, :], xs_ref[at : at + DEEP, :])
            for i in range(i0, i1 + 1):
                piece = part[(i - i0) * GROUP : (i - i0 + 1) * GROUP]
                sums[i] = piece if sums[i] is None else sums[i] + piece
        for i in range(rows):
            at = i * channels + g * GROUP
            acc_ref[at : at + GROUP, :] = sums[i]


def enter_kernel(core_axis, image_ref, mid_ref, pair_ref, far_ref):
    rows = mid_ref.shape[0]
    core = lax.axis_index(core_axis)
    for i in range(rows):
        mid_ref[i] = image_ref[:, i, :]
    for k in range(HALO):
        pair_ref[k] = mid_ref[k + (rows - HALO) * (1 - core)]
        far_ref[k] = mid_ref[k + (rows - HALO) * core]


def prepare_kernel(
    cot_ref, taps_ref, dwb_ref, gain_ref, lnb_ref, we_ref, be_ref, wr_ref, br_ref, scale_ref,
    cot_t_ref, forward_ref, backward_ref, we2_ref, wr2_ref, columns_ref, lift_ref, line_ref,
):
    for i in range(cot_t_ref.shape[0]):
        cot_t_ref[i] = cot_ref[:, i, :]
    tap_matrices(taps_ref, line_ref, forward_ref, False)
    tap_matrices(taps_ref, line_ref, backward_ref, True)
    channels, hidden_n = we_ref.shape
    extra = lift_ref.shape[0] - channels
    lift_ref[0:channels, :] = we_ref[...]
    lift_ref[channels:, :] = jnp.where(iota((extra, hidden_n), 0) == 0, be_ref[...].astype(F32), 0.0).astype(BF16)
    we2_ref[...] = lift_ref[...].T
    wr2_ref[...] = wr_ref[...].T
    lane = iota(columns_ref.shape, 1)
    total = jnp.zeros(columns_ref.shape, F32)
    for k, ref in enumerate((dwb_ref, gain_ref, lnb_ref, br_ref, scale_ref)):
        total = jnp.where(lane == k, column(ref[...]), total)
    columns_ref[...] = total


def gather_kernel(axes, mid_ref, pair_ref, far_ref, tall_ref, first_ref, second_ref):
    rows = mid_ref.shape[0]
    upper = lax.axis_index(axes[1]) == 0
    for k in range(HALO):
        pair, far = pair_ref[k], far_ref[k]
        tall_ref[k] = jnp.where(upper, far, pair)
        tall_ref[HALO + rows + k] = jnp.where(upper, pair, far)
    for i in range(rows):
        tall_ref[HALO + i] = mid_ref[i]
    edges = pack_edges([tall_ref[r] for r in range(rows + 2 * HALO)])
    high = edges.shape[0] // 2
    even = lax.rem(lax.axis_index(axes[2]), 2) == 0
    first_ref[...] = jnp.where(even, edges[:high], edges[high:])
    second_ref[...] = jnp.where(even, edges[high:], edges[:high])


def gelu_parts(v):
    z = jnp.abs(v)
    t = 1.0 / (1.0 + (0.3275911 / math.sqrt(2.0)) * z)
    e = jnp.exp(-0.5 * (v * v))
    half = 0.5
    poly = t * (
        half * 0.254829592
        + t * (half * -0.284496736 + t * (half * 1.421413741 + t * (half * -1.453152027 + t * (half * 1.061405429))))
    )
    tail = poly * e
    return jnp.where(v >= 0.0, 1.0 - tail, tail), (v * (1.0 / math.sqrt(2.0 * math.pi))) * e


def main_kernel(
    direct, axes,
    tall_ref, first_ref, second_ref, cot_ref, w_ref, we_ref, wr_ref, we2_ref, wr2_ref, columns_ref, scale_ref,
    out_ref, dconv_ref, far_ref, share_ref, edges_ref, *rest,
):
    if direct:
        (keep_ref, *scratch) = rest
    else:
        (grads_ref, small_out_ref, *scratch) = rest
    xs_ref, acc_ref, xhat_ref, nm_ref, db_ref, act_ref, dh_ref, wide_ref, dcs_ref, line_ref, small_ref = scratch
    rows, channels, width = cot_ref.shape
    groups = channels // GROUP
    hidden_n = we_ref.shape[1]
    extent = width + LANES
    core = lax.axis_index(axes[1])
    even = lax.rem(lax.axis_index(axes[2]), 2) == 0
    dwb, gain, lnb, br, scale = (columns_ref[:, k : k + 1] for k in range(5))
    first, second = first_ref[...], second_ref[...]
    edges_t = jnp.concatenate([jnp.where(even, second, first), jnp.where(even, first, second)], axis=0).T
    for r in range(rows + 2 * HALO):
        x = jnp.concatenate([tall_ref[r], halo_tile(edges_t, r)], axis=1)
        spread(xs_ref, r, x)
        for i in range(rows):
            if 0 <= r - i < SIDE:
                for g in range(groups):
                    at = g * DEEP + (r - i) * GROUP
                    wide_ref[at : at + GROUP, i * extent : (i + 1) * extent] = x[g * GROUP : (g + 1) * GROUP]
    depthwise(w_ref, xs_ref, acc_ref, rows)
    extra = nm_ref.shape[0] - channels
    nm_ref[channels:, :] = jnp.where(iota((extra, rows * width), 0) == 0, 1.0, 0.0).astype(BF16)
    zero = jnp.zeros((channels, LANES), F32)
    sums = {k: zero for k in VECTORS}

    def add(name, value):
        for k in range(0, width, LANES):
            sums[name] = sums[name] + value[:, k : k + LANES]

    chunk = 128
    dconv_rows = []
    for i in range(rows):
        cols = slice(i * width, (i + 1) * width)
        conv = acc_ref[i * channels : (i + 1) * channels, :] + dwb
        conv = conv - jnp.mean(conv, axis=0, keepdims=True)
        inv = lax.rsqrt(jnp.mean(conv * conv, axis=0, keepdims=True) + 1e-6)
        xhat = conv * inv
        xhat_ref[...] = xhat
        nm_ref[0:channels, cols] = (xhat * gain + lnb).astype(BF16)
        cot = cot_ref[i].astype(F32)
        add("rb", cot)
        db_ref[:, cols] = (cot * scale).astype(BF16)
        for h0 in range(0, hidden_n, chunk):
            hs = slice(h0, h0 + chunk)
            hidden = dot(we2_ref[hs, :], nm_ref[:, cols])
            back = dot(wr2_ref[hs, :], db_ref[:, cols])
            phi, bump = gelu_parts(hidden)
            act_ref[hs, cols] = (hidden * phi).astype(BF16)
            dh_ref[hs, cols] = (back * (phi + bump)).astype(BF16)
        branch = dot(wr_ref[...], act_ref[:, cols]) + br
        out_ref[i] = (tall_ref[HALO + i].astype(F32) + scale * branch).astype(BF16)
        add("scale", cot * branch)
        d_normed = dot(we_ref[...], dh_ref[:, cols])
        xhat = xhat_ref[...]
        add("lnb", d_normed)
        add("gain", d_normed * xhat)
        d_xhat = d_normed * gain
        m1 = jnp.mean(d_xhat, axis=0, keepdims=True)
        m2 = jnp.mean(d_xhat * xhat, axis=0, keepdims=True)
        dconv = (inv * (d_xhat - m1 - xhat * m2)).astype(BF16)
        add("dwb", dconv.astype(F32))
        dconv_ref[i] = dconv
        dconv_rows.append(dconv)
        padded = jnp.concatenate([dconv, jnp.zeros((channels, LANES), BF16)], axis=1)
        for b in range(SIDE):
            moved = shifted(padded, b - HALO)
            for g in range(groups):
                at = g * DEEP + b * GROUP
                dcs_ref[at : at + GROUP, i * extent : (i + 1) * extent] = moved[g * GROUP : (g + 1) * GROUP]
    for k in range(HALO):
        pair = dconv_ref[k + (rows - HALO) * (1 - core)]
        far_ref[k] = dconv_ref[k + (rows - HALO) * core]
        for p in range(width // LANES):
            at = (k * (width // LANES) + p) * channels
            share_ref[at : at + channels, :] = pair[:, p * LANES : (p + 1) * LANES]
    edges_ref[...] = widened(pack_edges(dconv_rows))
    g_reduce = widened(dot(act_ref[...], db_ref[...], NT))
    g_expand = widened(dot(dh_ref[...], nm_ref[...], NT))
    small_ref[...] = jnp.zeros_like(small_ref)
    diagonal = group_diagonal()
    for g in range(groups):
        taps = dot(wide_ref[g * DEEP : (g + 1) * DEEP, :], dcs_ref[g * DEEP : (g + 1) * DEEP, :], NT)
        for a in range(SIDE):
            part = jnp.where(diagonal, taps[a * GROUP : (a + 1) * GROUP, :], 0.0)
            line_ref[a : a + 1, :] = jnp.sum(part, axis=0, keepdims=True)
        for b in range(SIDE):
            small_ref[b * 8 : b * 8 + SIDE, g * GROUP : (g + 1) * GROUP] = line_ref[0:SIDE, b * GROUP : (b + 1) * GROUP]
    for b, name in enumerate(VECTORS):
        total = jnp.sum(sums[name].T, axis=0, keepdims=True)
        small_ref[b * 8 + SIDE : b * 8 + 8, 0:channels] = total * scale_ref[...] if name == "rb" else total
    if not direct:
        grads_ref[0] = g_reduce
        grads_ref[1] = g_expand
        small_out_ref[...] = small_ref[...]
        return
    half = small_ref.shape[0] // 2
    low, high = small_ref[0:half, :], small_ref[half:, :]
    lead = HALO * (width // LANES) * channels
    keep_ref[0:hidden_n, :] = jnp.where(core == 0, g_reduce, g_expand)
    keep_ref[hidden_n:, :] = jnp.where(core == 0, low, high)
    share_ref[lead : lead + hidden_n, :] = jnp.where(core == 0, g_expand, g_reduce).astype(BF16)
    share_ref[lead + hidden_n :, :] = jnp.where(core == 0, high, low).astype(BF16)


def block_kernel(sizes, filt_axis, share_ref, keep_ref, edges_ref, block_ref):
    chips, filt = sizes
    me = lax.axis_index(filt_axis)
    count = keep_ref.shape[0]
    lead = share_ref.shape[0] - count
    total = keep_ref[...] + share_ref[lead:, :].astype(F32)
    edges = edges_ref[...]
    high = edges.shape[0] // 2
    hidden_n = count - 8 * chips
    step = hidden_n // (filt * chips)
    for f in range(filt):
        edge = jnp.where(f > me, edges[:high], edges[high:])
        for q in range(chips):
            at = (f * chips + q) * step
            low = hidden_n + 8 * q
            head = jnp.concatenate([total[at : at + step], total[low : low + 8]], axis=0)
            block_ref[q * filt + f, 0 : step + 8, :] = head.astype(BF16)
            block_ref[q * filt + f, step + 8 :, :] = edge


def sum_kernel(axes, sizes, block_ref, total_ref, edges_ref):
    chips, filt = sizes
    head = total_ref.shape[1]
    total = block_ref[0, :head, :].astype(F32)
    for d in range(1, block_ref.shape[0]):
        total = total + block_ref[d, :head, :].astype(F32)
    total = total.astype(BF16)
    for s in range(total_ref.shape[0]):
        total_ref[s] = total
    q, core, f = (lax.axis_index(a) for a in axes)
    high = edges_ref.shape[0] // 4
    for k, chip in enumerate((q, q + 1 - 2 * core)):
        for side in range(2):
            ff = f + 2 * side - 1
            inside = (chip >= 0) & (chip < chips) & (ff >= 0) & (ff < filt)
            at = jnp.clip(chip, 0, chips - 1) * filt + jnp.clip(ff, 0, filt - 1)
            value = block_ref[at, head:, :]
            low = (2 * k + side) * high
            edges_ref[low : low + high, :] = jnp.where(inside, value, jnp.zeros_like(value))


def back_kernel(core_axis, share_ref, far_ref, mid_ref, own_ref, other_ref, cot_ref, w_ref, out_ref, xs_ref, acc_ref):
    rows, channels, width = cot_ref.shape
    upper = lax.axis_index(core_axis) == 0
    high = own_ref.shape[0] // 2
    near, beyond = other_ref[:high, 0:channels], other_ref[high:, 0:channels]
    edges = (jnp.where(upper, beyond, near).T, own_ref[:high, 0:channels].T, jnp.where(upper, near, beyond).T)
    parts = width // LANES
    for k in range(HALO):
        pair = [share_ref[(k * parts + p) * channels : (k * parts + p + 1) * channels, :] for p in range(parts)]
        pair = jnp.concatenate(pair, axis=1)
        far = far_ref[k]
        up, down = jnp.where(upper, far, pair), jnp.where(upper, pair, far)
        spread(xs_ref, k, jnp.concatenate([up, halo_tile(edges[0], rows - HALO + k)], axis=1))
        spread(xs_ref, HALO + rows + k, jnp.concatenate([down, halo_tile(edges[2], k)], axis=1))
    for i in range(rows):
        spread(xs_ref, HALO + i, jnp.concatenate([mid_ref[i], halo_tile(edges[1], i)], axis=1))
    depthwise(w_ref, xs_ref, acc_ref, rows)
    for i in range(rows):
        out_ref[i] = (cot_ref[i].astype(F32) + acc_ref[i * channels : (i + 1) * channels, :]).astype(BF16)


def finish_kernel(factor, total_ref, kg_ref, dwb_ref, gain_ref, lnb_ref, ge_ref, eb_ref, gr_ref, rb_ref, sc_ref):
    channels = kg_ref.shape[2]
    chips = total_ref.shape[0] // 2
    step = total_ref.shape[1] - 8
    vectors = (dwb_ref, gain_ref, lnb_ref, rb_ref, sc_ref)
    for s in range(2 * chips):
        q, core = s // 2, s % 2
        part = total_ref[s].astype(F32) * factor
        b = core * chips + q
        if b < SIDE:
            kg_ref[:, b, :] = part[step : step + SIDE, 0:channels]
        if b < len(vectors):
            vectors[b][...] = part[step + SIDE :, 0:channels]
        if core == 0:
            gr_ref[q * step : (q + 1) * step, :] = part[0:step, 0:channels]
        else:
            ge_ref[q * step : (q + 1) * step, :] = part[0:step, 0:channels]
            eye = iota((step, chips * step), 0) + q * step == iota((step, chips * step), 1)
            line = jnp.sum(jnp.where(eye, part[0:step, channels : channels + 1], 0.0), axis=0, keepdims=True)
            eb_ref[...] = line if q == 0 else eb_ref[...] + line


def call(kernel, outs, *args, scratch=(), flops=0):
    size = sum(math.prod(a.shape) * a.dtype.itemsize for a in args)
    size += sum(math.prod(s) * jnp.dtype(d).itemsize for s, d in outs)
    return pl.pallas_call(
        kernel,
        out_shape=[jax.ShapeDtypeStruct(s, d) for s, d in outs],
        scratch_shapes=[pltpu.VMEM(s, d) for s, d in scratch],
        compiler_params=pltpu.CompilerParams(vmem_limit_bytes=40 * 2**20),
        cost_estimate=pl.CostEstimate(flops=flops, bytes_accessed=size, transcendentals=0),
    )(*args)


def swap(x, axis, parity):
    size = lax.axis_size(axis)
    pairs = [(i, i + 1) for i in range(parity, size - 1, 2)]
    return lax.ppermute(x, axis, pairs + [(j, i) for i, j in pairs])


def moved(x, axis, step):
    size = lax.axis_size(axis)
    return lax.ppermute(x, axis, [(i, i + step) for i in range(size) if 0 <= i + step < size])


def shards(
    axes, image, cotangent, kernel, dw_bias, layer_norm_gain, layer_norm_bias,
    w_expand, b_expand, w_reduce, b_reduce, layer_scale,
):
    chip, core, filt = axes
    space = (chip, core)
    chip_n, filt_n = lax.axis_size(chip), lax.axis_size(filt)
    channels, rows, width = image.shape
    hidden_n = w_expand.shape[0]
    groups = channels // GROUP
    panel = hidden_n // filt_n
    tall = rows + 2 * HALO
    deep = SIDE * channels
    extent = width + LANES
    tokens = rows * width
    lift = channels + 16
    direct = chip_n == 4
    pieces = 8
    step = 2 * panel // pieces
    strip = ((HALO, channels, width), BF16)
    block = ((rows, channels, width), BF16)
    row = lambda v: v.reshape(1, -1)

    mid, pair, far = call(functools.partial(enter_kernel, core), [block, strip, strip], image)
    far = swap(far, space, 1)
    pair = swap(pair, core, 0)
    we_t, wr_t = w_expand.T, w_reduce.T
    cot_t, forward, backward, we2, wr2, columns = call(
        prepare_kernel,
        [
            block,
            ((groups, DEEP, DEEP), BF16),
            ((groups, DEEP, DEEP), BF16),
            ((hidden_n, lift), BF16),
            ((hidden_n, channels), BF16),
            ((channels, LANES), F32),
        ],
        cotangent, jnp.transpose(kernel, (1, 2, 0)), row(dw_bias), row(layer_norm_gain), row(layer_norm_bias),
        we_t, row(b_expand), wr_t, row(b_reduce), row(layer_scale),
        scratch=[((lift, hidden_n), BF16), ((8, DEEP), F32)],
    )
    edge = ((edge_height(tall), channels), BF16)
    image_t, first, second = call(
        functools.partial(gather_kernel, axes), [((tall, channels, width), BF16), edge, edge], mid, pair, far
    )
    first = swap(first, filt, 0)
    second = swap(second, filt, 1)
    lead = HALO * channels * (width // LANES)
    half = pieces * 8 // 2
    high = edge_height(rows)
    outs = [block, block, strip]
    if direct:
        outs += [((lead + hidden_n + half, LANES), BF16), ((2 * high, LANES), BF16), ((hidden_n + half, LANES), F32)]
    else:
        outs += [((lead, LANES), BF16), ((2 * high, LANES), BF16)]
        outs += [((2, hidden_n, LANES), F32), ((2 * half, LANES), F32)]
    out_t, dconv, far, share, edges, *rest = call(
        functools.partial(main_kernel, direct, axes),
        outs,
        image_t, first, second, cot_t, forward, we_t, wr_t, we2, wr2, columns, row(layer_scale),
        scratch=[
            ((tall * deep, width), BF16),
            ((rows * channels, width), F32),
            ((channels, width), F32),
            ((lift, tokens), BF16),
            ((channels, tokens), BF16),
            ((hidden_n, tokens), BF16),
            ((hidden_n, tokens), BF16),
            ((deep, rows * extent), BF16),
            ((deep, rows * extent), BF16),
            ((8, DEEP), F32),
            ((2 * half, LANES), F32),
        ],
    )
    share = swap(share, core, 0)
    far = swap(far, space, 1)
    if direct:
        (blocks,) = call(
            functools.partial(block_kernel, (chip_n, filt_n), filt),
            [((chip_n * filt_n, step + 8 + high, LANES), BF16)],
            share, *rest, edges,
        )
        blocks = lax.all_to_all(blocks, (chip, filt), 0, 0, tiled=True)
        total, edges = call(
            functools.partial(sum_kernel, axes, (chip_n, filt_n)),
            [((pieces, step + 8, LANES), BF16), ((4 * high, LANES), BF16)],
            blocks,
        )
        other = swap(edges, core, 0)
        total = lax.all_to_all(total, space, 0, 0, tiled=True)
    else:
        grads, small = rest
        edges = jnp.concatenate([moved(edges[:high], filt, 1), moved(edges[high:], filt, -1)], axis=0)
        above, below = moved(edges, space, 1), moved(edges, space, -1)
        upper = lax.axis_index(core) == 0
        other = jnp.concatenate([jnp.where(upper, below, above), jnp.where(upper, above, below)], axis=0)
        edges = jnp.concatenate([edges, edges], axis=0)
        grads, small = lax.psum((grads, small), axes)
        grads = lax.dynamic_slice_in_dim(grads, lax.axis_index(filt) * panel, panel, 1)
        grads = grads.reshape(2, pieces // 2, step, LANES).swapaxes(0, 1).reshape(pieces, step, LANES)
        small = small.reshape(2, pieces // 2, 8, LANES).swapaxes(0, 1).reshape(pieces, 8, LANES)
        total = jnp.concatenate([grads, small], axis=1)
    (back_t,) = call(
        functools.partial(back_kernel, core),
        [block],
        share, far, dconv, edges, other, cot_t, backward,
        scratch=[((tall * deep, width), BF16), ((rows * channels, width), F32)],
    )
    factor = 1.0 / math.sqrt(tokens * chip_n * lax.axis_size(core) * filt_n)
    line = ((1, channels), F32)
    matrix = ((panel, channels), F32)
    kg, dwb, gain, lnb, ge, eb, gr, rb, sc = call(
        functools.partial(finish_kernel, factor),
        [((SIDE, SIDE, channels), F32), line, line, line, matrix, ((1, panel), F32), matrix, line, line],
        total,
    )
    flat = lambda v: v.reshape(-1)
    swapped = lambda v: jnp.transpose(v, (1, 0, 2))
    return (
        swapped(out_t), swapped(back_t), jnp.transpose(kg, (2, 0, 1)),
        flat(dwb), flat(gain), flat(lnb), ge, flat(eb), gr, flat(rb), flat(sc),
    )


def solution(mesh):
    space, filt = mesh.devices.shape
    axes = ("chip", "core", "filt")
    pairs = Mesh(mesh.devices.reshape(space // 2, 2, filt), axes)
    pixels = P(None, ("chip", "core"), "filt")
    whole, shard = P(), P("filt")
    return jax.shard_map(
        functools.partial(shards, axes),
        mesh=pairs,
        in_specs=(pixels, pixels) + (whole,) * 9,
        out_specs=(pixels, pixels, whole, whole, whole, whole, shard, shard, shard, whole, whole),
        check_vma=False,
    )
```

time: 58.9 us -> 51.4 us (0.87)
  waiting for transfers between devices: 16 us -> 11.6 us
  Pallas kernels: 11.5 us -> 10 us
  starting transfers between devices: 26.8 us -> 25.3 us
    ppermute x6 -> x7, waiting for transfers between devices: 5.42 us -> 1.51 us  [swap(): return lax.ppermute(x, axis, pairs + [(j, i) for i, j in pairs])]
    pallas_call x6 -> x8, Pallas kernels: 11.5 us -> 10 us  [call(): pl.pallas_call(kernel, out_shape=[jax.ShapeDtypeStruct(s, d) for s, d in...]
    all_to_all x2, starting transfers between devices: 13.8 us -> 12.5 us  [the longest x1 9.11 us: shards(): blocks = lax.all_to_all(blocks, (chip, filt), 0, 0, tiled=True)]
    ppermute x6 -> x7, starting transfers between devices: 12.9 us -> 12.8 us  [swap(): return lax.ppermute(x, axis, pairs + [(j, i) for i, j in pairs])]
  transfers between devices with their start and end apart: 8 -> 9, of which waited for: 4 -> 4; matrix products, arithmetic and copies ran while one was open for 3% -> 3% of each run, Pallas kernels for 4% -> 6%
where the time goes in v2:
time: 51.4 us; the launch traced here: 51 us
  starting transfers between devices  25.3 us (49%)
  waiting for transfers between devices  11.6 us (23%)
  Pallas kernels  10 us (19%)
  local copies, waits for them, and re-layouts  3.25 us (6%)
  between operations  0.84 us (2%)
    ppermute x7, starting transfers between devices, swap(): return lax.ppermute(x, axis, pairs + [(j, i) for i, j in pairs])  12.8 us
    pallas_call x8, Pallas kernels, call(): pl.pallas_call(kernel, out_shape=[jax.ShapeDtypeStruct(s, d) for s, d in...  10 us
    all_to_all x1, starting transfers between devices, shards(): blocks = lax.all_to_all(blocks, (chip, filt), 0, 0, tiled=True)  9.11 us
    all_to_all x1, waiting for transfers between devices, shards(): blocks = lax.all_to_all(blocks, (chip, filt), 0, 0, tiled=True)  8.79 us
    all_to_all x1, starting transfers between devices, shards(): total = lax.all_to_all(total, space, 0, 0, tiled=True)  3.35 us
    unnamed x24, local copies, waits for them, and re-layouts  3.24 us
    ppermute x7, waiting for transfers between devices, swap(): return lax.ppermute(x, axis, pairs + [(j, i) for i, j in pairs])  1.51 us
    all_to_all x1, waiting for transfers between devices, shards(): total = lax.all_to_all(total, space, 0, 0, tiled=True)  1.31 us
  transfers between devices with their start and end apart: 9, of which 4 were waited for; matrix products, arithmetic and copies ran while one was open for 3% of the time, Pallas kernels for 6%

profile of v2, /device:TPU:0, one launch (start us, length us, event | category | flops | bytes accessed | tf_op | source)
XLA Modules:
  0.0 51.0 jit_solution(7252347544551286108)
XLA Ops:
  0.6 0.0 copy-start.2
  0.7 0.9 %copy-done.2 = bf16[96,4,256]{2,1,0:T(4,128)(2,1)S(1)} copy-done((bf16[96,4,256]{2,1,0:T(4,128)(2,1)S(1)}, bf16[96,4,256]{2,1,0:T(4,128)(2,1)}, u32[]{:S(2)}) %copy-start.2) | copy-done | bytes 196632
  1.6 0.4 shard_map.194
  2.0 0.5 %collective-permute-start = (bf16[3,96,256]{2,1,0:T(8,128)(2,1)S(1)}, bf16[3,96,256]{2,1,0:T(8,128)(2,1)S(1)}, u32[]{:S(2)}, u32[]{:S(2)}) collective-permute-start(bf16[3,96,256]{2,1,0:T(8,128)(2,1)S(1)} %get-tuple-element.41), channel_id=1, source_target_pairs={{0,4},{4,0},{1,5},{5,1},{2,6},{6,2},{3,7},{7,3},{8,12},{12,8},{9,1... | collective-permute-start | bytes 442376 | tf_op jit(solution)/shard_map/ppermute | solution.py:389
  2.5 0.7 %collective-permute-start.1 = (bf16[3,96,256]{2,1,0:T(8,128)(2,1)S(1)}, bf16[3,96,256]{2,1,0:T(8,128)(2,1)S(1)}, u32[]{:S(2)}, u32[]{:S(2)}) collective-permute-start(bf16[3,96,256]{2,1,0:T(8,128)(2,1)S(1)} %get-tuple-element.42), channel_id=1, source_target_pairs={{4,8},{12,16},{20,24},{8,4},{16,12},{24,20},{5,9},{13,17},{21,25},... | collective-permute-start | bytes 442376 | tf_op jit(solution)/shard_map/ppermute | solution.py:389
  3.2 0.3 collective-permute-done.pair_ref
  3.5 0.0 collective-permute-done.1.far_ref
  3.6 0.0 copy-start
  3.6 0.0 copy-start.1
  3.6 0.0 copy-start.3
  3.6 0.0 copy-start.4
  3.6 0.3 shard_map.195
  3.9 0.0 copy-start.10
  3.9 3.0 %collective-permute-start.2 = (bf16[32,96]{1,0:T(8,128)(2,1)S(1)}, bf16[32,96]{1,0:T(8,128)(2,1)S(1)}, u32[]{:S(2)}, u32[]{:S(2)}) collective-permute-start(bf16[32,96]{1,0:T(8,128)(2,1)S(1)} %get-tuple-element.44), channel_id=1, source_target_pairs={{0,1},{2,3},{1,0},{3,2},{4,5},{6,7},{5,4},{7,6},{8,9},{10,11},{9,8... | collective-permute-start | bytes 18440 | tf_op jit(solution)/shard_map/ppermute | solution.py:389
  6.9 0.6 %collective-permute-start.3 = (bf16[32,96]{1,0:T(8,128)(2,1)S(1)}, bf16[32,96]{1,0:T(8,128)(2,1)S(1)}, u32[]{:S(2)}, u32[]{:S(2)}) collective-permute-start(bf16[32,96]{1,0:T(8,128)(2,1)S(1)} %get-tuple-element.45), channel_id=1, source_target_pairs={{1,2},{2,1},{5,6},{6,5},{9,10},{10,9},{13,14},{14,13},{17,18},{18,... | collective-permute-start | bytes 18440 | tf_op jit(solution)/shard_map/ppermute | solution.py:389
  7.5 0.0 copy-done.10
  7.6 0.0 copy-start.8
  7.6 0.0 copy-start.9
  7.6 0.0 copy-start.5
  7.6 0.0 copy-start.6
  7.6 0.0 copy-start.7
  7.6 0.0 copy-done
  7.6 0.0 copy-done.1
  7.6 0.0 copy-done.3
  7.7 0.0 copy-done.4
  7.7 0.6 %copy-done.8 = f32[96]{0:T(128)S(1)} copy-done((f32[96]{0:T(128)S(1)}, f32[96]{0:T(128)}, u32[]{:S(2)}) %copy-start.8) | copy-done | bytes 408
  8.2 0.0 copy-done.9
  8.2 0.0 copy-done.5
  8.3 0.0 copy-done.6
  8.3 0.0 copy-done.7
  8.3 0.7 %shard_map.196 = (bf16[4,96,256]{2,1,0:T(8,128)(2,1)S(1)}, bf16[3,224,224]{2,1,0:T(8,128)(2,1)S(1)}, bf16[3,224,224]{2,1,0:T(8,128)(2,1)S(1)}, bf16[384,112]{1,0...) custom-call(bf16[96,4,256]{2,1,0:T(4,128)(2,1)S(1)} %copy-done.3, f32[7,7,96]{2,1,0:T(8,128)S(1)} %bitcast.23, ...), custom_call_target="tpu_custom_call" | custom-call | bytes 1373184 | tf_op jit(solution)/shard_map/pallas_call | solution.py:377
  9.0 0.0 collective-permute-done.2.first_ref
  9.0 0.0 collective-permute-done.3.second_ref
  9.0 5.0 %shard_map.197 = (bf16[4,96,256]{2,1,0:T(8,128)(2,1)S(1)}, bf16[4,96,256]{2,1,0:T(8,128)(2,1)S(1)}, bf16[3,96,256]{2,1,0:T(8,128)(2,1)S(1)}, bf16[992,128]{1,0:T...) custom-call(bf16[10,96,256]{2,1,0:T(8,128)(2,1)S(1)} %get-tuple-element.43.tall_ref, ...), custom_call_target="tpu_custom_call" | custom-call | bytes 2374016 | tf_op jit(solution)/shard_map/pallas_call | solution.py:377
  14.0 6.9 %collective-permute-start.4 = (bf16[992,128]{1,0:T(8,128)(2,1)S(1)}, bf16[992,128]{1,0:T(8,128)(2,1)S(1)}, u32[]{:S(2)}, u32[]{:S(2)}) collective-permute-start(bf16[992,128]{1,0:T(8,128)(2,1)S(1)} %get-tuple-element.52), channel_id=1, source_target_pairs={{0,4},{4,0},{1,5},{5,1},{2,6},{6,2},{3,7},{7,3},{8,12},{12,8},{9,1... | collective-permute-start | bytes 761864 | tf_op jit(solution)/shard_map/ppermute | solution.py:389
  20.9 1.2 %collective-permute-done.4.share_ref = bf16[992,128]{1,0:T(8,128)(2,1)S(1)} collective-permute-done((bf16[992,128]{1,0:T(8,128)(2,1)S(1)}, bf16[992,128]{1,0:T(8,128)(2,1)S(1)}, u32[]{:S(2)}, u32[]{:S(2)}) %collective-permute-start.4) | collective-permute-done | bytes 253984 | tf_op jit(solution)/shard_map/ppermute | solution.py:389
  22.1 0.7 %shard_map.198 = bf16[16,48,128]{2,1,0:T(8,128)(2,1)} custom-call(bf16[992,128]{1,0:T(8,128)(2,1)S(1)} %collective-permute-done.4.share_ref, f32[416,128]{1,0:T(8,128)S(1)} %get-tuple-element.55.keep_ref, bf16[32,128]{1,0:T(8,128)(2,1)S(1)} %get-tuple-element.56.edges_ref), custom_call_target="tpu_custom_call" | custom-call | bytes 671744 | tf_op jit(solution)/shard_map/pallas_call | solution.py:377
  22.8 9.1 %all-to-all-start = ((bf16[16,48,128]{2,1,0:T(8,128)(2,1)}), bf16[16,48,128]{2,1,0:T(8,128)(2,1)S(1)}, u32[]{:S(2)}, u32[]{:S(2)}) async-start(bf16[16,48,128]{2,1,0:T(8,128)(2,1)} %shard_map.198), calls=%async_computation | async-start | bytes 393216 | tf_op jit(solution)/shard_map/all_to_all | solution.py:479
  31.9 0.7 %collective-permute-start.5 = (bf16[3,96,256]{2,1,0:T(8,128)(2,1)S(1)}, bf16[3,96,256]{2,1,0:T(8,128)(2,1)S(1)}, u32[]{:S(2)}, u32[]{:S(2)}) collective-permute-start(bf16[3,96,256]{2,1,0:T(8,128)(2,1)S(1)} %get-tuple-element.53), channel_id=1, source_target_pairs={{4,8},{12,16},{20,24},{8,4},{16,12},{24,20},{5,9},{13,17},{21,25},... | collective-permute-start | bytes 442376 | tf_op jit(solution)/shard_map/ppermute | solution.py:389
  32.6 8.8 %all-to-all-done.block_ref = bf16[16,48,128]{2,1,0:T(8,128)(2,1)S(1)} async-done(((bf16[16,48,128]{2,1,0:T(8,128)(2,1)}), bf16[16,48,128]{2,1,0:T(8,128)(2,1)S(1)}, u32[]{:S(2)}, u32[]{:S(2)}) %all-to-all-start) | async-done | bytes 196640 | tf_op jit(solution)/shard_map/all_to_all | solution.py:479
  41.4 0.6 %shard_map.199 = (bf16[8,32,128]{2,1,0:T(8,128)(2,1)}, bf16[64,128]{1,0:T(8,128)(2,1)S(1)}) custom-call(bf16[16,48,128]{2,1,0:T(8,128)(2,1)S(1)} %all-to-all-done.block_ref), custom_call_target="tpu_custom_call" | custom-call | bytes 278528 | tf_op jit(solution)/shard_map/pallas_call | solution.py:377
  42.0 3.3 %all-to-all-start.1 = ((bf16[8,32,128]{2,1,0:T(8,128)(2,1)}), bf16[8,32,128]{2,1,0:T(8,128)(2,1)S(1)}, u32[]{:S(2)}, u32[]{:S(2)}) async-start(bf16[8,32,128]{2,1,0:T(8,128)(2,1)} %get-tuple-element.59), calls=%async_computation.1 | async-start | bytes 131072 | tf_op jit(solution)/shard_map/all_to_all | solution.py:486
  45.4 0.4 collective-permute-start.6
  45.8 0.8 %copy.22 = bf16[96,4,256]{2,1,0:T(4,128)(2,1)} copy(bf16[96,4,256]{2,0,1:T(8,128)(2,1)S(1)} %bitcast.22) | data formatting | bytes 393216
  46.6 0.0 collective-permute-done.5.far_ref
  46.6 0.0 collective-permute-done.6.other_ref
  46.6 1.6 %shard_map.200 = bf16[4,96,256]{2,1,0:T(8,128)(2,1)S(1)} custom-call(bf16[992,128]{1,0:T(8,128)(2,1)S(1)} %collective-permute-done.4.share_ref, bf16[3,96,256]{2,1,0:T(8,128)(2,1)S(1)} %collective-permute-done.5.far_ref, bf16[4,96,256]{2,1,0:T(8,128)(2,1)S(1)} %get-tuple-element.54.mid_ref, bf16[64,128]{1,0:T(8,128)(2,1)S(1)} %get-tuple-element.57.own_ref, ...), custom_call_target="tpu_custom_call" | custom-call | bytes 1325056 | tf_op jit(solution)/shard_map/pallas_call | solution.py:377
  48.2 0.8 %copy.23 = bf16[96,4,256]{2,1,0:T(4,128)(2,1)} copy(bf16[96,4,256]{2,0,1:T(8,128)(2,1)S(1)} %bitcast.17) | data formatting | bytes 393216
  49.0 1.3 %all-to-all-done.1.total_ref = bf16[8,32,128]{2,1,0:T(8,128)(2,1)S(1)} async-done(((bf16[8,32,128]{2,1,0:T(8,128)(2,1)}), bf16[8,32,128]{2,1,0:T(8,128)(2,1)S(1)}, u32[]{:S(2)}, u32[]{:S(2)}) %all-to-all-start.1) | async-done | bytes 65568 | tf_op jit(solution)/shard_map/all_to_all | solution.py:486
  50.3 0.7 %shard_map.201 = (f32[7,7,96]{2,1,0:T(8,128)}, f32[1,96]{1,0:T(1,128)}, f32[1,96]{1,0:T(1,128)}, f32[1,96]{1,0:T(1,128)}, f32[96,96]{1,0:T(8,128)}, /*index=5*/f...) custom-call(bf16[8,32,128]{2,1,0:T(8,128)(2,1)S(1)} %all-to-all-done.1.total_ref), custom_call_target="tpu_custom_call" | custom-call | bytes 160384 | tf_op jit(solution)/shard_map/pallas_call | solution.py:377
  (1 shorter events, 0.0 us)
Async XLA Ops:
  0.6 0.9 %copy-start.2 = (bf16[96,4,256]{2,1,0:T(4,128)(2,1)S(1)}, bf16[96,4,256]{2,1,0:T(4,128)(2,1)}, u32[]{:S(2)}) copy-start(bf16[96,4,256]{2,1,0:T(4,128)(2,1)} %image_ref.1) | copy-start | bytes 589828
  2.0 1.5 %collective-permute-start = (bf16[3,96,256]{2,1,0:T(8,128)(2,1)S(1)}, bf16[3,96,256]{2,1,0:T(8,128)(2,1)S(1)}, u32[]{:S(2)}, u32[]{:S(2)}) collective-permute-start(bf16[3,96,256]{2,1,0:T(8,128)(2,1)S(1)} %get-tuple-element.41), channel_id=1, source_target_pairs={{0,4},{4,0},{1,5},{5,1},{2,6},{6,2},{3,7},{7,3},{8,12},{12,8},{9,1... | collective-permute-start | bytes 442376 | tf_op jit(solution)/shard_map/ppermute | solution.py:389
  2.5 1.0 %collective-permute-start.1 = (bf16[3,96,256]{2,1,0:T(8,128)(2,1)S(1)}, bf16[3,96,256]{2,1,0:T(8,128)(2,1)S(1)}, u32[]{:S(2)}, u32[]{:S(2)}) collective-permute-start(bf16[3,96,256]{2,1,0:T(8,128)(2,1)S(1)} %get-tuple-element.42), channel_id=1, source_target_pairs={{4,8},{12,16},{20,24},{8,4},{16,12},{24,20},{5,9},{13,17},{21,25},... | collective-permute-start | bytes 442376 | tf_op jit(solution)/shard_map/ppermute | solution.py:389
  3.6 4.1 %copy-start = (bf16[384,96]{0,1:T(8,128)(2,1)S(1)}, bf16[384,96]{0,1:T(8,128)(2,1)}, u32[]{:S(2)}) copy-start(bf16[384,96]{0,1:T(8,128)(2,1)} %param.17) | copy-start | bytes 221188
  3.6 4.1 %copy-start.1 = (bf16[384,96]{0,1:T(8,128)(2,1)S(1)}, bf16[384,96]{0,1:T(8,128)(2,1)}, u32[]{:S(2)}) copy-start(bf16[384,96]{0,1:T(8,128)(2,1)} %param.19) | copy-start | bytes 221188
  3.6 4.1 %copy-start.3 = (bf16[96,4,256]{2,1,0:T(4,128)(2,1)S(1)}, bf16[96,4,256]{2,1,0:T(4,128)(2,1)}, u32[]{:S(2)}) copy-start(bf16[96,4,256]{2,1,0:T(4,128)(2,1)} %cot_ref.1) | copy-start | bytes 589828
  3.6 4.1 %copy-start.4 = (f32[96,7,7]{0,2,1:T(8,128)S(1)}, f32[96,7,7]{0,2,1:T(8,128)}, u32[]{:S(2)}) copy-start(f32[96,7,7]{0,2,1:T(8,128)} %param.13) | copy-start | bytes 56452
  3.9 3.7 %copy-start.10 = (bf16[384]{0:T(512)(128)(2,1)S(1)}, bf16[384]{0:T(512)(128)(2,1)}, u32[]{:S(2)}) copy-start(bf16[384]{0:T(512)(128)(2,1)} %param.18) | copy-start | bytes 2308
  3.9 5.1 %collective-permute-start.2 = (bf16[32,96]{1,0:T(8,128)(2,1)S(1)}, bf16[32,96]{1,0:T(8,128)(2,1)S(1)}, u32[]{:S(2)}, u32[]{:S(2)}) collective-permute-start(bf16[32,96]{1,0:T(8,128)(2,1)S(1)} %get-tuple-element.44), channel_id=1, source_target_pairs={{0,1},{2,3},{1,0},{3,2},{4,5},{6,7},{5,4},{7,6},{8,9},{10,11},{9,8... | collective-permute-start | bytes 18440 | tf_op jit(solution)/shard_map/ppermute | solution.py:389
  6.9 2.1 %collective-permute-start.3 = (bf16[32,96]{1,0:T(8,128)(2,1)S(1)}, bf16[32,96]{1,0:T(8,128)(2,1)S(1)}, u32[]{:S(2)}, u32[]{:S(2)}) collective-permute-start(bf16[32,96]{1,0:T(8,128)(2,1)S(1)} %get-tuple-element.45), channel_id=1, source_target_pairs={{1,2},{2,1},{5,6},{6,5},{9,10},{10,9},{13,14},{14,13},{17,18},{18,... | collective-permute-start | bytes 18440 | tf_op jit(solution)/shard_map/ppermute | solution.py:389
  7.6 0.7 %copy-start.8 = (f32[96]{0:T(128)S(1)}, f32[96]{0:T(128)}, u32[]{:S(2)}) copy-start(f32[96]{0:T(128)} %param.16) | copy-start | bytes 1156
  7.6 0.7 %copy-start.9 = (f32[96]{0:T(128)S(1)}, f32[96]{0:T(128)}, u32[]{:S(2)}) copy-start(f32[96]{0:T(128)} %param.20) | copy-start | bytes 1156
  7.6 0.7 %copy-start.5 = (f32[96]{0:T(128)S(1)}, f32[96]{0:T(128)}, u32[]{:S(2)}) copy-start(f32[96]{0:T(128)} %param.21) | copy-start | bytes 1156
  7.6 0.7 %copy-start.6 = (f32[96]{0:T(128)S(1)}, f32[96]{0:T(128)}, u32[]{:S(2)}) copy-start(f32[96]{0:T(128)} %param.14) | copy-start | bytes 1156
  7.6 0.7 %copy-start.7 = (f32[96]{0:T(128)S(1)}, f32[96]{0:T(128)}, u32[]{:S(2)}) copy-start(f32[96]{0:T(128)} %param.15) | copy-start | bytes 1156
  14.0 8.1 %collective-permute-start.4 = (bf16[992,128]{1,0:T(8,128)(2,1)S(1)}, bf16[992,128]{1,0:T(8,128)(2,1)S(1)}, u32[]{:S(2)}, u32[]{:S(2)}) collective-permute-start(bf16[992,128]{1,0:T(8,128)(2,1)S(1)} %get-tuple-element.52), channel_id=1, source_target_pairs={{0,4},{4,0},{1,5},{5,1},{2,6},{6,2},{3,7},{7,3},{8,12},{12,8},{9,1... | collective-permute-start | bytes 761864 | tf_op jit(solution)/shard_map/ppermute | solution.py:389
  22.8 18.6 %all-to-all-start = ((bf16[16,48,128]{2,1,0:T(8,128)(2,1)}), bf16[16,48,128]{2,1,0:T(8,128)(2,1)S(1)}, u32[]{:S(2)}, u32[]{:S(2)}) async-start(bf16[16,48,128]{2,1,0:T(8,128)(2,1)} %shard_map.198), calls=%async_computation | async-start | bytes 393216 | tf_op jit(solution)/shard_map/all_to_all | solution.py:479
  31.9 14.7 %collective-permute-start.5 = (bf16[3,96,256]{2,1,0:T(8,128)(2,1)S(1)}, bf16[3,96,256]{2,1,0:T(8,128)(2,1)S(1)}, u32[]{:S(2)}, u32[]{:S(2)}) collective-permute-start(bf16[3,96,256]{2,1,0:T(8,128)(2,1)S(1)} %get-tuple-element.53), channel_id=1, source_target_pairs={{4,8},{12,16},{20,24},{8,4},{16,12},{24,20},{5,9},{13,17},{21,25},... | collective-permute-start | bytes 442376 | tf_op jit(solution)/shard_map/ppermute | solution.py:389
  42.0 8.3 %all-to-all-start.1 = ((bf16[8,32,128]{2,1,0:T(8,128)(2,1)}), bf16[8,32,128]{2,1,0:T(8,128)(2,1)S(1)}, u32[]{:S(2)}, u32[]{:S(2)}) async-start(bf16[8,32,128]{2,1,0:T(8,128)(2,1)} %get-tuple-element.59), calls=%async_computation.1 | async-start | bytes 131072 | tf_op jit(solution)/shard_map/all_to_all | solution.py:486
  45.4 1.2 %collective-permute-start.6 = (bf16[64,128]{1,0:T(8,128)(2,1)S(1)}, bf16[64,128]{1,0:T(8,128)(2,1)S(1)}, u32[]{:S(2)}, u32[]{:S(2)}) collective-permute-start(bf16[64,128]{1,0:T(8,128)(2,1)S(1)} %get-tuple-element.57.own_ref), channel_id=1, source_target_pairs={{0,4},{4,0},{1,5},{5,1},{2,6},{6,2},{3,7},{7,3},{8,12},{12,8},{9,1... | collective-permute-start | bytes 49160 | tf_op jit(solution)/shard_map/ppermute | solution.py:389

commit v3 on v2

--- a/solution.py
+++ b/solution.py
@@ -31,6 +31,11 @@
     n = row.shape[1]
     eye = iota((n, n), 0) == iota((n, n), 1)
     return jnp.sum(jnp.where(eye, row, 0.0), axis=1, keepdims=True)
+
+
+def widened(value):
+    fill = jnp.zeros((value.shape[0], LANES - value.shape[1]), value.dtype)
+    return jnp.concatenate([value, fill], axis=1)
 
 
 def widened(value):
@@ -123,6 +128,35 @@
     for k in range(HALO):
         pair_ref[k] = mid_ref[k + (rows - HALO) * (1 - core)]
         far_ref[k] = mid_ref[k + (rows - HALO) * core]
+
+
+def gather_kernel(axes, mid_ref, pair_ref, far_ref, tall_ref, first_ref, second_ref):
+    rows = mid_ref.shape[0]
+    upper = lax.axis_index(axes[1]) == 0
+    for k in range(HALO):
+        pair, far = pair_ref[k], far_ref[k]
+        tall_ref[k] = jnp.where(upper, far, pair)
+        tall_ref[HALO + rows + k] = jnp.where(upper, pair, far)
+    for i in range(rows):
+        tall_ref[HALO + i] = mid_ref[i]
+    edges = pack_edges([tall_ref[r] for r in range(rows + 2 * HALO)])
+    high = edges.shape[0] // 2
+    even = lax.rem(lax.axis_index(axes[2]), 2) == 0
+    first_ref[...] = jnp.where(even, edges[:high], edges[high:])
+    second_ref[...] = jnp.where(even, edges[high:], edges[:high])
+
+
+def put_strip(ref, k, row):
+    channels, width = row.shape
+    parts = width // LANES
+    for p in range(parts):
+        ref[(k * parts + p) * channels : (k * parts + p + 1) * channels, :] = row[:, p * LANES : (p + 1) * LANES]
+
+
+def get_strip(ref, k, channels, width):
+    parts = width // LANES
+    pieces = [ref[(k * parts + p) * channels : (k * parts + p + 1) * channels, :] for p in range(parts)]
+    return jnp.concatenate(pieces, axis=1)
 
 
 def prepare_kernel(
@@ -146,22 +180,6 @@
     columns_ref[...] = total
 
 
-def gather_kernel(axes, mid_ref, pair_ref, far_ref, tall_ref, first_ref, second_ref):
-    rows = mid_ref.shape[0]
-    upper = lax.axis_index(axes[1]) == 0
-    for k in range(HALO):
-        pair, far = pair_ref[k], far_ref[k]
-        tall_ref[k] = jnp.where(upper, far, pair)
-        tall_ref[HALO + rows + k] = jnp.where(upper, pair, far)
-    for i in range(rows):
-        tall_ref[HALO + i] = mid_ref[i]
-    edges = pack_edges([tall_ref[r] for r in range(rows + 2 * HALO)])
-    high = edges.shape[0] // 2
-    even = lax.rem(lax.axis_index(axes[2]), 2) == 0
-    first_ref[...] = jnp.where(even, edges[:high], edges[high:])
-    second_ref[...] = jnp.where(even, edges[high:], edges[:high])
-
-
 def gelu_parts(v):
     z = jnp.abs(v)
     t = 1.0 / (1.0 + (0.3275911 / math.sqrt(2.0)) * z)
@@ -178,7 +196,7 @@
 def main_kernel(
     direct, axes,
     tall_ref, first_ref, second_ref, cot_ref, w_ref, we_ref, wr_ref, we2_ref, wr2_ref, columns_ref, scale_ref,
-    out_ref, dconv_ref, far_ref, share_ref, edges_ref, *rest,
+    out_ref, dconv_ref, far_ref, edges_ref, share_ref, *rest,
 ):
     if direct:
         (keep_ref, *scratch) = rest
@@ -190,8 +208,9 @@
     hidden_n = we_ref.shape[1]
     extent = width + LANES
     core = lax.axis_index(axes[1])
+    dwb, gain, lnb, br, scale = (columns_ref[:, k : k + 1] for k in range(5))
+    lead = HALO * channels * (width // LANES)
     even = lax.rem(lax.axis_index(axes[2]), 2) == 0
-    dwb, gain, lnb, br, scale = (columns_ref[:, k : k + 1] for k in range(5))
     first, second = first_ref[...], second_ref[...]
     edges_t = jnp.concatenate([jnp.where(even, second, first), jnp.where(even, first, second)], axis=0).T
     for r in range(rows + 2 * HALO):
@@ -253,11 +272,8 @@
                 at = g * DEEP + b * GROUP
                 dcs_ref[at : at + GROUP, i * extent : (i + 1) * extent] = moved[g * GROUP : (g + 1) * GROUP]
     for k in range(HALO):
-        pair = dconv_ref[k + (rows - HALO) * (1 - core)]
+        put_strip(share_ref, k, dconv_ref[k + (rows - HALO) * (1 - core)])
         far_ref[k] = dconv_ref[k + (rows - HALO) * core]
-        for p in range(width // LANES):
-            at = (k * (width // LANES) + p) * channels
-            share_ref[at : at + channels, :] = pair[:, p * LANES : (p + 1) * LANES]
     edges_ref[...] = widened(pack_edges(dconv_rows))
     g_reduce = widened(dot(act_ref[...], db_ref[...], NT))
     g_expand = widened(dot(dh_ref[...], nm_ref[...], NT))
@@ -280,107 +296,149 @@
         return
     half = small_ref.shape[0] // 2
     low, high = small_ref[0:half, :], small_ref[half:, :]
-    lead = HALO * (width // LANES) * channels
     keep_ref[0:hidden_n, :] = jnp.where(core == 0, g_reduce, g_expand)
     keep_ref[hidden_n:, :] = jnp.where(core == 0, low, high)
     share_ref[lead : lead + hidden_n, :] = jnp.where(core == 0, g_expand, g_reduce).astype(BF16)
     share_ref[lead + hidden_n :, :] = jnp.where(core == 0, high, low).astype(BF16)
 
 
-def block_kernel(sizes, filt_axis, share_ref, keep_ref, edges_ref, block_ref):
-    chips, filt = sizes
-    me = lax.axis_index(filt_axis)
+def block_kernel(axis, small, share_ref, keep_ref, edges_ref, block_ref):
+    filt = lax.axis_size(axis)
+    me = lax.axis_index(axis)
     count = keep_ref.shape[0]
     lead = share_ref.shape[0] - count
-    total = keep_ref[...] + share_ref[lead:, :].astype(F32)
+    high = edges_ref.shape[0] // 2
+    panel = (count - small) // filt
+    total = (keep_ref[...] + share_ref[lead:, :].astype(F32)).astype(BF16)
     edges = edges_ref[...]
-    high = edges.shape[0] // 2
-    hidden_n = count - 8 * chips
-    step = hidden_n // (filt * chips)
     for f in range(filt):
-        edge = jnp.where(f > me, edges[:high], edges[high:])
-        for q in range(chips):
-            at = (f * chips + q) * step
-            low = hidden_n + 8 * q
-            head = jnp.concatenate([total[at : at + step], total[low : low + 8]], axis=0)
-            block_ref[q * filt + f, 0 : step + 8, :] = head.astype(BF16)
-            block_ref[q * filt + f, step + 8 :, :] = edge
-
-
-def sum_kernel(axes, sizes, block_ref, total_ref, edges_ref):
-    chips, filt = sizes
-    head = total_ref.shape[1]
+        block_ref[f, 0:panel, :] = total[f * panel : (f + 1) * panel]
+        block_ref[f, panel : panel + small, :] = total[count - small :]
+        block_ref[f, panel + small :, :] = jnp.where(f > me, edges[:high], edges[high:])
+
+
+def columns_kernel(axis, block_ref, spread_ref):
+    filt = block_ref.shape[0]
+    count = spread_ref.shape[1]
+    high = count - block_ref.shape[1]
+    head = block_ref.shape[1] - high
+    f = lax.axis_index(axis)
     total = block_ref[0, :head, :].astype(F32)
-    for d in range(1, block_ref.shape[0]):
+    for d in range(1, filt):
         total = total + block_ref[d, :head, :].astype(F32)
-    total = total.astype(BF16)
-    for s in range(total_ref.shape[0]):
-        total_ref[s] = total
-    q, core, f = (lax.axis_index(a) for a in axes)
-    high = edges_ref.shape[0] // 4
-    for k, chip in enumerate((q, q + 1 - 2 * core)):
-        for side in range(2):
-            ff = f + 2 * side - 1
-            inside = (chip >= 0) & (chip < chips) & (ff >= 0) & (ff < filt)
-            at = jnp.clip(chip, 0, chips - 1) * filt + jnp.clip(ff, 0, filt - 1)
-            value = block_ref[at, head:, :]
-            low = (2 * k + side) * high
-            edges_ref[low : low + high, :] = jnp.where(inside, value, jnp.zeros_like(value))
-
-
-def back_kernel(core_axis, share_ref, far_ref, mid_ref, own_ref, other_ref, cot_ref, w_ref, out_ref, xs_ref, acc_ref):
+    pieces = [total.astype(BF16)]
+    for ff in (f - 1, f + 1):
+        value = block_ref[jnp.clip(ff, 0, filt - 1), head:, :]
+        pieces.append(jnp.where((ff >= 0) & (ff < filt), value, jnp.zeros_like(value)))
+    value = jnp.concatenate(pieces, axis=0)
+    for q in range(spread_ref.shape[0]):
+        spread_ref[q] = value
+
+
+def chips_kernel(axes, block_ref, total_ref):
+    chips, count, _ = block_ref.shape
+    low = 2 * count - total_ref.shape[0]
+    q, core = lax.axis_index(axes[0]), lax.axis_index(axes[1])
+    total = block_ref[0, :low, :].astype(F32)
+    for d in range(1, chips):
+        total = total + block_ref[d, :low, :].astype(F32)
+    total_ref[:low, :] = total
+    total_ref[low:count, :] = block_ref[q, low:, :].astype(F32)
+    other = q + 1 - 2 * core
+    value = block_ref[jnp.clip(other, 0, chips - 1), low:, :].astype(F32)
+    total_ref[count:, :] = jnp.where((other >= 0) & (other < chips), value, jnp.zeros_like(value))
+
+
+def back_kernel(core_axis, mid_ref, share_ref, far_ref, cot_ref, w_ref, acc_ref, xs_ref):
     rows, channels, width = cot_ref.shape
     upper = lax.axis_index(core_axis) == 0
-    high = own_ref.shape[0] // 2
-    near, beyond = other_ref[:high, 0:channels], other_ref[high:, 0:channels]
-    edges = (jnp.where(upper, beyond, near).T, own_ref[:high, 0:channels].T, jnp.where(upper, near, beyond).T)
-    parts = width // LANES
+    nothing = jnp.zeros((channels, LANES), BF16)
+    put = lambda r, x: spread(xs_ref, r, jnp.concatenate([x, nothing], axis=1))
     for k in range(HALO):
-        pair = [share_ref[(k * parts + p) * channels : (k * parts + p + 1) * channels, :] for p in range(parts)]
-        pair = jnp.concatenate(pair, axis=1)
-        far = far_ref[k]
-        up, down = jnp.where(upper, far, pair), jnp.where(upper, pair, far)
-        spread(xs_ref, k, jnp.concatenate([up, halo_tile(edges[0], rows - HALO + k)], axis=1))
-        spread(xs_ref, HALO + rows + k, jnp.concatenate([down, halo_tile(edges[2], k)], axis=1))
+        pair, far = get_strip(share_ref, k, channels, width), far_ref[k]
+        put(k, jnp.where(upper, far, pair))
+        put(HALO + rows + k, jnp.where(upper, pair, far))
     for i in range(rows):
-        spread(xs_ref, HALO + i, jnp.concatenate([mid_ref[i], halo_tile(edges[1], i)], axis=1))
+        put(HALO + i, mid_ref[i])
     depthwise(w_ref, xs_ref, acc_ref, rows)
     for i in range(rows):
-        out_ref[i] = (cot_ref[i].astype(F32) + acc_ref[i * channels : (i + 1) * channels, :]).astype(BF16)
-
-
-def finish_kernel(factor, total_ref, kg_ref, dwb_ref, gain_ref, lnb_ref, ge_ref, eb_ref, gr_ref, rb_ref, sc_ref):
+        acc_ref[i * channels : (i + 1) * channels, :] += cot_ref[i].astype(F32)
+
+
+def finish_kernel(
+    factor, core_axis, mine_ref, other_ref, acc_ref, w_ref,
+    back_ref, kg_ref, dwb_ref, gain_ref, lnb_ref, ge_ref, eb_ref, gr_ref, rb_ref, sc_ref, xs_ref, side_ref,
+):
     channels = kg_ref.shape[2]
-    chips = total_ref.shape[0] // 2
-    step = total_ref.shape[1] - 8
-    vectors = (dwb_ref, gain_ref, lnb_ref, rb_ref, sc_ref)
-    for s in range(2 * chips):
-        q, core = s // 2, s % 2
-        part = total_ref[s].astype(F32) * factor
-        b = core * chips + q
-        if b < SIDE:
-            kg_ref[:, b, :] = part[step : step + SIDE, 0:channels]
-        if b < len(vectors):
-            vectors[b][...] = part[step + SIDE :, 0:channels]
-        if core == 0:
-            gr_ref[q * step : (q + 1) * step, :] = part[0:step, 0:channels]
-        else:
-            ge_ref[q * step : (q + 1) * step, :] = part[0:step, 0:channels]
-            eye = iota((step, chips * step), 0) + q * step == iota((step, chips * step), 1)
-            line = jnp.sum(jnp.where(eye, part[0:step, channels : channels + 1], 0.0), axis=0, keepdims=True)
-            eb_ref[...] = line if q == 0 else eb_ref[...] + line
-
-
-def call(kernel, outs, *args, scratch=(), flops=0):
+    panel = gr_ref.shape[0]
+    low = panel + 32
+    core = lax.axis_index(core_axis)
+    rows, width = back_ref.shape[1:]
+    wide = 2 * edge_height(rows)
+    own, near, beyond = (
+        ref[at : at + wide, :].astype(BF16)[:, :channels].T
+        for ref, at in ((mine_ref, low), (other_ref, low), (other_ref, low + wide))
+    )
+    above, below = jnp.where(core == 0, beyond, near), jnp.where(core == 0, near, beyond)
+    sources = [(above, rows - HALO + k) for k in range(HALO)] + [(own, i) for i in range(rows)]
+    sources += [(below, k) for k in range(HALO)]
+    lane = iota((channels, LANES), 1)
+    for r, (edges_t, i) in enumerate(sources):
+        tile = halo_tile(edges_t, i)
+        left = jnp.where(lane >= LANES - HALO, tile, jnp.zeros_like(tile))
+        right = jnp.where(lane < HALO, tile, jnp.zeros_like(tile))
+        for b in range(SIDE):
+            if b < HALO:
+                moved = jnp.where(lane < HALO, shifted(left, HALO - b), jnp.zeros_like(tile))
+            elif b > HALO:
+                moved = jnp.where(lane >= LANES - HALO, shifted(right, HALO - b), jnp.zeros_like(tile))
+            else:
+                moved = jnp.zeros_like(tile)
+            for g in range(channels // GROUP):
+                at = r * SIDE * channels + g * DEEP + b * GROUP
+                xs_ref[at : at + GROUP, :] = moved[g * GROUP : (g + 1) * GROUP]
+    depthwise(w_ref, xs_ref, side_ref, rows)
+    for i in range(rows):
+        at = slice(i * channels, (i + 1) * channels)
+        side = side_ref[at, :]
+        value = acc_ref[at, :]
+        first = value[:, :LANES] + jnp.where(lane < HALO, side, 0.0)
+        last = value[:, width - LANES :] + jnp.where(lane >= LANES - HALO, side, 0.0)
+        middle = [value[:, k : k + LANES] for k in range(LANES, width - LANES, LANES)]
+        value = jnp.concatenate([first, *middle, last], axis=1)
+        back_ref[:, i, :] = value.astype(BF16)
+    mine, other = mine_ref[0:low, :] * factor, other_ref[0:low, :] * factor
+    low, high = jnp.where(core == 0, mine, other), jnp.where(core == 0, other, mine)
+    small = jnp.concatenate([low[panel:], high[panel:]], axis=0)
+    for b in range(SIDE):
+        kg_ref[:, b, :] = small[b * 8 : b * 8 + SIDE, 0:channels]
+    for b, ref in enumerate((dwb_ref, gain_ref, lnb_ref, rb_ref, sc_ref)):
+        ref[...] = small[b * 8 + SIDE : b * 8 + 8, 0:channels]
+    gr_ref[...] = low[0:panel, 0:channels]
+    ge_ref[...] = high[0:panel, 0:channels]
+    eye = iota((panel, panel), 0) == iota((panel, panel), 1)
+    eb_ref[...] = jnp.sum(jnp.where(eye, high[0:panel, channels : channels + 1], 0.0), axis=0, keepdims=True)
+
+
+def call(kernel, outs, *args, scratch=(), after=()):
     size = sum(math.prod(a.shape) * a.dtype.itemsize for a in args)
     size += sum(math.prod(s) * jnp.dtype(d).itemsize for s, d in outs)
+    count = len(args)
+
+    def body(*refs):
+        kernel(*refs[:count], *refs[count + len(after) :])
+
+    in_vmem = pl.BlockSpec(memory_space=pltpu.VMEM)
+    anywhere = pl.BlockSpec(memory_space=pl.ANY)
     return pl.pallas_call(
-        kernel,
+        body,
         out_shape=[jax.ShapeDtypeStruct(s, d) for s, d in outs],
+        in_specs=[in_vmem] * count + [anywhere] * len(after),
+        out_specs=[in_vmem] * len(outs),
         scratch_shapes=[pltpu.VMEM(s, d) for s, d in scratch],
         compiler_params=pltpu.CompilerParams(vmem_limit_bytes=40 * 2**20),
-        cost_estimate=pl.CostEstimate(flops=flops, bytes_accessed=size, transcendentals=0),
-    )(*args)
+        cost_estimate=pl.CostEstimate(flops=0, bytes_accessed=size, transcendentals=0),
+    )(*args, *after)
 
 
 def swap(x, axis, parity):
@@ -389,9 +447,14 @@
     return lax.ppermute(x, axis, pairs + [(j, i) for i, j in pairs])
 
 
-def moved(x, axis, step):
-    size = lax.axis_size(axis)
-    return lax.ppermute(x, axis, [(i, i + step) for i in range(size) if 0 <= i + step < size])
+def edges_by_permutes(axes, edges):
+    chip, core, filt = axes
+    count = lax.axis_size(filt)
+    right = [(i, i + 1) for i in range(count - 1)]
+    left = [(j, i) for i, j in right]
+    high = edges.shape[0] // 2
+    own = jnp.concatenate([lax.ppermute(edges[:high], filt, right), lax.ppermute(edges[high:], filt, left)], axis=0)
+    return jnp.concatenate([own, swap(own, (chip, core), 1)], axis=0)
 
 
 def shards(
@@ -399,8 +462,7 @@
     w_expand, b_expand, w_reduce, b_reduce, layer_scale,
 ):
     chip, core, filt = axes
-    space = (chip, core)
-    chip_n, filt_n = lax.axis_size(chip), lax.axis_size(filt)
+    chip_n, core_n, filt_n = (lax.axis_size(a) for a in axes)
     channels, rows, width = image.shape
     hidden_n = w_expand.shape[0]
     groups = channels // GROUP
@@ -411,12 +473,14 @@
     tokens = rows * width
     lift = channels + 16
     direct = chip_n == 4
-    pieces = 8
-    step = 2 * panel // pieces
     strip = ((HALO, channels, width), BF16)
     block = ((rows, channels, width), BF16)
+    high = edge_height(rows)
+    edge = ((2 * high, LANES), BF16)
     row = lambda v: v.reshape(1, -1)
 
+    space = (chip, core)
+    lead = HALO * channels * (width // LANES)
     mid, pair, far = call(functools.partial(enter_kernel, core), [block, strip, strip], image)
     far = swap(far, space, 1)
     pair = swap(pair, core, 0)
@@ -435,22 +499,19 @@
         we_t, row(b_expand), wr_t, row(b_reduce), row(layer_scale),
         scratch=[((lift, hidden_n), BF16), ((8, DEEP), F32)],
     )
-    edge = ((edge_height(tall), channels), BF16)
+    ends = ((edge_height(tall), channels), BF16)
     image_t, first, second = call(
-        functools.partial(gather_kernel, axes), [((tall, channels, width), BF16), edge, edge], mid, pair, far
-    )
-    first = swap(first, filt, 0)
-    second = swap(second, filt, 1)
-    lead = HALO * channels * (width // LANES)
-    half = pieces * 8 // 2
-    high = edge_height(rows)
-    outs = [block, block, strip]
+        functools.partial(gather_kernel, axes), [((tall, channels, width), BF16), ends, ends], mid, pair, far,
+        after=[columns],
+    )
+    first, second = swap(first, filt, 0), swap(second, filt, 1)
+    half = 32
+    outs = [block, block, strip, edge]
     if direct:
-        outs += [((lead + hidden_n + half, LANES), BF16), ((2 * high, LANES), BF16), ((hidden_n + half, LANES), F32)]
+        outs += [((lead + hidden_n + half, LANES), BF16), ((hidden_n + half, LANES), F32)]
     else:
-        outs += [((lead, LANES), BF16), ((2 * high, LANES), BF16)]
-        outs += [((2, hidden_n, LANES), F32), ((2 * half, LANES), F32)]
-    out_t, dconv, far, share, edges, *rest = call(
+        outs += [((lead, LANES), BF16), ((2, hidden_n, LANES), F32), ((2 * half, LANES), F32)]
+    out_t, dconv, far_out, edges, share, *rest = call(
         functools.partial(main_kernel, direct, axes),
         outs,
         image_t, first, second, cot_t, forward, we_t, wr_t, we2, wr2, columns, row(layer_scale),
@@ -468,52 +529,51 @@
             ((2 * half, LANES), F32),
         ],
     )
+    output = jnp.transpose(out_t, (1, 0, 2))
     share = swap(share, core, 0)
-    far = swap(far, space, 1)
+    far = swap(far_out, space, 1)
+    low = panel + half
+    (back,) = call(
+        functools.partial(back_kernel, core),
+        [((rows * channels, width), F32)],
+        dconv, share, far, cot_t, backward,
+        scratch=[((tall * deep, width), BF16)],
+    )
     if direct:
         (blocks,) = call(
-            functools.partial(block_kernel, (chip_n, filt_n), filt),
-            [((chip_n * filt_n, step + 8 + high, LANES), BF16)],
-            share, *rest, edges,
+            functools.partial(block_kernel, filt, half), [((filt_n, low + high, LANES), BF16)], share, *rest, edges
         )
-        blocks = lax.all_to_all(blocks, (chip, filt), 0, 0, tiled=True)
-        total, edges = call(
-            functools.partial(sum_kernel, axes, (chip_n, filt_n)),
-            [((pieces, step + 8, LANES), BF16), ((4 * high, LANES), BF16)],
-            blocks,
+        blocks = lax.all_to_all(blocks, filt, 0, 0, tiled=True)
+        (blocks,) = call(
+            functools.partial(columns_kernel, filt), [((chip_n, low + 2 * high, LANES), BF16)], blocks, after=[output]
         )
-        other = swap(edges, core, 0)
-        total = lax.all_to_all(total, space, 0, 0, tiled=True)
+        blocks = lax.all_to_all(blocks, chip, 0, 0, tiled=True)
+        (mine,) = call(functools.partial(chips_kernel, axes), [((low + 4 * high, LANES), F32)], blocks, after=[back])
+        other = swap(mine, core, 0)
     else:
-        grads, small = rest
-        edges = jnp.concatenate([moved(edges[:high], filt, 1), moved(edges[high:], filt, -1)], axis=0)
-        above, below = moved(edges, space, 1), moved(edges, space, -1)
+        edges = edges_by_permutes(axes, edges).astype(F32)
+        grads, small = lax.psum(tuple(rest), axes)
+        grads = lax.dynamic_slice_in_dim(grads, lax.axis_index(filt) * panel, panel, 1)
         upper = lax.axis_index(core) == 0
-        other = jnp.concatenate([jnp.where(upper, below, above), jnp.where(upper, above, below)], axis=0)
-        edges = jnp.concatenate([edges, edges], axis=0)
-        grads, small = lax.psum((grads, small), axes)
-        grads = lax.dynamic_slice_in_dim(grads, lax.axis_index(filt) * panel, panel, 1)
-        grads = grads.reshape(2, pieces // 2, step, LANES).swapaxes(0, 1).reshape(pieces, step, LANES)
-        small = small.reshape(2, pieces // 2, 8, LANES).swapaxes(0, 1).reshape(pieces, 8, LANES)
-        total = jnp.concatenate([grads, small], axis=1)
-    (back_t,) = call(
-        functools.partial(back_kernel, core),
-        [block],
-        share, far, dconv, edges, other, cot_t, backward,
-        scratch=[((tall * deep, width), BF16), ((rows * channels, width), F32)],
-    )
-    factor = 1.0 / math.sqrt(tokens * chip_n * lax.axis_size(core) * filt_n)
+        halves = [jnp.concatenate([grads[k], small[k * half : (k + 1) * half]], axis=0) for k in range(2)]
+        mine = jnp.concatenate([jnp.where(upper, halves[0], halves[1]), edges], axis=0)
+        other = jnp.concatenate([jnp.where(upper, halves[1], halves[0]), swap(edges, core, 0)], axis=0)
+    factor = 1.0 / math.sqrt(tokens * chip_n * core_n * filt_n)
     line = ((1, channels), F32)
     matrix = ((panel, channels), F32)
-    kg, dwb, gain, lnb, ge, eb, gr, rb, sc = call(
-        functools.partial(finish_kernel, factor),
-        [((SIDE, SIDE, channels), F32), line, line, line, matrix, ((1, panel), F32), matrix, line, line],
-        total,
+    image_grad, kg, dwb, gain, lnb, ge, eb, gr, rb, sc = call(
+        functools.partial(finish_kernel, factor, core),
+        [
+            ((channels, rows, width), BF16),
+            ((SIDE, SIDE, channels), F32),
+            line, line, line, matrix, ((1, panel), F32), matrix, line, line,
+        ],
+        mine, other, back, backward,
+        scratch=[((tall * deep, LANES), BF16), ((rows * channels, LANES), F32)],
     )
     flat = lambda v: v.reshape(-1)
-    swapped = lambda v: jnp.transpose(v, (1, 0, 2))
     return (
-        swapped(out_t), swapped(back_t), jnp.transpose(kg, (2, 0, 1)),
+        output, image_grad, jnp.transpose(kg, (2, 0, 1)),
         flat(dwb), flat(gain), flat(lnb), ge, flat(eb), gr, flat(rb), flat(sc),
     )
 

time: 51.4 us -> 49.4 us (0.961)
  starting transfers between devices: 25.3 us -> 21.6 us
  waiting for transfers between devices: 11.6 us -> 13.2 us
  Pallas kernels: 10 us -> 10.6 us
  local copies, waits for them, and re-layouts: 3.25 us -> 2.72 us
    ppermute x7, starting transfers between devices: 12.8 us -> 9.58 us  [swap(): return lax.ppermute(x, axis, pairs + [(j, i) for i, j in pairs])]
    ppermute x7, waiting for transfers between devices: 1.51 us -> 3.42 us  [swap(): return lax.ppermute(x, axis, pairs + [(j, i) for i, j in pairs])]
    unnamed x24, local copies, waits for them, and re-layouts: 3.24 us -> 2.56 us
    pallas_call x8 -> x9, Pallas kernels: 10 us -> 10.6 us  [call(): pl.pallas_call(body, out_shape=[jax.ShapeDtypeStruct(s, d) for s, d in ou...]
  transfers between devices with their start and end apart: 9 -> 9, of which waited for: 4 -> 5; matrix products, arithmetic and copies ran while one was open for 3% -> 0% of each run, Pallas kernels for 6% -> 5%
where the time goes in v3:
time: 49.4 us; the launch traced here: 49 us
  starting transfers between devices  21.6 us (44%)
  waiting for transfers between devices  13.2 us (27%)
  Pallas kernels  10.6 us (21%)
  local copies, waits for them, and re-layouts  2.72 us (6%)
  between operations  0.85 us (2%)
    pallas_call x9, Pallas kernels, call(): pl.pallas_call(body, out_shape=[jax.ShapeDtypeStruct(s, d) for s, d in ou...  10.6 us
    ppermute x7, starting transfers between devices, swap(): return lax.ppermute(x, axis, pairs + [(j, i) for i, j in pairs])  9.58 us
    all_to_all x1, starting transfers between devices, shards(): blocks = lax.all_to_all(blocks, filt, 0, 0, tiled=True)  7.21 us
    all_to_all x1, waiting for transfers between devices, shards(): blocks = lax.all_to_all(blocks, filt, 0, 0, tiled=True)  5.8 us
    all_to_all x1, starting transfers between devices, shards(): blocks = lax.all_to_all(blocks, chip, 0, 0, tiled=True)  4.78 us
    all_to_all x1, waiting for transfers between devices, shards(): blocks = lax.all_to_all(blocks, chip, 0, 0, tiled=True)  3.99 us
    ppermute x7, waiting for transfers between devices, swap(): return lax.ppermute(x, axis, pairs + [(j, i) for i, j in pairs])  3.42 us
    unnamed x24, local copies, waits for them, and re-layouts  2.56 us
  transfers between devices with their start and end apart: 9, of which 5 were waited for; matrix products, arithmetic and copies ran while one was open for 0% of the time, Pallas kernels for 5%

profile of v3, /device:TPU:0, one launch (start us, length us, event | category | flops | bytes accessed | tf_op | source)
XLA Modules:
  0.0 49.0 jit_solution(5336659614370176745)
XLA Ops:
  0.6 0.0 copy-start.2
  0.7 0.0 copy-start.1
  0.7 0.0 copy-start.3
  0.7 1.0 %copy-done.3 = bf16[96,4,256]{2,1,0:T(4,128)(2,1)S(1)} copy-done((bf16[96,4,256]{2,1,0:T(4,128)(2,1)S(1)}, bf16[96,4,256]{2,1,0:T(4,128)(2,1)}, u32[]{:S(2)}) %copy-start.3) | copy-done | bytes 196632
  1.6 0.0 copy-start.5
  1.6 0.4 shard_map.194
  2.1 0.0 copy-start.11
  2.1 0.5 %collective-permute-start = (bf16[3,96,256]{2,1,0:T(8,128)(2,1)S(1)}, bf16[3,96,256]{2,1,0:T(8,128)(2,1)S(1)}, u32[]{:S(2)}, u32[]{:S(2)}) collective-permute-start(bf16[3,96,256]{2,1,0:T(8,128)(2,1)S(1)} %get-tuple-element.40), channel_id=1, source_target_pairs={{0,4},{4,0},{1,5},{5,1},{2,6},{6,2},{3,7},{7,3},{8,12},{12,8},{9,1... | collective-permute-start | bytes 442376 | tf_op jit(solution)/shard_map/ppermute | solution.py:447
  2.6 0.7 %collective-permute-start.1 = (bf16[3,96,256]{2,1,0:T(8,128)(2,1)S(1)}, bf16[3,96,256]{2,1,0:T(8,128)(2,1)S(1)}, u32[]{:S(2)}, u32[]{:S(2)}) collective-permute-start(bf16[3,96,256]{2,1,0:T(8,128)(2,1)S(1)} %get-tuple-element.41), channel_id=1, source_target_pairs={{4,8},{12,16},{20,24},{8,4},{16,12},{24,20},{5,9},{13,17},{21,25},... | collective-permute-start | bytes 442376 | tf_op jit(solution)/shard_map/ppermute | solution.py:447
  3.3 0.0 copy-done.11
  3.3 0.0 copy-start.9
  3.3 0.0 copy-start.10
  3.3 0.0 copy-start.6
  3.3 0.0 copy-start.7
  3.3 0.0 copy-start.8
  3.4 0.0 copy-done.2
  3.4 0.0 copy-done.1
  3.4 0.0 copy-done.5
  3.4 0.6 %copy-done.9 = f32[96]{0:T(128)S(1)} copy-done((f32[96]{0:T(128)S(1)}, f32[96]{0:T(128)}, u32[]{:S(2)}) %copy-start.9) | copy-done | bytes 408
  4.0 0.0 copy-done.10
  4.0 0.0 copy-done.6
  4.0 0.0 copy-done.7
  4.0 0.0 copy-done.8
  4.0 0.0 copy-start.4
  4.0 0.9 %copy-done.4 = bf16[96,4,256]{2,1,0:T(4,128)(2,1)S(1)} copy-done((bf16[96,4,256]{2,1,0:T(4,128)(2,1)S(1)}, bf16[96,4,256]{2,1,0:T(4,128)(2,1)}, u32[]{:S(2)}) %copy-start.4) | copy-done | bytes 196632
  4.9 0.7 %shard_map.195 = (bf16[4,96,256]{2,1,0:T(8,128)(2,1)S(1)}, bf16[3,224,224]{2,1,0:T(8,128)(2,1)S(1)}, bf16[3,224,224]{2,1,0:T(8,128)(2,1)S(1)}, bf16[384,112]{1,0...) custom-call(bf16[96,4,256]{2,1,0:T(4,128)(2,1)S(1)} %copy-done.4, f32[7,7,96]{2,1,0:T(8,128)S(1)} %bitcast.24, ...), custom_call_target="tpu_custom_call" | custom-call | bytes 1373184 | tf_op jit(solution)/shard_map/pallas_call | solution.py:433
  5.6 0.0 collective-permute-done.refs_1_
  5.7 0.0 collective-permute-done.1.refs_2_
  5.7 0.3 shard_map.196
  6.0 2.7 %collective-permute-start.2 = (bf16[32,96]{1,0:T(8,128)(2,1)S(1)}, bf16[32,96]{1,0:T(8,128)(2,1)S(1)}, u32[]{:S(2)}, u32[]{:S(2)}) collective-permute-start(bf16[32,96]{1,0:T(8,128)(2,1)S(1)} %get-tuple-element.44), channel_id=1, source_target_pairs={{0,1},{2,3},{1,0},{3,2},{4,5},{6,7},{5,4},{7,6},{8,9},{10,11},{9,8... | collective-permute-start | bytes 18440 | tf_op jit(solution)/shard_map/ppermute | solution.py:447
  8.6 0.6 %collective-permute-start.3 = (bf16[32,96]{1,0:T(8,128)(2,1)S(1)}, bf16[32,96]{1,0:T(8,128)(2,1)S(1)}, u32[]{:S(2)}, u32[]{:S(2)}) collective-permute-start(bf16[32,96]{1,0:T(8,128)(2,1)S(1)} %get-tuple-element.45), channel_id=1, source_target_pairs={{1,2},{2,1},{5,6},{6,5},{9,10},{10,9},{13,14},{14,13},{17,18},{18,... | collective-permute-start | bytes 18440 | tf_op jit(solution)/shard_map/ppermute | solution.py:447
  9.3 1.0 %collective-permute-done.2.refs_1_ = bf16[32,96]{1,0:T(8,128)(2,1)S(1)} collective-permute-done((bf16[32,96]{1,0:T(8,128)(2,1)S(1)}, bf16[32,96]{1,0:T(8,128)(2,1)S(1)}, u32[]{:S(2)}, u32[]{:S(2)}) %collective-permute-start.2) | collective-permute-done | bytes 6176 | tf_op jit(solution)/shard_map/ppermute | solution.py:447
  10.3 0.0 collective-permute-done.3.refs_2_
  10.3 5.0 %shard_map.197 = (bf16[4,96,256]{2,1,0:T(8,128)(2,1)S(1)}, bf16[4,96,256]{2,1,0:T(8,128)(2,1)S(1)}, bf16[3,96,256]{2,1,0:T(8,128)(2,1)S(1)}, bf16[32,128]{1,0:T(...) custom-call(bf16[10,96,256]{2,1,0:T(8,128)(2,1)S(1)} %get-tuple-element.43.refs_0_, ...), custom_call_target="tpu_custom_call" | custom-call | bytes 2374016 | tf_op jit(solution)/shard_map/pallas_call | solution.py:433
  15.2 4.4 %collective-permute-start.4 = (bf16[992,128]{1,0:T(8,128)(2,1)S(1)}, bf16[992,128]{1,0:T(8,128)(2,1)S(1)}, u32[]{:S(2)}, u32[]{:S(2)}) collective-permute-start(bf16[992,128]{1,0:T(8,128)(2,1)S(1)} %get-tuple-element.51), channel_id=1, source_target_pairs={{0,4},{4,0},{1,5},{5,1},{2,6},{6,2},{3,7},{7,3},{8,12},{12,8},{9,1... | collective-permute-start | bytes 761864 | tf_op jit(solution)/shard_map/ppermute | solution.py:447
  19.6 1.2 %collective-permute-done.4.refs_0_.refs_1_ = bf16[992,128]{1,0:T(8,128)(2,1)S(1)} collective-permute-done((bf16[992,128]{1,0:T(8,128)(2,1)S(1)}, bf16[992,128]{1,0:T(8,128)(2,1)S(1)}, u32[]{:S(2)}, u32[]{:S(2)}) %collective-permute-start.4) | collective-permute-done | bytes 253984 | tf_op jit(solution)/shard_map/ppermute | solution.py:447
  20.7 0.7 %shard_map.198 = bf16[4,144,128]{2,1,0:T(8,128)(2,1)} custom-call(bf16[992,128]{1,0:T(8,128)(2,1)S(1)} %collective-permute-done.4.refs_0_.refs_1_, f32[416,128]{1,0:T(8,128)S(1)} %get-tuple-element.52.refs_1_, bf16[32,128]{1,0:T(8,128)(2,1)S(1)} %get-tuple-element.53.refs_2_), custom_call_target="tpu_custom_call" | custom-call | bytes 622592 | tf_op jit(solution)/shard_map/pallas_call | solution.py:433
  21.4 7.2 %all-to-all-start = ((bf16[4,144,128]{2,1,0:T(8,128)(2,1)}), bf16[4,144,128]{2,1,0:T(8,128)(2,1)S(1)}, u32[]{:S(2)}, u32[]{:S(2)}) async-start(bf16[4,144,128]{2,1,0:T(8,128)(2,1)} %shard_map.198), calls=%async_computation | async-start | bytes 294912 | tf_op jit(solution)/shard_map/all_to_all | solution.py:546
  28.6 0.7 %collective-permute-start.5 = (bf16[3,96,256]{2,1,0:T(8,128)(2,1)S(1)}, bf16[3,96,256]{2,1,0:T(8,128)(2,1)S(1)}, u32[]{:S(2)}, u32[]{:S(2)}) collective-permute-start(bf16[3,96,256]{2,1,0:T(8,128)(2,1)S(1)} %get-tuple-element.55), channel_id=1, source_target_pairs={{4,8},{12,16},{20,24},{8,4},{16,12},{24,20},{5,9},{13,17},{21,25},... | collective-permute-start | bytes 442376 | tf_op jit(solution)/shard_map/ppermute | solution.py:447
  29.3 0.2 copy.24
  29.5 0.0 copy-start
  29.5 5.8 %all-to-all-done.refs_0_ = bf16[4,144,128]{2,1,0:T(8,128)(2,1)S(1)} async-done(((bf16[4,144,128]{2,1,0:T(8,128)(2,1)}), bf16[4,144,128]{2,1,0:T(8,128)(2,1)S(1)}, u32[]{:S(2)}, u32[]{:S(2)}) %all-to-all-start) | async-done | bytes 147488 | tf_op jit(solution)/shard_map/all_to_all | solution.py:546
  35.3 0.7 %shard_map.199 = bf16[4,160,128]{2,1,0:T(8,128)(2,1)} custom-call(bf16[4,144,128]{2,1,0:T(8,128)(2,1)S(1)} %all-to-all-done.refs_0_, bf16[96,4,256]{2,1,0:T(4,128)(2,1)S(1)} %bitcast.18), custom_call_target="tpu_custom_call" | custom-call | bytes 311296 | tf_op jit(solution)/shard_map/pallas_call | solution.py:433
  36.0 0.0 copy-done
  36.0 4.8 %all-to-all-start.1 = ((bf16[4,160,128]{2,1,0:T(8,128)(2,1)}), bf16[4,160,128]{2,1,0:T(8,128)(2,1)S(1)}, u32[]{:S(2)}, u32[]{:S(2)}) async-start(bf16[4,160,128]{2,1,0:T(8,128)(2,1)} %shard_map.199), calls=%async_computation.1 | async-start | bytes 327680 | tf_op jit(solution)/shard_map/all_to_all | solution.py:550
  40.7 0.0 collective-permute-done.5.refs_2_
  40.7 1.1 %shard_map.200.refs_1_.refs_2_ = f32[384,256]{1,0:T(8,128)S(1)} custom-call(bf16[4,96,256]{2,1,0:T(8,128)(2,1)S(1)} %get-tuple-element.54.refs_0_, bf16[992,128]{1,0:T(8,128)(2,1)S(1)} %collective-permute-done.4.refs_0_.refs_1_, bf16[3,96,256]{2,1,0:T(8,128)(2,1)S(1)} %collective-permute-done.5.refs_2_, bf16[4,96,256]{2,1,0:T(8,128)(2,1)S(1)} %get-tuple-element.46.refs_3_, ...), custom_call_target="tpu_custom_call" | custom-call | bytes 1488896 | tf_op jit(solution)/shard_map/pallas_call | solution.py:433
  41.9 4.0 %all-to-all-done.1.refs_0_ = bf16[4,160,128]{2,1,0:T(8,128)(2,1)S(1)} async-done(((bf16[4,160,128]{2,1,0:T(8,128)(2,1)}), bf16[4,160,128]{2,1,0:T(8,128)(2,1)S(1)}, u32[]{:S(2)}, u32[]{:S(2)}) %all-to-all-start.1) | async-done | bytes 163872 | tf_op jit(solution)/shard_map/all_to_all | solution.py:550
  45.9 0.1 collective-permute-start.6
  46.0 1.3 %collective-permute-done.6.refs_1_ = f32[192,128]{1,0:T(8,128)S(1)} collective-permute-done((f32[192,128]{1,0:T(8,128)S(1)}, f32[192,128]{1,0:T(8,128)S(1)}, u32[]{:S(2)}, u32[]{:S(2)}) %collective-permute-start.6) | collective-permute-done | bytes 98336 | tf_op jit(solution)/shard_map/ppermute | solution.py:447
  47.2 1.7 %shard_map.202 = (bf16[96,4,256]{2,1,0:T(4,128)(2,1)}, f32[7,7,96]{2,1,0:T(8,128)}, f32[1,96]{1,0:T(1,128)}, f32[1,96]{1,0:T(1,128)}, f32[1,96]{1,0:T(1,128)}, /...) custom-call(f32[192,128]{1,0:T(8,128)S(1)} %shard_map.201.refs_0_, ...), custom_call_target="tpu_custom_call" | custom-call | bytes 1182336 | tf_op jit(solution)/shard_map/pallas_call | solution.py:433
  (2 shorter events, 0.0 us)
Async XLA Ops:
  0.6 2.7 %copy-start.2 = (bf16[384,96]{0,1:T(8,128)(2,1)S(1)}, bf16[384,96]{0,1:T(8,128)(2,1)}, u32[]{:S(2)}) copy-start(bf16[384,96]{0,1:T(8,128)(2,1)} %param.19) | copy-start | bytes 221188
  0.7 2.7 %copy-start.1 = (bf16[384,96]{0,1:T(8,128)(2,1)S(1)}, bf16[384,96]{0,1:T(8,128)(2,1)}, u32[]{:S(2)}) copy-start(bf16[384,96]{0,1:T(8,128)(2,1)} %param.17) | copy-start | bytes 221188
  0.7 1.0 %copy-start.3 = (bf16[96,4,256]{2,1,0:T(4,128)(2,1)S(1)}, bf16[96,4,256]{2,1,0:T(4,128)(2,1)}, u32[]{:S(2)}) copy-start(bf16[96,4,256]{2,1,0:T(4,128)(2,1)} %refs_0_.2) | copy-start | bytes 589828
  1.6 1.8 %copy-start.5 = (f32[96,7,7]{0,2,1:T(8,128)S(1)}, f32[96,7,7]{0,2,1:T(8,128)}, u32[]{:S(2)}) copy-start(f32[96,7,7]{0,2,1:T(8,128)} %param.13) | copy-start | bytes 56452
  2.1 1.2 %copy-start.11 = (bf16[384]{0:T(512)(128)(2,1)S(1)}, bf16[384]{0:T(512)(128)(2,1)}, u32[]{:S(2)}) copy-start(bf16[384]{0:T(512)(128)(2,1)} %param.18) | copy-start | bytes 2308
  2.1 3.6 %collective-permute-start = (bf16[3,96,256]{2,1,0:T(8,128)(2,1)S(1)}, bf16[3,96,256]{2,1,0:T(8,128)(2,1)S(1)}, u32[]{:S(2)}, u32[]{:S(2)}) collective-permute-start(bf16[3,96,256]{2,1,0:T(8,128)(2,1)S(1)} %get-tuple-element.40), channel_id=1, source_target_pairs={{0,4},{4,0},{1,5},{5,1},{2,6},{6,2},{3,7},{7,3},{8,12},{12,8},{9,1... | collective-permute-start | bytes 442376 | tf_op jit(solution)/shard_map/ppermute | solution.py:447
  2.6 3.0 %collective-permute-start.1 = (bf16[3,96,256]{2,1,0:T(8,128)(2,1)S(1)}, bf16[3,96,256]{2,1,0:T(8,128)(2,1)S(1)}, u32[]{:S(2)}, u32[]{:S(2)}) collective-permute-start(bf16[3,96,256]{2,1,0:T(8,128)(2,1)S(1)} %get-tuple-element.41), channel_id=1, source_target_pairs={{4,8},{12,16},{20,24},{8,4},{16,12},{24,20},{5,9},{13,17},{21,25},... | collective-permute-start | bytes 442376 | tf_op jit(solution)/shard_map/ppermute | solution.py:447
  3.3 0.7 %copy-start.9 = (f32[96]{0:T(128)S(1)}, f32[96]{0:T(128)}, u32[]{:S(2)}) copy-start(f32[96]{0:T(128)} %param.16) | copy-start | bytes 1156
  3.3 0.7 %copy-start.10 = (f32[96]{0:T(128)S(1)}, f32[96]{0:T(128)}, u32[]{:S(2)}) copy-start(f32[96]{0:T(128)} %param.20) | copy-start | bytes 1156
  3.3 0.7 %copy-start.6 = (f32[96]{0:T(128)S(1)}, f32[96]{0:T(128)}, u32[]{:S(2)}) copy-start(f32[96]{0:T(128)} %param.21) | copy-start | bytes 1156
  3.3 0.7 %copy-start.7 = (f32[96]{0:T(128)S(1)}, f32[96]{0:T(128)}, u32[]{:S(2)}) copy-start(f32[96]{0:T(128)} %param.14) | copy-start | bytes 1156
  3.3 0.7 %copy-start.8 = (f32[96]{0:T(128)S(1)}, f32[96]{0:T(128)}, u32[]{:S(2)}) copy-start(f32[96]{0:T(128)} %param.15) | copy-start | bytes 1156
  4.0 0.9 %copy-start.4 = (bf16[96,4,256]{2,1,0:T(4,128)(2,1)S(1)}, bf16[96,4,256]{2,1,0:T(4,128)(2,1)}, u32[]{:S(2)}) copy-start(bf16[96,4,256]{2,1,0:T(4,128)(2,1)} %refs_0_.3) | copy-start | bytes 589828
  6.0 4.3 %collective-permute-start.2 = (bf16[32,96]{1,0:T(8,128)(2,1)S(1)}, bf16[32,96]{1,0:T(8,128)(2,1)S(1)}, u32[]{:S(2)}, u32[]{:S(2)}) collective-permute-start(bf16[32,96]{1,0:T(8,128)(2,1)S(1)} %get-tuple-element.44), channel_id=1, source_target_pairs={{0,1},{2,3},{1,0},{3,2},{4,5},{6,7},{5,4},{7,6},{8,9},{10,11},{9,8... | collective-permute-start | bytes 18440 | tf_op jit(solution)/shard_map/ppermute | solution.py:447
  8.6 1.6 %collective-permute-start.3 = (bf16[32,96]{1,0:T(8,128)(2,1)S(1)}, bf16[32,96]{1,0:T(8,128)(2,1)S(1)}, u32[]{:S(2)}, u32[]{:S(2)}) collective-permute-start(bf16[32,96]{1,0:T(8,128)(2,1)S(1)} %get-tuple-element.45), channel_id=1, source_target_pairs={{1,2},{2,1},{5,6},{6,5},{9,10},{10,9},{13,14},{14,13},{17,18},{18,... | collective-permute-start | bytes 18440 | tf_op jit(solution)/shard_map/ppermute | solution.py:447
  15.2 5.5 %collective-permute-start.4 = (bf16[992,128]{1,0:T(8,128)(2,1)S(1)}, bf16[992,128]{1,0:T(8,128)(2,1)S(1)}, u32[]{:S(2)}, u32[]{:S(2)}) collective-permute-start(bf16[992,128]{1,0:T(8,128)(2,1)S(1)} %get-tuple-element.51), channel_id=1, source_target_pairs={{0,4},{4,0},{1,5},{5,1},{2,6},{6,2},{3,7},{7,3},{8,12},{12,8},{9,1... | collective-permute-start | bytes 761864 | tf_op jit(solution)/shard_map/ppermute | solution.py:447
  21.4 13.9 %all-to-all-start = ((bf16[4,144,128]{2,1,0:T(8,128)(2,1)}), bf16[4,144,128]{2,1,0:T(8,128)(2,1)S(1)}, u32[]{:S(2)}, u32[]{:S(2)}) async-start(bf16[4,144,128]{2,1,0:T(8,128)(2,1)} %shard_map.198), calls=%async_computation | async-start | bytes 294912 | tf_op jit(solution)/shard_map/all_to_all | solution.py:546
  28.6 12.1 %collective-permute-start.5 = (bf16[3,96,256]{2,1,0:T(8,128)(2,1)S(1)}, bf16[3,96,256]{2,1,0:T(8,128)(2,1)S(1)}, u32[]{:S(2)}, u32[]{:S(2)}) collective-permute-start(bf16[3,96,256]{2,1,0:T(8,128)(2,1)S(1)} %get-tuple-element.55), channel_id=1, source_target_pairs={{4,8},{12,16},{20,24},{8,4},{16,12},{24,20},{5,9},{13,17},{21,25},... | collective-permute-start | bytes 442376 | tf_op jit(solution)/shard_map/ppermute | solution.py:447
  29.5 6.5 %copy-start = (bf16[4,96,256]{2,0,1:T(4,128)(2,1)}, bf16[4,96,256]{2,0,1:T(4,128)(2,1)S(1)}, u32[]{:S(2)}) copy-start(bf16[4,96,256]{2,0,1:T(4,128)(2,1)S(1)} %copy.24) | copy-start | bytes 589828
  36.0 9.9 %all-to-all-start.1 = ((bf16[4,160,128]{2,1,0:T(8,128)(2,1)}), bf16[4,160,128]{2,1,0:T(8,128)(2,1)S(1)}, u32[]{:S(2)}, u32[]{:S(2)}) async-start(bf16[4,160,128]{2,1,0:T(8,128)(2,1)} %shard_map.199), calls=%async_computation.1 | async-start | bytes 327680 | tf_op jit(solution)/shard_map/all_to_all | solution.py:550
  45.9 1.4 %collective-permute-start.6 = (f32[192,128]{1,0:T(8,128)S(1)}, f32[192,128]{1,0:T(8,128)S(1)}, u32[]{:S(2)}, u32[]{:S(2)}) collective-permute-start(f32[192,128]{1,0:T(8,128)S(1)} %shard_map.201.refs_0_), channel_id=1, source_target_pairs={{0,4},{4,0},{1,5},{5,1},{2,6},{6,2},{3,7},{7,3},{8,12},{12,8},{9,1... | collective-permute-start | bytes 294920 | tf_op jit(solution)/shard_map/ppermute | solution.py:447

commit v4 on v3

--- a/solution.py
+++ b/solution.py
@@ -38,33 +38,29 @@
     return jnp.concatenate([value, fill], axis=1)
 
 
-def widened(value):
-    fill = jnp.zeros((value.shape[0], LANES - value.shape[1]), value.dtype)
-    return jnp.concatenate([value, fill], axis=1)
-
-
 def edge_height(rows):
     return -(-HALO * rows // 16) * 16
 
 
 def pack_edges(rows):
-    width, high = rows[0].shape[1], edge_height(len(rows))
+    count = len(rows)
+    width, high = rows[0].shape[1], edge_height(count)
     q, j = iota((2 * high, width), 0), iota((2 * high, width), 1)
     total = None
     for i, row in enumerate(rows):
-        last = (q == HALO * i + j - (width - HALO)) & (j >= width - HALO)
-        first = (q == high + HALO * i + j) & (j < HALO)
+        last = (q == count * (j - (width - HALO)) + i) & (j >= width - HALO)
+        first = (q == high + count * j + i) & (j < HALO)
         pick = jnp.where(last | first, 1.0, 0.0).astype(BF16)
         part = dot(pick, row, NT)
         total = part if total is None else total + part
     return total.astype(BF16)
 
 
-def halo_tile(edges_t, i):
+def halo_tile(edges_t, i, count):
     high = edges_t.shape[1] // 2
     q, l = iota((2 * high, LANES), 0), iota((2 * high, LANES), 1)
-    left = (q == HALO * i + l - (LANES - HALO)) & (l >= LANES - HALO)
-    right = (q == high + HALO * i + l) & (l < HALO)
+    left = (q == count * (l - (LANES - HALO)) + i) & (l >= LANES - HALO)
+    right = (q == high + count * l + i) & (l < HALO)
     pick = jnp.where(left | right, 1.0, 0.0).astype(BF16)
     return dot(edges_t, pick).astype(BF16)
 
@@ -120,11 +116,9 @@
             acc_ref[at : at + GROUP, :] = sums[i]
 
 
-def enter_kernel(core_axis, image_ref, mid_ref, pair_ref, far_ref):
+def enter_kernel(core_axis, mid_ref, pair_ref, far_ref):
     rows = mid_ref.shape[0]
     core = lax.axis_index(core_axis)
-    for i in range(rows):
-        mid_ref[i] = image_ref[:, i, :]
     for k in range(HALO):
         pair_ref[k] = mid_ref[k + (rows - HALO) * (1 - core)]
         far_ref[k] = mid_ref[k + (rows - HALO) * core]
@@ -194,19 +188,13 @@
 
 
 def main_kernel(
-    direct, axes,
+    axes,
     tall_ref, first_ref, second_ref, cot_ref, w_ref, we_ref, wr_ref, we2_ref, wr2_ref, columns_ref, scale_ref,
-    out_ref, dconv_ref, far_ref, edges_ref, share_ref, *rest,
+    out_ref, dconv_ref, far_ref, x_ref, vectors_ref, share_ref, keep_ref,
+    xs_ref, acc_ref, xhat_ref, nm_ref, db_ref, act_ref, dh_ref,
 ):
-    if direct:
-        (keep_ref, *scratch) = rest
-    else:
-        (grads_ref, small_out_ref, *scratch) = rest
-    xs_ref, acc_ref, xhat_ref, nm_ref, db_ref, act_ref, dh_ref, wide_ref, dcs_ref, line_ref, small_ref = scratch
     rows, channels, width = cot_ref.shape
-    groups = channels // GROUP
     hidden_n = we_ref.shape[1]
-    extent = width + LANES
     core = lax.axis_index(axes[1])
     dwb, gain, lnb, br, scale = (columns_ref[:, k : k + 1] for k in range(5))
     lead = HALO * channels * (width // LANES)
@@ -214,13 +202,9 @@
     first, second = first_ref[...], second_ref[...]
     edges_t = jnp.concatenate([jnp.where(even, second, first), jnp.where(even, first, second)], axis=0).T
     for r in range(rows + 2 * HALO):
-        x = jnp.concatenate([tall_ref[r], halo_tile(edges_t, r)], axis=1)
+        x = jnp.concatenate([tall_ref[r], halo_tile(edges_t, r, rows + 2 * HALO)], axis=1)
         spread(xs_ref, r, x)
-        for i in range(rows):
-            if 0 <= r - i < SIDE:
-                for g in range(groups):
-                    at = g * DEEP + (r - i) * GROUP
-                    wide_ref[at : at + GROUP, i * extent : (i + 1) * extent] = x[g * GROUP : (g + 1) * GROUP]
+        x_ref[r] = x
     depthwise(w_ref, xs_ref, acc_ref, rows)
     extra = nm_ref.shape[0] - channels
     nm_ref[channels:, :] = jnp.where(iota((extra, rows * width), 0) == 0, 1.0, 0.0).astype(BF16)
@@ -232,7 +216,6 @@
             sums[name] = sums[name] + value[:, k : k + LANES]
 
     chunk = 128
-    dconv_rows = []
     for i in range(rows):
         cols = slice(i * width, (i + 1) * width)
         conv = acc_ref[i * channels : (i + 1) * channels, :] + dwb
@@ -264,19 +247,36 @@
         dconv = (inv * (d_xhat - m1 - xhat * m2)).astype(BF16)
         add("dwb", dconv.astype(F32))
         dconv_ref[i] = dconv
-        dconv_rows.append(dconv)
-        padded = jnp.concatenate([dconv, jnp.zeros((channels, LANES), BF16)], axis=1)
+    for k in range(HALO):
+        put_strip(share_ref, k, dconv_ref[k + (rows - HALO) * (1 - core)])
+        far_ref[k] = dconv_ref[k + (rows - HALO) * core]
+    g_reduce = widened(dot(act_ref[...], db_ref[...], NT))
+    g_expand = widened(dot(dh_ref[...], nm_ref[...], NT))
+    keep_ref[...] = jnp.where(core == 0, g_reduce, g_expand)
+    share_ref[lead:, :] = jnp.where(core == 0, g_expand, g_reduce).astype(BF16)
+    vectors_ref[...] = jnp.zeros_like(vectors_ref)
+    for b, name in enumerate(VECTORS):
+        total = jnp.sum(sums[name].T, axis=0, keepdims=True)
+        vectors_ref[b : b + 1, 0:channels] = total * scale_ref[...] if name == "rb" else total
+
+
+def depthwise_gradient_kernel(x_ref, dconv_ref, vectors_ref, edges_ref, small_ref, wide_ref, dcs_ref, line_ref):
+    rows, channels, width = dconv_ref.shape
+    groups = channels // GROUP
+    extent = width + LANES
+    edges_ref[...] = widened(pack_edges([dconv_ref[i] for i in range(rows)]))
+    for i in range(rows):
+        padded = jnp.concatenate([dconv_ref[i], jnp.zeros((channels, LANES), BF16)], axis=1)
+        columns = slice(i * extent, (i + 1) * extent)
         for b in range(SIDE):
             moved = shifted(padded, b - HALO)
             for g in range(groups):
                 at = g * DEEP + b * GROUP
-                dcs_ref[at : at + GROUP, i * extent : (i + 1) * extent] = moved[g * GROUP : (g + 1) * GROUP]
-    for k in range(HALO):
-        put_strip(share_ref, k, dconv_ref[k + (rows - HALO) * (1 - core)])
-        far_ref[k] = dconv_ref[k + (rows - HALO) * core]
-    edges_ref[...] = widened(pack_edges(dconv_rows))
-    g_reduce = widened(dot(act_ref[...], db_ref[...], NT))
-    g_expand = widened(dot(dh_ref[...], nm_ref[...], NT))
+                dcs_ref[at : at + GROUP, columns] = moved[g * GROUP : (g + 1) * GROUP]
+        for a in range(SIDE):
+            for g in range(groups):
+                at = g * DEEP + a * GROUP
+                wide_ref[at : at + GROUP, columns] = x_ref[i + a, g * GROUP : (g + 1) * GROUP, :]
     small_ref[...] = jnp.zeros_like(small_ref)
     diagonal = group_diagonal()
     for g in range(groups):
@@ -286,67 +286,69 @@
             line_ref[a : a + 1, :] = jnp.sum(part, axis=0, keepdims=True)
         for b in range(SIDE):
             small_ref[b * 8 : b * 8 + SIDE, g * GROUP : (g + 1) * GROUP] = line_ref[0:SIDE, b * GROUP : (b + 1) * GROUP]
-    for b, name in enumerate(VECTORS):
-        total = jnp.sum(sums[name].T, axis=0, keepdims=True)
-        small_ref[b * 8 + SIDE : b * 8 + 8, 0:channels] = total * scale_ref[...] if name == "rb" else total
-    if not direct:
-        grads_ref[0] = g_reduce
-        grads_ref[1] = g_expand
-        small_out_ref[...] = small_ref[...]
-        return
-    half = small_ref.shape[0] // 2
-    low, high = small_ref[0:half, :], small_ref[half:, :]
-    keep_ref[0:hidden_n, :] = jnp.where(core == 0, g_reduce, g_expand)
-    keep_ref[hidden_n:, :] = jnp.where(core == 0, low, high)
-    share_ref[lead : lead + hidden_n, :] = jnp.where(core == 0, g_expand, g_reduce).astype(BF16)
-    share_ref[lead + hidden_n :, :] = jnp.where(core == 0, high, low).astype(BF16)
-
-
-def block_kernel(axis, small, share_ref, keep_ref, edges_ref, block_ref):
-    filt = lax.axis_size(axis)
-    me = lax.axis_index(axis)
-    count = keep_ref.shape[0]
-    lead = share_ref.shape[0] - count
+    for b in range(len(VECTORS)):
+        small_ref[b * 8 + SIDE : b * 8 + 8, :] = vectors_ref[b : b + 1, :]
+
+
+def first_kernel(axis, panel, share_ref, keep_ref, small_ref, edges_ref, send_ref, rest_ref, total_ref):
+    f = lax.axis_index(axis)
+    count = total_ref.shape[0]
+    total_ref[...] = keep_ref[...] + share_ref[share_ref.shape[0] - count :, :].astype(F32)
+    part = lambda k: total_ref[pl.ds(pl.multiple_of(k * panel, 8), panel), :]
+    tail = small_ref[...].astype(BF16)
+    small = tail.shape[0]
+    even = lax.rem(f, 2) == 0
+    mate = f + 1 - 2 * lax.rem(f, 2)
+    send_ref[0:panel, :] = part(mate).astype(BF16)
+    send_ref[panel : 2 * panel, :] = part(3 - mate).astype(BF16)
+    send_ref[2 * panel : 2 * panel + small, :] = tail
     high = edges_ref.shape[0] // 2
-    panel = (count - small) // filt
-    total = (keep_ref[...] + share_ref[lead:, :].astype(F32)).astype(BF16)
-    edges = edges_ref[...]
-    for f in range(filt):
-        block_ref[f, 0:panel, :] = total[f * panel : (f + 1) * panel]
-        block_ref[f, panel : panel + small, :] = total[count - small :]
-        block_ref[f, panel + small :, :] = jnp.where(f > me, edges[:high], edges[high:])
-
-
-def columns_kernel(axis, block_ref, spread_ref):
-    filt = block_ref.shape[0]
-    count = spread_ref.shape[1]
-    high = count - block_ref.shape[1]
-    head = block_ref.shape[1] - high
+    send_ref[2 * panel + small :, :] = jnp.where(even, edges_ref[:high, :], edges_ref[high:, :])
+    rest_ref[0:panel, :] = part(f)
+    rest_ref[panel : 2 * panel, :] = part(3 - f)
+    rest_ref[2 * panel :, :] = tail.astype(F32)
+
+
+def second_kernel(axis, panel, got_ref, rest_ref, edges_ref, send_ref, kept_ref):
+    even = lax.rem(lax.axis_index(axis), 2) == 0
+    count = rest_ref.shape[0]
+    total = rest_ref[...] + got_ref[0:count, :].astype(F32)
+    tail = total[2 * panel :].astype(BF16)
+    small = tail.shape[0]
+    high = edges_ref.shape[0] // 2
+    send_ref[0:panel, :] = total[panel : 2 * panel].astype(BF16)
+    send_ref[panel : panel + small, :] = tail
+    send_ref[panel + small :, :] = jnp.where(even, edges_ref[high:, :], edges_ref[:high, :])
+    kept_ref[0:panel, :] = total[0:panel]
+    kept_ref[panel:, :] = tail.astype(F32)
+
+
+def third_kernel(axis, got_ref, kept_ref, before_ref, send_ref):
     f = lax.axis_index(axis)
-    total = block_ref[0, :head, :].astype(F32)
-    for d in range(1, filt):
-        total = total + block_ref[d, :head, :].astype(F32)
-    pieces = [total.astype(BF16)]
-    for ff in (f - 1, f + 1):
-        value = block_ref[jnp.clip(ff, 0, filt - 1), head:, :]
-        pieces.append(jnp.where((ff >= 0) & (ff < filt), value, jnp.zeros_like(value)))
-    value = jnp.concatenate(pieces, axis=0)
-    for q in range(spread_ref.shape[0]):
-        spread_ref[q] = value
-
-
-def chips_kernel(axes, block_ref, total_ref):
-    chips, count, _ = block_ref.shape
-    low = 2 * count - total_ref.shape[0]
+    even = lax.rem(f, 2) == 0
+    count = kept_ref.shape[0]
+    near = before_ref[before_ref.shape[0] - (got_ref.shape[0] - count) :, :]
+    far = got_ref[count:, :]
+    far = jnp.where((f == 0) | (f == lax.axis_size(axis) - 1), jnp.zeros_like(far), far)
+    total = kept_ref[...] + got_ref[0:count, :].astype(F32)
+    edges = [jnp.where(even, far, near), jnp.where(even, near, far)]
+    send_ref[...] = jnp.concatenate([total.astype(BF16), *edges], axis=0)
+
+
+def fourth_kernel(count, got_ref, mine_ref, send_ref):
+    total = mine_ref[0:count, :].astype(F32) + got_ref[0:count, :].astype(F32)
+    send_ref[...] = jnp.concatenate([total.astype(BF16), mine_ref[count:, :], got_ref[count:, :]], axis=0)
+
+
+def fifth_kernel(axes, count, got_ref, mine_ref, total_ref):
     q, core = lax.axis_index(axes[0]), lax.axis_index(axes[1])
-    total = block_ref[0, :low, :].astype(F32)
-    for d in range(1, chips):
-        total = total + block_ref[d, :low, :].astype(F32)
-    total_ref[:low, :] = total
-    total_ref[low:count, :] = block_ref[q, low:, :].astype(F32)
+    total_ref[0:count, :] = mine_ref[0:count, :].astype(F32) + got_ref[0:count, :].astype(F32)
+    wide = (got_ref.shape[0] - count) // 2
+    total_ref[count : count + wide, :] = mine_ref[count : count + wide, :].astype(F32)
     other = q + 1 - 2 * core
-    value = block_ref[jnp.clip(other, 0, chips - 1), low:, :].astype(F32)
-    total_ref[count:, :] = jnp.where((other >= 0) & (other < chips), value, jnp.zeros_like(value))
+    beside = lax.rem(q + core, 2) == 0
+    value = jnp.where(beside, got_ref[count : count + wide, :], got_ref[count + wide :, :]).astype(F32)
+    total_ref[count + wide :, :] = jnp.where((other >= 0) & (other < lax.axis_size(axes[0])), value, 0.0)
 
 
 def back_kernel(core_axis, mid_ref, share_ref, far_ref, cot_ref, w_ref, acc_ref, xs_ref):
@@ -366,50 +368,56 @@
 
 
 def finish_kernel(
-    factor, core_axis, mine_ref, other_ref, acc_ref, w_ref,
-    back_ref, kg_ref, dwb_ref, gain_ref, lnb_ref, ge_ref, eb_ref, gr_ref, rb_ref, sc_ref, xs_ref, side_ref,
+    factor, core_axis, mine_ref, other_ref, acc_ref, taps_ref,
+    back_ref, kg_ref, dwb_ref, gain_ref, lnb_ref, ge_ref, eb_ref, gr_ref, rb_ref, sc_ref, ends_ref, side_ref,
 ):
     channels = kg_ref.shape[2]
     panel = gr_ref.shape[0]
-    low = panel + 32
     core = lax.axis_index(core_axis)
     rows, width = back_ref.shape[1:]
-    wide = 2 * edge_height(rows)
-    own, near, beyond = (
-        ref[at : at + wide, :].astype(BF16)[:, :channels].T
-        for ref, at in ((mine_ref, low), (other_ref, low), (other_ref, low + wide))
-    )
+    high = edge_height(rows)
+    low = mine_ref.shape[0] - 4 * high
+    own, near, beyond = mine_ref[low : low + 2 * high, :], other_ref[low : low + 2 * high, :], other_ref[low + 2 * high :, :]
     above, below = jnp.where(core == 0, beyond, near), jnp.where(core == 0, near, beyond)
-    sources = [(above, rows - HALO + k) for k in range(HALO)] + [(own, i) for i in range(rows)]
-    sources += [(below, k) for k in range(HALO)]
-    lane = iota((channels, LANES), 1)
-    for r, (edges_t, i) in enumerate(sources):
-        tile = halo_tile(edges_t, i)
-        left = jnp.where(lane >= LANES - HALO, tile, jnp.zeros_like(tile))
-        right = jnp.where(lane < HALO, tile, jnp.zeros_like(tile))
-        for b in range(SIDE):
-            if b < HALO:
-                moved = jnp.where(lane < HALO, shifted(left, HALO - b), jnp.zeros_like(tile))
-            elif b > HALO:
-                moved = jnp.where(lane >= LANES - HALO, shifted(right, HALO - b), jnp.zeros_like(tile))
-            else:
-                moved = jnp.zeros_like(tile)
-            for g in range(channels // GROUP):
-                at = r * SIDE * channels + g * DEEP + b * GROUP
-                xs_ref[at : at + GROUP, :] = moved[g * GROUP : (g + 1) * GROUP]
-    depthwise(w_ref, xs_ref, side_ref, rows)
+    for side in range(2):
+        for k in range(HALO):
+            at = side * high + k * rows
+            ends_ref[side * HALO + k, 0:HALO, :] = above[at + rows - HALO : at + rows]
+            ends_ref[side * HALO + k, HALO : HALO + rows, :] = own[at : at + rows]
+            ends_ref[side * HALO + k, HALO + rows : 2 * HALO + rows, :] = below[at : at + HALO]
+    side_ref[...] = jnp.zeros_like(side_ref)
+    for side in range(2):
+        for j in range(HALO):
+            total = None
+            for k in range(HALO):
+                b = k + side * (SIDE - 1) - j
+                if not 0 <= b < SIDE:
+                    continue
+                for a in range(SIDE):
+                    tap = taps_ref[SIDE - 1 - a, SIDE - 1 - b : SIDE - b, :]
+                    part = tap * ends_ref[side * HALO + k, a : a + rows, 0:channels]
+                    total = part if total is None else total + part
+            at = (side * HALO + j) * rows
+            side_ref[at : at + rows, 0:channels] = total
+    side = side_ref[...]
+    upper = side.astype(BF16)
+    lower = (side - upper.astype(F32)).astype(BF16)
+    side_t = jnp.concatenate([upper, lower], axis=0).T
+    count = side_ref.shape[0]
+    q, l = iota((2 * count, LANES), 0), iota((2 * count, LANES), 1)
+    q = jnp.where(q >= count, q - count, q)
     for i in range(rows):
-        at = slice(i * channels, (i + 1) * channels)
-        side = side_ref[at, :]
-        value = acc_ref[at, :]
-        first = value[:, :LANES] + jnp.where(lane < HALO, side, 0.0)
-        last = value[:, width - LANES :] + jnp.where(lane >= LANES - HALO, side, 0.0)
-        middle = [value[:, k : k + LANES] for k in range(LANES, width - LANES, LANES)]
-        value = jnp.concatenate([first, *middle, last], axis=1)
-        back_ref[:, i, :] = value.astype(BF16)
+        first = (q == l * rows + i) & (l < HALO)
+        last = (q == (HALO + l - (LANES - HALO)) * rows + i) & (l >= LANES - HALO)
+        extra = [dot(side_t, jnp.where(at, 1.0, 0.0).astype(BF16))[0:channels] for at in (first, last)]
+        value = acc_ref[i * channels : (i + 1) * channels, :]
+        tiles = [value[:, k : k + LANES] for k in range(0, width, LANES)]
+        tiles[0] = tiles[0] + extra[0]
+        tiles[-1] = tiles[-1] + extra[1]
+        back_ref[:, i, :] = jnp.concatenate(tiles, axis=1).astype(BF16)
     mine, other = mine_ref[0:low, :] * factor, other_ref[0:low, :] * factor
     low, high = jnp.where(core == 0, mine, other), jnp.where(core == 0, other, mine)
-    small = jnp.concatenate([low[panel:], high[panel:]], axis=0)
+    small = mine[panel:] + other[panel:]
     for b in range(SIDE):
         kg_ref[:, b, :] = small[b * 8 : b * 8 + SIDE, 0:channels]
     for b, ref in enumerate((dwb_ref, gain_ref, lnb_ref, rb_ref, sc_ref)):
@@ -445,6 +453,10 @@
     size = lax.axis_size(axis)
     pairs = [(i, i + 1) for i in range(parity, size - 1, 2)]
     return lax.ppermute(x, axis, pairs + [(j, i) for i, j in pairs])
+
+
+def crossed(x, axis, bits):
+    return lax.ppermute(x, axis, [(i, i ^ bits) for i in range(lax.axis_size(axis))])
 
 
 def edges_by_permutes(axes, edges):
@@ -472,7 +484,7 @@
     extent = width + LANES
     tokens = rows * width
     lift = channels + 16
-    direct = chip_n == 4
+    direct = chip_n == 4 and filt_n == 4
     strip = ((HALO, channels, width), BF16)
     block = ((rows, channels, width), BF16)
     high = edge_height(rows)
@@ -481,10 +493,12 @@
 
     space = (chip, core)
     lead = HALO * channels * (width // LANES)
-    mid, pair, far = call(functools.partial(enter_kernel, core), [block, strip, strip], image)
+    mid = jnp.transpose(image, (1, 0, 2))
+    pair, far = call(functools.partial(enter_kernel, core), [strip, strip], mid)
     far = swap(far, space, 1)
     pair = swap(pair, core, 0)
     we_t, wr_t = w_expand.T, w_reduce.T
+    taps = jnp.transpose(kernel, (1, 2, 0))
     cot_t, forward, backward, we2, wr2, columns = call(
         prepare_kernel,
         [
@@ -495,7 +509,7 @@
             ((hidden_n, channels), BF16),
             ((channels, LANES), F32),
         ],
-        cotangent, jnp.transpose(kernel, (1, 2, 0)), row(dw_bias), row(layer_norm_gain), row(layer_norm_bias),
+        cotangent, taps, row(dw_bias), row(layer_norm_gain), row(layer_norm_bias),
         we_t, row(b_expand), wr_t, row(b_reduce), row(layer_scale),
         scratch=[((lift, hidden_n), BF16), ((8, DEEP), F32)],
     )
@@ -505,15 +519,14 @@
         after=[columns],
     )
     first, second = swap(first, filt, 0), swap(second, filt, 1)
-    half = 32
-    outs = [block, block, strip, edge]
-    if direct:
-        outs += [((lead + hidden_n + half, LANES), BF16), ((hidden_n + half, LANES), F32)]
-    else:
-        outs += [((lead, LANES), BF16), ((2, hidden_n, LANES), F32), ((2 * half, LANES), F32)]
-    out_t, dconv, far_out, edges, share, *rest = call(
-        functools.partial(main_kernel, direct, axes),
-        outs,
+    small_n = 64
+    flat = ((hidden_n, LANES), F32)
+    out_t, dconv, far_out, x, vectors, share, keep = call(
+        functools.partial(main_kernel, axes),
+        [
+            block, block, strip, ((tall, channels, extent), BF16), ((8, LANES), F32),
+            ((HALO * channels * (width // LANES) + hidden_n, LANES), BF16), flat,
+        ],
         image_t, first, second, cot_t, forward, we_t, wr_t, we2, wr2, columns, row(layer_scale),
         scratch=[
             ((tall * deep, width), BF16),
@@ -523,41 +536,55 @@
             ((channels, tokens), BF16),
             ((hidden_n, tokens), BF16),
             ((hidden_n, tokens), BF16),
-            ((deep, rows * extent), BF16),
-            ((deep, rows * extent), BF16),
-            ((8, DEEP), F32),
-            ((2 * half, LANES), F32),
         ],
     )
     output = jnp.transpose(out_t, (1, 0, 2))
+    edges, small = call(
+        depthwise_gradient_kernel,
+        [edge, ((small_n, LANES), F32)],
+        x, dconv, vectors,
+        scratch=[((deep, rows * extent), BF16), ((deep, rows * extent), BF16), ((8, DEEP), F32)],
+    )
     share = swap(share, core, 0)
     far = swap(far_out, space, 1)
-    low = panel + half
+    low = panel + small_n
+    if direct:
+        send, kept = call(
+            functools.partial(first_kernel, filt, panel),
+            [((panel + low + high, LANES), BF16), ((panel + low, LANES), F32)],
+            share, keep, small, edges,
+            scratch=[flat],
+        )
+        first = crossed(send, filt, 1)
+        send, kept = call(
+            functools.partial(second_kernel, filt, panel),
+            [((low + high, LANES), BF16), ((low, LANES), F32)],
+            first, kept, edges,
+        )
+        got = crossed(send, filt, 3)
+        own = ((low + 2 * high, LANES), BF16)
+        (third,) = call(functools.partial(third_kernel, filt), [own], got, kept, first)
+        got = crossed(third, chip, 2)
+        (send,) = call(
+            functools.partial(fourth_kernel, low), [((low + 4 * high, LANES), BF16)], got, third, after=[far]
+        )
+        got = crossed(send, chip, 1)
+        (mine,) = call(
+            functools.partial(fifth_kernel, axes, low), [((low + 4 * high, LANES), F32)], got, send, after=[output]
+        )
+    else:
+        edges = edges_by_permutes(axes, edges).astype(F32)
+        total, small = lax.psum((keep + share[-hidden_n:].astype(F32), small), (chip, filt))
+        total = lax.dynamic_slice_in_dim(total, lax.axis_index(filt) * panel, panel, 0)
+        mine = jnp.concatenate([total, small, edges], axis=0)
+    other = swap(mine, core, 0)
     (back,) = call(
         functools.partial(back_kernel, core),
         [((rows * channels, width), F32)],
         dconv, share, far, cot_t, backward,
         scratch=[((tall * deep, width), BF16)],
-    )
-    if direct:
-        (blocks,) = call(
-            functools.partial(block_kernel, filt, half), [((filt_n, low + high, LANES), BF16)], share, *rest, edges
-        )
-        blocks = lax.all_to_all(blocks, filt, 0, 0, tiled=True)
-        (blocks,) = call(
-            functools.partial(columns_kernel, filt), [((chip_n, low + 2 * high, LANES), BF16)], blocks, after=[output]
-        )
-        blocks = lax.all_to_all(blocks, chip, 0, 0, tiled=True)
-        (mine,) = call(functools.partial(chips_kernel, axes), [((low + 4 * high, LANES), F32)], blocks, after=[back])
-        other = swap(mine, core, 0)
-    else:
-        edges = edges_by_permutes(axes, edges).astype(F32)
-        grads, small = lax.psum(tuple(rest), axes)
-        grads = lax.dynamic_slice_in_dim(grads, lax.axis_index(filt) * panel, panel, 1)
-        upper = lax.axis_index(core) == 0
-        halves = [jnp.concatenate([grads[k], small[k * half : (k + 1) * half]], axis=0) for k in range(2)]
-        mine = jnp.concatenate([jnp.where(upper, halves[0], halves[1]), edges], axis=0)
-        other = jnp.concatenate([jnp.where(upper, halves[1], halves[0]), swap(edges, core, 0)], axis=0)
+        after=[mine],
+    )
     factor = 1.0 / math.sqrt(tokens * chip_n * core_n * filt_n)
     line = ((1, channels), F32)
     matrix = ((panel, channels), F32)
@@ -568,8 +595,8 @@
             ((SIDE, SIDE, channels), F32),
             line, line, line, matrix, ((1, panel), F32), matrix, line, line,
         ],
-        mine, other, back, backward,
-        scratch=[((tall * deep, LANES), BF16), ((rows * channels, LANES), F32)],
+        mine, other, back, taps,
+        scratch=[((2 * HALO, 16, LANES), F32), ((2 * HALO * rows, LANES), F32)],
     )
     flat = lambda v: v.reshape(-1)
     return (

time: 49.4 us -> 45.4 us (0.919)
  Pallas kernels: 10.6 us -> 8.36 us
  waiting for transfers between devices: 13.2 us -> 11.4 us
  starting transfers between devices: 21.6 us -> 22.7 us
  local copies, waits for them, and re-layouts: 2.72 us -> 1.82 us
    ppermute x0 -> x4, starting transfers between devices: none -> 12.2 us  [crossed(): lax.ppermute(x, axis, [(i, i ^ bits) for i in range(lax.axis_size(axis))])]
    all_to_all x2 -> x0, starting transfers between devices: 12 us -> none  [the longest x1 7.21 us: shards(): blocks = lax.all_to_all(blocks, filt, 0, 0, tiled=True)]
    ppermute x0 -> x4, waiting for transfers between devices: none -> 10 us  [crossed(): lax.ppermute(x, axis, [(i, i ^ bits) for i in range(lax.axis_size(axis))])]
    all_to_all x2 -> x0, waiting for transfers between devices: 9.79 us -> none  [the longest x1 5.8 us: shards(): blocks = lax.all_to_all(blocks, filt, 0, 0, tiled=True)]
    pallas_call x9 -> x12, Pallas kernels: 10.6 us -> 8.36 us  [call(): pl.pallas_call(body, out_shape=[jax.ShapeDtypeStruct(s, d) for s, d in ou...]
    ppermute x7, waiting for transfers between devices: 3.42 us -> 1.37 us  [swap(): return lax.ppermute(x, axis, pairs + [(j, i) for i, j in pairs])]
    ppermute x7, starting transfers between devices: 9.58 us -> 10.5 us  [swap(): return lax.ppermute(x, axis, pairs + [(j, i) for i, j in pairs])]
    unnamed x24 -> x23, local copies, waits for them, and re-layouts: 2.56 us -> 1.66 us
  transfers between devices with their start and end apart: 9 -> 11, of which waited for: 5 -> 7; matrix products, arithmetic and copies ran while one was open for 0% -> 0% of each run, Pallas kernels for 5% -> 6%
where the time goes in v4:
time: 45.4 us; the launch traced here: 45.2 us
  starting transfers between devices  22.7 us (50%)
  waiting for transfers between devices  11.4 us (25%)
  Pallas kernels  8.36 us (18%)
  local copies, waits for them, and re-layouts  1.82 us (4%)
  between operations  0.89 us (2%)
    ppermute x4, starting transfers between devices, crossed(): lax.ppermute(x, axis, [(i, i ^ bits) for i in range(lax.axis_size(axis))])  12.2 us
    ppermute x7, starting transfers between devices, swap(): return lax.ppermute(x, axis, pairs + [(j, i) for i, j in pairs])  10.5 us
    ppermute x4, waiting for transfers between devices, crossed(): lax.ppermute(x, axis, [(i, i ^ bits) for i in range(lax.axis_size(axis))])  10 us
    pallas_call x12, Pallas kernels, call(): pl.pallas_call(body, out_shape=[jax.ShapeDtypeStruct(s, d) for s, d in ou...  8.36 us
    unnamed x23, local copies, waits for them, and re-layouts  1.66 us
    ppermute x7, waiting for transfers between devices, swap(): return lax.ppermute(x, axis, pairs + [(j, i) for i, j in pairs])  1.37 us
  transfers between devices with their start and end apart: 11, of which 7 were waited for; matrix products, arithmetic and copies ran while one was open for 0% of the time, Pallas kernels for 6%

profile of v4, /device:TPU:0, one launch (start us, length us, event | category | flops | bytes accessed | tf_op | source)
XLA Modules:
  0.0 45.2 jit_solution(13756227092558059689)
XLA Ops:
  0.6 0.0 copy-start.3
  0.7 1.0 %copy.27 = bf16[96,4,256]{2,0,1:T(8,128)(2,1)S(1)} copy(bf16[96,4,256]{2,1,0:T(4,128)(2,1)} %param.11) | data formatting | bytes 393216 | tf_op args[0]
  1.6 0.0 copy-start.1
  1.7 0.0 copy-start.2
  1.7 0.0 copy-start.4
  1.7 0.0 copy-start.10
  1.7 0.5 %collective-permute-start = (bf16[3,96,256]{2,1,0:T(8,128)(2,1)S(1)}, bf16[3,96,256]{2,1,0:T(8,128)(2,1)S(1)}, u32[]{:S(2)}, u32[]{:S(2)}) collective-permute-start(bf16[3,96,256]{2,1,0:T(8,128)(2,1)S(1)} %get-tuple-element.45), channel_id=1, source_target_pairs={{0,4},{4,0},{1,5},{5,1},{2,6},{6,2},{3,7},{7,3},{8,12},{12,8},{9,1... | collective-permute-start | bytes 442376 | tf_op jit(solution)/shard_map/ppermute | solution.py:455
  2.3 0.7 %collective-permute-start.1 = (bf16[3,96,256]{2,1,0:T(8,128)(2,1)S(1)}, bf16[3,96,256]{2,1,0:T(8,128)(2,1)S(1)}, u32[]{:S(2)}, u32[]{:S(2)}) collective-permute-start(bf16[3,96,256]{2,1,0:T(8,128)(2,1)S(1)} %get-tuple-element.46), channel_id=1, source_target_pairs={{4,8},{12,16},{20,24},{8,4},{16,12},{24,20},{5,9},{13,17},{21,25},... | collective-permute-start | bytes 442376 | tf_op jit(solution)/shard_map/ppermute | solution.py:455
  2.9 0.0 copy-done.10
  2.9 0.0 copy-start.8
  3.0 0.0 copy-start.9
  3.0 0.0 copy-start.5
  3.0 0.0 copy-start.6
  3.0 0.0 copy-start.7
  3.0 0.0 copy-done.3
  3.0 0.0 copy-done.1
  3.0 0.0 copy-done.2
  3.0 0.0 copy-done.4
  3.0 0.6 %copy-done.8 = f32[96]{0:T(128)S(1)} copy-done((f32[96]{0:T(128)S(1)}, f32[96]{0:T(128)}, u32[]{:S(2)}) %copy-start.8) | copy-done | bytes 408
  3.6 0.0 copy-done.9
  3.6 0.0 copy-done.5
  3.6 0.0 copy-done.6
  3.6 0.0 copy-done.7
  3.7 0.7 %shard_map.195 = (bf16[4,96,256]{2,1,0:T(8,128)(2,1)S(1)}, bf16[3,224,224]{2,1,0:T(8,128)(2,1)S(1)}, bf16[3,224,224]{2,1,0:T(8,128)(2,1)S(1)}, bf16[384,112]{1,0...) custom-call(bf16[96,4,256]{2,1,0:T(4,128)(2,1)S(1)} %copy-done.3, f32[7,7,96]{2,1,0:T(8,128)S(1)} %bitcast.29, ...), custom_call_target="tpu_custom_call" | custom-call | bytes 1373184 | tf_op jit(solution)/shard_map/pallas_call | solution.py:441
  4.4 0.0 collective-permute-done.refs_1_
  4.4 0.0 collective-permute-done.1.refs_2_
  4.4 0.3 shard_map.196
  4.7 2.7 %collective-permute-start.2 = (bf16[32,96]{1,0:T(8,128)(2,1)S(1)}, bf16[32,96]{1,0:T(8,128)(2,1)S(1)}, u32[]{:S(2)}, u32[]{:S(2)}) collective-permute-start(bf16[32,96]{1,0:T(8,128)(2,1)S(1)} %get-tuple-element.49), channel_id=1, source_target_pairs={{0,1},{2,3},{1,0},{3,2},{4,5},{6,7},{5,4},{7,6},{8,9},{10,11},{9,8... | collective-permute-start | bytes 18440 | tf_op jit(solution)/shard_map/ppermute | solution.py:455
  7.3 0.6 %collective-permute-start.3 = (bf16[32,96]{1,0:T(8,128)(2,1)S(1)}, bf16[32,96]{1,0:T(8,128)(2,1)S(1)}, u32[]{:S(2)}, u32[]{:S(2)}) collective-permute-start(bf16[32,96]{1,0:T(8,128)(2,1)S(1)} %get-tuple-element.50), channel_id=1, source_target_pairs={{1,2},{2,1},{5,6},{6,5},{9,10},{10,9},{13,14},{14,13},{17,18},{18,... | collective-permute-start | bytes 18440 | tf_op jit(solution)/shard_map/ppermute | solution.py:455
  8.0 1.0 %collective-permute-done.2.refs_1_ = bf16[32,96]{1,0:T(8,128)(2,1)S(1)} collective-permute-done((bf16[32,96]{1,0:T(8,128)(2,1)S(1)}, bf16[32,96]{1,0:T(8,128)(2,1)S(1)}, u32[]{:S(2)}, u32[]{:S(2)}) %collective-permute-start.2) | collective-permute-done | bytes 6176 | tf_op jit(solution)/shard_map/ppermute | solution.py:455
  9.0 0.0 collective-permute-done.3.refs_2_
  9.0 4.0 %shard_map.197 = (bf16[4,96,256]{2,1,0:T(8,128)(2,1)S(1)}, bf16[4,96,256]{2,1,0:T(8,128)(2,1)S(1)}, bf16[3,96,256]{2,1,0:T(8,128)(2,1)S(1)}, bf16[10,96,384]{2,1...) custom-call(bf16[10,96,256]{2,1,0:T(8,128)(2,1)S(1)} %get-tuple-element.48.refs_0_,, ...), custom_call_target="tpu_custom_call" | custom-call | bytes 3082624 | tf_op jit(solution)/shard_map/pallas_call | solution.py:441
  13.0 5.3 %collective-permute-start.4 = (bf16[960,128]{1,0:T(8,128)(2,1)S(1)}, bf16[960,128]{1,0:T(8,128)(2,1)S(1)}, u32[]{:S(2)}, u32[]{:S(2)}) collective-permute-start(bf16[960,128]{1,0:T(8,128)(2,1)S(1)} %get-tuple-element.56), channel_id=1, source_target_pairs={{0,4},{4,0},{1,5},{5,1},{2,6},{6,2},{3,7},{7,3},{8,12},{12,8},{9,1... | collective-permute-start | bytes 737288 | tf_op jit(solution)/shard_map/ppermute | solution.py:455
  18.2 0.9 %shard_map.198 = (bf16[32,128]{1,0:T(8,128)(2,1)S(1)}, f32[64,128]{1,0:T(8,128)S(1)}) custom-call(bf16[10,96,384]{2,1,0:T(8,128)(2,1)S(1)} %get-tuple-element.58.refs_0_, bf16[4,96,256]{2,1,0:T(8,128)(2,1)S(1)} %get-tuple-element.59.refs_1_.refs_0_, f32[8,128]{1,0:T(8,128)S(1)} %get-tuple-element.60.refs_2_), custom_call_target="tpu_custom_call" | custom-call | bytes 978944 | tf_op jit(solution)/shard_map/pallas_call | solution.py:441
  19.2 0.2 collective-permute-done.4.refs_0_.refs_1_
  19.4 4.8 %collective-permute-start.5 = (bf16[272,128]{1,0:T(8,128)(2,1)S(1)}, bf16[272,128]{1,0:T(8,128)(2,1)S(1)}, u32[]{:S(2)}, u32[]{:S(2)}) collective-permute-start(bf16[272,128]{1,0:T(8,128)(2,1)S(1)} %get-tuple-element.63), channel_id=1, source_target_pairs={{0,1},{1,0},{2,3},{3,2},{4,5},{5,4},{6,7},{7,6},{8,9},{9,8},{10,11... | collective-permute-start | bytes 208904 | tf_op jit(solution)/shard_map/ppermute | solution.py:459
  24.3 0.7 %collective-permute-start.8 = (bf16[3,96,256]{2,1,0:T(8,128)(2,1)S(1)}, bf16[3,96,256]{2,1,0:T(8,128)(2,1)S(1)}, u32[]{:S(2)}, u32[]{:S(2)}) collective-permute-start(bf16[3,96,256]{2,1,0:T(8,128)(2,1)S(1)} %get-tuple-element.67), channel_id=1, source_target_pairs={{4,8},{12,16},{20,24},{8,4},{16,12},{24,20},{5,9},{13,17},{21,25},... | collective-permute-start | bytes 442376 | tf_op jit(solution)/shard_map/ppermute | solution.py:455
  24.9 2.0 %collective-permute-done.5.refs_0_.refs_2_ = bf16[272,128]{1,0:T(8,128)(2,1)S(1)} collective-permute-done((bf16[272,128]{1,0:T(8,128)(2,1)S(1)}, bf16[272,128]{1,0:T(8,128)(2,1)S(1)}, u32[]{:S(2)}, u32[]{:S(2)}) %collective-permute-start.5) | collective-permute-done | bytes 69664 | tf_op jit(solution)/shard_map/ppermute | solution.py:459
  27.0 2.7 %collective-permute-start.6 = (bf16[176,128]{1,0:T(8,128)(2,1)S(1)}, bf16[176,128]{1,0:T(8,128)(2,1)S(1)}, u32[]{:S(2)}, u32[]{:S(2)}) collective-permute-start(bf16[176,128]{1,0:T(8,128)(2,1)S(1)} %get-tuple-element.65), channel_id=1, source_target_pairs={{0,3},{1,2},{2,1},{3,0},{4,7},{5,6},{6,5},{7,4},{8,11},{9,10},{10,... | collective-permute-start | bytes 135176 | tf_op jit(solution)/shard_map/ppermute | solution.py:459
  29.7 3.3 %collective-permute-done.6.refs_0_ = bf16[176,128]{1,0:T(8,128)(2,1)S(1)} collective-permute-done((bf16[176,128]{1,0:T(8,128)(2,1)S(1)}, bf16[176,128]{1,0:T(8,128)(2,1)S(1)}, u32[]{:S(2)}, u32[]{:S(2)}) %collective-permute-start.6) | collective-permute-done | bytes 45088 | tf_op jit(solution)/shard_map/ppermute | solution.py:459
  33.0 3.2 %collective-permute-start.7 = (bf16[192,128]{1,0:T(8,128)(2,1)S(1)}, bf16[192,128]{1,0:T(8,128)(2,1)S(1)}, u32[]{:S(2)}, u32[]{:S(2)}) collective-permute-start(bf16[192,128]{1,0:T(8,128)(2,1)S(1)} %shard_map.201.refs_1_), channel_id=1, source_target_pairs={{0,16},{8,24},{16,0},{24,8},{1,17},{9,25},{17,1},{25,9},{2,18},{10... | collective-permute-start | bytes 147464 | tf_op jit(solution)/shard_map/ppermute | solution.py:459
  36.2 0.0 collective-permute-done.8.refs_2_
  36.2 2.1 %collective-permute-done.7.refs_0_ = bf16[192,128]{1,0:T(8,128)(2,1)S(1)} collective-permute-done((bf16[192,128]{1,0:T(8,128)(2,1)S(1)}, bf16[192,128]{1,0:T(8,128)(2,1)S(1)}, u32[]{:S(2)}, u32[]{:S(2)}) %collective-permute-start.7) | collective-permute-done | bytes 49184 | tf_op jit(solution)/shard_map/ppermute | solution.py:459
  38.3 1.5 %collective-permute-start.9 = (bf16[224,128]{1,0:T(8,128)(2,1)S(1)}, bf16[224,128]{1,0:T(8,128)(2,1)S(1)}, u32[]{:S(2)}, u32[]{:S(2)}) collective-permute-start(bf16[224,128]{1,0:T(8,128)(2,1)S(1)} %shard_map.202.refs_1_), channel_id=1, source_target_pairs={{0,8},{8,0},{16,24},{24,16},{1,9},{9,1},{17,25},{25,17},{2,10},{10... | collective-permute-start | bytes 172040 | tf_op jit(solution)/shard_map/ppermute | solution.py:459
  39.8 0.2 copy.26
  40.0 0.0 copy-start
  40.0 2.6 %collective-permute-done.9.refs_0_ = bf16[224,128]{1,0:T(8,128)(2,1)S(1)} collective-permute-done((bf16[224,128]{1,0:T(8,128)(2,1)S(1)}, bf16[224,128]{1,0:T(8,128)(2,1)S(1)}, u32[]{:S(2)}, u32[]{:S(2)}) %collective-permute-start.9) | collective-permute-done | bytes 57376 | tf_op jit(solution)/shard_map/ppermute | solution.py:459
  42.6 0.0 copy-done
  42.6 0.1 collective-permute-start.10
  42.6 1.1 %shard_map.204.refs_2_ = f32[384,256]{1,0:T(8,128)S(1)} custom-call(bf16[4,96,256]{2,1,0:T(8,128)(2,1)S(1)} %get-tuple-element.59.refs_1_.refs_0_, bf16[960,128]{1,0:T(8,128)(2,1)S(1)} %collective-permute-done.4.refs_0_.refs_1_, bf16[3,96,256]{2,1,0:T(8,128)(2,1)S(1)} %collective-permute-done.8.refs_2_, bf16[4,96,256]{2,1,0:T(8,128)(2,1)S(1)} %get-tuple-element.51.refs_3_, ...), custom_call_target="tpu_custom_call" | custom-call | bytes 1480704 | tf_op jit(solution)/shard_map/pallas_call | solution.py:441
  43.8 0.2 collective-permute-done.10.refs_1_
  44.0 1.2 %shard_map.205 = (bf16[96,4,256]{2,1,0:T(4,128)(2,1)}, f32[7,7,96]{2,1,0:T(8,128)}, f32[1,96]{1,0:T(1,128)}, f32[1,96]{1,0:T(1,128)}, f32[1,96]{1,0:T(1,128)}, /...) custom-call(f32[224,128]{1,0:T(8,128)S(1)} %shard_map.203.refs_5_.refs_0_, ...), custom_call_target="tpu_custom_call" | custom-call | bytes 932864 | tf_op jit(solution)/shard_map/pallas_call | solution.py:441
  (7 shorter events, 0.1 us)
Async XLA Ops:
  0.6 2.4 %copy-start.3 = (bf16[96,4,256]{2,1,0:T(4,128)(2,1)S(1)}, bf16[96,4,256]{2,1,0:T(4,128)(2,1)}, u32[]{:S(2)}) copy-start(bf16[96,4,256]{2,1,0:T(4,128)(2,1)} %refs_0_.1) | copy-start | bytes 589828
  1.6 1.4 %copy-start.1 = (bf16[384,96]{0,1:T(8,128)(2,1)S(1)}, bf16[384,96]{0,1:T(8,128)(2,1)}, u32[]{:S(2)}) copy-start(bf16[384,96]{0,1:T(8,128)(2,1)} %param.17) | copy-start | bytes 221188
  1.7 1.4 %copy-start.2 = (bf16[384,96]{0,1:T(8,128)(2,1)S(1)}, bf16[384,96]{0,1:T(8,128)(2,1)}, u32[]{:S(2)}) copy-start(bf16[384,96]{0,1:T(8,128)(2,1)} %param.19) | copy-start | bytes 221188
  1.7 1.4 %copy-start.4 = (f32[96,7,7]{0,2,1:T(8,128)S(1)}, f32[96,7,7]{0,2,1:T(8,128)}, u32[]{:S(2)}) copy-start(f32[96,7,7]{0,2,1:T(8,128)} %param.13) | copy-start | bytes 56452
  1.7 1.2 %copy-start.10 = (bf16[384]{0:T(512)(128)(2,1)S(1)}, bf16[384]{0:T(512)(128)(2,1)}, u32[]{:S(2)}) copy-start(bf16[384]{0:T(512)(128)(2,1)} %param.18) | copy-start | bytes 2308
  1.7 2.6 %collective-permute-start = (bf16[3,96,256]{2,1,0:T(8,128)(2,1)S(1)}, bf16[3,96,256]{2,1,0:T(8,128)(2,1)S(1)}, u32[]{:S(2)}, u32[]{:S(2)}) collective-permute-start(bf16[3,96,256]{2,1,0:T(8,128)(2,1)S(1)} %get-tuple-element.45), channel_id=1, source_target_pairs={{0,4},{4,0},{1,5},{5,1},{2,6},{6,2},{3,7},{7,3},{8,12},{12,8},{9,1... | collective-permute-start | bytes 442376 | tf_op jit(solution)/shard_map/ppermute | solution.py:455
  2.3 2.1 %collective-permute-start.1 = (bf16[3,96,256]{2,1,0:T(8,128)(2,1)S(1)}, bf16[3,96,256]{2,1,0:T(8,128)(2,1)S(1)}, u32[]{:S(2)}, u32[]{:S(2)}) collective-permute-start(bf16[3,96,256]{2,1,0:T(8,128)(2,1)S(1)} %get-tuple-element.46), channel_id=1, source_target_pairs={{4,8},{12,16},{20,24},{8,4},{16,12},{24,20},{5,9},{13,17},{21,25},... | collective-permute-start | bytes 442376 | tf_op jit(solution)/shard_map/ppermute | solution.py:455
  2.9 0.7 %copy-start.8 = (f32[96]{0:T(128)S(1)}, f32[96]{0:T(128)}, u32[]{:S(2)}) copy-start(f32[96]{0:T(128)} %param.16) | copy-start | bytes 1156
  3.0 0.7 %copy-start.9 = (f32[96]{0:T(128)S(1)}, f32[96]{0:T(128)}, u32[]{:S(2)}) copy-start(f32[96]{0:T(128)} %param.20) | copy-start | bytes 1156
  3.0 0.7 %copy-start.5 = (f32[96]{0:T(128)S(1)}, f32[96]{0:T(128)}, u32[]{:S(2)}) copy-start(f32[96]{0:T(128)} %param.21) | copy-start | bytes 1156
  3.0 0.7 %copy-start.6 = (f32[96]{0:T(128)S(1)}, f32[96]{0:T(128)}, u32[]{:S(2)}) copy-start(f32[96]{0:T(128)} %param.14) | copy-start | bytes 1156
  3.0 0.7 %copy-start.7 = (f32[96]{0:T(128)S(1)}, f32[96]{0:T(128)}, u32[]{:S(2)}) copy-start(f32[96]{0:T(128)} %param.15) | copy-start | bytes 1156
  4.7 4.3 %collective-permute-start.2 = (bf16[32,96]{1,0:T(8,128)(2,1)S(1)}, bf16[32,96]{1,0:T(8,128)(2,1)S(1)}, u32[]{:S(2)}, u32[]{:S(2)}) collective-permute-start(bf16[32,96]{1,0:T(8,128)(2,1)S(1)} %get-tuple-element.49), channel_id=1, source_target_pairs={{0,1},{2,3},{1,0},{3,2},{4,5},{6,7},{5,4},{7,6},{8,9},{10,11},{9,8... | collective-permute-start | bytes 18440 | tf_op jit(solution)/shard_map/ppermute | solution.py:455
  7.3 1.6 %collective-permute-start.3 = (bf16[32,96]{1,0:T(8,128)(2,1)S(1)}, bf16[32,96]{1,0:T(8,128)(2,1)S(1)}, u32[]{:S(2)}, u32[]{:S(2)}) collective-permute-start(bf16[32,96]{1,0:T(8,128)(2,1)S(1)} %get-tuple-element.50), channel_id=1, source_target_pairs={{1,2},{2,1},{5,6},{6,5},{9,10},{10,9},{13,14},{14,13},{17,18},{18,... | collective-permute-start | bytes 18440 | tf_op jit(solution)/shard_map/ppermute | solution.py:455
  13.0 6.4 %collective-permute-start.4 = (bf16[960,128]{1,0:T(8,128)(2,1)S(1)}, bf16[960,128]{1,0:T(8,128)(2,1)S(1)}, u32[]{:S(2)}, u32[]{:S(2)}) collective-permute-start(bf16[960,128]{1,0:T(8,128)(2,1)S(1)} %get-tuple-element.56), channel_id=1, source_target_pairs={{0,4},{4,0},{1,5},{5,1},{2,6},{6,2},{3,7},{7,3},{8,12},{12,8},{9,1... | collective-permute-start | bytes 737288 | tf_op jit(solution)/shard_map/ppermute | solution.py:455
  19.4 7.5 %collective-permute-start.5 = (bf16[272,128]{1,0:T(8,128)(2,1)S(1)}, bf16[272,128]{1,0:T(8,128)(2,1)S(1)}, u32[]{:S(2)}, u32[]{:S(2)}) collective-permute-start(bf16[272,128]{1,0:T(8,128)(2,1)S(1)} %get-tuple-element.63), channel_id=1, source_target_pairs={{0,1},{1,0},{2,3},{3,2},{4,5},{5,4},{6,7},{7,6},{8,9},{9,8},{10,11... | collective-permute-start | bytes 208904 | tf_op jit(solution)/shard_map/ppermute | solution.py:459
  24.3 11.9 %collective-permute-start.8 = (bf16[3,96,256]{2,1,0:T(8,128)(2,1)S(1)}, bf16[3,96,256]{2,1,0:T(8,128)(2,1)S(1)}, u32[]{:S(2)}, u32[]{:S(2)}) collective-permute-start(bf16[3,96,256]{2,1,0:T(8,128)(2,1)S(1)} %get-tuple-element.67), channel_id=1, source_target_pairs={{4,8},{12,16},{20,24},{8,4},{16,12},{24,20},{5,9},{13,17},{21,25},... | collective-permute-start | bytes 442376 | tf_op jit(solution)/shard_map/ppermute | solution.py:455
  27.0 6.0 %collective-permute-start.6 = (bf16[176,128]{1,0:T(8,128)(2,1)S(1)}, bf16[176,128]{1,0:T(8,128)(2,1)S(1)}, u32[]{:S(2)}, u32[]{:S(2)}) collective-permute-start(bf16[176,128]{1,0:T(8,128)(2,1)S(1)} %get-tuple-element.65), channel_id=1, source_target_pairs={{0,3},{1,2},{2,1},{3,0},{4,7},{5,6},{6,5},{7,4},{8,11},{9,10},{10,... | collective-permute-start | bytes 135176 | tf_op jit(solution)/shard_map/ppermute | solution.py:459
  33.0 5.2 %collective-permute-start.7 = (bf16[192,128]{1,0:T(8,128)(2,1)S(1)}, bf16[192,128]{1,0:T(8,128)(2,1)S(1)}, u32[]{:S(2)}, u32[]{:S(2)}) collective-permute-start(bf16[192,128]{1,0:T(8,128)(2,1)S(1)} %shard_map.201.refs_1_), channel_id=1, source_target_pairs={{0,16},{8,24},{16,0},{24,8},{1,17},{9,25},{17,1},{25,9},{2,18},{10... | collective-permute-start | bytes 147464 | tf_op jit(solution)/shard_map/ppermute | solution.py:459
  38.3 4.2 %collective-permute-start.9 = (bf16[224,128]{1,0:T(8,128)(2,1)S(1)}, bf16[224,128]{1,0:T(8,128)(2,1)S(1)}, u32[]{:S(2)}, u32[]{:S(2)}) collective-permute-start(bf16[224,128]{1,0:T(8,128)(2,1)S(1)} %shard_map.202.refs_1_), channel_id=1, source_target_pairs={{0,8},{8,0},{16,24},{24,16},{1,9},{9,1},{17,25},{25,17},{2,10},{10... | collective-permute-start | bytes 172040 | tf_op jit(solution)/shard_map/ppermute | solution.py:459
  40.0 2.6 %copy-start = (bf16[4,96,256]{2,0,1:T(4,128)(2,1)}, bf16[4,96,256]{2,0,1:T(4,128)(2,1)S(1)}, u32[]{:S(2)}) copy-start(bf16[4,96,256]{2,0,1:T(4,128)(2,1)S(1)} %copy.26) | copy-start | bytes 589828
  42.6 1.4 %collective-permute-start.10 = (f32[224,128]{1,0:T(8,128)S(1)}, f32[224,128]{1,0:T(8,128)S(1)}, u32[]{:S(2)}, u32[]{:S(2)}) collective-permute-start(f32[224,128]{1,0:T(8,128)S(1)} %shard_map.203.refs_5_.refs_0_), channel_id=1, source_target_pairs={{0,4},{4,0},{1,5},{5,1},{2,6},{6,2},{3,7},{7,3},{8,12},{12,8},{9,1... | collective-permute-start | bytes 344072 | tf_op jit(solution)/shard_map/ppermute | solution.py:455

commit v5 on v4

--- a/solution.py
+++ b/solution.py
@@ -177,7 +177,7 @@
 def gelu_parts(v):
     z = jnp.abs(v)
     t = 1.0 / (1.0 + (0.3275911 / math.sqrt(2.0)) * z)
-    e = jnp.exp(-0.5 * (v * v))
+    e = jnp.exp2((-0.5 * math.log2(math.e)) * (v * v))
     half = 0.5
     poly = t * (
         half * 0.254829592
@@ -290,64 +290,56 @@
         small_ref[b * 8 + SIDE : b * 8 + 8, :] = vectors_ref[b : b + 1, :]
 
 
-def first_kernel(axis, panel, share_ref, keep_ref, small_ref, edges_ref, send_ref, rest_ref, total_ref):
+def columns_kernel(axis, panel, share_ref, keep_ref, small_ref, edges_ref, *refs):
+    *send_refs, kept_ref, total_ref = refs
     f = lax.axis_index(axis)
     count = total_ref.shape[0]
     total_ref[...] = keep_ref[...] + share_ref[share_ref.shape[0] - count :, :].astype(F32)
     part = lambda k: total_ref[pl.ds(pl.multiple_of(k * panel, 8), panel), :]
     tail = small_ref[...].astype(BF16)
     small = tail.shape[0]
-    even = lax.rem(f, 2) == 0
-    mate = f + 1 - 2 * lax.rem(f, 2)
-    send_ref[0:panel, :] = part(mate).astype(BF16)
-    send_ref[panel : 2 * panel, :] = part(3 - mate).astype(BF16)
-    send_ref[2 * panel : 2 * panel + small, :] = tail
     high = edges_ref.shape[0] // 2
-    send_ref[2 * panel + small :, :] = jnp.where(even, edges_ref[:high, :], edges_ref[high:, :])
-    rest_ref[0:panel, :] = part(f)
-    rest_ref[panel : 2 * panel, :] = part(3 - f)
-    rest_ref[2 * panel :, :] = tail.astype(F32)
-
-
-def second_kernel(axis, panel, got_ref, rest_ref, edges_ref, send_ref, kept_ref):
-    even = lax.rem(lax.axis_index(axis), 2) == 0
-    count = rest_ref.shape[0]
-    total = rest_ref[...] + got_ref[0:count, :].astype(F32)
-    tail = total[2 * panel :].astype(BF16)
-    small = tail.shape[0]
-    high = edges_ref.shape[0] // 2
-    send_ref[0:panel, :] = total[panel : 2 * panel].astype(BF16)
-    send_ref[panel : panel + small, :] = tail
-    send_ref[panel + small :, :] = jnp.where(even, edges_ref[high:, :], edges_ref[:high, :])
-    kept_ref[0:panel, :] = total[0:panel]
+    for mate, send_ref in zip(mates(f), send_refs):
+        send_ref[0:panel, :] = part(mate).astype(BF16)
+        send_ref[panel : panel + small, :] = tail
+        send_ref[panel + small :, :] = jnp.where(mate > f, edges_ref[:high, :], edges_ref[high:, :])
+    kept_ref[0:panel, :] = part(f)
     kept_ref[panel:, :] = tail.astype(F32)
 
 
-def third_kernel(axis, got_ref, kept_ref, before_ref, send_ref):
+def mates(index):
+    low = 1 - 2 * lax.rem(index, 2)
+    high = jnp.where(index < 2, 2, -2)
+    return index + low, index + high, index + low + high
+
+
+def four_sums(mine, parts):
+    first, second, third = (part.astype(F32) for part in parts)
+    return (mine + first) + (second + third)
+
+
+def chips_kernel(axis, kept_ref, first_ref, second_ref, third_ref, send_ref, plain_ref):
     f = lax.axis_index(axis)
     even = lax.rem(f, 2) == 0
     count = kept_ref.shape[0]
-    near = before_ref[before_ref.shape[0] - (got_ref.shape[0] - count) :, :]
-    far = got_ref[count:, :]
+    total = four_sums(kept_ref[...], [ref[0:count, :] for ref in (first_ref, second_ref, third_ref)]).astype(BF16)
+    near, far = first_ref[count:, :], third_ref[count:, :]
     far = jnp.where((f == 0) | (f == lax.axis_size(axis) - 1), jnp.zeros_like(far), far)
-    total = kept_ref[...] + got_ref[0:count, :].astype(F32)
     edges = [jnp.where(even, far, near), jnp.where(even, near, far)]
-    send_ref[...] = jnp.concatenate([total.astype(BF16), *edges], axis=0)
-
-
-def fourth_kernel(count, got_ref, mine_ref, send_ref):
-    total = mine_ref[0:count, :].astype(F32) + got_ref[0:count, :].astype(F32)
-    send_ref[...] = jnp.concatenate([total.astype(BF16), mine_ref[count:, :], got_ref[count:, :]], axis=0)
-
-
-def fifth_kernel(axes, count, got_ref, mine_ref, total_ref):
+    plain_ref[...] = total
+    send_ref[...] = jnp.concatenate([total, *edges], axis=0)
+
+
+def total_kernel(axes, mine_ref, first_ref, second_ref, third_ref, total_ref):
     q, core = lax.axis_index(axes[0]), lax.axis_index(axes[1])
-    total_ref[0:count, :] = mine_ref[0:count, :].astype(F32) + got_ref[0:count, :].astype(F32)
-    wide = (got_ref.shape[0] - count) // 2
-    total_ref[count : count + wide, :] = mine_ref[count : count + wide, :].astype(F32)
+    count = second_ref.shape[0]
+    wide = mine_ref.shape[0] - count
+    mine = mine_ref[0:count, :].astype(F32)
+    total_ref[0:count, :] = four_sums(mine, [ref[0:count, :] for ref in (first_ref, second_ref, third_ref)])
+    total_ref[count : count + wide, :] = mine_ref[count:, :].astype(F32)
     other = q + 1 - 2 * core
     beside = lax.rem(q + core, 2) == 0
-    value = jnp.where(beside, got_ref[count : count + wide, :], got_ref[count + wide :, :]).astype(F32)
+    value = jnp.where(beside, first_ref[count:, :], third_ref[count:, :]).astype(F32)
     total_ref[count + wide :, :] = jnp.where((other >= 0) & (other < lax.axis_size(axes[0])), value, 0.0)
 
 
@@ -428,7 +420,7 @@
     eb_ref[...] = jnp.sum(jnp.where(eye, high[0:panel, channels : channels + 1], 0.0), axis=0, keepdims=True)
 
 
-def call(kernel, outs, *args, scratch=(), after=()):
+def call(kernel, outs, *args, scratch=(), after=(), flops=0):
     size = sum(math.prod(a.shape) * a.dtype.itemsize for a in args)
     size += sum(math.prod(s) * jnp.dtype(d).itemsize for s, d in outs)
     count = len(args)
@@ -445,7 +437,7 @@
         out_specs=[in_vmem] * len(outs),
         scratch_shapes=[pltpu.VMEM(s, d) for s, d in scratch],
         compiler_params=pltpu.CompilerParams(vmem_limit_bytes=40 * 2**20),
-        cost_estimate=pl.CostEstimate(flops=0, bytes_accessed=size, transcendentals=0),
+        cost_estimate=pl.CostEstimate(flops=flops, bytes_accessed=size, transcendentals=0),
     )(*args, *after)
 
 
@@ -546,33 +538,30 @@
         scratch=[((deep, rows * extent), BF16), ((deep, rows * extent), BF16), ((8, DEEP), F32)],
     )
     share = swap(share, core, 0)
-    far = swap(far_out, space, 1)
+    far = swap(far_out, space, 1) if direct else None
     low = panel + small_n
     if direct:
-        send, kept = call(
-            functools.partial(first_kernel, filt, panel),
-            [((panel + low + high, LANES), BF16), ((panel + low, LANES), F32)],
+        sums = ((low, LANES), BF16)
+        *sends, kept = call(
+            functools.partial(columns_kernel, filt, panel),
+            [((low + high, LANES), BF16)] * 3 + [((low, LANES), F32)],
             share, keep, small, edges,
             scratch=[flat],
         )
-        first = crossed(send, filt, 1)
-        send, kept = call(
-            functools.partial(second_kernel, filt, panel),
-            [((low + high, LANES), BF16), ((low, LANES), F32)],
-            first, kept, edges,
+        third, second, first = (crossed(sends[k - 1], filt, k) for k in (3, 2, 1))
+        send, plain = call(
+            functools.partial(chips_kernel, filt), [((low + 2 * high, LANES), BF16), sums], kept, first, second, third,
+            flops=4 * 10**9,
         )
-        got = crossed(send, filt, 3)
-        own = ((low + 2 * high, LANES), BF16)
-        (third,) = call(functools.partial(third_kernel, filt), [own], got, kept, first)
-        got = crossed(third, chip, 2)
-        (send,) = call(
-            functools.partial(fourth_kernel, low), [((low + 4 * high, LANES), BF16)], got, third, after=[far]
-        )
-        got = crossed(send, chip, 1)
+        third, second, first = (crossed(plain if k == 2 else send, chip, k) for k in (3, 2, 1))
         (mine,) = call(
-            functools.partial(fifth_kernel, axes, low), [((low + 4 * high, LANES), F32)], got, send, after=[output]
+            functools.partial(total_kernel, axes),
+            [((low + 4 * high, LANES), F32)],
+            send, first, second, third,
+            after=[output, far],
         )
     else:
+        far = swap(far_out, space, 1)
         edges = edges_by_permutes(axes, edges).astype(F32)
         total, small = lax.psum((keep + share[-hidden_n:].astype(F32), small), (chip, filt))
         total = lax.dynamic_slice_in_dim(total, lax.axis_index(filt) * panel, panel, 0)

time: 45.4 us -> 43.5 us (0.958)
  waiting for transfers between devices: 11.4 us -> 9.03 us
  starting transfers between devices: 22.7 us -> 23.3 us
    ppermute x4 -> x6, waiting for transfers between devices: 10 us -> 7.66 us  [crossed(): lax.ppermute(x, axis, [(i, i ^ bits) for i in range(lax.axis_size(axis))])]
    ppermute x4 -> x6, starting transfers between devices: 12.2 us -> 12.8 us  [crossed(): lax.ppermute(x, axis, [(i, i ^ bits) for i in range(lax.axis_size(axis))])]
    pallas_call x12 -> x10, Pallas kernels: 8.36 us -> 8.28 us  [call(): pl.pallas_call(body, out_shape=[jax.ShapeDtypeStruct(s, d) for s, d in ou...]
  transfers between devices with their start and end apart: 11 -> 13, of which waited for: 7 -> 6; matrix products, arithmetic and copies ran while one was open for 0% -> 0% of each run, Pallas kernels for 6% -> 6%
where the time goes in v5:
time: 43.5 us; the launch traced here: 43.3 us
  starting transfers between devices  23.3 us (54%)
  waiting for transfers between devices  9.03 us (21%)
  Pallas kernels  8.28 us (19%)
  local copies, waits for them, and re-layouts  1.82 us (4%)
  between operations  0.91 us (2%)
    ppermute x6, starting transfers between devices, crossed(): lax.ppermute(x, axis, [(i, i ^ bits) for i in range(lax.axis_size(axis))])  12.8 us
    ppermute x7, starting transfers between devices, swap(): return lax.ppermute(x, axis, pairs + [(j, i) for i, j in pairs])  10.5 us
    pallas_call x10, Pallas kernels, call(): pl.pallas_call(body, out_shape=[jax.ShapeDtypeStruct(s, d) for s, d in ou...  8.28 us
    ppermute x6, waiting for transfers between devices, crossed(): lax.ppermute(x, axis, [(i, i ^ bits) for i in range(lax.axis_size(axis))])  7.66 us
    unnamed x23, local copies, waits for them, and re-layouts  1.66 us
    ppermute x7, waiting for transfers between devices, swap(): return lax.ppermute(x, axis, pairs + [(j, i) for i, j in pairs])  1.37 us
  transfers between devices with their start and end apart: 13, of which 6 were waited for; matrix products, arithmetic and copies ran while one was open for 0% of the time, Pallas kernels for 6%

profile of v5, /device:TPU:0, one launch (start us, length us, event | category | flops | bytes accessed | tf_op | source)
XLA Modules:
  0.0 43.3 jit_solution(3701660396224516861)
XLA Ops:
  0.6 0.0 copy-start.3
  0.7 1.0 %copy.27 = bf16[96,4,256]{2,0,1:T(8,128)(2,1)S(1)} copy(bf16[96,4,256]{2,1,0:T(4,128)(2,1)} %param.11) | data formatting | bytes 393216 | tf_op args[0]
  1.6 0.0 copy-start.1
  1.7 0.0 copy-start.2
  1.7 0.0 copy-start.4
  1.7 0.0 copy-start.10
  1.7 0.5 %collective-permute-start = (bf16[3,96,256]{2,1,0:T(8,128)(2,1)S(1)}, bf16[3,96,256]{2,1,0:T(8,128)(2,1)S(1)}, u32[]{:S(2)}, u32[]{:S(2)}) collective-permute-start(bf16[3,96,256]{2,1,0:T(8,128)(2,1)S(1)} %get-tuple-element.47), channel_id=1, source_target_pairs={{0,4},{4,0},{1,5},{5,1},{2,6},{6,2},{3,7},{7,3},{8,12},{12,8},{9,1... | collective-permute-start | bytes 442376 | tf_op jit(solution)/shard_map/ppermute | solution.py:447
  2.3 0.7 %collective-permute-start.1 = (bf16[3,96,256]{2,1,0:T(8,128)(2,1)S(1)}, bf16[3,96,256]{2,1,0:T(8,128)(2,1)S(1)}, u32[]{:S(2)}, u32[]{:S(2)}) collective-permute-start(bf16[3,96,256]{2,1,0:T(8,128)(2,1)S(1)} %get-tuple-element.48), channel_id=1, source_target_pairs={{4,8},{12,16},{20,24},{8,4},{16,12},{24,20},{5,9},{13,17},{21,25},... | collective-permute-start | bytes 442376 | tf_op jit(solution)/shard_map/ppermute | solution.py:447
  2.9 0.0 copy-done.10
  2.9 0.0 copy-start.8
  3.0 0.0 copy-start.9
  3.0 0.0 copy-start.5
  3.0 0.0 copy-start.6
  3.0 0.0 copy-start.7
  3.0 0.0 copy-done.3
  3.0 0.0 copy-done.1
  3.0 0.0 copy-done.2
  3.0 0.0 copy-done.4
  3.0 0.6 %copy-done.8 = f32[96]{0:T(128)S(1)} copy-done((f32[96]{0:T(128)S(1)}, f32[96]{0:T(128)}, u32[]{:S(2)}) %copy-start.8) | copy-done | bytes 408
  3.6 0.0 copy-done.9
  3.6 0.0 copy-done.5
  3.6 0.0 copy-done.6
  3.6 0.0 copy-done.7
  3.7 0.7 %shard_map.195 = (bf16[4,96,256]{2,1,0:T(8,128)(2,1)S(1)}, bf16[3,224,224]{2,1,0:T(8,128)(2,1)S(1)}, bf16[3,224,224]{2,1,0:T(8,128)(2,1)S(1)}, bf16[384,112]{1,0...) custom-call(bf16[96,4,256]{2,1,0:T(4,128)(2,1)S(1)} %copy-done.3, f32[7,7,96]{2,1,0:T(8,128)S(1)} %bitcast.29, ...), custom_call_target="tpu_custom_call" | custom-call | bytes 1373184 | tf_op jit(solution)/shard_map/pallas_call | solution.py:433
  4.4 0.0 collective-permute-done.refs_1_
  4.4 0.0 collective-permute-done.1.refs_2_
  4.4 0.3 shard_map.196
  4.7 2.7 %collective-permute-start.2 = (bf16[32,96]{1,0:T(8,128)(2,1)S(1)}, bf16[32,96]{1,0:T(8,128)(2,1)S(1)}, u32[]{:S(2)}, u32[]{:S(2)}) collective-permute-start(bf16[32,96]{1,0:T(8,128)(2,1)S(1)} %get-tuple-element.51), channel_id=1, source_target_pairs={{0,1},{2,3},{1,0},{3,2},{4,5},{6,7},{5,4},{7,6},{8,9},{10,11},{9,8... | collective-permute-start | bytes 18440 | tf_op jit(solution)/shard_map/ppermute | solution.py:447
  7.3 0.6 %collective-permute-start.3 = (bf16[32,96]{1,0:T(8,128)(2,1)S(1)}, bf16[32,96]{1,0:T(8,128)(2,1)S(1)}, u32[]{:S(2)}, u32[]{:S(2)}) collective-permute-start(bf16[32,96]{1,0:T(8,128)(2,1)S(1)} %get-tuple-element.52), channel_id=1, source_target_pairs={{1,2},{2,1},{5,6},{6,5},{9,10},{10,9},{13,14},{14,13},{17,18},{18,... | collective-permute-start | bytes 18440 | tf_op jit(solution)/shard_map/ppermute | solution.py:447
  8.0 1.0 %collective-permute-done.2.refs_1_ = bf16[32,96]{1,0:T(8,128)(2,1)S(1)} collective-permute-done((bf16[32,96]{1,0:T(8,128)(2,1)S(1)}, bf16[32,96]{1,0:T(8,128)(2,1)S(1)}, u32[]{:S(2)}, u32[]{:S(2)}) %collective-permute-start.2) | collective-permute-done | bytes 6176 | tf_op jit(solution)/shard_map/ppermute | solution.py:447
  9.0 0.0 collective-permute-done.3.refs_2_
  9.0 3.9 %shard_map.197 = (bf16[4,96,256]{2,1,0:T(8,128)(2,1)S(1)}, bf16[4,96,256]{2,1,0:T(8,128)(2,1)S(1)}, bf16[3,96,256]{2,1,0:T(8,128)(2,1)S(1)}, bf16[10,96,384]{2,1...) custom-call(bf16[10,96,256]{2,1,0:T(8,128)(2,1)S(1)} %get-tuple-element.50.refs_0_,, ...), custom_call_target="tpu_custom_call" | custom-call | bytes 3082624 | tf_op jit(solution)/shard_map/pallas_call | solution.py:433
  12.9 5.3 %collective-permute-start.4 = (bf16[960,128]{1,0:T(8,128)(2,1)S(1)}, bf16[960,128]{1,0:T(8,128)(2,1)S(1)}, u32[]{:S(2)}, u32[]{:S(2)}) collective-permute-start(bf16[960,128]{1,0:T(8,128)(2,1)S(1)} %get-tuple-element.58), channel_id=1, source_target_pairs={{0,4},{4,0},{1,5},{5,1},{2,6},{6,2},{3,7},{7,3},{8,12},{12,8},{9,1... | collective-permute-start | bytes 737288 | tf_op jit(solution)/shard_map/ppermute | solution.py:447
  18.2 0.9 %shard_map.198 = (bf16[32,128]{1,0:T(8,128)(2,1)S(1)}, f32[64,128]{1,0:T(8,128)S(1)}) custom-call(bf16[10,96,384]{2,1,0:T(8,128)(2,1)S(1)} %get-tuple-element.60.refs_0_, bf16[4,96,256]{2,1,0:T(8,128)(2,1)S(1)} %get-tuple-element.61.refs_1_.refs_0_, f32[8,128]{1,0:T(8,128)S(1)} %get-tuple-element.62.refs_2_), custom_call_target="tpu_custom_call" | custom-call | bytes 978944 | tf_op jit(solution)/shard_map/pallas_call | solution.py:433
  19.1 0.2 collective-permute-done.4.refs_0_.refs_1_
  19.4 4.8 %collective-permute-start.5 = (bf16[176,128]{1,0:T(8,128)(2,1)S(1)}, bf16[176,128]{1,0:T(8,128)(2,1)S(1)}, u32[]{:S(2)}, u32[]{:S(2)}) collective-permute-start(bf16[176,128]{1,0:T(8,128)(2,1)S(1)} %get-tuple-element.66), channel_id=1, source_target_pairs={{0,1},{1,0},{2,3},{3,2},{4,5},{5,4},{6,7},{7,6},{8,9},{9,8},{10,11... | collective-permute-start | bytes 135176 | tf_op jit(solution)/shard_map/ppermute | solution.py:451
  24.2 1.3 %collective-permute-start.6 = (bf16[176,128]{1,0:T(8,128)(2,1)S(1)}, bf16[176,128]{1,0:T(8,128)(2,1)S(1)}, u32[]{:S(2)}, u32[]{:S(2)}) collective-permute-start(bf16[176,128]{1,0:T(8,128)(2,1)S(1)} %get-tuple-element.67), channel_id=1, source_target_pairs={{0,2},{1,3},{2,0},{3,1},{4,6},{5,7},{6,4},{7,5},{8,10},{9,11},{10,... | collective-permute-start | bytes 135176 | tf_op jit(solution)/shard_map/ppermute | solution.py:451
  25.5 1.4 %collective-permute-start.7 = (bf16[176,128]{1,0:T(8,128)(2,1)S(1)}, bf16[176,128]{1,0:T(8,128)(2,1)S(1)}, u32[]{:S(2)}, u32[]{:S(2)}) collective-permute-start(bf16[176,128]{1,0:T(8,128)(2,1)S(1)} %get-tuple-element.68), channel_id=1, source_target_pairs={{0,3},{1,2},{2,1},{3,0},{4,7},{5,6},{6,5},{7,4},{8,11},{9,10},{10,... | collective-permute-start | bytes 135176 | tf_op jit(solution)/shard_map/ppermute | solution.py:451
  26.9 0.7 %collective-permute-start.11 = (bf16[3,96,256]{2,1,0:T(8,128)(2,1)S(1)}, bf16[3,96,256]{2,1,0:T(8,128)(2,1)S(1)}, u32[]{:S(2)}, u32[]{:S(2)}) collective-permute-start(bf16[3,96,256]{2,1,0:T(8,128)(2,1)S(1)} %get-tuple-element.71), channel_id=1, source_target_pairs={{4,8},{12,16},{20,24},{8,4},{16,12},{24,20},{5,9},{13,17},{21,25},... | collective-permute-start | bytes 442376 | tf_op jit(solution)/shard_map/ppermute | solution.py:447
  27.5 0.0 collective-permute-done.5.refs_1_
  27.5 3.0 %collective-permute-done.6.refs_2_ = bf16[176,128]{1,0:T(8,128)(2,1)S(1)} collective-permute-done((bf16[176,128]{1,0:T(8,128)(2,1)S(1)}, bf16[176,128]{1,0:T(8,128)(2,1)S(1)}, u32[]{:S(2)}, u32[]{:S(2)}) %collective-permute-start.6) | collective-permute-done | bytes 45088 | tf_op jit(solution)/shard_map/ppermute | solution.py:451
  30.5 0.8 %collective-permute-done.7.refs_3_ = bf16[176,128]{1,0:T(8,128)(2,1)S(1)} collective-permute-done((bf16[176,128]{1,0:T(8,128)(2,1)S(1)}, bf16[176,128]{1,0:T(8,128)(2,1)S(1)}, u32[]{:S(2)}, u32[]{:S(2)}) %collective-permute-start.7) | collective-permute-done | bytes 45088 | tf_op jit(solution)/shard_map/ppermute | solution.py:451
  31.4 3.6 %collective-permute-start.10 = (bf16[192,128]{1,0:T(8,128)(2,1)S(1)}, bf16[192,128]{1,0:T(8,128)(2,1)S(1)}, u32[]{:S(2)}, u32[]{:S(2)}) collective-permute-start(bf16[192,128]{1,0:T(8,128)(2,1)S(1)} %get-tuple-element.69.refs_0_), channel_id=1, source_target_pairs={{0,24},{8,16},{16,8},{24,0},{1,25},{9,17},{17,9},{25,1},{2,26},{10... | collective-permute-start | bytes 147464 | tf_op jit(solution)/shard_map/ppermute | solution.py:451
  35.0 1.7 %collective-permute-start.8 = (bf16[192,128]{1,0:T(8,128)(2,1)S(1)}, bf16[192,128]{1,0:T(8,128)(2,1)S(1)}, u32[]{:S(2)}, u32[]{:S(2)}) collective-permute-start(bf16[192,128]{1,0:T(8,128)(2,1)S(1)} %get-tuple-element.69.refs_0_), channel_id=1, source_target_pairs={{0,8},{8,0},{16,24},{24,16},{1,9},{9,1},{17,25},{25,17},{2,10},{10... | collective-permute-start | bytes 147464 | tf_op jit(solution)/shard_map/ppermute | solution.py:451
  36.7 0.0 collective-permute-start.9
  36.7 0.2 copy.26
  36.9 0.0 copy-start
  36.9 0.0 collective-permute-done.11.refs_5_.refs_2_
  36.9 3.8 %collective-permute-done.9.refs_2_ = bf16[160,128]{1,0:T(8,128)(2,1)S(1)} collective-permute-done((bf16[160,128]{1,0:T(8,128)(2,1)S(1)}, bf16[160,128]{1,0:T(8,128)(2,1)S(1)}, u32[]{:S(2)}, u32[]{:S(2)}) %collective-permute-start.9) | collective-permute-done | bytes 40992 | tf_op jit(solution)/shard_map/ppermute | solution.py:451
  40.7 0.0 collective-permute-done.10.refs_3_
  40.7 0.0 collective-permute-done.8.refs_1_
  40.7 0.0 copy-done
  40.7 0.1 collective-permute-start.12
  40.8 1.1 %shard_map.202.refs_2_ = f32[384,256]{1,0:T(8,128)S(1)} custom-call(bf16[4,96,256]{2,1,0:T(8,128)(2,1)S(1)} %get-tuple-element.61.refs_1_.refs_0_, bf16[960,128]{1,0:T(8,128)(2,1)S(1)} %collective-permute-done.4.refs_0_.refs_1_, bf16[3,96,256]{2,1,0:T(8,128)(2,1)S(1)} %collective-permute-done.11.refs_5_.refs_2_, ...), custom_call_target="tpu_custom_call" | custom-call | bytes 1480704 | tf_op jit(solution)/shard_map/pallas_call | solution.py:433
  41.9 0.2 collective-permute-done.12.refs_1_
  42.1 1.2 %shard_map.203 = (bf16[96,4,256]{2,1,0:T(4,128)(2,1)}, f32[7,7,96]{2,1,0:T(8,128)}, f32[1,96]{1,0:T(1,128)}, f32[1,96]{1,0:T(1,128)}, f32[1,96]{1,0:T(1,128)}, /...) custom-call(f32[224,128]{1,0:T(8,128)S(1)} %shard_map.201.refs_5_.refs_0_, ...), custom_call_target="tpu_custom_call" | custom-call | bytes 932864 | tf_op jit(solution)/shard_map/pallas_call | solution.py:433
  (5 shorter events, 0.1 us)
Async XLA Ops:
  0.6 2.4 %copy-start.3 = (bf16[96,4,256]{2,1,0:T(4,128)(2,1)S(1)}, bf16[96,4,256]{2,1,0:T(4,128)(2,1)}, u32[]{:S(2)}) copy-start(bf16[96,4,256]{2,1,0:T(4,128)(2,1)} %refs_0_.1) | copy-start | bytes 589828
  1.6 1.4 %copy-start.1 = (bf16[384,96]{0,1:T(8,128)(2,1)S(1)}, bf16[384,96]{0,1:T(8,128)(2,1)}, u32[]{:S(2)}) copy-start(bf16[384,96]{0,1:T(8,128)(2,1)} %param.17) | copy-start | bytes 221188
  1.7 1.4 %copy-start.2 = (bf16[384,96]{0,1:T(8,128)(2,1)S(1)}, bf16[384,96]{0,1:T(8,128)(2,1)}, u32[]{:S(2)}) copy-start(bf16[384,96]{0,1:T(8,128)(2,1)} %param.19) | copy-start | bytes 221188
  1.7 1.4 %copy-start.4 = (f32[96,7,7]{0,2,1:T(8,128)S(1)}, f32[96,7,7]{0,2,1:T(8,128)}, u32[]{:S(2)}) copy-start(f32[96,7,7]{0,2,1:T(8,128)} %param.13) | copy-start | bytes 56452
  1.7 1.2 %copy-start.10 = (bf16[384]{0:T(512)(128)(2,1)S(1)}, bf16[384]{0:T(512)(128)(2,1)}, u32[]{:S(2)}) copy-start(bf16[384]{0:T(512)(128)(2,1)} %param.18) | copy-start | bytes 2308
  1.7 2.6 %collective-permute-start = (bf16[3,96,256]{2,1,0:T(8,128)(2,1)S(1)}, bf16[3,96,256]{2,1,0:T(8,128)(2,1)S(1)}, u32[]{:S(2)}, u32[]{:S(2)}) collective-permute-start(bf16[3,96,256]{2,1,0:T(8,128)(2,1)S(1)} %get-tuple-element.47), channel_id=1, source_target_pairs={{0,4},{4,0},{1,5},{5,1},{2,6},{6,2},{3,7},{7,3},{8,12},{12,8},{9,1... | collective-permute-start | bytes 442376 | tf_op jit(solution)/shard_map/ppermute | solution.py:447
  2.3 2.1 %collective-permute-start.1 = (bf16[3,96,256]{2,1,0:T(8,128)(2,1)S(1)}, bf16[3,96,256]{2,1,0:T(8,128)(2,1)S(1)}, u32[]{:S(2)}, u32[]{:S(2)}) collective-permute-start(bf16[3,96,256]{2,1,0:T(8,128)(2,1)S(1)} %get-tuple-element.48), channel_id=1, source_target_pairs={{4,8},{12,16},{20,24},{8,4},{16,12},{24,20},{5,9},{13,17},{21,25},... | collective-permute-start | bytes 442376 | tf_op jit(solution)/shard_map/ppermute | solution.py:447
  2.9 0.7 %copy-start.8 = (f32[96]{0:T(128)S(1)}, f32[96]{0:T(128)}, u32[]{:S(2)}) copy-start(f32[96]{0:T(128)} %param.16) | copy-start | bytes 1156
  3.0 0.7 %copy-start.9 = (f32[96]{0:T(128)S(1)}, f32[96]{0:T(128)}, u32[]{:S(2)}) copy-start(f32[96]{0:T(128)} %param.20) | copy-start | bytes 1156
  3.0 0.7 %copy-start.5 = (f32[96]{0:T(128)S(1)}, f32[96]{0:T(128)}, u32[]{:S(2)}) copy-start(f32[96]{0:T(128)} %param.21) | copy-start | bytes 1156
  3.0 0.7 %copy-start.6 = (f32[96]{0:T(128)S(1)}, f32[96]{0:T(128)}, u32[]{:S(2)}) copy-start(f32[96]{0:T(128)} %param.14) | copy-start | bytes 1156
  3.0 0.7 %copy-start.7 = (f32[96]{0:T(128)S(1)}, f32[96]{0:T(128)}, u32[]{:S(2)}) copy-start(f32[96]{0:T(128)} %param.15) | copy-start | bytes 1156
  4.7 4.3 %collective-permute-start.2 = (bf16[32,96]{1,0:T(8,128)(2,1)S(1)}, bf16[32,96]{1,0:T(8,128)(2,1)S(1)}, u32[]{:S(2)}, u32[]{:S(2)}) collective-permute-start(bf16[32,96]{1,0:T(8,128)(2,1)S(1)} %get-tuple-element.51), channel_id=1, source_target_pairs={{0,1},{2,3},{1,0},{3,2},{4,5},{6,7},{5,4},{7,6},{8,9},{10,11},{9,8... | collective-permute-start | bytes 18440 | tf_op jit(solution)/shard_map/ppermute | solution.py:447
  7.3 1.6 %collective-permute-start.3 = (bf16[32,96]{1,0:T(8,128)(2,1)S(1)}, bf16[32,96]{1,0:T(8,128)(2,1)S(1)}, u32[]{:S(2)}, u32[]{:S(2)}) collective-permute-start(bf16[32,96]{1,0:T(8,128)(2,1)S(1)} %get-tuple-element.52), channel_id=1, source_target_pairs={{1,2},{2,1},{5,6},{6,5},{9,10},{10,9},{13,14},{14,13},{17,18},{18,... | collective-permute-start | bytes 18440 | tf_op jit(solution)/shard_map/ppermute | solution.py:447
  12.9 6.4 %collective-permute-start.4 = (bf16[960,128]{1,0:T(8,128)(2,1)S(1)}, bf16[960,128]{1,0:T(8,128)(2,1)S(1)}, u32[]{:S(2)}, u32[]{:S(2)}) collective-permute-start(bf16[960,128]{1,0:T(8,128)(2,1)S(1)} %get-tuple-element.58), channel_id=1, source_target_pairs={{0,4},{4,0},{1,5},{5,1},{2,6},{6,2},{3,7},{7,3},{8,12},{12,8},{9,1... | collective-permute-start | bytes 737288 | tf_op jit(solution)/shard_map/ppermute | solution.py:447
  19.4 8.1 %collective-permute-start.5 = (bf16[176,128]{1,0:T(8,128)(2,1)S(1)}, bf16[176,128]{1,0:T(8,128)(2,1)S(1)}, u32[]{:S(2)}, u32[]{:S(2)}) collective-permute-start(bf16[176,128]{1,0:T(8,128)(2,1)S(1)} %get-tuple-element.66), channel_id=1, source_target_pairs={{0,1},{1,0},{2,3},{3,2},{4,5},{5,4},{6,7},{7,6},{8,9},{9,8},{10,11... | collective-permute-start | bytes 135176 | tf_op jit(solution)/shard_map/ppermute | solution.py:451
  24.2 6.3 %collective-permute-start.6 = (bf16[176,128]{1,0:T(8,128)(2,1)S(1)}, bf16[176,128]{1,0:T(8,128)(2,1)S(1)}, u32[]{:S(2)}, u32[]{:S(2)}) collective-permute-start(bf16[176,128]{1,0:T(8,128)(2,1)S(1)} %get-tuple-element.67), channel_id=1, source_target_pairs={{0,2},{1,3},{2,0},{3,1},{4,6},{5,7},{6,4},{7,5},{8,10},{9,11},{10,... | collective-permute-start | bytes 135176 | tf_op jit(solution)/shard_map/ppermute | solution.py:451
  25.5 5.9 %collective-permute-start.7 = (bf16[176,128]{1,0:T(8,128)(2,1)S(1)}, bf16[176,128]{1,0:T(8,128)(2,1)S(1)}, u32[]{:S(2)}, u32[]{:S(2)}) collective-permute-start(bf16[176,128]{1,0:T(8,128)(2,1)S(1)} %get-tuple-element.68), channel_id=1, source_target_pairs={{0,3},{1,2},{2,1},{3,0},{4,7},{5,6},{6,5},{7,4},{8,11},{9,10},{10,... | collective-permute-start | bytes 135176 | tf_op jit(solution)/shard_map/ppermute | solution.py:451
  26.9 10.0 %collective-permute-start.11 = (bf16[3,96,256]{2,1,0:T(8,128)(2,1)S(1)}, bf16[3,96,256]{2,1,0:T(8,128)(2,1)S(1)}, u32[]{:S(2)}, u32[]{:S(2)}) collective-permute-start(bf16[3,96,256]{2,1,0:T(8,128)(2,1)S(1)} %get-tuple-element.71), channel_id=1, source_target_pairs={{4,8},{12,16},{20,24},{8,4},{16,12},{24,20},{5,9},{13,17},{21,25},... | collective-permute-start | bytes 442376 | tf_op jit(solution)/shard_map/ppermute | solution.py:447
  31.4 9.3 %collective-permute-start.10 = (bf16[192,128]{1,0:T(8,128)(2,1)S(1)}, bf16[192,128]{1,0:T(8,128)(2,1)S(1)}, u32[]{:S(2)}, u32[]{:S(2)}) collective-permute-start(bf16[192,128]{1,0:T(8,128)(2,1)S(1)} %get-tuple-element.69.refs_0_), channel_id=1, source_target_pairs={{0,24},{8,16},{16,8},{24,0},{1,25},{9,17},{17,9},{25,1},{2,26},{10... | collective-permute-start | bytes 147464 | tf_op jit(solution)/shard_map/ppermute | solution.py:451
  35.0 5.7 %collective-permute-start.8 = (bf16[192,128]{1,0:T(8,128)(2,1)S(1)}, bf16[192,128]{1,0:T(8,128)(2,1)S(1)}, u32[]{:S(2)}, u32[]{:S(2)}) collective-permute-start(bf16[192,128]{1,0:T(8,128)(2,1)S(1)} %get-tuple-element.69.refs_0_), channel_id=1, source_target_pairs={{0,8},{8,0},{16,24},{24,16},{1,9},{9,1},{17,25},{25,17},{2,10},{10... | collective-permute-start | bytes 147464 | tf_op jit(solution)/shard_map/ppermute | solution.py:451
  36.7 4.0 %collective-permute-start.9 = (bf16[160,128]{1,0:T(8,128)(2,1)S(1)}, bf16[160,128]{1,0:T(8,128)(2,1)S(1)}, u32[]{:S(2)}, u32[]{:S(2)}) collective-permute-start(bf16[160,128]{1,0:T(8,128)(2,1)S(1)} %get-tuple-element.70), channel_id=1, source_target_pairs={{0,16},{8,24},{16,0},{24,8},{1,17},{9,25},{17,1},{25,9},{2,18},{10... | collective-permute-start | bytes 122888 | tf_op jit(solution)/shard_map/ppermute | solution.py:451
  36.9 3.9 %copy-start = (bf16[4,96,256]{2,0,1:T(4,128)(2,1)}, bf16[4,96,256]{2,0,1:T(4,128)(2,1)S(1)}, u32[]{:S(2)}) copy-start(bf16[4,96,256]{2,0,1:T(4,128)(2,1)S(1)} %copy.26) | copy-start | bytes 589828
  40.7 1.4 %collective-permute-start.12 = (f32[224,128]{1,0:T(8,128)S(1)}, f32[224,128]{1,0:T(8,128)S(1)}, u32[]{:S(2)}, u32[]{:S(2)}) collective-permute-start(f32[224,128]{1,0:T(8,128)S(1)} %shard_map.201.refs_5_.refs_0_), channel_id=1, source_target_pairs={{0,4},{4,0},{1,5},{5,1},{2,6},{6,2},{3,7},{7,3},{8,12},{12,8},{9,1... | collective-permute-start | bytes 344072 | tf_op jit(solution)/shard_map/ppermute | solution.py:447

commit v6 on v5

--- a/solution.py
+++ b/solution.py
@@ -98,46 +98,58 @@
             xs_ref[at : at + GROUP, :] = moved[g * GROUP : (g + 1) * GROUP]
 
 
-def depthwise(w_ref, xs_ref, acc_ref, rows):
+def depthwise(w_ref, xs_ref, acc_ref, rows, taken, before_ref=None):
     groups = w_ref.shape[0]
     channels = groups * GROUP
     for g in range(groups):
-        sums = [None] * rows
-        for r in range(rows + 2 * HALO):
+        at = [slice(i * channels + g * GROUP, i * channels + (g + 1) * GROUP) for i in range(rows)]
+        sums = [None if before_ref is None else before_ref[at[i], :] for i in range(rows)]
+        for k, r in enumerate(taken):
             i0, i1 = max(0, r - (SIDE - 1)), min(rows - 1, r)
             m0 = SIDE - 1 - r + i0
-            at = r * SIDE * channels + g * DEEP
-            part = dot(w_ref[g, m0 * GROUP : (m0 + i1 - i0 + 1) * GROUP, :], xs_ref[at : at + DEEP, :])
+            low = k * SIDE * channels + g * DEEP
+            part = dot(w_ref[g, m0 * GROUP : (m0 + i1 - i0 + 1) * GROUP, :], xs_ref[low : low + DEEP, :])
             for i in range(i0, i1 + 1):
                 piece = part[(i - i0) * GROUP : (i - i0 + 1) * GROUP]
                 sums[i] = piece if sums[i] is None else sums[i] + piece
         for i in range(rows):
-            at = i * channels + g * GROUP
-            acc_ref[at : at + GROUP, :] = sums[i]
-
-
-def enter_kernel(core_axis, mid_ref, pair_ref, far_ref):
-    rows = mid_ref.shape[0]
-    core = lax.axis_index(core_axis)
-    for k in range(HALO):
-        pair_ref[k] = mid_ref[k + (rows - HALO) * (1 - core)]
-        far_ref[k] = mid_ref[k + (rows - HALO) * core]
-
-
-def gather_kernel(axes, mid_ref, pair_ref, far_ref, tall_ref, first_ref, second_ref):
-    rows = mid_ref.shape[0]
-    upper = lax.axis_index(axes[1]) == 0
-    for k in range(HALO):
-        pair, far = pair_ref[k], far_ref[k]
-        tall_ref[k] = jnp.where(upper, far, pair)
-        tall_ref[HALO + rows + k] = jnp.where(upper, pair, far)
+            acc_ref[at[i], :] = sums[i]
+
+
+def own_rows_kernel(mid_ref, own_ref, w_ref, acc_ref, x_ref, xs_ref):
+    rows, channels, _ = mid_ref.shape
+    edges_t = own_ref[:, 0:channels].T
     for i in range(rows):
-        tall_ref[HALO + i] = mid_ref[i]
-    edges = pack_edges([tall_ref[r] for r in range(rows + 2 * HALO)])
+        x = jnp.concatenate([mid_ref[i], halo_tile(edges_t, i, rows)], axis=1)
+        x_ref[i] = x
+        spread(xs_ref, i, x)
+    depthwise(w_ref, xs_ref, acc_ref, rows, range(HALO, HALO + rows))
+
+
+def edges_kernel(axis, mid_ref, first_ref, second_ref):
+    edges = pack_edges([mid_ref[i] for i in range(mid_ref.shape[0])])
     high = edges.shape[0] // 2
-    even = lax.rem(lax.axis_index(axes[2]), 2) == 0
+    even = lax.rem(lax.axis_index(axis), 2) == 0
     first_ref[...] = jnp.where(even, edges[:high], edges[high:])
     second_ref[...] = jnp.where(even, edges[high:], edges[:high])
+
+
+def far_kernel(axes, mid_ref, first_ref, second_ref, own_ref, far_ref):
+    even = lax.rem(lax.axis_index(axes[2]), 2) == 0
+    first, second = first_ref[...], second_ref[...]
+    edges = jnp.concatenate([jnp.where(even, second, first), jnp.where(even, first, second)], axis=0)
+    own_ref[...] = widened(edges)
+    put_strips(mid_ref, own_ref, far_ref, lax.axis_index(axes[1]))
+
+
+def pair_kernel(core_axis, mid_ref, own_ref, pair_ref):
+    put_strips(mid_ref, own_ref, pair_ref, 1 - lax.axis_index(core_axis))
+
+
+def put_strips(mid_ref, edges_ref, to_ref, last):
+    for k in range(HALO):
+        put_strip(to_ref, k, mid_ref[k + (mid_ref.shape[0] - HALO) * last])
+    to_ref[to_ref.shape[0] - edges_ref.shape[0] :, :] = edges_ref[...]
 
 
 def put_strip(ref, k, row):
@@ -189,7 +201,7 @@
 
 def main_kernel(
     axes,
-    tall_ref, first_ref, second_ref, cot_ref, w_ref, we_ref, wr_ref, we2_ref, wr2_ref, columns_ref, scale_ref,
+    mid_ref, pair_ref, beyond_ref, own_ref, before_ref, cot_ref, w_ref, we_ref, wr_ref, we2_ref, wr2_ref, columns_ref, scale_ref,
     out_ref, dconv_ref, far_ref, x_ref, vectors_ref, share_ref, keep_ref,
     xs_ref, acc_ref, xhat_ref, nm_ref, db_ref, act_ref, dh_ref,
 ):
@@ -198,14 +210,21 @@
     core = lax.axis_index(axes[1])
     dwb, gain, lnb, br, scale = (columns_ref[:, k : k + 1] for k in range(5))
     lead = HALO * channels * (width // LANES)
-    even = lax.rem(lax.axis_index(axes[2]), 2) == 0
-    first, second = first_ref[...], second_ref[...]
-    edges_t = jnp.concatenate([jnp.where(even, second, first), jnp.where(even, first, second)], axis=0).T
-    for r in range(rows + 2 * HALO):
-        x = jnp.concatenate([tall_ref[r], halo_tile(edges_t, r, rows + 2 * HALO)], axis=1)
-        spread(xs_ref, r, x)
-        x_ref[r] = x
-    depthwise(w_ref, xs_ref, acc_ref, rows)
+    upper = core == 0
+    high = own_ref.shape[0]
+    near, beyond = (ref[ref.shape[0] - high :, 0:channels].T for ref in (pair_ref, beyond_ref))
+    above, below = jnp.where(upper, beyond, near), jnp.where(upper, near, beyond)
+    for k in range(HALO):
+        pair, far = (get_strip(ref, k, channels, width) for ref in (pair_ref, beyond_ref))
+        up, down = jnp.where(upper, far, pair), jnp.where(upper, pair, far)
+        up = jnp.concatenate([up, halo_tile(above, rows - HALO + k, rows)], axis=1)
+        down = jnp.concatenate([down, halo_tile(below, k, rows)], axis=1)
+        x_ref[k] = up
+        x_ref[HALO + k] = down
+        spread(xs_ref, k, up)
+        spread(xs_ref, HALO + k, down)
+    taken = [*range(HALO), *range(HALO + rows, rows + 2 * HALO)]
+    depthwise(w_ref, xs_ref, acc_ref, rows, taken, before_ref)
     extra = nm_ref.shape[0] - channels
     nm_ref[channels:, :] = jnp.where(iota((extra, rows * width), 0) == 0, 1.0, 0.0).astype(BF16)
     zero = jnp.zeros((channels, LANES), F32)
@@ -235,7 +254,7 @@
             act_ref[hs, cols] = (hidden * phi).astype(BF16)
             dh_ref[hs, cols] = (back * (phi + bump)).astype(BF16)
         branch = dot(wr_ref[...], act_ref[:, cols]) + br
-        out_ref[i] = (tall_ref[HALO + i].astype(F32) + scale * branch).astype(BF16)
+        out_ref[i] = (mid_ref[i].astype(F32) + scale * branch).astype(BF16)
         add("scale", cot * branch)
         d_normed = dot(we_ref[...], dh_ref[:, cols])
         xhat = xhat_ref[...]
@@ -260,7 +279,7 @@
         vectors_ref[b : b + 1, 0:channels] = total * scale_ref[...] if name == "rb" else total
 
 
-def depthwise_gradient_kernel(x_ref, dconv_ref, vectors_ref, edges_ref, small_ref, wide_ref, dcs_ref, line_ref):
+def depthwise_gradient_kernel(x_ref, own_x_ref, dconv_ref, vectors_ref, edges_ref, small_ref, wide_ref, dcs_ref, line_ref):
     rows, channels, width = dconv_ref.shape
     groups = channels // GROUP
     extent = width + LANES
@@ -274,9 +293,14 @@
                 at = g * DEEP + b * GROUP
                 dcs_ref[at : at + GROUP, columns] = moved[g * GROUP : (g + 1) * GROUP]
         for a in range(SIDE):
+            r = i + a
+            if HALO <= r < HALO + rows:
+                x = own_x_ref[r - HALO]
+            else:
+                x = x_ref[r if r < HALO else r - rows]
             for g in range(groups):
                 at = g * DEEP + a * GROUP
-                wide_ref[at : at + GROUP, columns] = x_ref[i + a, g * GROUP : (g + 1) * GROUP, :]
+                wide_ref[at : at + GROUP, columns] = x[g * GROUP : (g + 1) * GROUP, :]
     small_ref[...] = jnp.zeros_like(small_ref)
     diagonal = group_diagonal()
     for g in range(groups):
@@ -302,7 +326,8 @@
     for mate, send_ref in zip(mates(f), send_refs):
         send_ref[0:panel, :] = part(mate).astype(BF16)
         send_ref[panel : panel + small, :] = tail
-        send_ref[panel + small :, :] = jnp.where(mate > f, edges_ref[:high, :], edges_ref[high:, :])
+        if send_ref.shape[0] > panel + small:
+            send_ref[panel + small :, :] = jnp.where(mate > f, edges_ref[:high, :], edges_ref[high:, :])
     kept_ref[0:panel, :] = part(f)
     kept_ref[panel:, :] = tail.astype(F32)
 
@@ -354,7 +379,7 @@
         put(HALO + rows + k, jnp.where(upper, pair, far))
     for i in range(rows):
         put(HALO + i, mid_ref[i])
-    depthwise(w_ref, xs_ref, acc_ref, rows)
+    depthwise(w_ref, xs_ref, acc_ref, rows, range(rows + 2 * HALO))
     for i in range(rows):
         acc_ref[i * channels : (i + 1) * channels, :] += cot_ref[i].astype(F32)
 
@@ -486,9 +511,13 @@
     space = (chip, core)
     lead = HALO * channels * (width // LANES)
     mid = jnp.transpose(image, (1, 0, 2))
-    pair, far = call(functools.partial(enter_kernel, core), [strip, strip], mid)
+    ends = ((high, channels), BF16)
+    lead = HALO * channels * (width // LANES)
+    flat_strip = ((lead + 2 * high, LANES), BF16)
+    first, second = call(functools.partial(edges_kernel, filt), [ends, ends], mid)
+    first, second = swap(first, filt, 0), swap(second, filt, 1)
+    own, far = call(functools.partial(far_kernel, axes), [edge, flat_strip], mid, first, second)
     far = swap(far, space, 1)
-    pair = swap(pair, core, 0)
     we_t, wr_t = w_expand.T, w_reduce.T
     taps = jnp.transpose(kernel, (1, 2, 0))
     cot_t, forward, backward, we2, wr2, columns = call(
@@ -504,24 +533,27 @@
         cotangent, taps, row(dw_bias), row(layer_norm_gain), row(layer_norm_bias),
         we_t, row(b_expand), wr_t, row(b_reduce), row(layer_scale),
         scratch=[((lift, hidden_n), BF16), ((8, DEEP), F32)],
-    )
-    ends = ((edge_height(tall), channels), BF16)
-    image_t, first, second = call(
-        functools.partial(gather_kernel, axes), [((tall, channels, width), BF16), ends, ends], mid, pair, far,
-        after=[columns],
-    )
-    first, second = swap(first, filt, 0), swap(second, filt, 1)
+        after=[own],
+    )
+    (pair,) = call(functools.partial(pair_kernel, core), [flat_strip], mid, own, after=[columns])
+    pair = swap(pair, core, 0)
+    before, own_x = call(
+        own_rows_kernel,
+        [((rows * channels, width), F32), ((rows, channels, extent), BF16)],
+        mid, own, forward,
+        scratch=[((rows * deep, width), BF16)],
+    )
     small_n = 64
     flat = ((hidden_n, LANES), F32)
     out_t, dconv, far_out, x, vectors, share, keep = call(
         functools.partial(main_kernel, axes),
         [
-            block, block, strip, ((tall, channels, extent), BF16), ((8, LANES), F32),
+            block, block, strip, ((2 * HALO, channels, extent), BF16), ((8, LANES), F32),
             ((HALO * channels * (width // LANES) + hidden_n, LANES), BF16), flat,
         ],
-        image_t, first, second, cot_t, forward, we_t, wr_t, we2, wr2, columns, row(layer_scale),
+        mid, pair, far, own, before, cot_t, forward, we_t, wr_t, we2, wr2, columns, row(layer_scale),
         scratch=[
-            ((tall * deep, width), BF16),
+            ((2 * HALO * deep, width), BF16),
             ((rows * channels, width), F32),
             ((channels, width), F32),
             ((lift, tokens), BF16),
@@ -534,7 +566,7 @@
     edges, small = call(
         depthwise_gradient_kernel,
         [edge, ((small_n, LANES), F32)],
-        x, dconv, vectors,
+        x, own_x, dconv, vectors,
         scratch=[((deep, rows * extent), BF16), ((deep, rows * extent), BF16), ((8, DEEP), F32)],
     )
     share = swap(share, core, 0)
@@ -544,7 +576,7 @@
         sums = ((low, LANES), BF16)
         *sends, kept = call(
             functools.partial(columns_kernel, filt, panel),
-            [((low + high, LANES), BF16)] * 3 + [((low, LANES), F32)],
+            [((low + high, LANES), BF16), sums, ((low + high, LANES), BF16), ((low, LANES), F32)],
             share, keep, small, edges,
             scratch=[flat],
         )

time: 43.5 us -> 42.8 us (0.984)
  starting transfers between devices: 23.3 us -> 21.7 us
  waiting for transfers between devices: 9.03 us -> 9.52 us
    ppermute x7, starting transfers between devices: 10.5 us -> 9.7 us  [swap(): return lax.ppermute(x, axis, pairs + [(j, i) for i, j in pairs])]
    ppermute x6, starting transfers between devices: 12.8 us -> 12 us  [crossed(): lax.ppermute(x, axis, [(i, i ^ bits) for i in range(lax.axis_size(axis))])]
    pallas_call x10 -> x12, Pallas kernels: 8.28 us -> 8.64 us  [call(): pl.pallas_call(body, out_shape=[jax.ShapeDtypeStruct(s, d) for s, d in ou...]
  transfers between devices with their start and end apart: 13 -> 13, of which waited for: 6 -> 6; matrix products, arithmetic and copies ran while one was open for 0% -> 0% of each run, Pallas kernels for 6% -> 9%
where the time goes in v6:
time: 42.8 us; the launch traced here: 42.6 us
  starting transfers between devices  21.7 us (51%)
  waiting for transfers between devices  9.52 us (22%)
  Pallas kernels  8.64 us (20%)
  local copies, waits for them, and re-layouts  1.81 us (4%)
  between operations  0.89 us (2%)
    ppermute x6, starting transfers between devices, crossed(): lax.ppermute(x, axis, [(i, i ^ bits) for i in range(lax.axis_size(axis))])  12 us
    ppermute x7, starting transfers between devices, swap(): return lax.ppermute(x, axis, pairs + [(j, i) for i, j in pairs])  9.7 us
    pallas_call x12, Pallas kernels, call(): pl.pallas_call(body, out_shape=[jax.ShapeDtypeStruct(s, d) for s, d in ou...  8.64 us
    ppermute x6, waiting for transfers between devices, crossed(): lax.ppermute(x, axis, [(i, i ^ bits) for i in range(lax.axis_size(axis))])  8.06 us
    unnamed x23, local copies, waits for them, and re-layouts  1.65 us
    ppermute x7, waiting for transfers between devices, swap(): return lax.ppermute(x, axis, pairs + [(j, i) for i, j in pairs])  1.46 us
  transfers between devices with their start and end apart: 13, of which 6 were waited for; matrix products, arithmetic and copies ran while one was open for 0% of the time, Pallas kernels for 9%

profile of v6, /device:TPU:0, one launch (start us, length us, event | category | flops | bytes accessed | tf_op | source)
XLA Modules:
  0.0 42.6 jit_solution(5626230125114008365)
XLA Ops:
  0.6 0.9 %copy.27 = bf16[96,4,256]{2,0,1:T(8,128)(2,1)S(1)} copy(bf16[96,4,256]{2,1,0:T(4,128)(2,1)} %param.11) | data formatting | bytes 393216 | tf_op args[0]
  1.6 0.0 copy-start.3
  1.6 0.2 shard_map.194
  1.8 0.0 copy-start.10
  1.8 3.1 %collective-permute-start = (bf16[16,96]{1,0:T(8,128)(2,1)S(1)}, bf16[16,96]{1,0:T(8,128)(2,1)S(1)}, u32[]{:S(2)}, u32[]{:S(2)}) collective-permute-start(bf16[16,96]{1,0:T(8,128)(2,1)S(1)} %get-tuple-element.48), channel_id=1, source_target_pairs={{0,1},{2,3},{1,0},{3,2},{4,5},{6,7},{5,4},{7,6},{8,9},{10,11},{9,8... | collective-permute-start | bytes 9224 | tf_op jit(solution)/shard_map/ppermute | solution.py:472
  4.9 0.6 %collective-permute-start.1 = (bf16[16,96]{1,0:T(8,128)(2,1)S(1)}, bf16[16,96]{1,0:T(8,128)(2,1)S(1)}, u32[]{:S(2)}, u32[]{:S(2)}) collective-permute-start(bf16[16,96]{1,0:T(8,128)(2,1)S(1)} %get-tuple-element.49), channel_id=1, source_target_pairs={{1,2},{2,1},{5,6},{6,5},{9,10},{10,9},{13,14},{14,13},{17,18},{18,... | collective-permute-start | bytes 9224 | tf_op jit(solution)/shard_map/ppermute | solution.py:472
  5.5 0.0 copy-done.10
  5.6 0.0 copy-start.1
  5.6 0.0 copy-start.2
  5.6 0.9 %collective-permute-done.refs_1_ = bf16[16,96]{1,0:T(8,128)(2,1)S(1)} collective-permute-done((bf16[16,96]{1,0:T(8,128)(2,1)S(1)}, bf16[16,96]{1,0:T(8,128)(2,1)S(1)}, u32[]{:S(2)}, u32[]{:S(2)}) %collective-permute-start) | collective-permute-done | bytes 3104 | tf_op jit(solution)/shard_map/ppermute | solution.py:472
  6.5 0.0 collective-permute-done.1.refs_2_
  6.5 0.0 copy-start.4
  6.5 0.7 %collective-permute-start.3 = (bf16[608,128]{1,0:T(8,128)(2,1)S(1)}, bf16[608,128]{1,0:T(8,128)(2,1)S(1)}, u32[]{:S(2)}, u32[]{:S(2)}) collective-permute-start(bf16[608,128]{1,0:T(8,128)(2,1)S(1)} %get-tuple-element.52), channel_id=1, source_target_pairs={{4,8},{12,16},{20,24},{8,4},{16,12},{24,20},{5,9},{13,17},{21,25},... | collective-permute-start | bytes 466952 | tf_op jit(solution)/shard_map/ppermute | solution.py:472
  7.2 0.0 copy-start.8
  7.2 0.0 copy-start.9
  7.2 0.0 copy-start.5
  7.2 0.0 copy-start.6
  7.2 0.0 copy-start.7
  7.2 0.0 copy-done.3
  7.3 0.0 copy-done.1
  7.3 0.0 copy-done.2
  7.3 0.0 copy-done.4
  7.3 0.6 %copy-done.8 = f32[96]{0:T(128)S(1)} copy-done((f32[96]{0:T(128)S(1)}, f32[96]{0:T(128)}, u32[]{:S(2)}) %copy-start.8) | copy-done | bytes 408
  7.8 0.0 copy-done.9
  7.9 0.0 copy-done.5
  7.9 0.0 copy-done.6
  7.9 0.0 copy-done.7
  7.9 0.7 %shard_map.196 = (bf16[4,96,256]{2,1,0:T(8,128)(2,1)S(1)}, bf16[3,224,224]{2,1,0:T(8,128)(2,1)S(1)}, bf16[3,224,224]{2,1,0:T(8,128)(2,1)S(1)}, bf16[384,112]{1,0...) custom-call(bf16[96,4,256]{2,1,0:T(4,128)(2,1)S(1)} %copy-done.3, f32[7,7,96]{2,1,0:T(8,128)S(1)} %bitcast.32, ...), custom_call_target="tpu_custom_call" | custom-call | bytes 1373184 | tf_op jit(solution)/shard_map/pallas_call | solution.py:458
  8.6 3.4 %collective-permute-start.2 = (bf16[608,128]{1,0:T(8,128)(2,1)S(1)}, bf16[608,128]{1,0:T(8,128)(2,1)S(1)}, u32[]{:S(2)}, u32[]{:S(2)}) collective-permute-start(bf16[608,128]{1,0:T(8,128)(2,1)S(1)} %shard_map.197), channel_id=1, source_target_pairs={{0,4},{4,0},{1,5},{5,1},{2,6},{6,2},{3,7},{7,3},{8,12},{12,8},{9,1... | collective-permute-start | bytes 466952 | tf_op jit(solution)/shard_map/ppermute | solution.py:472
  12.0 0.8 %shard_map.198 = (f32[384,256]{1,0:T(8,128)S(1)}, bf16[4,96,384]{2,1,0:T(8,128)(2,1)S(1)}) custom-call(bf16[4,96,256]{2,1,0:T(8,128)(2,1)S(1)} %bitcast.24, bf16[32,128]{1,0:T(8,128)(2,1)S(1)} %get-tuple-element.50.refs_10_.refs_1_.refs_3_, bf16[3,224,224]{2,1,0:T(8,128)(2,1)S(1)} %get-tuple-element.53.refs_2_.refs_6_), custom_call_target="tpu_custom_call" | custom-call | bytes 1193984 | tf_op jit(solution)/shard_map/pallas_call | solution.py:458
  12.8 0.0 collective-permute-done.3.refs_2_
  12.8 0.2 collective-permute-done.2.refs_1_
  13.0 3.6 %shard_map.199 = (bf16[4,96,256]{2,1,0:T(8,128)(2,1)S(1)}, bf16[4,96,256]{2,1,0:T(8,128)(2,1)S(1)}, bf16[3,96,256]{2,1,0:T(8,128)(2,1)S(1)}, bf16[6,96,384]{2,1,...) custom-call(bf16[4,96,256]{2,1,0:T(8,128)(2,1)S(1)} %bitcast.25, ...), custom_call_target="tpu_custom_call" | custom-call | bytes 3193216 | tf_op jit(solution)/shard_map/pallas_call | solution.py:458
  16.6 1.2 %collective-permute-start.4 = (bf16[960,128]{1,0:T(8,128)(2,1)S(1)}, bf16[960,128]{1,0:T(8,128)(2,1)S(1)}, u32[]{:S(2)}, u32[]{:S(2)}) collective-permute-start(bf16[960,128]{1,0:T(8,128)(2,1)S(1)} %get-tuple-element.59), channel_id=1, source_target_pairs={{0,4},{4,0},{1,5},{5,1},{2,6},{6,2},{3,7},{7,3},{8,12},{12,8},{9,1... | collective-permute-start | bytes 737288 | tf_op jit(solution)/shard_map/ppermute | solution.py:472
  17.8 1.0 %shard_map.200 = (bf16[32,128]{1,0:T(8,128)(2,1)S(1)}, f32[64,128]{1,0:T(8,128)S(1)}) custom-call(bf16[6,96,384]{2,1,0:T(8,128)(2,1)S(1)} %get-tuple-element.61.refs_0_, bf16[4,96,384]{2,1,0:T(8,128)(2,1)S(1)} %get-tuple-element.62.refs_1_, bf16[4,96,256]{2,1,0:T(8,128)(2,1)S(1)} %get-tuple-element.63.refs_2_.refs_0_, f32[8,128]{1,0:T(8,128)S(1)} %get-tuple-element.64.refs_3_), custom_call_target="tpu_custom_call" | custom-call | bytes 978944 | tf_op jit(solution)/shard_map/pallas_call | solution.py:458
  18.8 0.2 collective-permute-done.4.refs_0_.refs_1_
  19.0 4.7 %collective-permute-start.5 = (bf16[176,128]{1,0:T(8,128)(2,1)S(1)}, bf16[176,128]{1,0:T(8,128)(2,1)S(1)}, u32[]{:S(2)}, u32[]{:S(2)}) collective-permute-start(bf16[176,128]{1,0:T(8,128)(2,1)S(1)} %get-tuple-element.68), channel_id=1, source_target_pairs={{0,1},{1,0},{2,3},{3,2},{4,5},{5,4},{6,7},{7,6},{8,9},{9,8},{10,11... | collective-permute-start | bytes 135176 | tf_op jit(solution)/shard_map/ppermute | solution.py:476
  23.7 2.9 %collective-permute-start.7 = (bf16[176,128]{1,0:T(8,128)(2,1)S(1)}, bf16[176,128]{1,0:T(8,128)(2,1)S(1)}, u32[]{:S(2)}, u32[]{:S(2)}) collective-permute-start(bf16[176,128]{1,0:T(8,128)(2,1)S(1)} %get-tuple-element.70), channel_id=1, source_target_pairs={{0,3},{1,2},{2,1},{3,0},{4,7},{5,6},{6,5},{7,4},{8,11},{9,10},{10,... | collective-permute-start | bytes 135176 | tf_op jit(solution)/shard_map/ppermute | solution.py:476
  26.6 0.0 collective-permute-start.6
  26.6 0.7 %collective-permute-start.11 = (bf16[3,96,256]{2,1,0:T(8,128)(2,1)S(1)}, bf16[3,96,256]{2,1,0:T(8,128)(2,1)S(1)}, u32[]{:S(2)}, u32[]{:S(2)}) collective-permute-start(bf16[3,96,256]{2,1,0:T(8,128)(2,1)S(1)} %get-tuple-element.73), channel_id=1, source_target_pairs={{4,8},{12,16},{20,24},{8,4},{16,12},{24,20},{5,9},{13,17},{21,25},... | collective-permute-start | bytes 442376 | tf_op jit(solution)/shard_map/ppermute | solution.py:472
  27.2 4.2 %collective-permute-done.6.refs_2_ = bf16[160,128]{1,0:T(8,128)(2,1)S(1)} collective-permute-done((bf16[160,128]{1,0:T(8,128)(2,1)S(1)}, bf16[160,128]{1,0:T(8,128)(2,1)S(1)}, u32[]{:S(2)}, u32[]{:S(2)}) %collective-permute-start.6) | collective-permute-done | bytes 40992 | tf_op jit(solution)/shard_map/ppermute | solution.py:476
  31.5 0.0 collective-permute-done.5.refs_1_
  31.5 0.0 collective-permute-done.7.refs_3_
  31.5 3.0 %collective-permute-start.10 = (bf16[192,128]{1,0:T(8,128)(2,1)S(1)}, bf16[192,128]{1,0:T(8,128)(2,1)S(1)}, u32[]{:S(2)}, u32[]{:S(2)}) collective-permute-start(bf16[192,128]{1,0:T(8,128)(2,1)S(1)} %get-tuple-element.71.refs_0_), channel_id=1, source_target_pairs={{0,24},{8,16},{16,8},{24,0},{1,25},{9,17},{17,9},{25,1},{2,26},{10... | collective-permute-start | bytes 147464 | tf_op jit(solution)/shard_map/ppermute | solution.py:476
  34.5 1.4 %collective-permute-start.8 = (bf16[192,128]{1,0:T(8,128)(2,1)S(1)}, bf16[192,128]{1,0:T(8,128)(2,1)S(1)}, u32[]{:S(2)}, u32[]{:S(2)}) collective-permute-start(bf16[192,128]{1,0:T(8,128)(2,1)S(1)} %get-tuple-element.71.refs_0_), channel_id=1, source_target_pairs={{0,8},{8,0},{16,24},{24,16},{1,9},{9,1},{17,25},{25,17},{2,10},{10... | collective-permute-start | bytes 147464 | tf_op jit(solution)/shard_map/ppermute | solution.py:476
  35.9 0.0 collective-permute-start.9
  35.9 0.2 copy.26
  36.1 0.0 copy-start
  36.1 0.0 collective-permute-done.11.refs_5_.refs_2_
  36.1 3.8 %collective-permute-done.9.refs_2_ = bf16[160,128]{1,0:T(8,128)(2,1)S(1)} collective-permute-done((bf16[160,128]{1,0:T(8,128)(2,1)S(1)}, bf16[160,128]{1,0:T(8,128)(2,1)S(1)}, u32[]{:S(2)}, u32[]{:S(2)}) %collective-permute-start.9) | collective-permute-done | bytes 40992 | tf_op jit(solution)/shard_map/ppermute | solution.py:476
  39.9 0.0 collective-permute-done.10.refs_3_
  39.9 0.0 collective-permute-done.8.refs_1_
  40.0 0.0 copy-done
  40.0 0.1 collective-permute-start.12
  40.1 1.1 %shard_map.204.refs_2_ = f32[384,256]{1,0:T(8,128)S(1)} custom-call(bf16[4,96,256]{2,1,0:T(8,128)(2,1)S(1)} %get-tuple-element.63.refs_2_.refs_0_, bf16[960,128]{1,0:T(8,128)(2,1)S(1)} %collective-permute-done.4.refs_0_.refs_1_, bf16[3,96,256]{2,1,0:T(8,128)(2,1)S(1)} %collective-permute-done.11.refs_5_.refs_2_, ...), custom_call_target="tpu_custom_call" | custom-call | bytes 1480704 | tf_op jit(solution)/shard_map/pallas_call | solution.py:458
  41.2 0.2 collective-permute-done.12.refs_1_
  41.4 1.2 %shard_map.205 = (bf16[96,4,256]{2,1,0:T(4,128)(2,1)}, f32[7,7,96]{2,1,0:T(8,128)}, f32[1,96]{1,0:T(1,128)}, f32[1,96]{1,0:T(1,128)}, f32[1,96]{1,0:T(1,128)}, /...) custom-call(f32[224,128]{1,0:T(8,128)S(1)} %shard_map.203.refs_5_.refs_0_, ...), custom_call_target="tpu_custom_call" | custom-call | bytes 932864 | tf_op jit(solution)/shard_map/pallas_call | solution.py:458
  (6 shorter events, 0.2 us)
Async XLA Ops:
  1.6 5.7 %copy-start.3 = (bf16[96,4,256]{2,1,0:T(4,128)(2,1)S(1)}, bf16[96,4,256]{2,1,0:T(4,128)(2,1)}, u32[]{:S(2)}) copy-start(bf16[96,4,256]{2,1,0:T(4,128)(2,1)} %refs_0_.1) | copy-start | bytes 589828
  1.8 3.8 %copy-start.10 = (bf16[384]{0:T(512)(128)(2,1)S(1)}, bf16[384]{0:T(512)(128)(2,1)}, u32[]{:S(2)}) copy-start(bf16[384]{0:T(512)(128)(2,1)} %param.18) | copy-start | bytes 2308
  1.8 4.7 %collective-permute-start = (bf16[16,96]{1,0:T(8,128)(2,1)S(1)}, bf16[16,96]{1,0:T(8,128)(2,1)S(1)}, u32[]{:S(2)}, u32[]{:S(2)}) collective-permute-start(bf16[16,96]{1,0:T(8,128)(2,1)S(1)} %get-tuple-element.48), channel_id=1, source_target_pairs={{0,1},{2,3},{1,0},{3,2},{4,5},{6,7},{5,4},{7,6},{8,9},{10,11},{9,8... | collective-permute-start | bytes 9224 | tf_op jit(solution)/shard_map/ppermute | solution.py:472
  4.9 1.6 %collective-permute-start.1 = (bf16[16,96]{1,0:T(8,128)(2,1)S(1)}, bf16[16,96]{1,0:T(8,128)(2,1)S(1)}, u32[]{:S(2)}, u32[]{:S(2)}) collective-permute-start(bf16[16,96]{1,0:T(8,128)(2,1)S(1)} %get-tuple-element.49), channel_id=1, source_target_pairs={{1,2},{2,1},{5,6},{6,5},{9,10},{10,9},{13,14},{14,13},{17,18},{18,... | collective-permute-start | bytes 9224 | tf_op jit(solution)/shard_map/ppermute | solution.py:472
  5.6 1.7 %copy-start.1 = (bf16[384,96]{0,1:T(8,128)(2,1)S(1)}, bf16[384,96]{0,1:T(8,128)(2,1)}, u32[]{:S(2)}) copy-start(bf16[384,96]{0,1:T(8,128)(2,1)} %param.17) | copy-start | bytes 221188
  5.6 1.7 %copy-start.2 = (bf16[384,96]{0,1:T(8,128)(2,1)S(1)}, bf16[384,96]{0,1:T(8,128)(2,1)}, u32[]{:S(2)}) copy-start(bf16[384,96]{0,1:T(8,128)(2,1)} %param.19) | copy-start | bytes 221188
  6.5 0.8 %copy-start.4 = (f32[96,7,7]{0,2,1:T(8,128)S(1)}, f32[96,7,7]{0,2,1:T(8,128)}, u32[]{:S(2)}) copy-start(f32[96,7,7]{0,2,1:T(8,128)} %param.13) | copy-start | bytes 56452
  6.5 6.3 %collective-permute-start.3 = (bf16[608,128]{1,0:T(8,128)(2,1)S(1)}, bf16[608,128]{1,0:T(8,128)(2,1)S(1)}, u32[]{:S(2)}, u32[]{:S(2)}) collective-permute-start(bf16[608,128]{1,0:T(8,128)(2,1)S(1)} %get-tuple-element.52), channel_id=1, source_target_pairs={{4,8},{12,16},{20,24},{8,4},{16,12},{24,20},{5,9},{13,17},{21,25},... | collective-permute-start | bytes 466952 | tf_op jit(solution)/shard_map/ppermute | solution.py:472
  7.2 0.7 %copy-start.8 = (f32[96]{0:T(128)S(1)}, f32[96]{0:T(128)}, u32[]{:S(2)}) copy-start(f32[96]{0:T(128)} %param.16) | copy-start | bytes 1156
  7.2 0.7 %copy-start.9 = (f32[96]{0:T(128)S(1)}, f32[96]{0:T(128)}, u32[]{:S(2)}) copy-start(f32[96]{0:T(128)} %param.20) | copy-start | bytes 1156
  7.2 0.7 %copy-start.5 = (f32[96]{0:T(128)S(1)}, f32[96]{0:T(128)}, u32[]{:S(2)}) copy-start(f32[96]{0:T(128)} %param.21) | copy-start | bytes 1156
  7.2 0.7 %copy-start.6 = (f32[96]{0:T(128)S(1)}, f32[96]{0:T(128)}, u32[]{:S(2)}) copy-start(f32[96]{0:T(128)} %param.14) | copy-start | bytes 1156
  7.2 0.7 %copy-start.7 = (f32[96]{0:T(128)S(1)}, f32[96]{0:T(128)}, u32[]{:S(2)}) copy-start(f32[96]{0:T(128)} %param.15) | copy-start | bytes 1156
  8.6 4.4 %collective-permute-start.2 = (bf16[608,128]{1,0:T(8,128)(2,1)S(1)}, bf16[608,128]{1,0:T(8,128)(2,1)S(1)}, u32[]{:S(2)}, u32[]{:S(2)}) collective-permute-start(bf16[608,128]{1,0:T(8,128)(2,1)S(1)} %shard_map.197), channel_id=1, source_target_pairs={{0,4},{4,0},{1,5},{5,1},{2,6},{6,2},{3,7},{7,3},{8,12},{12,8},{9,1... | collective-permute-start | bytes 466952 | tf_op jit(solution)/shard_map/ppermute | solution.py:472
  16.6 2.3 %collective-permute-start.4 = (bf16[960,128]{1,0:T(8,128)(2,1)S(1)}, bf16[960,128]{1,0:T(8,128)(2,1)S(1)}, u32[]{:S(2)}, u32[]{:S(2)}) collective-permute-start(bf16[960,128]{1,0:T(8,128)(2,1)S(1)} %get-tuple-element.59), channel_id=1, source_target_pairs={{0,4},{4,0},{1,5},{5,1},{2,6},{6,2},{3,7},{7,3},{8,12},{12,8},{9,1... | collective-permute-start | bytes 737288 | tf_op jit(solution)/shard_map/ppermute | solution.py:472
  19.0 12.5 %collective-permute-start.5 = (bf16[176,128]{1,0:T(8,128)(2,1)S(1)}, bf16[176,128]{1,0:T(8,128)(2,1)S(1)}, u32[]{:S(2)}, u32[]{:S(2)}) collective-permute-start(bf16[176,128]{1,0:T(8,128)(2,1)S(1)} %get-tuple-element.68), channel_id=1, source_target_pairs={{0,1},{1,0},{2,3},{3,2},{4,5},{5,4},{6,7},{7,6},{8,9},{9,8},{10,11... | collective-permute-start | bytes 135176 | tf_op jit(solution)/shard_map/ppermute | solution.py:476
  23.7 7.8 %collective-permute-start.7 = (bf16[176,128]{1,0:T(8,128)(2,1)S(1)}, bf16[176,128]{1,0:T(8,128)(2,1)S(1)}, u32[]{:S(2)}, u32[]{:S(2)}) collective-permute-start(bf16[176,128]{1,0:T(8,128)(2,1)S(1)} %get-tuple-element.70), channel_id=1, source_target_pairs={{0,3},{1,2},{2,1},{3,0},{4,7},{5,6},{6,5},{7,4},{8,11},{9,10},{10,... | collective-permute-start | bytes 135176 | tf_op jit(solution)/shard_map/ppermute | solution.py:476
  26.6 4.9 %collective-permute-start.6 = (bf16[160,128]{1,0:T(8,128)(2,1)S(1)}, bf16[160,128]{1,0:T(8,128)(2,1)S(1)}, u32[]{:S(2)}, u32[]{:S(2)}) collective-permute-start(bf16[160,128]{1,0:T(8,128)(2,1)S(1)} %get-tuple-element.69), channel_id=1, source_target_pairs={{0,2},{1,3},{2,0},{3,1},{4,6},{5,7},{6,4},{7,5},{8,10},{9,11},{10,... | collective-permute-start | bytes 122888 | tf_op jit(solution)/shard_map/ppermute | solution.py:476
  26.6 9.5 %collective-permute-start.11 = (bf16[3,96,256]{2,1,0:T(8,128)(2,1)S(1)}, bf16[3,96,256]{2,1,0:T(8,128)(2,1)S(1)}, u32[]{:S(2)}, u32[]{:S(2)}) collective-permute-start(bf16[3,96,256]{2,1,0:T(8,128)(2,1)S(1)} %get-tuple-element.73), channel_id=1, source_target_pairs={{4,8},{12,16},{20,24},{8,4},{16,12},{24,20},{5,9},{13,17},{21,25},... | collective-permute-start | bytes 442376 | tf_op jit(solution)/shard_map/ppermute | solution.py:472
  31.5 8.4 %collective-permute-start.10 = (bf16[192,128]{1,0:T(8,128)(2,1)S(1)}, bf16[192,128]{1,0:T(8,128)(2,1)S(1)}, u32[]{:S(2)}, u32[]{:S(2)}) collective-permute-start(bf16[192,128]{1,0:T(8,128)(2,1)S(1)} %get-tuple-element.71.refs_0_), channel_id=1, source_target_pairs={{0,24},{8,16},{16,8},{24,0},{1,25},{9,17},{17,9},{25,1},{2,26},{10... | collective-permute-start | bytes 147464 | tf_op jit(solution)/shard_map/ppermute | solution.py:476
  34.5 5.4 %collective-permute-start.8 = (bf16[192,128]{1,0:T(8,128)(2,1)S(1)}, bf16[192,128]{1,0:T(8,128)(2,1)S(1)}, u32[]{:S(2)}, u32[]{:S(2)}) collective-permute-start(bf16[192,128]{1,0:T(8,128)(2,1)S(1)} %get-tuple-element.71.refs_0_), channel_id=1, source_target_pairs={{0,8},{8,0},{16,24},{24,16},{1,9},{9,1},{17,25},{25,17},{2,10},{10... | collective-permute-start | bytes 147464 | tf_op jit(solution)/shard_map/ppermute | solution.py:476
  35.9 4.0 %collective-permute-start.9 = (bf16[160,128]{1,0:T(8,128)(2,1)S(1)}, bf16[160,128]{1,0:T(8,128)(2,1)S(1)}, u32[]{:S(2)}, u32[]{:S(2)}) collective-permute-start(bf16[160,128]{1,0:T(8,128)(2,1)S(1)} %get-tuple-element.72), channel_id=1, source_target_pairs={{0,16},{8,24},{16,0},{24,8},{1,17},{9,25},{17,1},{25,9},{2,18},{10... | collective-permute-start | bytes 122888 | tf_op jit(solution)/shard_map/ppermute | solution.py:476
  36.1 3.9 %copy-start = (bf16[4,96,256]{2,0,1:T(4,128)(2,1)}, bf16[4,96,256]{2,0,1:T(4,128)(2,1)S(1)}, u32[]{:S(2)}) copy-start(bf16[4,96,256]{2,0,1:T(4,128)(2,1)S(1)} %copy.26) | copy-start | bytes 589828
  40.0 1.4 %collective-permute-start.12 = (f32[224,128]{1,0:T(8,128)S(1)}, f32[224,128]{1,0:T(8,128)S(1)}, u32[]{:S(2)}, u32[]{:S(2)}) collective-permute-start(f32[224,128]{1,0:T(8,128)S(1)} %shard_map.203.refs_5_.refs_0_), channel_id=1, source_target_pairs={{0,4},{4,0},{1,5},{5,1},{2,6},{6,2},{3,7},{7,3},{8,12},{12,8},{9,1... | collective-permute-start | bytes 344072 | tf_op jit(solution)/shard_map/ppermute | solution.py:472

commit v7 on v6

--- a/solution.py
+++ b/solution.py
@@ -126,7 +126,7 @@
     depthwise(w_ref, xs_ref, acc_ref, rows, range(HALO, HALO + rows))
 
 
-def edges_kernel(axis, mid_ref, first_ref, second_ref):
+def edges_kernel(axis, mid_ref, second_ref, first_ref):
     edges = pack_edges([mid_ref[i] for i in range(mid_ref.shape[0])])
     high = edges.shape[0] // 2
     even = lax.rem(lax.axis_index(axis), 2) == 0
@@ -134,7 +134,7 @@
     second_ref[...] = jnp.where(even, edges[high:], edges[:high])
 
 
-def far_kernel(axes, mid_ref, first_ref, second_ref, own_ref, far_ref):
+def far_kernel(axes, mid_ref, second_ref, first_ref, own_ref, far_ref):
     even = lax.rem(lax.axis_index(axes[2]), 2) == 0
     first, second = first_ref[...], second_ref[...]
     edges = jnp.concatenate([jnp.where(even, second, first), jnp.where(even, first, second)], axis=0)
@@ -403,6 +403,7 @@
             ends_ref[side * HALO + k, HALO : HALO + rows, :] = own[at : at + rows]
             ends_ref[side * HALO + k, HALO + rows : 2 * HALO + rows, :] = below[at : at + HALO]
     side_ref[...] = jnp.zeros_like(side_ref)
+    taps = [taps_ref[a] for a in range(SIDE)]
     for side in range(2):
         for j in range(HALO):
             total = None
@@ -411,7 +412,7 @@
                 if not 0 <= b < SIDE:
                     continue
                 for a in range(SIDE):
-                    tap = taps_ref[SIDE - 1 - a, SIDE - 1 - b : SIDE - b, :]
+                    tap = taps[SIDE - 1 - a][SIDE - 1 - b : SIDE - b]
                     part = tap * ends_ref[side * HALO + k, a : a + rows, 0:channels]
                     total = part if total is None else total + part
             at = (side * HALO + j) * rows
@@ -514,9 +515,9 @@
     ends = ((high, channels), BF16)
     lead = HALO * channels * (width // LANES)
     flat_strip = ((lead + 2 * high, LANES), BF16)
-    first, second = call(functools.partial(edges_kernel, filt), [ends, ends], mid)
-    first, second = swap(first, filt, 0), swap(second, filt, 1)
-    own, far = call(functools.partial(far_kernel, axes), [edge, flat_strip], mid, first, second)
+    second, first = call(functools.partial(edges_kernel, filt), [ends, ends], mid)
+    second, first = swap(second, filt, 1), swap(first, filt, 0)
+    own, far = call(functools.partial(far_kernel, axes), [edge, flat_strip], mid, second, first)
     far = swap(far, space, 1)
     we_t, wr_t = w_expand.T, w_reduce.T
     taps = jnp.transpose(kernel, (1, 2, 0))
@@ -532,7 +533,7 @@
         ],
         cotangent, taps, row(dw_bias), row(layer_norm_gain), row(layer_norm_bias),
         we_t, row(b_expand), wr_t, row(b_reduce), row(layer_scale),
-        scratch=[((lift, hidden_n), BF16), ((8, DEEP), F32)],
+        scratch=[((lift, hidden_n), BF16), ((16, DEEP), F32)],
         after=[own],
     )
     (pair,) = call(functools.partial(pair_kernel, core), [flat_strip], mid, own, after=[columns])
@@ -548,7 +549,7 @@
     out_t, dconv, far_out, x, vectors, share, keep = call(
         functools.partial(main_kernel, axes),
         [
-            block, block, strip, ((2 * HALO, channels, extent), BF16), ((8, LANES), F32),
+            block, block, strip, ((2 * HALO, channels, extent), BF16), ((16, LANES), F32),
             ((HALO * channels * (width // LANES) + hidden_n, LANES), BF16), flat,
         ],
         mid, pair, far, own, before, cot_t, forward, we_t, wr_t, we2, wr2, columns, row(layer_scale),
@@ -567,7 +568,7 @@
         depthwise_gradient_kernel,
         [edge, ((small_n, LANES), F32)],
         x, own_x, dconv, vectors,
-        scratch=[((deep, rows * extent), BF16), ((deep, rows * extent), BF16), ((8, DEEP), F32)],
+        scratch=[((deep, rows * extent), BF16), ((deep, rows * extent), BF16), ((16, DEEP), F32)],
     )
     share = swap(share, core, 0)
     far = swap(far_out, space, 1) if direct else None
@@ -617,7 +618,7 @@
             line, line, line, matrix, ((1, panel), F32), matrix, line, line,
         ],
         mine, other, back, taps,
-        scratch=[((2 * HALO, 16, LANES), F32), ((2 * HALO * rows, LANES), F32)],
+        scratch=[((2 * HALO, 16, LANES), F32), ((edge_height(2 * rows), LANES), F32)],
     )
     flat = lambda v: v.reshape(-1)
     return (

time: 42.8 us -> 42.6 us (level)
  starting transfers between devices: 21.7 us -> 20.1 us
  waiting for transfers between devices: 9.52 us -> 10.9 us
    ppermute x6, starting transfers between devices: 12 us -> 7.84 us  [crossed(): lax.ppermute(x, axis, [(i, i ^ bits) for i in range(lax.axis_size(axis))])]
    ppermute x7, starting transfers between devices: 9.7 us -> 12.2 us  [swap(): return lax.ppermute(x, axis, pairs + [(j, i) for i, j in pairs])]
    ppermute x6, waiting for transfers between devices: 8.06 us -> 8.81 us  [crossed(): lax.ppermute(x, axis, [(i, i ^ bits) for i in range(lax.axis_size(axis))])]
    ppermute x7, waiting for transfers between devices: 1.46 us -> 2.12 us  [swap(): return lax.ppermute(x, axis, pairs + [(j, i) for i, j in pairs])]
where the time goes in v7:
time: 42.6 us; the launch traced here: 42.3 us
  starting transfers between devices  20.1 us (47%)
  waiting for transfers between devices  10.9 us (26%)
  Pallas kernels  8.66 us (20%)
  local copies, waits for them, and re-layouts  1.8 us (4%)
  between operations  0.88 us (2%)
    ppermute x7, starting transfers between devices, swap(): return lax.ppermute(x, axis, pairs + [(j, i) for i, j in pairs])  12.2 us
    ppermute x6, waiting for transfers between devices, crossed(): lax.ppermute(x, axis, [(i, i ^ bits) for i in range(lax.axis_size(axis))])  8.81 us
    pallas_call x12, Pallas kernels, call(): pl.pallas_call(body, out_shape=[jax.ShapeDtypeStruct(s, d) for s, d in ou...  8.66 us
    ppermute x6, starting transfers between devices, crossed(): lax.ppermute(x, axis, [(i, i ^ bits) for i in range(lax.axis_size(axis))])  7.84 us
    ppermute x7, waiting for transfers between devices, swap(): return lax.ppermute(x, axis, pairs + [(j, i) for i, j in pairs])  2.12 us
    unnamed x23, local copies, waits for them, and re-layouts  1.64 us
  transfers between devices with their start and end apart: 13, of which 6 were waited for; matrix products, arithmetic and copies ran while one was open for 0% of the time, Pallas kernels for 9%

profile of v7, /device:TPU:0, one launch (start us, length us, event | category | flops | bytes accessed | tf_op | source)
XLA Modules:
  0.0 42.3 jit_solution(13307456531647013989)
XLA Ops:
  0.6 0.9 %copy.27 = bf16[96,4,256]{2,0,1:T(8,128)(2,1)S(1)} copy(bf16[96,4,256]{2,1,0:T(4,128)(2,1)} %param.11) | data formatting | bytes 393216 | tf_op args[0]
  1.6 0.0 copy-start.3
  1.6 0.2 shard_map.194
  1.8 0.0 copy-start.10
  1.8 0.8 %collective-permute-start = (bf16[16,96]{1,0:T(8,128)(2,1)S(1)}, bf16[16,96]{1,0:T(8,128)(2,1)S(1)}, u32[]{:S(2)}, u32[]{:S(2)}) collective-permute-start(bf16[16,96]{1,0:T(8,128)(2,1)S(1)} %get-tuple-element.48), channel_id=1, source_target_pairs={{1,2},{2,1},{5,6},{6,5},{9,10},{10,9},{13,14},{14,13},{17,18},{18,... | collective-permute-start | bytes 9224 | tf_op jit(solution)/shard_map/ppermute | solution.py:473
  2.6 5.9 %collective-permute-start.1 = (bf16[16,96]{1,0:T(8,128)(2,1)S(1)}, bf16[16,96]{1,0:T(8,128)(2,1)S(1)}, u32[]{:S(2)}, u32[]{:S(2)}) collective-permute-start(bf16[16,96]{1,0:T(8,128)(2,1)S(1)} %get-tuple-element.49), channel_id=1, source_target_pairs={{0,1},{2,3},{1,0},{3,2},{4,5},{6,7},{5,4},{7,6},{8,9},{10,11},{9,8... | collective-permute-start | bytes 9224 | tf_op jit(solution)/shard_map/ppermute | solution.py:473
  8.5 0.0 copy-done.10
  8.5 0.0 copy-start.1
  8.5 0.0 copy-start.2
  8.5 0.0 collective-permute-done.refs_1_
  8.5 1.6 %collective-permute-done.1.refs_2_ = bf16[16,96]{1,0:T(8,128)(2,1)S(1)} collective-permute-done((bf16[16,96]{1,0:T(8,128)(2,1)S(1)}, bf16[16,96]{1,0:T(8,128)(2,1)S(1)}, u32[]{:S(2)}, u32[]{:S(2)}) %collective-permute-start.1) | collective-permute-done | bytes 3104 | tf_op jit(solution)/shard_map/ppermute | solution.py:473
  10.1 0.0 copy-start.4
  10.1 0.7 %collective-permute-start.3 = (bf16[608,128]{1,0:T(8,128)(2,1)S(1)}, bf16[608,128]{1,0:T(8,128)(2,1)S(1)}, u32[]{:S(2)}, u32[]{:S(2)}) collective-permute-start(bf16[608,128]{1,0:T(8,128)(2,1)S(1)} %get-tuple-element.52), channel_id=1, source_target_pairs={{4,8},{12,16},{20,24},{8,4},{16,12},{24,20},{5,9},{13,17},{21,25},... | collective-permute-start | bytes 466952 | tf_op jit(solution)/shard_map/ppermute | solution.py:473
  10.8 0.0 copy-start.8
  10.8 0.0 copy-start.9
  10.8 0.0 copy-start.5
  10.8 0.0 copy-start.6
  10.9 0.0 copy-start.7
  10.9 0.0 copy-done.3
  10.9 0.0 copy-done.1
  10.9 0.0 copy-done.2
  10.9 0.0 copy-done.4
  10.9 0.6 %copy-done.8 = f32[96]{0:T(128)S(1)} copy-done((f32[96]{0:T(128)S(1)}, f32[96]{0:T(128)}, u32[]{:S(2)}) %copy-start.8) | copy-done | bytes 408
  11.5 0.0 copy-done.9
  11.5 0.0 copy-done.5
  11.5 0.0 copy-done.6
  11.5 0.0 copy-done.7
  11.5 0.7 %shard_map.196 = (bf16[4,96,256]{2,1,0:T(8,128)(2,1)S(1)}, bf16[3,224,224]{2,1,0:T(8,128)(2,1)S(1)}, bf16[3,224,224]{2,1,0:T(8,128)(2,1)S(1)}, bf16[384,112]{1,0...) custom-call(bf16[96,4,256]{2,1,0:T(4,128)(2,1)S(1)} %copy-done.3, f32[7,7,96]{2,1,0:T(8,128)S(1)} %bitcast.32, ...), custom_call_target="tpu_custom_call" | custom-call | bytes 1373184 | tf_op jit(solution)/shard_map/pallas_call | solution.py:459
  12.3 2.9 %collective-permute-start.2 = (bf16[608,128]{1,0:T(8,128)(2,1)S(1)}, bf16[608,128]{1,0:T(8,128)(2,1)S(1)}, u32[]{:S(2)}, u32[]{:S(2)}) collective-permute-start(bf16[608,128]{1,0:T(8,128)(2,1)S(1)} %shard_map.197), channel_id=1, source_target_pairs={{0,4},{4,0},{1,5},{5,1},{2,6},{6,2},{3,7},{7,3},{8,12},{12,8},{9,1... | collective-permute-start | bytes 466952 | tf_op jit(solution)/shard_map/ppermute | solution.py:473
  15.2 0.8 %shard_map.198 = (f32[384,256]{1,0:T(8,128)S(1)}, bf16[4,96,384]{2,1,0:T(8,128)(2,1)S(1)}) custom-call(bf16[4,96,256]{2,1,0:T(8,128)(2,1)S(1)} %bitcast.24, bf16[32,128]{1,0:T(8,128)(2,1)S(1)} %get-tuple-element.50.refs_10_.refs_1_.refs_3_, bf16[3,224,224]{2,1,0:T(8,128)(2,1)S(1)} %get-tuple-element.53.refs_2_.refs_6_), custom_call_target="tpu_custom_call" | custom-call | bytes 1193984 | tf_op jit(solution)/shard_map/pallas_call | solution.py:459
  16.0 0.0 collective-permute-done.3.refs_2_
  16.0 0.2 collective-permute-done.2.refs_1_
  16.2 3.6 %shard_map.199 = (bf16[4,96,256]{2,1,0:T(8,128)(2,1)S(1)}, bf16[4,96,256]{2,1,0:T(8,128)(2,1)S(1)}, bf16[3,96,256]{2,1,0:T(8,128)(2,1)S(1)}, bf16[6,96,384]{2,1,...) custom-call(bf16[4,96,256]{2,1,0:T(8,128)(2,1)S(1)} %bitcast.25, ...), custom_call_target="tpu_custom_call" | custom-call | bytes 3197312 | tf_op jit(solution)/shard_map/pallas_call | solution.py:459
  19.8 1.2 %collective-permute-start.4 = (bf16[960,128]{1,0:T(8,128)(2,1)S(1)}, bf16[960,128]{1,0:T(8,128)(2,1)S(1)}, u32[]{:S(2)}, u32[]{:S(2)}) collective-permute-start(bf16[960,128]{1,0:T(8,128)(2,1)S(1)} %get-tuple-element.59), channel_id=1, source_target_pairs={{0,4},{4,0},{1,5},{5,1},{2,6},{6,2},{3,7},{7,3},{8,12},{12,8},{9,1... | collective-permute-start | bytes 737288 | tf_op jit(solution)/shard_map/ppermute | solution.py:473
  21.0 1.0 %shard_map.200 = (bf16[32,128]{1,0:T(8,128)(2,1)S(1)}, f32[64,128]{1,0:T(8,128)S(1)}) custom-call(bf16[6,96,384]{2,1,0:T(8,128)(2,1)S(1)} %get-tuple-element.61.refs_0_, bf16[4,96,384]{2,1,0:T(8,128)(2,1)S(1)} %get-tuple-element.62.refs_1_, bf16[4,96,256]{2,1,0:T(8,128)(2,1)S(1)} %get-tuple-element.63.refs_2_.refs_0_, f32[16,128]{1,0:T(8,128)S(1)} %get-tuple-element.64.refs_3_), custom_call_target="tpu_custom_call" | custom-call | bytes 983040 | tf_op jit(solution)/shard_map/pallas_call | solution.py:459
  22.0 0.2 collective-permute-done.4.refs_0_.refs_1_
  22.2 2.1 %collective-permute-start.5 = (bf16[176,128]{1,0:T(8,128)(2,1)S(1)}, bf16[176,128]{1,0:T(8,128)(2,1)S(1)}, u32[]{:S(2)}, u32[]{:S(2)}) collective-permute-start(bf16[176,128]{1,0:T(8,128)(2,1)S(1)} %get-tuple-element.68), channel_id=1, source_target_pairs={{0,1},{1,0},{2,3},{3,2},{4,5},{5,4},{6,7},{7,6},{8,9},{9,8},{10,11... | collective-permute-start | bytes 135176 | tf_op jit(solution)/shard_map/ppermute | solution.py:477
  24.3 1.3 %collective-permute-start.7 = (bf16[176,128]{1,0:T(8,128)(2,1)S(1)}, bf16[176,128]{1,0:T(8,128)(2,1)S(1)}, u32[]{:S(2)}, u32[]{:S(2)}) collective-permute-start(bf16[176,128]{1,0:T(8,128)(2,1)S(1)} %get-tuple-element.70), channel_id=1, source_target_pairs={{0,3},{1,2},{2,1},{3,0},{4,7},{5,6},{6,5},{7,4},{8,11},{9,10},{10,... | collective-permute-start | bytes 135176 | tf_op jit(solution)/shard_map/ppermute | solution.py:477
  25.6 0.2 collective-permute-start.6
  25.8 0.7 %collective-permute-start.11 = (bf16[3,96,256]{2,1,0:T(8,128)(2,1)S(1)}, bf16[3,96,256]{2,1,0:T(8,128)(2,1)S(1)}, u32[]{:S(2)}, u32[]{:S(2)}) collective-permute-start(bf16[3,96,256]{2,1,0:T(8,128)(2,1)S(1)} %get-tuple-element.73), channel_id=1, source_target_pairs={{4,8},{12,16},{20,24},{8,4},{16,12},{24,20},{5,9},{13,17},{21,25},... | collective-permute-start | bytes 442376 | tf_op jit(solution)/shard_map/ppermute | solution.py:473
  26.5 5.0 %collective-permute-done.6.refs_2_ = bf16[160,128]{1,0:T(8,128)(2,1)S(1)} collective-permute-done((bf16[160,128]{1,0:T(8,128)(2,1)S(1)}, bf16[160,128]{1,0:T(8,128)(2,1)S(1)}, u32[]{:S(2)}, u32[]{:S(2)}) %collective-permute-start.6) | collective-permute-done | bytes 40992 | tf_op jit(solution)/shard_map/ppermute | solution.py:477
  31.5 0.0 collective-permute-done.5.refs_1_
  31.5 0.0 collective-permute-done.7.refs_3_
  31.5 2.8 %collective-permute-start.10 = (bf16[192,128]{1,0:T(8,128)(2,1)S(1)}, bf16[192,128]{1,0:T(8,128)(2,1)S(1)}, u32[]{:S(2)}, u32[]{:S(2)}) collective-permute-start(bf16[192,128]{1,0:T(8,128)(2,1)S(1)} %get-tuple-element.71.refs_0_), channel_id=1, source_target_pairs={{0,24},{8,16},{16,8},{24,0},{1,25},{9,17},{17,9},{25,1},{2,26},{10... | collective-permute-start | bytes 147464 | tf_op jit(solution)/shard_map/ppermute | solution.py:477
  34.3 1.4 %collective-permute-start.8 = (bf16[192,128]{1,0:T(8,128)(2,1)S(1)}, bf16[192,128]{1,0:T(8,128)(2,1)S(1)}, u32[]{:S(2)}, u32[]{:S(2)}) collective-permute-start(bf16[192,128]{1,0:T(8,128)(2,1)S(1)} %get-tuple-element.71.refs_0_), channel_id=1, source_target_pairs={{0,8},{8,0},{16,24},{24,16},{1,9},{9,1},{17,25},{25,17},{2,10},{10... | collective-permute-start | bytes 147464 | tf_op jit(solution)/shard_map/ppermute | solution.py:477
  35.7 0.0 collective-permute-start.9
  35.7 0.2 copy.26
  35.9 0.0 copy-start
  35.9 0.0 collective-permute-done.11.refs_5_.refs_2_
  35.9 3.8 %collective-permute-done.9.refs_2_ = bf16[160,128]{1,0:T(8,128)(2,1)S(1)} collective-permute-done((bf16[160,128]{1,0:T(8,128)(2,1)S(1)}, bf16[160,128]{1,0:T(8,128)(2,1)S(1)}, u32[]{:S(2)}, u32[]{:S(2)}) %collective-permute-start.9) | collective-permute-done | bytes 40992 | tf_op jit(solution)/shard_map/ppermute | solution.py:477
  39.7 0.0 collective-permute-done.10.refs_3_
  39.7 0.0 collective-permute-done.8.refs_1_
  39.7 0.0 copy-done
  39.7 0.1 collective-permute-start.12
  39.8 1.1 %shard_map.204.refs_2_ = f32[384,256]{1,0:T(8,128)S(1)} custom-call(bf16[4,96,256]{2,1,0:T(8,128)(2,1)S(1)} %get-tuple-element.63.refs_2_.refs_0_, bf16[960,128]{1,0:T(8,128)(2,1)S(1)} %collective-permute-done.4.refs_0_.refs_1_, bf16[3,96,256]{2,1,0:T(8,128)(2,1)S(1)} %collective-permute-done.11.refs_5_.refs_2_, ...), custom_call_target="tpu_custom_call" | custom-call | bytes 1480704 | tf_op jit(solution)/shard_map/pallas_call | solution.py:459
  41.0 0.2 collective-permute-done.12.refs_1_
  41.1 1.2 %shard_map.205 = (bf16[96,4,256]{2,1,0:T(4,128)(2,1)}, f32[7,7,96]{2,1,0:T(8,128)}, f32[1,96]{1,0:T(1,128)}, f32[1,96]{1,0:T(1,128)}, f32[1,96]{1,0:T(1,128)}, /...) custom-call(f32[224,128]{1,0:T(8,128)S(1)} %shard_map.203.refs_5_.refs_0_, ...), custom_call_target="tpu_custom_call" | custom-call | bytes 932864 | tf_op jit(solution)/shard_map/pallas_call | solution.py:459
  (6 shorter events, 0.2 us)
Async XLA Ops:
  1.6 9.3 %copy-start.3 = (bf16[96,4,256]{2,1,0:T(4,128)(2,1)S(1)}, bf16[96,4,256]{2,1,0:T(4,128)(2,1)}, u32[]{:S(2)}) copy-start(bf16[96,4,256]{2,1,0:T(4,128)(2,1)} %refs_0_.1) | copy-start | bytes 589828
  1.8 6.7 %copy-start.10 = (bf16[384]{0:T(512)(128)(2,1)S(1)}, bf16[384]{0:T(512)(128)(2,1)}, u32[]{:S(2)}) copy-start(bf16[384]{0:T(512)(128)(2,1)} %param.18) | copy-start | bytes 2308
  1.8 6.7 %collective-permute-start = (bf16[16,96]{1,0:T(8,128)(2,1)S(1)}, bf16[16,96]{1,0:T(8,128)(2,1)S(1)}, u32[]{:S(2)}, u32[]{:S(2)}) collective-permute-start(bf16[16,96]{1,0:T(8,128)(2,1)S(1)} %get-tuple-element.48), channel_id=1, source_target_pairs={{1,2},{2,1},{5,6},{6,5},{9,10},{10,9},{13,14},{14,13},{17,18},{18,... | collective-permute-start | bytes 9224 | tf_op jit(solution)/shard_map/ppermute | solution.py:473
  2.6 7.5 %collective-permute-start.1 = (bf16[16,96]{1,0:T(8,128)(2,1)S(1)}, bf16[16,96]{1,0:T(8,128)(2,1)S(1)}, u32[]{:S(2)}, u32[]{:S(2)}) collective-permute-start(bf16[16,96]{1,0:T(8,128)(2,1)S(1)} %get-tuple-element.49), channel_id=1, source_target_pairs={{0,1},{2,3},{1,0},{3,2},{4,5},{6,7},{5,4},{7,6},{8,9},{10,11},{9,8... | collective-permute-start | bytes 9224 | tf_op jit(solution)/shard_map/ppermute | solution.py:473
  8.5 2.4 %copy-start.1 = (bf16[384,96]{0,1:T(8,128)(2,1)S(1)}, bf16[384,96]{0,1:T(8,128)(2,1)}, u32[]{:S(2)}) copy-start(bf16[384,96]{0,1:T(8,128)(2,1)} %param.17) | copy-start | bytes 221188
  8.5 2.4 %copy-start.2 = (bf16[384,96]{0,1:T(8,128)(2,1)S(1)}, bf16[384,96]{0,1:T(8,128)(2,1)}, u32[]{:S(2)}) copy-start(bf16[384,96]{0,1:T(8,128)(2,1)} %param.19) | copy-start | bytes 221188
  10.1 0.8 %copy-start.4 = (f32[96,7,7]{0,2,1:T(8,128)S(1)}, f32[96,7,7]{0,2,1:T(8,128)}, u32[]{:S(2)}) copy-start(f32[96,7,7]{0,2,1:T(8,128)} %param.13) | copy-start | bytes 56452
  10.1 5.8 %collective-permute-start.3 = (bf16[608,128]{1,0:T(8,128)(2,1)S(1)}, bf16[608,128]{1,0:T(8,128)(2,1)S(1)}, u32[]{:S(2)}, u32[]{:S(2)}) collective-permute-start(bf16[608,128]{1,0:T(8,128)(2,1)S(1)} %get-tuple-element.52), channel_id=1, source_target_pairs={{4,8},{12,16},{20,24},{8,4},{16,12},{24,20},{5,9},{13,17},{21,25},... | collective-permute-start | bytes 466952 | tf_op jit(solution)/shard_map/ppermute | solution.py:473
  10.8 0.7 %copy-start.8 = (f32[96]{0:T(128)S(1)}, f32[96]{0:T(128)}, u32[]{:S(2)}) copy-start(f32[96]{0:T(128)} %param.16) | copy-start | bytes 1156
  10.8 0.7 %copy-start.9 = (f32[96]{0:T(128)S(1)}, f32[96]{0:T(128)}, u32[]{:S(2)}) copy-start(f32[96]{0:T(128)} %param.20) | copy-start | bytes 1156
  10.8 0.7 %copy-start.5 = (f32[96]{0:T(128)S(1)}, f32[96]{0:T(128)}, u32[]{:S(2)}) copy-start(f32[96]{0:T(128)} %param.21) | copy-start | bytes 1156
  10.8 0.7 %copy-start.6 = (f32[96]{0:T(128)S(1)}, f32[96]{0:T(128)}, u32[]{:S(2)}) copy-start(f32[96]{0:T(128)} %param.14) | copy-start | bytes 1156
  10.9 0.7 %copy-start.7 = (f32[96]{0:T(128)S(1)}, f32[96]{0:T(128)}, u32[]{:S(2)}) copy-start(f32[96]{0:T(128)} %param.15) | copy-start | bytes 1156
  12.3 3.9 %collective-permute-start.2 = (bf16[608,128]{1,0:T(8,128)(2,1)S(1)}, bf16[608,128]{1,0:T(8,128)(2,1)S(1)}, u32[]{:S(2)}, u32[]{:S(2)}) collective-permute-start(bf16[608,128]{1,0:T(8,128)(2,1)S(1)} %shard_map.197), channel_id=1, source_target_pairs={{0,4},{4,0},{1,5},{5,1},{2,6},{6,2},{3,7},{7,3},{8,12},{12,8},{9,1... | collective-permute-start | bytes 466952 | tf_op jit(solution)/shard_map/ppermute | solution.py:473
  19.8 2.3 %collective-permute-start.4 = (bf16[960,128]{1,0:T(8,128)(2,1)S(1)}, bf16[960,128]{1,0:T(8,128)(2,1)S(1)}, u32[]{:S(2)}, u32[]{:S(2)}) collective-permute-start(bf16[960,128]{1,0:T(8,128)(2,1)S(1)} %get-tuple-element.59), channel_id=1, source_target_pairs={{0,4},{4,0},{1,5},{5,1},{2,6},{6,2},{3,7},{7,3},{8,12},{12,8},{9,1... | collective-permute-start | bytes 737288 | tf_op jit(solution)/shard_map/ppermute | solution.py:473
  22.2 9.3 %collective-permute-start.5 = (bf16[176,128]{1,0:T(8,128)(2,1)S(1)}, bf16[176,128]{1,0:T(8,128)(2,1)S(1)}, u32[]{:S(2)}, u32[]{:S(2)}) collective-permute-start(bf16[176,128]{1,0:T(8,128)(2,1)S(1)} %get-tuple-element.68), channel_id=1, source_target_pairs={{0,1},{1,0},{2,3},{3,2},{4,5},{5,4},{6,7},{7,6},{8,9},{9,8},{10,11... | collective-permute-start | bytes 135176 | tf_op jit(solution)/shard_map/ppermute | solution.py:477
  24.3 7.2 %collective-permute-start.7 = (bf16[176,128]{1,0:T(8,128)(2,1)S(1)}, bf16[176,128]{1,0:T(8,128)(2,1)S(1)}, u32[]{:S(2)}, u32[]{:S(2)}) collective-permute-start(bf16[176,128]{1,0:T(8,128)(2,1)S(1)} %get-tuple-element.70), channel_id=1, source_target_pairs={{0,3},{1,2},{2,1},{3,0},{4,7},{5,6},{6,5},{7,4},{8,11},{9,10},{10,... | collective-permute-start | bytes 135176 | tf_op jit(solution)/shard_map/ppermute | solution.py:477
  25.6 5.8 %collective-permute-start.6 = (bf16[160,128]{1,0:T(8,128)(2,1)S(1)}, bf16[160,128]{1,0:T(8,128)(2,1)S(1)}, u32[]{:S(2)}, u32[]{:S(2)}) collective-permute-start(bf16[160,128]{1,0:T(8,128)(2,1)S(1)} %get-tuple-element.69), channel_id=1, source_target_pairs={{0,2},{1,3},{2,0},{3,1},{4,6},{5,7},{6,4},{7,5},{8,10},{9,11},{10,... | collective-permute-start | bytes 122888 | tf_op jit(solution)/shard_map/ppermute | solution.py:477
  25.8 10.1 %collective-permute-start.11 = (bf16[3,96,256]{2,1,0:T(8,128)(2,1)S(1)}, bf16[3,96,256]{2,1,0:T(8,128)(2,1)S(1)}, u32[]{:S(2)}, u32[]{:S(2)}) collective-permute-start(bf16[3,96,256]{2,1,0:T(8,128)(2,1)S(1)} %get-tuple-element.73), channel_id=1, source_target_pairs={{4,8},{12,16},{20,24},{8,4},{16,12},{24,20},{5,9},{13,17},{21,25},... | collective-permute-start | bytes 442376 | tf_op jit(solution)/shard_map/ppermute | solution.py:473
  31.5 8.2 %collective-permute-start.10 = (bf16[192,128]{1,0:T(8,128)(2,1)S(1)}, bf16[192,128]{1,0:T(8,128)(2,1)S(1)}, u32[]{:S(2)}, u32[]{:S(2)}) collective-permute-start(bf16[192,128]{1,0:T(8,128)(2,1)S(1)} %get-tuple-element.71.refs_0_), channel_id=1, source_target_pairs={{0,24},{8,16},{16,8},{24,0},{1,25},{9,17},{17,9},{25,1},{2,26},{10... | collective-permute-start | bytes 147464 | tf_op jit(solution)/shard_map/ppermute | solution.py:477
  34.3 5.5 %collective-permute-start.8 = (bf16[192,128]{1,0:T(8,128)(2,1)S(1)}, bf16[192,128]{1,0:T(8,128)(2,1)S(1)}, u32[]{:S(2)}, u32[]{:S(2)}) collective-permute-start(bf16[192,128]{1,0:T(8,128)(2,1)S(1)} %get-tuple-element.71.refs_0_), channel_id=1, source_target_pairs={{0,8},{8,0},{16,24},{24,16},{1,9},{9,1},{17,25},{25,17},{2,10},{10... | collective-permute-start | bytes 147464 | tf_op jit(solution)/shard_map/ppermute | solution.py:477
  35.7 4.0 %collective-permute-start.9 = (bf16[160,128]{1,0:T(8,128)(2,1)S(1)}, bf16[160,128]{1,0:T(8,128)(2,1)S(1)}, u32[]{:S(2)}, u32[]{:S(2)}) collective-permute-start(bf16[160,128]{1,0:T(8,128)(2,1)S(1)} %get-tuple-element.72), channel_id=1, source_target_pairs={{0,16},{8,24},{16,0},{24,8},{1,17},{9,25},{17,1},{25,9},{2,18},{10... | collective-permute-start | bytes 122888 | tf_op jit(solution)/shard_map/ppermute | solution.py:477
  35.9 3.9 %copy-start = (bf16[4,96,256]{2,0,1:T(4,128)(2,1)}, bf16[4,96,256]{2,0,1:T(4,128)(2,1)S(1)}, u32[]{:S(2)}) copy-start(bf16[4,96,256]{2,0,1:T(4,128)(2,1)S(1)} %copy.26) | copy-start | bytes 589828
  39.7 1.4 %collective-permute-start.12 = (f32[224,128]{1,0:T(8,128)S(1)}, f32[224,128]{1,0:T(8,128)S(1)}, u32[]{:S(2)}, u32[]{:S(2)}) collective-permute-start(f32[224,128]{1,0:T(8,128)S(1)} %shard_map.203.refs_5_.refs_0_), channel_id=1, source_target_pairs={{0,4},{4,0},{1,5},{5,1},{2,6},{6,2},{3,7},{7,3},{8,12},{12,8},{9,1... | collective-permute-start | bytes 344072 | tf_op jit(solution)/shard_map/ppermute | solution.py:473

commit v8 on v7

--- a/solution.py
+++ b/solution.py
@@ -343,7 +343,7 @@
     return (mine + first) + (second + third)
 
 
-def chips_kernel(axis, kept_ref, first_ref, second_ref, third_ref, send_ref, plain_ref):
+def chips_kernel(axis, third_ref, second_ref, first_ref, kept_ref, send_ref, plain_ref):
     f = lax.axis_index(axis)
     even = lax.rem(f, 2) == 0
     count = kept_ref.shape[0]
@@ -355,7 +355,7 @@
     send_ref[...] = jnp.concatenate([total, *edges], axis=0)
 
 
-def total_kernel(axes, mine_ref, first_ref, second_ref, third_ref, total_ref):
+def total_kernel(axes, third_ref, second_ref, first_ref, mine_ref, total_ref):
     q, core = lax.axis_index(axes[0]), lax.axis_index(axes[1])
     count = second_ref.shape[0]
     wide = mine_ref.shape[0] - count
@@ -484,7 +484,7 @@
     left = [(j, i) for i, j in right]
     high = edges.shape[0] // 2
     own = jnp.concatenate([lax.ppermute(edges[:high], filt, right), lax.ppermute(edges[high:], filt, left)], axis=0)
-    return jnp.concatenate([own, swap(own, (chip, core), 1)], axis=0)
+    return jnp.concatenate([own, swap(swap(own, (chip, core), 1), core, 0)], axis=0)
 
 
 def shards(
@@ -583,14 +583,14 @@
         )
         third, second, first = (crossed(sends[k - 1], filt, k) for k in (3, 2, 1))
         send, plain = call(
-            functools.partial(chips_kernel, filt), [((low + 2 * high, LANES), BF16), sums], kept, first, second, third,
+            functools.partial(chips_kernel, filt), [((low + 2 * high, LANES), BF16), sums], third, second, first, kept,
             flops=4 * 10**9,
         )
         third, second, first = (crossed(plain if k == 2 else send, chip, k) for k in (3, 2, 1))
         (mine,) = call(
             functools.partial(total_kernel, axes),
             [((low + 4 * high, LANES), F32)],
-            send, first, second, third,
+            third, second, first, send,
             after=[output, far],
         )
     else:

time: 42.6 us -> 41.5 us (0.974)
  waiting for transfers between devices: 10.9 us -> 8.99 us
  starting transfers between devices: 20.1 us -> 20.9 us
    ppermute x6, waiting for transfers between devices: 8.81 us -> 6.87 us  [crossed(): lax.ppermute(x, axis, [(i, i ^ bits) for i in range(lax.axis_size(axis))])]
    ppermute x6, starting transfers between devices: 7.84 us -> 8.66 us  [crossed(): lax.ppermute(x, axis, [(i, i ^ bits) for i in range(lax.axis_size(axis))])]
where the time goes in v8:
time: 41.5 us; the launch traced here: 41.2 us
  starting transfers between devices  20.9 us (50%)
  waiting for transfers between devices  8.99 us (22%)
  Pallas kernels  8.66 us (21%)
  local copies, waits for them, and re-layouts  1.8 us (4%)
  between operations  0.88 us (2%)
    ppermute x7, starting transfers between devices, swap(): return lax.ppermute(x, axis, pairs + [(j, i) for i, j in pairs])  12.2 us
    ppermute x6, starting transfers between devices, crossed(): lax.ppermute(x, axis, [(i, i ^ bits) for i in range(lax.axis_size(axis))])  8.66 us
    pallas_call x12, Pallas kernels, call(): pl.pallas_call(body, out_shape=[jax.ShapeDtypeStruct(s, d) for s, d in ou...  8.66 us
    ppermute x6, waiting for transfers between devices, crossed(): lax.ppermute(x, axis, [(i, i ^ bits) for i in range(lax.axis_size(axis))])  6.87 us
    ppermute x7, waiting for transfers between devices, swap(): return lax.ppermute(x, axis, pairs + [(j, i) for i, j in pairs])  2.11 us
    unnamed x23, local copies, waits for them, and re-layouts  1.64 us
  transfers between devices with their start and end apart: 13, of which 6 were waited for; matrix products, arithmetic and copies ran while one was open for 0% of the time, Pallas kernels for 9%

profile of v8, /device:TPU:0, one launch (start us, length us, event | category | flops | bytes accessed | tf_op | source)
XLA Modules:
  0.0 41.2 jit_solution(3996491837876566099)
XLA Ops:
  0.6 0.9 %copy.27 = bf16[96,4,256]{2,0,1:T(8,128)(2,1)S(1)} copy(bf16[96,4,256]{2,1,0:T(4,128)(2,1)} %param.11) | data formatting | bytes 393216 | tf_op args[0]
  1.6 0.0 copy-start.3
  1.6 0.2 shard_map.194
  1.8 0.0 copy-start.10
  1.8 0.8 %collective-permute-start = (bf16[16,96]{1,0:T(8,128)(2,1)S(1)}, bf16[16,96]{1,0:T(8,128)(2,1)S(1)}, u32[]{:S(2)}, u32[]{:S(2)}) collective-permute-start(bf16[16,96]{1,0:T(8,128)(2,1)S(1)} %get-tuple-element.48), channel_id=1, source_target_pairs={{1,2},{2,1},{5,6},{6,5},{9,10},{10,9},{13,14},{14,13},{17,18},{18,... | collective-permute-start | bytes 9224 | tf_op jit(solution)/shard_map/ppermute | solution.py:473
  2.6 5.9 %collective-permute-start.1 = (bf16[16,96]{1,0:T(8,128)(2,1)S(1)}, bf16[16,96]{1,0:T(8,128)(2,1)S(1)}, u32[]{:S(2)}, u32[]{:S(2)}) collective-permute-start(bf16[16,96]{1,0:T(8,128)(2,1)S(1)} %get-tuple-element.49), channel_id=1, source_target_pairs={{0,1},{2,3},{1,0},{3,2},{4,5},{6,7},{5,4},{7,6},{8,9},{10,11},{9,8... | collective-permute-start | bytes 9224 | tf_op jit(solution)/shard_map/ppermute | solution.py:473
  8.5 0.0 copy-done.10
  8.5 0.0 copy-start.1
  8.5 0.0 copy-start.2
  8.5 0.0 collective-permute-done.refs_1_
  8.5 1.6 %collective-permute-done.1.refs_2_ = bf16[16,96]{1,0:T(8,128)(2,1)S(1)} collective-permute-done((bf16[16,96]{1,0:T(8,128)(2,1)S(1)}, bf16[16,96]{1,0:T(8,128)(2,1)S(1)}, u32[]{:S(2)}, u32[]{:S(2)}) %collective-permute-start.1) | collective-permute-done | bytes 3104 | tf_op jit(solution)/shard_map/ppermute | solution.py:473
  10.1 0.0 copy-start.4
  10.1 0.7 %collective-permute-start.3 = (bf16[608,128]{1,0:T(8,128)(2,1)S(1)}, bf16[608,128]{1,0:T(8,128)(2,1)S(1)}, u32[]{:S(2)}, u32[]{:S(2)}) collective-permute-start(bf16[608,128]{1,0:T(8,128)(2,1)S(1)} %get-tuple-element.52), channel_id=1, source_target_pairs={{4,8},{12,16},{20,24},{8,4},{16,12},{24,20},{5,9},{13,17},{21,25},... | collective-permute-start | bytes 466952 | tf_op jit(solution)/shard_map/ppermute | solution.py:473
  10.8 0.0 copy-start.8
  10.8 0.0 copy-start.9
  10.8 0.0 copy-start.5
  10.8 0.0 copy-start.6
  10.9 0.0 copy-start.7
  10.9 0.0 copy-done.3
  10.9 0.0 copy-done.1
  10.9 0.0 copy-done.2
  10.9 0.0 copy-done.4
  10.9 0.6 %copy-done.8 = f32[96]{0:T(128)S(1)} copy-done((f32[96]{0:T(128)S(1)}, f32[96]{0:T(128)}, u32[]{:S(2)}) %copy-start.8) | copy-done | bytes 408
  11.5 0.0 copy-done.9
  11.5 0.0 copy-done.5
  11.5 0.0 copy-done.6
  11.5 0.0 copy-done.7
  11.5 0.7 %shard_map.196 = (bf16[4,96,256]{2,1,0:T(8,128)(2,1)S(1)}, bf16[3,224,224]{2,1,0:T(8,128)(2,1)S(1)}, bf16[3,224,224]{2,1,0:T(8,128)(2,1)S(1)}, bf16[384,112]{1,0...) custom-call(bf16[96,4,256]{2,1,0:T(4,128)(2,1)S(1)} %copy-done.3, f32[7,7,96]{2,1,0:T(8,128)S(1)} %bitcast.32, ...), custom_call_target="tpu_custom_call" | custom-call | bytes 1373184 | tf_op jit(solution)/shard_map/pallas_call | solution.py:459
  12.3 2.9 %collective-permute-start.2 = (bf16[608,128]{1,0:T(8,128)(2,1)S(1)}, bf16[608,128]{1,0:T(8,128)(2,1)S(1)}, u32[]{:S(2)}, u32[]{:S(2)}) collective-permute-start(bf16[608,128]{1,0:T(8,128)(2,1)S(1)} %shard_map.197), channel_id=1, source_target_pairs={{0,4},{4,0},{1,5},{5,1},{2,6},{6,2},{3,7},{7,3},{8,12},{12,8},{9,1... | collective-permute-start | bytes 466952 | tf_op jit(solution)/shard_map/ppermute | solution.py:473
  15.2 0.8 %shard_map.198 = (f32[384,256]{1,0:T(8,128)S(1)}, bf16[4,96,384]{2,1,0:T(8,128)(2,1)S(1)}) custom-call(bf16[4,96,256]{2,1,0:T(8,128)(2,1)S(1)} %bitcast.24, bf16[32,128]{1,0:T(8,128)(2,1)S(1)} %get-tuple-element.50.refs_10_.refs_1_.refs_3_, bf16[3,224,224]{2,1,0:T(8,128)(2,1)S(1)} %get-tuple-element.53.refs_2_.refs_6_), custom_call_target="tpu_custom_call" | custom-call | bytes 1193984 | tf_op jit(solution)/shard_map/pallas_call | solution.py:459
  16.0 0.0 collective-permute-done.3.refs_2_
  16.0 0.2 collective-permute-done.2.refs_1_
  16.2 3.6 %shard_map.199 = (bf16[4,96,256]{2,1,0:T(8,128)(2,1)S(1)}, bf16[4,96,256]{2,1,0:T(8,128)(2,1)S(1)}, bf16[3,96,256]{2,1,0:T(8,128)(2,1)S(1)}, bf16[6,96,384]{2,1,...) custom-call(bf16[4,96,256]{2,1,0:T(8,128)(2,1)S(1)} %bitcast.25, ...), custom_call_target="tpu_custom_call" | custom-call | bytes 3197312 | tf_op jit(solution)/shard_map/pallas_call | solution.py:459
  19.8 1.2 %collective-permute-start.4 = (bf16[960,128]{1,0:T(8,128)(2,1)S(1)}, bf16[960,128]{1,0:T(8,128)(2,1)S(1)}, u32[]{:S(2)}, u32[]{:S(2)}) collective-permute-start(bf16[960,128]{1,0:T(8,128)(2,1)S(1)} %get-tuple-element.59), channel_id=1, source_target_pairs={{0,4},{4,0},{1,5},{5,1},{2,6},{6,2},{3,7},{7,3},{8,12},{12,8},{9,1... | collective-permute-start | bytes 737288 | tf_op jit(solution)/shard_map/ppermute | solution.py:473
  21.0 1.0 %shard_map.200 = (bf16[32,128]{1,0:T(8,128)(2,1)S(1)}, f32[64,128]{1,0:T(8,128)S(1)}) custom-call(bf16[6,96,384]{2,1,0:T(8,128)(2,1)S(1)} %get-tuple-element.61.refs_0_, bf16[4,96,384]{2,1,0:T(8,128)(2,1)S(1)} %get-tuple-element.62.refs_1_, bf16[4,96,256]{2,1,0:T(8,128)(2,1)S(1)} %get-tuple-element.63.refs_2_.refs_0_, f32[16,128]{1,0:T(8,128)S(1)} %get-tuple-element.64.refs_3_), custom_call_target="tpu_custom_call" | custom-call | bytes 983040 | tf_op jit(solution)/shard_map/pallas_call | solution.py:459
  22.0 0.2 collective-permute-done.4.refs_0_.refs_1_
  22.2 1.4 %collective-permute-start.5 = (bf16[176,128]{1,0:T(8,128)(2,1)S(1)}, bf16[176,128]{1,0:T(8,128)(2,1)S(1)}, u32[]{:S(2)}, u32[]{:S(2)}) collective-permute-start(bf16[176,128]{1,0:T(8,128)(2,1)S(1)} %get-tuple-element.67), channel_id=1, source_target_pairs={{0,3},{1,2},{2,1},{3,0},{4,7},{5,6},{6,5},{7,4},{8,11},{9,10},{10,... | collective-permute-start | bytes 135176 | tf_op jit(solution)/shard_map/ppermute | solution.py:477
  23.6 1.1 %collective-permute-start.7 = (bf16[176,128]{1,0:T(8,128)(2,1)S(1)}, bf16[176,128]{1,0:T(8,128)(2,1)S(1)}, u32[]{:S(2)}, u32[]{:S(2)}) collective-permute-start(bf16[176,128]{1,0:T(8,128)(2,1)S(1)} %get-tuple-element.69), channel_id=1, source_target_pairs={{0,1},{1,0},{2,3},{3,2},{4,5},{5,4},{6,7},{7,6},{8,9},{9,8},{10,11... | collective-permute-start | bytes 135176 | tf_op jit(solution)/shard_map/ppermute | solution.py:477
  24.7 1.9 %collective-permute-start.6 = (bf16[160,128]{1,0:T(8,128)(2,1)S(1)}, bf16[160,128]{1,0:T(8,128)(2,1)S(1)}, u32[]{:S(2)}, u32[]{:S(2)}) collective-permute-start(bf16[160,128]{1,0:T(8,128)(2,1)S(1)} %get-tuple-element.68), channel_id=1, source_target_pairs={{0,2},{1,3},{2,0},{3,1},{4,6},{5,7},{6,4},{7,5},{8,10},{9,11},{10,... | collective-permute-start | bytes 122888 | tf_op jit(solution)/shard_map/ppermute | solution.py:477
  26.6 0.7 %collective-permute-start.11 = (bf16[3,96,256]{2,1,0:T(8,128)(2,1)S(1)}, bf16[3,96,256]{2,1,0:T(8,128)(2,1)S(1)}, u32[]{:S(2)}, u32[]{:S(2)}) collective-permute-start(bf16[3,96,256]{2,1,0:T(8,128)(2,1)S(1)} %get-tuple-element.73), channel_id=1, source_target_pairs={{4,8},{12,16},{20,24},{8,4},{16,12},{24,20},{5,9},{13,17},{21,25},... | collective-permute-start | bytes 442376 | tf_op jit(solution)/shard_map/ppermute | solution.py:473
  27.3 3.0 %collective-permute-done.6.refs_1_ = bf16[160,128]{1,0:T(8,128)(2,1)S(1)} collective-permute-done((bf16[160,128]{1,0:T(8,128)(2,1)S(1)}, bf16[160,128]{1,0:T(8,128)(2,1)S(1)}, u32[]{:S(2)}, u32[]{:S(2)}) %collective-permute-start.6) | collective-permute-done | bytes 40992 | tf_op jit(solution)/shard_map/ppermute | solution.py:477
  30.3 0.0 collective-permute-done.5.refs_0_
  30.3 0.0 collective-permute-done.7.refs_2_
  30.4 1.6 %collective-permute-start.10 = (bf16[192,128]{1,0:T(8,128)(2,1)S(1)}, bf16[192,128]{1,0:T(8,128)(2,1)S(1)}, u32[]{:S(2)}, u32[]{:S(2)}) collective-permute-start(bf16[192,128]{1,0:T(8,128)(2,1)S(1)} %get-tuple-element.71.refs_3_), channel_id=1, source_target_pairs={{0,8},{8,0},{16,24},{24,16},{1,9},{9,1},{17,25},{25,17},{2,10},{10... | collective-permute-start | bytes 147464 | tf_op jit(solution)/shard_map/ppermute | solution.py:477
  31.9 2.6 %collective-permute-start.8 = (bf16[192,128]{1,0:T(8,128)(2,1)S(1)}, bf16[192,128]{1,0:T(8,128)(2,1)S(1)}, u32[]{:S(2)}, u32[]{:S(2)}) collective-permute-start(bf16[192,128]{1,0:T(8,128)(2,1)S(1)} %get-tuple-element.71.refs_3_), channel_id=1, source_target_pairs={{0,24},{8,16},{16,8},{24,0},{1,25},{9,17},{17,9},{25,1},{2,26},{10... | collective-permute-start | bytes 147464 | tf_op jit(solution)/shard_map/ppermute | solution.py:477
  34.6 0.0 collective-permute-start.9
  34.6 0.2 copy.26
  34.7 0.0 copy-start
  34.8 0.0 collective-permute-done.11.refs_5_.refs_2_
  34.8 3.8 %collective-permute-done.9.refs_1_ = bf16[160,128]{1,0:T(8,128)(2,1)S(1)} collective-permute-done((bf16[160,128]{1,0:T(8,128)(2,1)S(1)}, bf16[160,128]{1,0:T(8,128)(2,1)S(1)}, u32[]{:S(2)}, u32[]{:S(2)}) %collective-permute-start.9) | collective-permute-done | bytes 40992 | tf_op jit(solution)/shard_map/ppermute | solution.py:477
  38.6 0.0 collective-permute-done.10.refs_2_
  38.6 0.0 collective-permute-done.8.refs_0_
  38.6 0.0 copy-done
  38.6 0.1 collective-permute-start.12
  38.7 1.1 %shard_map.204.refs_2_ = f32[384,256]{1,0:T(8,128)S(1)} custom-call(bf16[4,96,256]{2,1,0:T(8,128)(2,1)S(1)} %get-tuple-element.63.refs_2_.refs_0_, bf16[960,128]{1,0:T(8,128)(2,1)S(1)} %collective-permute-done.4.refs_0_.refs_1_, bf16[3,96,256]{2,1,0:T(8,128)(2,1)S(1)} %collective-permute-done.11.refs_5_.refs_2_, ...), custom_call_target="tpu_custom_call" | custom-call | bytes 1480704 | tf_op jit(solution)/shard_map/pallas_call | solution.py:459
  39.8 0.2 collective-permute-done.12.refs_1_
  40.0 1.2 %shard_map.205 = (bf16[96,4,256]{2,1,0:T(4,128)(2,1)}, f32[7,7,96]{2,1,0:T(8,128)}, f32[1,96]{1,0:T(1,128)}, f32[1,96]{1,0:T(1,128)}, f32[1,96]{1,0:T(1,128)}, /...) custom-call(f32[224,128]{1,0:T(8,128)S(1)} %shard_map.203.refs_5_.refs_0_, ...), custom_call_target="tpu_custom_call" | custom-call | bytes 932864 | tf_op jit(solution)/shard_map/pallas_call | solution.py:459
  (6 shorter events, 0.2 us)
Async XLA Ops:
  1.6 9.3 %copy-start.3 = (bf16[96,4,256]{2,1,0:T(4,128)(2,1)S(1)}, bf16[96,4,256]{2,1,0:T(4,128)(2,1)}, u32[]{:S(2)}) copy-start(bf16[96,4,256]{2,1,0:T(4,128)(2,1)} %refs_0_.1) | copy-start | bytes 589828
  1.8 6.7 %copy-start.10 = (bf16[384]{0:T(512)(128)(2,1)S(1)}, bf16[384]{0:T(512)(128)(2,1)}, u32[]{:S(2)}) copy-start(bf16[384]{0:T(512)(128)(2,1)} %param.18) | copy-start | bytes 2308
  1.8 6.7 %collective-permute-start = (bf16[16,96]{1,0:T(8,128)(2,1)S(1)}, bf16[16,96]{1,0:T(8,128)(2,1)S(1)}, u32[]{:S(2)}, u32[]{:S(2)}) collective-permute-start(bf16[16,96]{1,0:T(8,128)(2,1)S(1)} %get-tuple-element.48), channel_id=1, source_target_pairs={{1,2},{2,1},{5,6},{6,5},{9,10},{10,9},{13,14},{14,13},{17,18},{18,... | collective-permute-start | bytes 9224 | tf_op jit(solution)/shard_map/ppermute | solution.py:473
  2.6 7.5 %collective-permute-start.1 = (bf16[16,96]{1,0:T(8,128)(2,1)S(1)}, bf16[16,96]{1,0:T(8,128)(2,1)S(1)}, u32[]{:S(2)}, u32[]{:S(2)}) collective-permute-start(bf16[16,96]{1,0:T(8,128)(2,1)S(1)} %get-tuple-element.49), channel_id=1, source_target_pairs={{0,1},{2,3},{1,0},{3,2},{4,5},{6,7},{5,4},{7,6},{8,9},{10,11},{9,8... | collective-permute-start | bytes 9224 | tf_op jit(solution)/shard_map/ppermute | solution.py:473
  8.5 2.4 %copy-start.1 = (bf16[384,96]{0,1:T(8,128)(2,1)S(1)}, bf16[384,96]{0,1:T(8,128)(2,1)}, u32[]{:S(2)}) copy-start(bf16[384,96]{0,1:T(8,128)(2,1)} %param.17) | copy-start | bytes 221188
  8.5 2.4 %copy-start.2 = (bf16[384,96]{0,1:T(8,128)(2,1)S(1)}, bf16[384,96]{0,1:T(8,128)(2,1)}, u32[]{:S(2)}) copy-start(bf16[384,96]{0,1:T(8,128)(2,1)} %param.19) | copy-start | bytes 221188
  10.1 0.8 %copy-start.4 = (f32[96,7,7]{0,2,1:T(8,128)S(1)}, f32[96,7,7]{0,2,1:T(8,128)}, u32[]{:S(2)}) copy-start(f32[96,7,7]{0,2,1:T(8,128)} %param.13) | copy-start | bytes 56452
  10.1 5.8 %collective-permute-start.3 = (bf16[608,128]{1,0:T(8,128)(2,1)S(1)}, bf16[608,128]{1,0:T(8,128)(2,1)S(1)}, u32[]{:S(2)}, u32[]{:S(2)}) collective-permute-start(bf16[608,128]{1,0:T(8,128)(2,1)S(1)} %get-tuple-element.52), channel_id=1, source_target_pairs={{4,8},{12,16},{20,24},{8,4},{16,12},{24,20},{5,9},{13,17},{21,25},... | collective-permute-start | bytes 466952 | tf_op jit(solution)/shard_map/ppermute | solution.py:473
  10.8 0.7 %copy-start.8 = (f32[96]{0:T(128)S(1)}, f32[96]{0:T(128)}, u32[]{:S(2)}) copy-start(f32[96]{0:T(128)} %param.16) | copy-start | bytes 1156
  10.8 0.7 %copy-start.9 = (f32[96]{0:T(128)S(1)}, f32[96]{0:T(128)}, u32[]{:S(2)}) copy-start(f32[96]{0:T(128)} %param.20) | copy-start | bytes 1156
  10.8 0.7 %copy-start.5 = (f32[96]{0:T(128)S(1)}, f32[96]{0:T(128)}, u32[]{:S(2)}) copy-start(f32[96]{0:T(128)} %param.21) | copy-start | bytes 1156
  10.8 0.7 %copy-start.6 = (f32[96]{0:T(128)S(1)}, f32[96]{0:T(128)}, u32[]{:S(2)}) copy-start(f32[96]{0:T(128)} %param.14) | copy-start | bytes 1156
  10.9 0.7 %copy-start.7 = (f32[96]{0:T(128)S(1)}, f32[96]{0:T(128)}, u32[]{:S(2)}) copy-start(f32[96]{0:T(128)} %param.15) | copy-start | bytes 1156
  12.3 3.9 %collective-permute-start.2 = (bf16[608,128]{1,0:T(8,128)(2,1)S(1)}, bf16[608,128]{1,0:T(8,128)(2,1)S(1)}, u32[]{:S(2)}, u32[]{:S(2)}) collective-permute-start(bf16[608,128]{1,0:T(8,128)(2,1)S(1)} %shard_map.197), channel_id=1, source_target_pairs={{0,4},{4,0},{1,5},{5,1},{2,6},{6,2},{3,7},{7,3},{8,12},{12,8},{9,1... | collective-permute-start | bytes 466952 | tf_op jit(solution)/shard_map/ppermute | solution.py:473
  19.8 2.3 %collective-permute-start.4 = (bf16[960,128]{1,0:T(8,128)(2,1)S(1)}, bf16[960,128]{1,0:T(8,128)(2,1)S(1)}, u32[]{:S(2)}, u32[]{:S(2)}) collective-permute-start(bf16[960,128]{1,0:T(8,128)(2,1)S(1)} %get-tuple-element.59), channel_id=1, source_target_pairs={{0,4},{4,0},{1,5},{5,1},{2,6},{6,2},{3,7},{7,3},{8,12},{12,8},{9,1... | collective-permute-start | bytes 737288 | tf_op jit(solution)/shard_map/ppermute | solution.py:473
  22.2 8.2 %collective-permute-start.5 = (bf16[176,128]{1,0:T(8,128)(2,1)S(1)}, bf16[176,128]{1,0:T(8,128)(2,1)S(1)}, u32[]{:S(2)}, u32[]{:S(2)}) collective-permute-start(bf16[176,128]{1,0:T(8,128)(2,1)S(1)} %get-tuple-element.67), channel_id=1, source_target_pairs={{0,3},{1,2},{2,1},{3,0},{4,7},{5,6},{6,5},{7,4},{8,11},{9,10},{10,... | collective-permute-start | bytes 135176 | tf_op jit(solution)/shard_map/ppermute | solution.py:477
  23.6 6.8 %collective-permute-start.7 = (bf16[176,128]{1,0:T(8,128)(2,1)S(1)}, bf16[176,128]{1,0:T(8,128)(2,1)S(1)}, u32[]{:S(2)}, u32[]{:S(2)}) collective-permute-start(bf16[176,128]{1,0:T(8,128)(2,1)S(1)} %get-tuple-element.69), channel_id=1, source_target_pairs={{0,1},{1,0},{2,3},{3,2},{4,5},{5,4},{6,7},{7,6},{8,9},{9,8},{10,11... | collective-permute-start | bytes 135176 | tf_op jit(solution)/shard_map/ppermute | solution.py:477
  24.7 5.6 %collective-permute-start.6 = (bf16[160,128]{1,0:T(8,128)(2,1)S(1)}, bf16[160,128]{1,0:T(8,128)(2,1)S(1)}, u32[]{:S(2)}, u32[]{:S(2)}) collective-permute-start(bf16[160,128]{1,0:T(8,128)(2,1)S(1)} %get-tuple-element.68), channel_id=1, source_target_pairs={{0,2},{1,3},{2,0},{3,1},{4,6},{5,7},{6,4},{7,5},{8,10},{9,11},{10,... | collective-permute-start | bytes 122888 | tf_op jit(solution)/shard_map/ppermute | solution.py:477
  26.6 8.1 %collective-permute-start.11 = (bf16[3,96,256]{2,1,0:T(8,128)(2,1)S(1)}, bf16[3,96,256]{2,1,0:T(8,128)(2,1)S(1)}, u32[]{:S(2)}, u32[]{:S(2)}) collective-permute-start(bf16[3,96,256]{2,1,0:T(8,128)(2,1)S(1)} %get-tuple-element.73), channel_id=1, source_target_pairs={{4,8},{12,16},{20,24},{8,4},{16,12},{24,20},{5,9},{13,17},{21,25},... | collective-permute-start | bytes 442376 | tf_op jit(solution)/shard_map/ppermute | solution.py:473
  30.4 8.2 %collective-permute-start.10 = (bf16[192,128]{1,0:T(8,128)(2,1)S(1)}, bf16[192,128]{1,0:T(8,128)(2,1)S(1)}, u32[]{:S(2)}, u32[]{:S(2)}) collective-permute-start(bf16[192,128]{1,0:T(8,128)(2,1)S(1)} %get-tuple-element.71.refs_3_), channel_id=1, source_target_pairs={{0,8},{8,0},{16,24},{24,16},{1,9},{9,1},{17,25},{25,17},{2,10},{10... | collective-permute-start | bytes 147464 | tf_op jit(solution)/shard_map/ppermute | solution.py:477
  31.9 6.6 %collective-permute-start.8 = (bf16[192,128]{1,0:T(8,128)(2,1)S(1)}, bf16[192,128]{1,0:T(8,128)(2,1)S(1)}, u32[]{:S(2)}, u32[]{:S(2)}) collective-permute-start(bf16[192,128]{1,0:T(8,128)(2,1)S(1)} %get-tuple-element.71.refs_3_), channel_id=1, source_target_pairs={{0,24},{8,16},{16,8},{24,0},{1,25},{9,17},{17,9},{25,1},{2,26},{10... | collective-permute-start | bytes 147464 | tf_op jit(solution)/shard_map/ppermute | solution.py:477
  34.6 4.0 %collective-permute-start.9 = (bf16[160,128]{1,0:T(8,128)(2,1)S(1)}, bf16[160,128]{1,0:T(8,128)(2,1)S(1)}, u32[]{:S(2)}, u32[]{:S(2)}) collective-permute-start(bf16[160,128]{1,0:T(8,128)(2,1)S(1)} %get-tuple-element.72), channel_id=1, source_target_pairs={{0,16},{8,24},{16,0},{24,8},{1,17},{9,25},{17,1},{25,9},{2,18},{10... | collective-permute-start | bytes 122888 | tf_op jit(solution)/shard_map/ppermute | solution.py:477
  34.7 3.9 %copy-start = (bf16[4,96,256]{2,0,1:T(4,128)(2,1)}, bf16[4,96,256]{2,0,1:T(4,128)(2,1)S(1)}, u32[]{:S(2)}) copy-start(bf16[4,96,256]{2,0,1:T(4,128)(2,1)S(1)} %copy.26) | copy-start | bytes 589828
  38.6 1.4 %collective-permute-start.12 = (f32[224,128]{1,0:T(8,128)S(1)}, f32[224,128]{1,0:T(8,128)S(1)}, u32[]{:S(2)}, u32[]{:S(2)}) collective-permute-start(f32[224,128]{1,0:T(8,128)S(1)} %shard_map.203.refs_5_.refs_0_), channel_id=1, source_target_pairs={{0,4},{4,0},{1,5},{5,1},{2,6},{6,2},{3,7},{7,3},{8,12},{12,8},{9,1... | collective-permute-start | bytes 344072 | tf_op jit(solution)/shard_map/ppermute | solution.py:473

commit v9 on v8

--- a/solution.py
+++ b/solution.py
@@ -355,7 +355,7 @@
     send_ref[...] = jnp.concatenate([total, *edges], axis=0)
 
 
-def total_kernel(axes, third_ref, second_ref, first_ref, mine_ref, total_ref):
+def total_kernel(axes, second_ref, third_ref, first_ref, mine_ref, total_ref):
     q, core = lax.axis_index(axes[0]), lax.axis_index(axes[1])
     count = second_ref.shape[0]
     wide = mine_ref.shape[0] - count
@@ -590,7 +590,7 @@
         (mine,) = call(
             functools.partial(total_kernel, axes),
             [((low + 4 * high, LANES), F32)],
-            third, second, first, send,
+            second, third, first, send,
             after=[output, far],
         )
     else:

time: 41.5 us -> 41.5 us (level)
  no operation moved by 1% of the time
where the time goes in v9:
time: 41.5 us; the launch traced here: 41.2 us
  starting transfers between devices  20.9 us (50%)
  waiting for transfers between devices  8.99 us (22%)
  Pallas kernels  8.66 us (21%)
  local copies, waits for them, and re-layouts  1.8 us (4%)
  between operations  0.88 us (2%)
    ppermute x7, starting transfers between devices, swap(): return lax.ppermute(x, axis, pairs + [(j, i) for i, j in pairs])  12.2 us
    ppermute x6, starting transfers between devices, crossed(): lax.ppermute(x, axis, [(i, i ^ bits) for i in range(lax.axis_size(axis))])  8.66 us
    pallas_call x12, Pallas kernels, call(): pl.pallas_call(body, out_shape=[jax.ShapeDtypeStruct(s, d) for s, d in ou...  8.66 us
    ppermute x6, waiting for transfers between devices, crossed(): lax.ppermute(x, axis, [(i, i ^ bits) for i in range(lax.axis_size(axis))])  6.87 us
    ppermute x7, waiting for transfers between devices, swap(): return lax.ppermute(x, axis, pairs + [(j, i) for i, j in pairs])  2.11 us
    unnamed x23, local copies, waits for them, and re-layouts  1.64 us
  transfers between devices with their start and end apart: 13, of which 6 were waited for; matrix products, arithmetic and copies ran while one was open for 0% of the time, Pallas kernels for 9%

profile of v9, /device:TPU:0, one launch (start us, length us, event | category | flops | bytes accessed | tf_op | source)
XLA Modules:
  0.0 41.2 jit_solution(5748641507059184742)
XLA Ops:
  0.6 0.9 %copy.27 = bf16[96,4,256]{2,0,1:T(8,128)(2,1)S(1)} copy(bf16[96,4,256]{2,1,0:T(4,128)(2,1)} %param.11) | data formatting | bytes 393216 | tf_op args[0]
  1.6 0.0 copy-start.3
  1.6 0.2 shard_map.194
  1.8 0.0 copy-start.10
  1.8 0.8 %collective-permute-start = (bf16[16,96]{1,0:T(8,128)(2,1)S(1)}, bf16[16,96]{1,0:T(8,128)(2,1)S(1)}, u32[]{:S(2)}, u32[]{:S(2)}) collective-permute-start(bf16[16,96]{1,0:T(8,128)(2,1)S(1)} %get-tuple-element.48), channel_id=1, source_target_pairs={{1,2},{2,1},{5,6},{6,5},{9,10},{10,9},{13,14},{14,13},{17,18},{18,... | collective-permute-start | bytes 9224 | tf_op jit(solution)/shard_map/ppermute | solution.py:473
  2.6 5.9 %collective-permute-start.1 = (bf16[16,96]{1,0:T(8,128)(2,1)S(1)}, bf16[16,96]{1,0:T(8,128)(2,1)S(1)}, u32[]{:S(2)}, u32[]{:S(2)}) collective-permute-start(bf16[16,96]{1,0:T(8,128)(2,1)S(1)} %get-tuple-element.49), channel_id=1, source_target_pairs={{0,1},{2,3},{1,0},{3,2},{4,5},{6,7},{5,4},{7,6},{8,9},{10,11},{9,8... | collective-permute-start | bytes 9224 | tf_op jit(solution)/shard_map/ppermute | solution.py:473
  8.5 0.0 copy-done.10
  8.5 0.0 copy-start.1
  8.5 0.0 copy-start.2
  8.5 0.0 collective-permute-done.refs_1_
  8.5 1.6 %collective-permute-done.1.refs_2_ = bf16[16,96]{1,0:T(8,128)(2,1)S(1)} collective-permute-done((bf16[16,96]{1,0:T(8,128)(2,1)S(1)}, bf16[16,96]{1,0:T(8,128)(2,1)S(1)}, u32[]{:S(2)}, u32[]{:S(2)}) %collective-permute-start.1) | collective-permute-done | bytes 3104 | tf_op jit(solution)/shard_map/ppermute | solution.py:473
  10.1 0.0 copy-start.4
  10.1 0.7 %collective-permute-start.3 = (bf16[608,128]{1,0:T(8,128)(2,1)S(1)}, bf16[608,128]{1,0:T(8,128)(2,1)S(1)}, u32[]{:S(2)}, u32[]{:S(2)}) collective-permute-start(bf16[608,128]{1,0:T(8,128)(2,1)S(1)} %get-tuple-element.52), channel_id=1, source_target_pairs={{4,8},{12,16},{20,24},{8,4},{16,12},{24,20},{5,9},{13,17},{21,25},... | collective-permute-start | bytes 466952 | tf_op jit(solution)/shard_map/ppermute | solution.py:473
  10.8 0.0 copy-start.8
  10.8 0.0 copy-start.9
  10.8 0.0 copy-start.5
  10.8 0.0 copy-start.6
  10.9 0.0 copy-start.7
  10.9 0.0 copy-done.3
  10.9 0.0 copy-done.1
  10.9 0.0 copy-done.2
  10.9 0.0 copy-done.4
  10.9 0.6 %copy-done.8 = f32[96]{0:T(128)S(1)} copy-done((f32[96]{0:T(128)S(1)}, f32[96]{0:T(128)}, u32[]{:S(2)}) %copy-start.8) | copy-done | bytes 408
  11.5 0.0 copy-done.9
  11.5 0.0 copy-done.5
  11.5 0.0 copy-done.6
  11.5 0.0 copy-done.7
  11.5 0.7 %shard_map.196 = (bf16[4,96,256]{2,1,0:T(8,128)(2,1)S(1)}, bf16[3,224,224]{2,1,0:T(8,128)(2,1)S(1)}, bf16[3,224,224]{2,1,0:T(8,128)(2,1)S(1)}, bf16[384,112]{1,0...) custom-call(bf16[96,4,256]{2,1,0:T(4,128)(2,1)S(1)} %copy-done.3, f32[7,7,96]{2,1,0:T(8,128)S(1)} %bitcast.32, ...), custom_call_target="tpu_custom_call" | custom-call | bytes 1373184 | tf_op jit(solution)/shard_map/pallas_call | solution.py:459
  12.3 2.9 %collective-permute-start.2 = (bf16[608,128]{1,0:T(8,128)(2,1)S(1)}, bf16[608,128]{1,0:T(8,128)(2,1)S(1)}, u32[]{:S(2)}, u32[]{:S(2)}) collective-permute-start(bf16[608,128]{1,0:T(8,128)(2,1)S(1)} %shard_map.197), channel_id=1, source_target_pairs={{0,4},{4,0},{1,5},{5,1},{2,6},{6,2},{3,7},{7,3},{8,12},{12,8},{9,1... | collective-permute-start | bytes 466952 | tf_op jit(solution)/shard_map/ppermute | solution.py:473
  15.2 0.8 %shard_map.198 = (f32[384,256]{1,0:T(8,128)S(1)}, bf16[4,96,384]{2,1,0:T(8,128)(2,1)S(1)}) custom-call(bf16[4,96,256]{2,1,0:T(8,128)(2,1)S(1)} %bitcast.24, bf16[32,128]{1,0:T(8,128)(2,1)S(1)} %get-tuple-element.50.refs_10_.refs_1_.refs_3_, bf16[3,224,224]{2,1,0:T(8,128)(2,1)S(1)} %get-tuple-element.53.refs_2_.refs_6_), custom_call_target="tpu_custom_call" | custom-call | bytes 1193984 | tf_op jit(solution)/shard_map/pallas_call | solution.py:459
  16.0 0.0 collective-permute-done.3.refs_2_
  16.0 0.2 collective-permute-done.2.refs_1_
  16.2 3.6 %shard_map.199 = (bf16[4,96,256]{2,1,0:T(8,128)(2,1)S(1)}, bf16[4,96,256]{2,1,0:T(8,128)(2,1)S(1)}, bf16[3,96,256]{2,1,0:T(8,128)(2,1)S(1)}, bf16[6,96,384]{2,1,...) custom-call(bf16[4,96,256]{2,1,0:T(8,128)(2,1)S(1)} %bitcast.25, ...), custom_call_target="tpu_custom_call" | custom-call | bytes 3197312 | tf_op jit(solution)/shard_map/pallas_call | solution.py:459
  19.8 1.2 %collective-permute-start.4 = (bf16[960,128]{1,0:T(8,128)(2,1)S(1)}, bf16[960,128]{1,0:T(8,128)(2,1)S(1)}, u32[]{:S(2)}, u32[]{:S(2)}) collective-permute-start(bf16[960,128]{1,0:T(8,128)(2,1)S(1)} %get-tuple-element.59), channel_id=1, source_target_pairs={{0,4},{4,0},{1,5},{5,1},{2,6},{6,2},{3,7},{7,3},{8,12},{12,8},{9,1... | collective-permute-start | bytes 737288 | tf_op jit(solution)/shard_map/ppermute | solution.py:473
  21.0 1.0 %shard_map.200 = (bf16[32,128]{1,0:T(8,128)(2,1)S(1)}, f32[64,128]{1,0:T(8,128)S(1)}) custom-call(bf16[6,96,384]{2,1,0:T(8,128)(2,1)S(1)} %get-tuple-element.61.refs_0_, bf16[4,96,384]{2,1,0:T(8,128)(2,1)S(1)} %get-tuple-element.62.refs_1_, bf16[4,96,256]{2,1,0:T(8,128)(2,1)S(1)} %get-tuple-element.63.refs_2_.refs_0_, f32[16,128]{1,0:T(8,128)S(1)} %get-tuple-element.64.refs_3_), custom_call_target="tpu_custom_call" | custom-call | bytes 983040 | tf_op jit(solution)/shard_map/pallas_call | solution.py:459
  22.0 0.2 collective-permute-done.4.refs_0_.refs_1_
  22.2 1.4 %collective-permute-start.5 = (bf16[176,128]{1,0:T(8,128)(2,1)S(1)}, bf16[176,128]{1,0:T(8,128)(2,1)S(1)}, u32[]{:S(2)}, u32[]{:S(2)}) collective-permute-start(bf16[176,128]{1,0:T(8,128)(2,1)S(1)} %get-tuple-element.67), channel_id=1, source_target_pairs={{0,3},{1,2},{2,1},{3,0},{4,7},{5,6},{6,5},{7,4},{8,11},{9,10},{10,... | collective-permute-start | bytes 135176 | tf_op jit(solution)/shard_map/ppermute | solution.py:477
  23.6 1.1 %collective-permute-start.7 = (bf16[176,128]{1,0:T(8,128)(2,1)S(1)}, bf16[176,128]{1,0:T(8,128)(2,1)S(1)}, u32[]{:S(2)}, u32[]{:S(2)}) collective-permute-start(bf16[176,128]{1,0:T(8,128)(2,1)S(1)} %get-tuple-element.69), channel_id=1, source_target_pairs={{0,1},{1,0},{2,3},{3,2},{4,5},{5,4},{6,7},{7,6},{8,9},{9,8},{10,11... | collective-permute-start | bytes 135176 | tf_op jit(solution)/shard_map/ppermute | solution.py:477
  24.7 1.9 %collective-permute-start.6 = (bf16[160,128]{1,0:T(8,128)(2,1)S(1)}, bf16[160,128]{1,0:T(8,128)(2,1)S(1)}, u32[]{:S(2)}, u32[]{:S(2)}) collective-permute-start(bf16[160,128]{1,0:T(8,128)(2,1)S(1)} %get-tuple-element.68), channel_id=1, source_target_pairs={{0,2},{1,3},{2,0},{3,1},{4,6},{5,7},{6,4},{7,5},{8,10},{9,11},{10,... | collective-permute-start | bytes 122888 | tf_op jit(solution)/shard_map/ppermute | solution.py:477
  26.6 0.7 %collective-permute-start.11 = (bf16[3,96,256]{2,1,0:T(8,128)(2,1)S(1)}, bf16[3,96,256]{2,1,0:T(8,128)(2,1)S(1)}, u32[]{:S(2)}, u32[]{:S(2)}) collective-permute-start(bf16[3,96,256]{2,1,0:T(8,128)(2,1)S(1)} %get-tuple-element.73), channel_id=1, source_target_pairs={{4,8},{12,16},{20,24},{8,4},{16,12},{24,20},{5,9},{13,17},{21,25},... | collective-permute-start | bytes 442376 | tf_op jit(solution)/shard_map/ppermute | solution.py:473
  27.3 3.0 %collective-permute-done.6.refs_1_ = bf16[160,128]{1,0:T(8,128)(2,1)S(1)} collective-permute-done((bf16[160,128]{1,0:T(8,128)(2,1)S(1)}, bf16[160,128]{1,0:T(8,128)(2,1)S(1)}, u32[]{:S(2)}, u32[]{:S(2)}) %collective-permute-start.6) | collective-permute-done | bytes 40992 | tf_op jit(solution)/shard_map/ppermute | solution.py:477
  30.3 0.0 collective-permute-done.5.refs_0_
  30.3 0.0 collective-permute-done.7.refs_2_
  30.4 1.6 %collective-permute-start.10 = (bf16[192,128]{1,0:T(8,128)(2,1)S(1)}, bf16[192,128]{1,0:T(8,128)(2,1)S(1)}, u32[]{:S(2)}, u32[]{:S(2)}) collective-permute-start(bf16[192,128]{1,0:T(8,128)(2,1)S(1)} %get-tuple-element.72.refs_3_), channel_id=1, source_target_pairs={{0,8},{8,0},{16,24},{24,16},{1,9},{9,1},{17,25},{25,17},{2,10},{10... | collective-permute-start | bytes 147464 | tf_op jit(solution)/shard_map/ppermute | solution.py:477
  31.9 2.6 %collective-permute-start.9 = (bf16[192,128]{1,0:T(8,128)(2,1)S(1)}, bf16[192,128]{1,0:T(8,128)(2,1)S(1)}, u32[]{:S(2)}, u32[]{:S(2)}) collective-permute-start(bf16[192,128]{1,0:T(8,128)(2,1)S(1)} %get-tuple-element.72.refs_3_), channel_id=1, source_target_pairs={{0,24},{8,16},{16,8},{24,0},{1,25},{9,17},{17,9},{25,1},{2,26},{10... | collective-permute-start | bytes 147464 | tf_op jit(solution)/shard_map/ppermute | solution.py:477
  34.6 0.0 collective-permute-start.8
  34.6 0.2 copy.26
  34.7 0.0 copy-start
  34.8 0.0 collective-permute-done.11.refs_5_.refs_2_
  34.8 3.8 %collective-permute-done.8.refs_0_ = bf16[160,128]{1,0:T(8,128)(2,1)S(1)} collective-permute-done((bf16[160,128]{1,0:T(8,128)(2,1)S(1)}, bf16[160,128]{1,0:T(8,128)(2,1)S(1)}, u32[]{:S(2)}, u32[]{:S(2)}) %collective-permute-start.8) | collective-permute-done | bytes 40992 | tf_op jit(solution)/shard_map/ppermute | solution.py:477
  38.6 0.0 collective-permute-done.10.refs_2_
  38.6 0.0 collective-permute-done.9.refs_1_
  38.6 0.0 copy-done
  38.6 0.1 collective-permute-start.12
  38.7 1.1 %shard_map.204.refs_2_ = f32[384,256]{1,0:T(8,128)S(1)} custom-call(bf16[4,96,256]{2,1,0:T(8,128)(2,1)S(1)} %get-tuple-element.63.refs_2_.refs_0_, bf16[960,128]{1,0:T(8,128)(2,1)S(1)} %collective-permute-done.4.refs_0_.refs_1_, bf16[3,96,256]{2,1,0:T(8,128)(2,1)S(1)} %collective-permute-done.11.refs_5_.refs_2_, ...), custom_call_target="tpu_custom_call" | custom-call | bytes 1480704 | tf_op jit(solution)/shard_map/pallas_call | solution.py:459
  39.8 0.2 collective-permute-done.12.refs_1_
  40.0 1.2 %shard_map.205 = (bf16[96,4,256]{2,1,0:T(4,128)(2,1)}, f32[7,7,96]{2,1,0:T(8,128)}, f32[1,96]{1,0:T(1,128)}, f32[1,96]{1,0:T(1,128)}, f32[1,96]{1,0:T(1,128)}, /...) custom-call(f32[224,128]{1,0:T(8,128)S(1)} %shard_map.203.refs_5_.refs_0_, ...), custom_call_target="tpu_custom_call" | custom-call | bytes 932864 | tf_op jit(solution)/shard_map/pallas_call | solution.py:459
  (6 shorter events, 0.2 us)
Async XLA Ops:
  1.6 9.3 %copy-start.3 = (bf16[96,4,256]{2,1,0:T(4,128)(2,1)S(1)}, bf16[96,4,256]{2,1,0:T(4,128)(2,1)}, u32[]{:S(2)}) copy-start(bf16[96,4,256]{2,1,0:T(4,128)(2,1)} %refs_0_.1) | copy-start | bytes 589828
  1.8 6.7 %copy-start.10 = (bf16[384]{0:T(512)(128)(2,1)S(1)}, bf16[384]{0:T(512)(128)(2,1)}, u32[]{:S(2)}) copy-start(bf16[384]{0:T(512)(128)(2,1)} %param.18) | copy-start | bytes 2308
  1.8 6.7 %collective-permute-start = (bf16[16,96]{1,0:T(8,128)(2,1)S(1)}, bf16[16,96]{1,0:T(8,128)(2,1)S(1)}, u32[]{:S(2)}, u32[]{:S(2)}) collective-permute-start(bf16[16,96]{1,0:T(8,128)(2,1)S(1)} %get-tuple-element.48), channel_id=1, source_target_pairs={{1,2},{2,1},{5,6},{6,5},{9,10},{10,9},{13,14},{14,13},{17,18},{18,... | collective-permute-start | bytes 9224 | tf_op jit(solution)/shard_map/ppermute | solution.py:473
  2.6 7.5 %collective-permute-start.1 = (bf16[16,96]{1,0:T(8,128)(2,1)S(1)}, bf16[16,96]{1,0:T(8,128)(2,1)S(1)}, u32[]{:S(2)}, u32[]{:S(2)}) collective-permute-start(bf16[16,96]{1,0:T(8,128)(2,1)S(1)} %get-tuple-element.49), channel_id=1, source_target_pairs={{0,1},{2,3},{1,0},{3,2},{4,5},{6,7},{5,4},{7,6},{8,9},{10,11},{9,8... | collective-permute-start | bytes 9224 | tf_op jit(solution)/shard_map/ppermute | solution.py:473
  8.5 2.4 %copy-start.1 = (bf16[384,96]{0,1:T(8,128)(2,1)S(1)}, bf16[384,96]{0,1:T(8,128)(2,1)}, u32[]{:S(2)}) copy-start(bf16[384,96]{0,1:T(8,128)(2,1)} %param.17) | copy-start | bytes 221188
  8.5 2.4 %copy-start.2 = (bf16[384,96]{0,1:T(8,128)(2,1)S(1)}, bf16[384,96]{0,1:T(8,128)(2,1)}, u32[]{:S(2)}) copy-start(bf16[384,96]{0,1:T(8,128)(2,1)} %param.19) | copy-start | bytes 221188
  10.1 0.8 %copy-start.4 = (f32[96,7,7]{0,2,1:T(8,128)S(1)}, f32[96,7,7]{0,2,1:T(8,128)}, u32[]{:S(2)}) copy-start(f32[96,7,7]{0,2,1:T(8,128)} %param.13) | copy-start | bytes 56452
  10.1 5.8 %collective-permute-start.3 = (bf16[608,128]{1,0:T(8,128)(2,1)S(1)}, bf16[608,128]{1,0:T(8,128)(2,1)S(1)}, u32[]{:S(2)}, u32[]{:S(2)}) collective-permute-start(bf16[608,128]{1,0:T(8,128)(2,1)S(1)} %get-tuple-element.52), channel_id=1, source_target_pairs={{4,8},{12,16},{20,24},{8,4},{16,12},{24,20},{5,9},{13,17},{21,25},... | collective-permute-start | bytes 466952 | tf_op jit(solution)/shard_map/ppermute | solution.py:473
  10.8 0.7 %copy-start.8 = (f32[96]{0:T(128)S(1)}, f32[96]{0:T(128)}, u32[]{:S(2)}) copy-start(f32[96]{0:T(128)} %param.16) | copy-start | bytes 1156
  10.8 0.7 %copy-start.9 = (f32[96]{0:T(128)S(1)}, f32[96]{0:T(128)}, u32[]{:S(2)}) copy-start(f32[96]{0:T(128)} %param.20) | copy-start | bytes 1156
  10.8 0.7 %copy-start.5 = (f32[96]{0:T(128)S(1)}, f32[96]{0:T(128)}, u32[]{:S(2)}) copy-start(f32[96]{0:T(128)} %param.21) | copy-start | bytes 1156
  10.8 0.7 %copy-start.6 = (f32[96]{0:T(128)S(1)}, f32[96]{0:T(128)}, u32[]{:S(2)}) copy-start(f32[96]{0:T(128)} %param.14) | copy-start | bytes 1156
  10.9 0.7 %copy-start.7 = (f32[96]{0:T(128)S(1)}, f32[96]{0:T(128)}, u32[]{:S(2)}) copy-start(f32[96]{0:T(128)} %param.15) | copy-start | bytes 1156
  12.3 3.9 %collective-permute-start.2 = (bf16[608,128]{1,0:T(8,128)(2,1)S(1)}, bf16[608,128]{1,0:T(8,128)(2,1)S(1)}, u32[]{:S(2)}, u32[]{:S(2)}) collective-permute-start(bf16[608,128]{1,0:T(8,128)(2,1)S(1)} %shard_map.197), channel_id=1, source_target_pairs={{0,4},{4,0},{1,5},{5,1},{2,6},{6,2},{3,7},{7,3},{8,12},{12,8},{9,1... | collective-permute-start | bytes 466952 | tf_op jit(solution)/shard_map/ppermute | solution.py:473
  19.8 2.3 %collective-permute-start.4 = (bf16[960,128]{1,0:T(8,128)(2,1)S(1)}, bf16[960,128]{1,0:T(8,128)(2,1)S(1)}, u32[]{:S(2)}, u32[]{:S(2)}) collective-permute-start(bf16[960,128]{1,0:T(8,128)(2,1)S(1)} %get-tuple-element.59), channel_id=1, source_target_pairs={{0,4},{4,0},{1,5},{5,1},{2,6},{6,2},{3,7},{7,3},{8,12},{12,8},{9,1... | collective-permute-start | bytes 737288 | tf_op jit(solution)/shard_map/ppermute | solution.py:473
  22.2 8.2 %collective-permute-start.5 = (bf16[176,128]{1,0:T(8,128)(2,1)S(1)}, bf16[176,128]{1,0:T(8,128)(2,1)S(1)}, u32[]{:S(2)}, u32[]{:S(2)}) collective-permute-start(bf16[176,128]{1,0:T(8,128)(2,1)S(1)} %get-tuple-element.67), channel_id=1, source_target_pairs={{0,3},{1,2},{2,1},{3,0},{4,7},{5,6},{6,5},{7,4},{8,11},{9,10},{10,... | collective-permute-start | bytes 135176 | tf_op jit(solution)/shard_map/ppermute | solution.py:477
  23.6 6.8 %collective-permute-start.7 = (bf16[176,128]{1,0:T(8,128)(2,1)S(1)}, bf16[176,128]{1,0:T(8,128)(2,1)S(1)}, u32[]{:S(2)}, u32[]{:S(2)}) collective-permute-start(bf16[176,128]{1,0:T(8,128)(2,1)S(1)} %get-tuple-element.69), channel_id=1, source_target_pairs={{0,1},{1,0},{2,3},{3,2},{4,5},{5,4},{6,7},{7,6},{8,9},{9,8},{10,11... | collective-permute-start | bytes 135176 | tf_op jit(solution)/shard_map/ppermute | solution.py:477
  24.7 5.6 %collective-permute-start.6 = (bf16[160,128]{1,0:T(8,128)(2,1)S(1)}, bf16[160,128]{1,0:T(8,128)(2,1)S(1)}, u32[]{:S(2)}, u32[]{:S(2)}) collective-permute-start(bf16[160,128]{1,0:T(8,128)(2,1)S(1)} %get-tuple-element.68), channel_id=1, source_target_pairs={{0,2},{1,3},{2,0},{3,1},{4,6},{5,7},{6,4},{7,5},{8,10},{9,11},{10,... | collective-permute-start | bytes 122888 | tf_op jit(solution)/shard_map/ppermute | solution.py:477
  26.6 8.1 %collective-permute-start.11 = (bf16[3,96,256]{2,1,0:T(8,128)(2,1)S(1)}, bf16[3,96,256]{2,1,0:T(8,128)(2,1)S(1)}, u32[]{:S(2)}, u32[]{:S(2)}) collective-permute-start(bf16[3,96,256]{2,1,0:T(8,128)(2,1)S(1)} %get-tuple-element.73), channel_id=1, source_target_pairs={{4,8},{12,16},{20,24},{8,4},{16,12},{24,20},{5,9},{13,17},{21,25},... | collective-permute-start | bytes 442376 | tf_op jit(solution)/shard_map/ppermute | solution.py:473
  30.4 8.2 %collective-permute-start.10 = (bf16[192,128]{1,0:T(8,128)(2,1)S(1)}, bf16[192,128]{1,0:T(8,128)(2,1)S(1)}, u32[]{:S(2)}, u32[]{:S(2)}) collective-permute-start(bf16[192,128]{1,0:T(8,128)(2,1)S(1)} %get-tuple-element.72.refs_3_), channel_id=1, source_target_pairs={{0,8},{8,0},{16,24},{24,16},{1,9},{9,1},{17,25},{25,17},{2,10},{10... | collective-permute-start | bytes 147464 | tf_op jit(solution)/shard_map/ppermute | solution.py:477
  31.9 6.6 %collective-permute-start.9 = (bf16[192,128]{1,0:T(8,128)(2,1)S(1)}, bf16[192,128]{1,0:T(8,128)(2,1)S(1)}, u32[]{:S(2)}, u32[]{:S(2)}) collective-permute-start(bf16[192,128]{1,0:T(8,128)(2,1)S(1)} %get-tuple-element.72.refs_3_), channel_id=1, source_target_pairs={{0,24},{8,16},{16,8},{24,0},{1,25},{9,17},{17,9},{25,1},{2,26},{10... | collective-permute-start | bytes 147464 | tf_op jit(solution)/shard_map/ppermute | solution.py:477
  34.6 4.0 %collective-permute-start.8 = (bf16[160,128]{1,0:T(8,128)(2,1)S(1)}, bf16[160,128]{1,0:T(8,128)(2,1)S(1)}, u32[]{:S(2)}, u32[]{:S(2)}) collective-permute-start(bf16[160,128]{1,0:T(8,128)(2,1)S(1)} %get-tuple-element.71), channel_id=1, source_target_pairs={{0,16},{8,24},{16,0},{24,8},{1,17},{9,25},{17,1},{25,9},{2,18},{10... | collective-permute-start | bytes 122888 | tf_op jit(solution)/shard_map/ppermute | solution.py:477
  34.7 3.9 %copy-start = (bf16[4,96,256]{2,0,1:T(4,128)(2,1)}, bf16[4,96,256]{2,0,1:T(4,128)(2,1)S(1)}, u32[]{:S(2)}) copy-start(bf16[4,96,256]{2,0,1:T(4,128)(2,1)S(1)} %copy.26) | copy-start | bytes 589828
  38.6 1.4 %collective-permute-start.12 = (f32[224,128]{1,0:T(8,128)S(1)}, f32[224,128]{1,0:T(8,128)S(1)}, u32[]{:S(2)}, u32[]{:S(2)}) collective-permute-start(f32[224,128]{1,0:T(8,128)S(1)} %shard_map.203.refs_5_.refs_0_), channel_id=1, source_target_pairs={{0,4},{4,0},{1,5},{5,1},{2,6},{6,2},{3,7},{7,3},{8,12},{12,8},{9,1... | collective-permute-start | bytes 344072 | tf_op jit(solution)/shard_map/ppermute | solution.py:473
